TPU v7x, 512 devices: a whole 4x4x16 slice. The times are simulated.
512 devices in a mesh: ctx: 64 (over z_lo, y, core), ch: 8 (over x, z_hi).
Axes of the slice: x: 4, y: 4, z: 16 (z_hi: 2, z_lo: 8; z = z_hi * 8 + z_lo), core: 2. Of those that a mesh axis runs over, the one named last changes fastest.
Arguments:
- gate_input: bfloat16 [16384, 4096], P('ctx', 'ch'), may hold values from -6 to 6
- key_input: bfloat16 [16384, 4096], P('ctx', 'ch'), may hold values from -6 to 6
- value_input: bfloat16 [16384, 4096], P('ctx', 'ch'), may hold values from -6 to 6
- out_grad: bfloat16 [16384, 4096], P(('ctx', 'ch')), may hold values from -6 to 6
- filter_taps: bfloat16 [768, 4096], P(None, 'ch'), may hold values from -6 to 6
Outputs:
- gate_grad: bfloat16 [16384, 4096], P('ctx', 'ch')
- key_grad: bfloat16 [16384, 4096], P('ctx', 'ch')
- value_grad: bfloat16 [16384, 4096], P('ctx', 'ch')
- filter_grad: float32 [768, 4096], P('ctx', 'ch')
All inputs are finite; a program needn't handle non-finite values.
Results may differ from a plain program's by a relative error of at most 0.012.
Values may be sent and summed in bfloat16 or wider, within the bound.
No kernel may reach another device: no remote copies, remote signals or barrier semaphores. Data moves between devices by JAX's collectives and lax.ppermute only.
A program may use at most 64 MiB of HBM per device.

v0:
```python
import math

import jax
import jax.numpy as jnp
from jax import lax
from jax.sharding import PartitionSpec as P

REACH = 3


def shifted(value, axis, steps):
    count = lax.axis_size(axis)
    leading, last = (max(0, -steps), min(count, count - steps))
    return lax.ppermute(value, axis, [(source, source + steps) for source in range(leading, last)])


def make_tables(span):
    period = 2 * span
    bins = span + 1
    freq = lax.broadcasted_iota(jnp.int32, (bins, period), 0)
    place = lax.broadcasted_iota(jnp.int32, (bins, period), 1)
    angle = 2.0 * math.pi / period * (freq * place % period).astype(jnp.float32)
    cos_table = jnp.cos(angle)
    sin_table = -jnp.sin(angle)
    cos_high = cos_table.astype(jnp.bfloat16)
    cos_low = (cos_table - cos_high.astype(jnp.float32)).astype(jnp.bfloat16)
    sin_high = sin_table.astype(jnp.bfloat16)
    sin_low = (sin_table - sin_high.astype(jnp.float32)).astype(jnp.bfloat16)
    weight = jnp.where((freq == 0) | (freq == span), 1.0, 2.0) / period
    inv_cos = (cos_table * weight).T
    inv_sin = (sin_table * weight).T
    return ((cos_high, cos_low), (sin_high, sin_low), inv_cos, inv_sin)


def split_product(table_pair, panels):
    rows = panels.shape[1]
    high_part = jnp.einsum(
        "kj,njc->nkc", table_pair[0][:, :rows], panels, preferred_element_type=jnp.float32
    )
    low_part = jnp.einsum(
        "kj,njc->nkc", table_pair[1][:, :rows], panels, preferred_element_type=jnp.float32
    )
    return high_part + low_part


def spectra(panels, cos_pair, sin_pair):
    return (split_product(cos_pair, panels), split_product(sin_pair, panels))


def inverse_rows(real_part, imag_part, inv_cos, inv_sin, rows):
    first = jnp.einsum("jk,nkc->njc", inv_cos[:rows], real_part, precision=lax.Precision.HIGH)
    second = jnp.einsum("jk,nkc->njc", inv_sin[:rows], imag_part, precision=lax.Precision.HIGH)
    return first + second


def body(gate_input, key_input, value_input, out_grad, filter_taps):
    span = gate_input.shape[0]
    width = gate_input.shape[1]
    lags = filter_taps.shape[0]
    period = 2 * span
    cotangent = lax.all_to_all(out_grad, "ch", split_axis=1, concat_axis=0, tiled=True)
    mixed_in = (key_input.astype(jnp.float32) * value_input.astype(jnp.float32)).astype(
        jnp.bfloat16
    )
    grad_conv = (cotangent.astype(jnp.float32) * gate_input.astype(jnp.float32)).astype(
        jnp.bfloat16
    )
    earlier = [mixed_in]
    later = [grad_conv]
    for offset in range(1, REACH + 1):
        earlier.append(shifted(mixed_in, "ctx", offset))
        later.append(shifted(grad_conv, "ctx", -offset))
    cos_pair, sin_pair, inv_cos, inv_sin = make_tables(span)
    scale = 1.0 / lags**0.5
    padded = jnp.pad(filter_taps, ((span, span), (0, 0)))
    blank = jnp.zeros((1, width), jnp.bfloat16)
    columns = jnp.stack(
        [
            jnp.concatenate(
                [
                    padded[block * span + span : block * span + 2 * span],
                    blank,
                    padded[block * span + 1 : block * span + span],
                ],
                axis=0,
            )
            for block in range(REACH + 1)
        ]
    )
    filt_re, filt_im = spectra(columns, cos_pair, sin_pair)
    filt_re = filt_re * scale
    filt_im = filt_im * scale
    mixed_re, mixed_im = spectra(jnp.stack(earlier), cos_pair, sin_pair)
    grad_re, grad_im = spectra(jnp.stack(later), cos_pair, sin_pair)
    conv_re = jnp.sum(filt_re * mixed_re - filt_im * mixed_im, axis=0, keepdims=True)
    conv_im = jnp.sum(filt_re * mixed_im + filt_im * mixed_re, axis=0, keepdims=True)
    conv_out = inverse_rows(conv_re, conv_im, inv_cos, inv_sin, span)[0]
    gate_grad = (cotangent.astype(jnp.float32) * conv_out).astype(jnp.bfloat16)
    back_re = jnp.sum(filt_re * grad_re + filt_im * grad_im, axis=0, keepdims=True)
    back_im = jnp.sum(filt_re * grad_im - filt_im * grad_re, axis=0, keepdims=True)
    grad_mixed = inverse_rows(back_re, back_im, inv_cos, inv_sin, span)[0]
    key_grad = (grad_mixed * value_input.astype(jnp.float32)).astype(jnp.bfloat16)
    value_grad = (grad_mixed * key_input.astype(jnp.float32)).astype(jnp.bfloat16)
    cross_re = grad_re * mixed_re[0] + grad_im * mixed_im[0]
    cross_im = grad_im * mixed_re[0] - grad_re * mixed_im[0]
    lag_terms = inverse_rows(cross_re, cross_im, inv_cos, inv_sin, period)
    local_grad = (lag_terms[:REACH, :span] + lag_terms[1:, span:]).reshape(lags, width) * scale
    share = lags // lax.axis_size("ctx")
    summed = lax.psum(local_grad, "ctx")
    filter_grad = lax.dynamic_slice_in_dim(summed, lax.axis_index("ctx") * share, share, 0)
    return (gate_grad, key_grad, value_grad, filter_grad)


def solution(mesh):
    return jax.shard_map(
        body,
        mesh=mesh,
        in_specs=(
            P("ctx", "ch"),
            P("ctx", "ch"),
            P("ctx", "ch"),
            P(("ctx", "ch"), None),
            P(None, "ch"),
        ),
        out_specs=(P("ctx", "ch"), P("ctx", "ch"), P("ctx", "ch"), P("ctx", "ch")),
        check_vma=False,
    )
```

profile of v0, /device:TPU:1, one launch (start us, length us, event | category | flops | bytes accessed | tf_op | source)
XLA Modules:
  0.0 952.4 jit_solution(9133178679255346400)
XLA Ops:
  7.2 1.2 fusion.42
  8.3 4.6 collective-permute-start
  12.9 3.2 collective-permute-start.1
  16.2 3.5 collective-permute-start.2
  19.7 1.7 copy.36
  21.4 17.3 %all-to-all-start = ((bf16[32,8,512]{2,0,1:T(8,128)(2,1)}), bf16[32,8,512]{2,0,1:T(8,128)(2,1)S(1)}, u32[]{:S(2)}, u32[]{:S(2)}) async-start(bf16[32,8,512]{2,0,1:T(8,128)(2,1)} %bitcast.151), calls=%async_computation | async-start | bytes 524288 | tf_op jit(solution)/shard_map/all_to_all | solution.py:61
  38.8 0.2 fusion.95
  39.2 0.4 maximum_bitcast_fusion
  39.6 2.7 fusion.51
  42.3 2.8 fusion.48
  45.1 2.2 subtract_convert_fusion.1
  47.3 2.0 fusion.58
  49.4 4.1 add_multiply_fusion.1
  53.5 4.1 add_multiply_fusion
  57.6 2.1 subtract_convert_fusion
  59.7 2.1 fusion.44
  61.8 0.5 fusion.68
  62.6 0.5 fusion.66
  63.1 1.6 add_bitcast_fusion.1
  64.8 1.9 add_bitcast_fusion.2
  66.7 1.1 multiply_convert_fusion
  67.8 2.0 collective-permute-start.3
  69.8 1.3 collective-permute-start.4
  71.1 1.7 collective-permute-start.5
  72.8 1.1 slice_bitcast_fusion
  73.9 2.9 collective-permute-done.3
  76.8 4.7 collective-permute-done.4
  81.6 0.5 fusion.65
  82.1 0.4 copy-done.15
  82.5 0.5 fusion.67
  83.1 0.6 convolution_add_fusion.1
  83.6 0.5 copy-done.3
  84.1 0.8 copy-done
  84.9 0.7 copy-done.2
  85.6 3.1 fusion.3
  88.7 6.2 fusion.5
  94.9 6.9 add_bitcast_fusion
  101.8 1.5 fusion.16
  103.3 0.4 fusion.27
  103.8 0.2 copy.28
  104.0 0.4 copy-done.6
  104.4 2.0 fusion.45
  106.3 2.0 fusion.20
  108.3 0.8 copy.31
  109.2 1.8 fusion.46
  111.0 3.6 fusion.41
  114.6 829.4 %all-reduce.2.cloned.1.call-done = f32[768,512]{1,0:T(8,128)} async-done(((f32[768,512]{1,0:T(8,128)}), f32[768,512]{1,0:T(8,128)}) %all-reduce.2.cloned.1.call-update) | async-done | bytes 1572880 | tf_op jit(solution)/shard_map/psum | solution.py:109
  944.0 1.4 constant_dynamic-slice_fusion
  (43 shorter events, 0.7 us)
Async XLA Ops:
  7.2 31.5 %copy-start.1 = (bf16[768,512]{1,0:T(8,128)(2,1)S(1)}, bf16[768,512]{1,0:T(8,128)(2,1)}, u32[]{:S(2)}) copy-start(bf16[768,512]{1,0:T(8,128)(2,1)} %param.9) | copy-start | bytes 2359300
  8.3 53.4 %collective-permute-start = (bf16[256,512]{1,0:T(8,128)(2,1)S(1)}, bf16[256,512]{1,0:T(8,128)(2,1)S(1)}, u32[]{:S(2)}, u32[]{:S(2)}) collective-permute-start(bf16[256,512]{1,0:T(8,128)(2,1)S(1)} %fusion.42), channel_id=1, source_target_pairs={{0,8},{8,16},{16,24},{24,32},{32,40},{40,48},{48,56},{56,64},{64,7... | collective-permute-start | bytes 786440 | tf_op jit(solution)/shard_map/ppermute | solution.py:14
  12.9 48.8 %collective-permute-start.1 = (bf16[256,512]{1,0:T(8,128)(2,1)S(1)}, bf16[256,512]{1,0:T(8,128)(2,1)S(1)}, u32[]{:S(2)}, u32[]{:S(2)}) collective-permute-start(bf16[256,512]{1,0:T(8,128)(2,1)S(1)} %fusion.42), channel_id=1, source_target_pairs={{0,16},{8,24},{16,32},{24,40},{32,48},{40,56},{48,64},{56,72},{64,... | collective-permute-start | bytes 786440 | tf_op jit(solution)/shard_map/ppermute | solution.py:14
  16.2 45.6 %collective-permute-start.2 = (bf16[256,512]{1,0:T(8,128)(2,1)S(1)}, bf16[256,512]{1,0:T(8,128)(2,1)S(1)}, u32[]{:S(2)}, u32[]{:S(2)}) collective-permute-start(bf16[256,512]{1,0:T(8,128)(2,1)S(1)} %fusion.42), channel_id=1, source_target_pairs={{0,24},{8,32},{16,40},{24,48},{32,56},{40,64},{48,72},{56,80},{64,... | collective-permute-start | bytes 786440 | tf_op jit(solution)/shard_map/ppermute | solution.py:14
  21.4 45.4 %all-to-all-start = ((bf16[32,8,512]{2,0,1:T(8,128)(2,1)}), bf16[32,8,512]{2,0,1:T(8,128)(2,1)S(1)}, u32[]{:S(2)}, u32[]{:S(2)}) async-start(bf16[32,8,512]{2,0,1:T(8,128)(2,1)} %bitcast.151), calls=%async_computation | async-start | bytes 524288 | tf_op jit(solution)/shard_map/all_to_all | solution.py:61
  38.7 905.3 %all-reduce.2.cloned.1.call-start = ((), (), s32[]{:S(2)}) async-start(), calls=%async_computation.1 | async-start | bytes 3145728 | tf_op jit(solution)/shard_map/psum | solution.py:109
  47.3 15.0 %copy-start.12 = (bf16[257,512]{1,0:T(8,128)(2,1)}, bf16[257,512]{1,0:T(8,128)(2,1)S(1)}, u32[]{:S(2)}) copy-start(bf16[257,512]{1,0:T(8,128)(2,1)S(1)} %subtract_convert_fusion.1) | copy-start | bytes 789508
  59.7 2.7 copy-start.14
  61.8 0.7 copy-start.7
  61.8 0.8 copy-start.9
  63.1 1.7 copy-start.8
  63.1 1.7 copy-start.10
  66.7 14.8 %copy-start.13 = (bf16[257,512]{1,0:T(8,128)(2,1)S(1)}, bf16[257,512]{1,0:T(8,128)(2,1)}, u32[]{:S(2)}) copy-start(bf16[257,512]{1,0:T(8,128)(2,1)} %copy-done.12) | copy-start | bytes 789508
  67.8 9.0 collective-permute-start.3
  69.8 11.8 %collective-permute-start.4 = (bf16[256,512]{1,0:T(8,128)(2,1)S(1)}, bf16[256,512]{1,0:T(8,128)(2,1)S(1)}, u32[]{:S(2)}, u32[]{:S(2)}) collective-permute-start(bf16[256,512]{1,0:T(8,128)(2,1)S(1)} %multiply_convert_fusion), channel_id=1, source_target_pairs={{16,0},{24,8},{32,16},{40,24},{48,32},{56,40},{64,48},{72,56},{80,... | collective-permute-start | bytes 786440 | tf_op jit(solution)/shard_map/ppermute | solution.py:14
  71.1 10.5 %collective-permute-start.5 = (bf16[256,512]{1,0:T(8,128)(2,1)S(1)}, bf16[256,512]{1,0:T(8,128)(2,1)S(1)}, u32[]{:S(2)}, u32[]{:S(2)}) collective-permute-start(bf16[256,512]{1,0:T(8,128)(2,1)S(1)} %multiply_convert_fusion), channel_id=1, source_target_pairs={{24,0},{32,8},{40,16},{48,24},{56,32},{64,40},{72,48},{80,56},{88,... | collective-permute-start | bytes 786440 | tf_op jit(solution)/shard_map/ppermute | solution.py:14
  81.6 1.0 copy-start.15
  82.5 1.6 copy-start.3
  83.0 1.9 copy-start
  83.0 2.5 copy-start.2
  103.3 1.0 copy-start.6
  104.0 5.2 copy-start.5
  106.3 4.7 copy-start.4
  106.3 4.7 copy-start.11
Sparse Core Ops, SparseCore 0:
  103.5 840.4 all-reduce.1
where the time goes:
time: 959 us; the launch traced here: 952 us
  waiting for transfers between devices  837 us (87%)
  matrix products  45.5 us (5%)
  starting transfers between devices  33.6 us (4%)
  between operations  14.7 us (2%)
  other arithmetic  13.1 us (1%)
    psum x1, waiting for transfers between devices, body(): summed = lax.psum(local_grad, 'ctx')  829 us
  transfers between devices with their start and end apart: 8, of which 3 were waited for; matrix products, arithmetic and copies ran while one was open for 4% of the time, Pallas kernels for 0%

commit v1 on v0

v1 whole, which is shorter than its diff:
```python
import functools
import math

import jax
import jax.numpy as jnp
import ml_dtypes
import numpy as np
from jax import lax
from jax.experimental import pallas as pl
from jax.experimental.pallas import tpu as pltpu
from jax.sharding import Mesh, PartitionSpec as P

BF16 = jnp.bfloat16
F32 = jnp.float32
AXES = ("z", "yh", "yl", "c", "x", "zh")
SIZES = (8, 2, 2, 2, 4, 2)
CTX = ("z", "yh", "yl", "c")
GROUP = ("yl", "c")
RUNS = ("z", "yh")
CH = ("x", "zh")

BLOCK = 256
PERIOD = 1024
LANES = 128
BLOCKS = 4
BINS = 128
STEPS = PERIOD // 2 // BINS
ROWS = 2 * BINS


def make_tables():
    freq = np.arange(PERIOD // 2)[:, None]
    place = np.arange(PERIOD)[None, :]
    angle = math.pi / PERIOD * ((2 * freq + 1) * place % (2 * PERIOD)).astype(np.float64)
    both = np.stack([np.cos(angle), -np.sin(angle)])
    both = both.reshape(2, STEPS, BINS, PERIOD).transpose(1, 0, 2, 3).reshape(PERIOD, PERIOD)
    return both.astype(ml_dtypes.bfloat16), np.ascontiguousarray(both.T).astype(ml_dtypes.bfloat16)


def dot(a, b):
    return jnp.dot(a, b, preferred_element_type=F32)


def spread(part):
    return jnp.concatenate([part] * BLOCKS, axis=1)


def fill_windows(windows, source):
    for block in range(BLOCKS):
        windows[:, block * LANES : (block + 1) * LANES] = source[
            block * BLOCK : block * BLOCK + PERIOD, :
        ]


def conv_kernel(scale, forward, inverse, mixed, taps, conv, spectrum, response, windows, total):
    step = pl.program_id(0)

    @pl.when(step == 0)
    def _():
        fill_windows(windows, mixed)

    resp = dot(forward[:, : taps.shape[0]], taps[...])
    response[...] = resp
    spec = dot(forward[...], windows[...])
    spectrum[...] = spec
    f_re, f_im = spread(resp[:BINS]), spread(resp[BINS:])
    x_re, x_im = spec[:BINS], spec[BINS:]
    y = jnp.concatenate([f_re * x_re - f_im * x_im, f_re * x_im + f_im * x_re]).astype(BF16)
    part = dot(inverse[...], y)

    @pl.when(step == 0)
    def _():
        total[...] = part

    @pl.when(step > 0)
    def _():
        total[...] += part

    @pl.when(step == STEPS - 1)
    def _():
        for block in range(BLOCKS):
            conv[block * BLOCK : (block + 1) * BLOCK, :] = (
                total[:, block * LANES : (block + 1) * LANES] * scale
            )


def cross_kernel(scale, forward, inverse, grad, spectrum, lag_grad, windows, total):
    step = pl.program_id(0)

    @pl.when(step == 0)
    def _():
        for block in range(BLOCKS):
            windows[:, block * LANES : (block + 1) * LANES] = grad[
                block * BLOCK : (block + 1) * BLOCK, :
            ]

    spec = dot(forward[...], windows[...])
    g_re, g_im = spec[:BINS], spec[BINS:]
    x_re, x_im = spectrum[:BINS], spectrum[BINS:]
    re = g_re * x_re + g_im * x_im
    im = g_im * x_re - g_re * x_im
    re = sum(re[:, b * LANES : (b + 1) * LANES] for b in range(BLOCKS))
    im = sum(im[:, b * LANES : (b + 1) * LANES] for b in range(BLOCKS))
    part = dot(inverse[...], jnp.concatenate([re, im]).astype(BF16))

    @pl.when(step == 0)
    def _():
        total[...] = part

    @pl.when(step > 0)
    def _():
        total[...] += part

    @pl.when(step == STEPS - 1)
    def _():
        lag_grad[...] = (total[...] * scale).astype(BF16)


def back_kernel(scale, forward, inverse, grad, response, back, windows, total):
    step = pl.program_id(0)

    @pl.when(step == 0)
    def _():
        fill_windows(windows, grad)

    spec = dot(forward[...], windows[...])
    f_re, f_im = spread(response[:BINS]), spread(response[BINS:])
    g_re, g_im = spec[:BINS], spec[BINS:]
    y = jnp.concatenate([f_re * g_re + f_im * g_im, f_re * g_im - f_im * g_re]).astype(BF16)
    part = dot(inverse[...], y)

    @pl.when(step == 0)
    def _():
        total[...] = part

    @pl.when(step > 0)
    def _():
        total[...] += part

    @pl.when(step == STEPS - 1)
    def _():
        for block in range(BLOCKS):
            back[block * BLOCK : (block + 1) * BLOCK, :] = (
                total[:, block * LANES : (block + 1) * LANES] * scale
            ).astype(BF16)


def whole(shape):
    return pl.BlockSpec(shape, lambda step: (0,) * len(shape))


def call(kernel, in_specs, out_specs, out_shape, scratch, macs, moved):
    return pl.pallas_call(
        kernel,
        grid=(STEPS,),
        in_specs=in_specs,
        out_specs=out_specs,
        out_shape=out_shape,
        scratch_shapes=scratch,
        compiler_params=pltpu.CompilerParams(
            dimension_semantics=("arbitrary",), vmem_limit_bytes=24 * 1024 * 1024
        ),
        cost_estimate=pl.CostEstimate(flops=2 * macs, bytes_accessed=moved, transcendentals=0),
    )


def shift(value, steps):
    count = lax.axis_size(RUNS)
    first, last = max(0, -steps), min(count, count - steps)
    return lax.ppermute(value, RUNS, [(i, i + steps) for i in range(first, last)])


def exchange(value, axes):
    return lax.all_to_all(value, axes, split_axis=0, concat_axis=0, tiled=True)


def body(forward, inverse, gate_input, key_input, value_input, out_grad, filter_taps):
    lags = filter_taps.shape[0]
    tokens = BLOCKS * BLOCK
    wide = BLOCKS * LANES
    norm = 2.0 / PERIOD / lags**0.5
    held = out_grad.shape[0]
    pieces = out_grad.reshape(held, -1, BLOCKS, LANES).transpose(2, 1, 0, 3)
    cotangent = exchange(pieces.reshape(-1, held, LANES), GROUP + CH).reshape(tokens, LANES)
    by_quarter = lambda a: a.reshape(BLOCK, BLOCKS, LANES).transpose(1, 0, 2)
    mixed = (key_input.astype(F32) * value_input.astype(F32)).astype(BF16)
    mixed = exchange(by_quarter(mixed), GROUP).reshape(tokens, LANES)
    gate = exchange(by_quarter(gate_input), GROUP).reshape(tokens, LANES)
    mixed_window = jnp.concatenate([shift(mixed[tokens - lags :], 1), mixed])
    quarter = lax.axis_index(GROUP)
    taps = lax.dynamic_slice_in_dim(filter_taps, quarter * LANES, LANES, 1)

    conv, spectrum, response = call(
        functools.partial(conv_kernel, norm),
        [
            pl.BlockSpec((ROWS, PERIOD), lambda step: (step, 0)),
            pl.BlockSpec((BLOCK, ROWS), lambda step: (lags // BLOCK, step)),
            whole((tokens + lags, LANES)),
            whole((lags, LANES)),
        ],
        [
            whole((tokens, LANES)),
            pl.BlockSpec((ROWS, wide), lambda step: (step, 0)),
            pl.BlockSpec((ROWS, LANES), lambda step: (step, 0)),
        ],
        [
            jax.ShapeDtypeStruct((tokens, LANES), F32),
            jax.ShapeDtypeStruct((PERIOD, wide), F32),
            jax.ShapeDtypeStruct((PERIOD, LANES), F32),
        ],
        [pltpu.VMEM((PERIOD, wide), BF16), pltpu.VMEM((BLOCK, wide), F32)],
        PERIOD * (PERIOD * wide + lags * LANES + BLOCK * wide),
        6_000_000,
    )(forward, inverse, mixed_window, taps)

    grad = (cotangent.astype(F32) * gate.astype(F32)).astype(BF16)
    grad_window = jnp.concatenate([grad, shift(grad[:lags], -1)])

    lag_grad = call(
        functools.partial(cross_kernel, norm),
        [
            pl.BlockSpec((ROWS, BLOCK), lambda step: (step, lags // BLOCK)),
            pl.BlockSpec((lags, ROWS), lambda step: (0, step)),
            whole((tokens, LANES)),
            pl.BlockSpec((ROWS, wide), lambda step: (step, 0)),
        ],
        whole((lags, LANES)),
        jax.ShapeDtypeStruct((lags, LANES), BF16),
        [pltpu.VMEM((BLOCK, wide), BF16), pltpu.VMEM((lags, LANES), F32)],
        PERIOD * (BLOCK * wide + lags * LANES),
        4_000_000,
    )(forward, inverse, grad, spectrum)
    share = lags // lax.axis_size(CTX)
    parts = exchange(lag_grad.reshape(-1, share, LANES), CTX)
    filter_grad = parts.reshape(-1, BLOCKS, share, LANES).astype(F32).sum(0)
    filter_grad = filter_grad.transpose(1, 0, 2).reshape(share, wide)

    back = call(
        functools.partial(back_kernel, norm),
        [
            pl.BlockSpec((ROWS, PERIOD), lambda step: (step, 0)),
            pl.BlockSpec((BLOCK, ROWS), lambda step: (0, step)),
            whole((tokens + lags, LANES)),
            pl.BlockSpec((ROWS, LANES), lambda step: (step, 0)),
        ],
        whole((tokens, LANES)),
        jax.ShapeDtypeStruct((tokens, LANES), BF16),
        [pltpu.VMEM((PERIOD, wide), BF16), pltpu.VMEM((BLOCK, wide), F32)],
        PERIOD * (PERIOD * wide + BLOCK * wide),
        4_000_000,
    )(forward, inverse, grad_window, response)

    gate_part = (cotangent.astype(F32) * conv).astype(BF16)
    by_token = lambda a: (
        exchange(a.reshape(BLOCKS, BLOCK, LANES), GROUP).transpose(1, 0, 2).reshape(BLOCK, wide)
    )
    gate_grad = by_token(gate_part)
    grad_mixed = by_token(back).astype(F32)
    key_grad = (grad_mixed * value_input.astype(F32)).astype(BF16)
    value_grad = (grad_mixed * key_input.astype(F32)).astype(BF16)
    return gate_grad, key_grad, value_grad, filter_grad


def solution(mesh):
    split = Mesh(mesh.devices.reshape(SIZES), AXES)
    spans = P(CTX, CH)
    mapped = jax.shard_map(
        body,
        mesh=split,
        in_specs=(P(), P(), spans, spans, spans, P(CTX + CH, None), P(None, CH)),
        out_specs=(spans, spans, spans, spans),
        check_vma=False,
    )
    forward, inverse = make_tables()

    def run(gate_input, key_input, value_input, out_grad, filter_taps):
        return mapped(
            forward, inverse, gate_input, key_input, value_input, out_grad, filter_taps
        )

    return run
```

time: 959 us -> 132 us (0.14)
  waiting for transfers between devices: 837 us -> 31.7 us
  matrix products: 45.5 us -> 0 us
  starting transfers between devices: 33.6 us -> 62 us
  between operations: 14.7 us -> 0.76 us
  local copies, waits for them, and re-layouts: 8.56 us -> 18.6 us
  Pallas kernels: 0 us -> 10 us
    psum x1 -> x0, waiting for transfers between devices: 829 us -> none  [body(): summed = lax.psum(local_grad, 'ctx')]
    dot_general x18 -> x0, matrix products: 45.5 us -> none  [the longest x6 12.8 us: split_product(): jnp.einsum('kj,njc->nkc', table_pair[0][:, :rows], panels, preferred_elem...]
    all_to_all x1 -> x6, starting transfers between devices: 17.3 us -> 55.2 us  [exchange(): return lax.all_to_all(value, axes, split_axis=0, concat_axis=0, tiled=True)]
    all_to_all x1 -> x6, waiting for transfers between devices: 0.01 us -> 22.8 us  [exchange(): return lax.all_to_all(value, axes, split_axis=0, concat_axis=0, tiled=True)]
    pallas_call x0 -> x3, Pallas kernels: none -> 10 us  [the longest x1 3.85 us: body(): call(functools.partial(back_kernel, norm), [pl.BlockSpec((ROWS, PERIOD),...]
  transfers between devices with their start and end apart: 8 -> 8, of which waited for: 3 -> 5; matrix products, arithmetic and copies ran while one was open for 4% -> 8% of each run, Pallas kernels for 0% -> 8%
where the time goes in v1:
time: 132 us; the launch traced here: 131 us
  starting transfers between devices  62 us (47%)
  waiting for transfers between devices  31.7 us (24%)
  local copies, waits for them, and re-layouts  18.6 us (14%)
  Pallas kernels  10 us (8%)
  other arithmetic  7.78 us (6%)
    all_to_all x6, starting transfers between devices, exchange(): return lax.all_to_all(value, axes, split_axis=0, concat_axis=0, tiled=True)  55.2 us
    all_to_all x6, waiting for transfers between devices, exchange(): return lax.all_to_all(value, axes, split_axis=0, concat_axis=0, tiled=True)  22.8 us
    unnamed x24, local copies, waits for them, and re-layouts  10.9 us
    ppermute x2, waiting for transfers between devices, shift(): lax.ppermute(value, RUNS, [(i, i + steps) for i in range(first, last)])  8.81 us
    ppermute x2, starting transfers between devices, shift(): lax.ppermute(value, RUNS, [(i, i + steps) for i in range(first, last)])  6.77 us
    pallas_call x1, Pallas kernels, body(): call(functools.partial(back_kernel, norm), [pl.BlockSpec((ROWS, PERIOD),...  3.85 us
    pallas_call x1, Pallas kernels, body(): call(functools.partial(conv_kernel, norm), [pl.BlockSpec((ROWS, PERIOD),...  3.59 us
  transfers between devices with their start and end apart: 8, of which 5 were waited for; matrix products, arithmetic and copies ran while one was open for 8% of the time, Pallas kernels for 8%

profile of v1, /device:TPU:1, one launch (start us, length us, event | category | flops | bytes accessed | tf_op | source)
XLA Modules:
  0.0 130.7 jit_solution(2662697767745330952)
XLA Ops:
  0.6 0.0 copy-start
  0.6 1.9 %bitcast_bitcast_fusion.1 = bf16[4,256,128]{2,1,0:T(8,128)(2,1)} fusion(bf16[256,512]{1,0:T(8,128)(2,1)} %param.9, bf16[256,512]{1,0:T(8,128)(2,1)} %param.8), kind=kLoop, calls=%fused_computation.17 | loop fusion | flops 524288 | bytes 786432 | tf_op jit(solution)/shard_map/transpose | solution.py:185
  2.5 10.3 %all-to-all-start.1 = ((bf16[4,256,128]{2,1,0:T(8,128)(2,1)}), bf16[4,256,128]{2,1,0:T(8,128)(2,1)S(1)}, u32[]{:S(2)}, u32[]{:S(2)}) async-start(bf16[4,256,128]{2,1,0:T(8,128)(2,1)} %bitcast_bitcast_fusion.1), calls=%async_computation.1 | async-start | bytes 524288 | tf_op jit(solution)/shard_map/all_to_all | solution.py:174
  12.8 1.8 %bitcast_bitcast_fusion = bf16[4,256,128]{2,1,0:T(8,128)(2,1)} fusion(bf16[256,512]{1,0:T(8,128)(2,1)} %param.7), kind=kLoop, calls=%fused_computation.16 | loop fusion | bytes 524288 | tf_op jit(solution)/shard_map/transpose | solution.py:185
  14.6 3.3 %all-to-all-done.1 = bf16[4,256,128]{2,1,0:T(8,128)(2,1)S(1)} async-done(((bf16[4,256,128]{2,1,0:T(8,128)(2,1)}), bf16[4,256,128]{2,1,0:T(8,128)(2,1)S(1)}, u32[]{:S(2)}, u32[]{:S(2)}) %all-to-all-start.1) | async-done | bytes 262176 | tf_op jit(solution)/shard_map/all_to_all | solution.py:174
  17.9 4.9 %all-to-all-start.3 = ((bf16[4,256,128]{2,1,0:T(8,128)(2,1)}), bf16[4,256,128]{2,1,0:T(8,128)(2,1)}, u32[]{:S(2)}, u32[]{:S(2)}) async-start(bf16[4,256,128]{2,1,0:T(8,128)(2,1)} %bitcast_bitcast_fusion), calls=%async_computation.3 | async-start | bytes 524288 | tf_op jit(solution)/shard_map/all_to_all | solution.py:174
  22.8 1.1 reshape.51
  23.9 0.8 copy.26
  24.7 3.4 %all-to-all-done.3 = bf16[4,256,128]{2,1,0:T(8,128)(2,1)} async-done(((bf16[4,256,128]{2,1,0:T(8,128)(2,1)}), bf16[4,256,128]{2,1,0:T(8,128)(2,1)}, u32[]{:S(2)}, u32[]{:S(2)}) %all-to-all-start.3) | async-done | bytes 262176 | tf_op jit(solution)/shard_map/all_to_all | solution.py:174
  28.1 13.2 %all-to-all-start = ((bf16[32,32,128]{2,1,0:T(8,128)(2,1)}), bf16[32,32,128]{2,1,0:T(8,128)(2,1)S(1)}, u32[]{:S(2)}, u32[]{:S(2)}) async-start(bf16[32,32,128]{2,1,0:T(8,128)(2,1)} %bitcast.1), calls=%async_computation | async-start | bytes 524288 | tf_op jit(solution)/shard_map/all_to_all | solution.py:174
  41.3 0.7 slice.12
  42.0 5.5 %collective-permute-start = (bf16[768,128]{1,0:T(8,128)(2,1)}, bf16[768,128]{1,0:T(8,128)(2,1)}, u32[]{:S(2)}, u32[]{:S(2)}) collective-permute-start(bf16[768,128]{1,0:T(8,128)(2,1)} %bitcast.4), channel_id=1, source_target_pairs={{0,32},{32,64},{64,96},{96,128},{128,160},{160,192},{192,224},{224... | collective-permute-start | bytes 589832 | tf_op jit(solution)/shard_map/ppermute | solution.py:170
  47.5 0.0 copy-done
  47.5 3.7 %collective-permute-done = bf16[768,128]{1,0:T(8,128)(2,1)} collective-permute-done((bf16[768,128]{1,0:T(8,128)(2,1)}, bf16[768,128]{1,0:T(8,128)(2,1)}, u32[]{:S(2)}, u32[]{:S(2)}) %collective-permute-start) | collective-permute-done | bytes 196640 | tf_op jit(solution)/shard_map/ppermute | solution.py:170
  51.2 1.0 pad_maximum_fusion.mixed
  52.1 0.0 copy-done.1
  52.1 0.0 copy-start.2
  52.2 1.6 %copy-done.2 = bf16[1024,1024]{1,0:T(8,128)(2,1)S(1)} copy-done((bf16[1024,1024]{1,0:T(8,128)(2,1)S(1)}, bf16[1024,1024]{1,0:T(8,128)(2,1)}, u32[]{:S(2)}) %copy-start.2) | copy-done | bytes 2097176
  53.7 3.6 %shard_map.102 = (f32[1024,128]{1,0:T(8,128)S(1)}, f32[1024,512]{1,0:T(8,128)S(1)}, f32[1024,128]{1,0:T(8,128)S(1)}) custom-call(bf16[1024,1024]{1,0:T(8,128)(2,1)S(1)} %copy-done.1, bf16[1024,1024]{1,0:T(8,128)(2,1)S(1)} %copy-done.2, bf16[1792,128]{1,0:T(8,128)(2,1)S(1)} %pad_maximum_fusion.mixed, bf16[768,128]{1,0:T(8,128)(2,1)S(1)} %constant_dynamic-slice_fusion.taps), custom_call_target="tpu_custom_call" | custom-call | flops 1543503872 | bytes 6000000 | tf_op jit(solution)/shard_map/pallas_call | solution.py:193
  57.3 0.0 copy-start.5
  57.3 1.3 %copy-done.5 = f32[1024,512]{1,0:T(8,128)} copy-done((f32[1024,512]{1,0:T(8,128)}, f32[1024,512]{1,0:T(8,128)S(1)}, u32[]{:S(2)}) %copy-start.5) | copy-done | bytes 2097176
  58.7 0.8 copy-done.7
  59.5 0.8 copy-done.8
  60.3 0.0 all-to-all-done
  60.3 1.9 %fusion.4 = (bf16[1024,128]{1,0:T(8,128)(2,1)S(1)}, bf16[1024,128]{1,0:T(8,128)(2,1)}) fusion(bf16[4,256,128]{2,1,0:T(8,128)(2,1)} %all-to-all-done.3, bf16[32,32,128]{2,1,0:T(8,128)(2,1)S(1)} %all-to-all-done, f32[1024,128]{1,0:T(8,128)} %copy-done.7), kind=kLoop, calls=%fused_computation.9 | loop fusion | flops 786432 | bytes 1572864 | tf_op jit(solution)/shard_map/convert_element_type | solution.py:216
  62.2 0.7 slice.13
  62.9 1.3 collective-permute-start.1
  64.2 4.4 %all-to-all-start.2 = ((bf16[4,256,128]{2,1,0:T(8,128)(2,1)}), bf16[4,256,128]{2,1,0:T(8,128)(2,1)S(1)}, u32[]{:S(2)}, u32[]{:S(2)}) async-start(bf16[4,256,128]{2,1,0:T(8,128)(2,1)} %bitcast.49), calls=%async_computation.2 | async-start | bytes 524288 | tf_op jit(solution)/shard_map/all_to_all | solution.py:174
  68.6 5.1 %collective-permute-done.1 = bf16[768,128]{1,0:T(8,128)(2,1)} collective-permute-done((bf16[768,128]{1,0:T(8,128)(2,1)}, bf16[768,128]{1,0:T(8,128)(2,1)}, u32[]{:S(2)}, u32[]{:S(2)}) %collective-permute-start.1) | collective-permute-done | bytes 196640 | tf_op jit(solution)/shard_map/ppermute | solution.py:170
  73.8 1.0 pad_maximum_fusion.1.grad
  74.7 0.0 copy-start.3
  74.7 1.6 %copy-done.3 = bf16[1024,1024]{1,0:T(8,128)(2,1)S(1)} copy-done((bf16[1024,1024]{1,0:T(8,128)(2,1)S(1)}, bf16[1024,1024]{1,0:T(8,128)(2,1)}, u32[]{:S(2)}) %copy-start.3) | copy-done | bytes 2097176
  76.3 1.0 copy-done.9
  77.4 3.8 %shard_map.103 = bf16[1024,128]{1,0:T(8,128)(2,1)} custom-call(bf16[1024,1024]{1,0:T(8,128)(2,1)S(1)} %copy-done.1, bf16[1024,1024]{1,0:T(8,128)(2,1)S(1)} %copy-done.3, bf16[1792,128]{1,0:T(8,128)(2,1)S(1)} %pad_maximum_fusion.1.grad, f32[1024,128]{1,0:T(8,128)S(1)} %copy-done.9), custom_call_target="tpu_custom_call" | custom-call | flops 1342177280 | bytes 4000000 | tf_op jit(solution)/shard_map/pallas_call | solution.py:238
  81.2 0.0 all-to-all-done.2
  81.2 5.8 %all-to-all-start.4 = ((bf16[4,256,128]{2,1,0:T(8,128)(2,1)}), bf16[4,256,128]{2,1,0:T(8,128)(2,1)}, u32[]{:S(2)}, u32[]{:S(2)}) async-start(bf16[4,256,128]{2,1,0:T(8,128)(2,1)} %bitcast.11), calls=%async_computation.4 | async-start | bytes 524288 | tf_op jit(solution)/shard_map/all_to_all | solution.py:174
  87.0 0.0 copy-done.10
  87.0 1.6 %copy-done.4 = bf16[1024,1024]{1,0:T(8,128)(2,1)S(1)} copy-done((bf16[1024,1024]{1,0:T(8,128)(2,1)S(1)}, bf16[1024,1024]{1,0:T(8,128)(2,1)}, u32[]{:S(2)}) %copy-start.4) | copy-done | bytes 2097176
  88.6 1.6 %copy-done.6 = f32[1024,512]{1,0:T(8,128)S(1)} copy-done((f32[1024,512]{1,0:T(8,128)S(1)}, f32[1024,512]{1,0:T(8,128)}, u32[]{:S(2)}) %copy-start.6) | copy-done | bytes 2097176
  90.2 2.6 %shard_map.104 = bf16[768,128]{1,0:T(8,128)(2,1)S(1)} custom-call(bf16[1024,1024]{1,0:T(8,128)(2,1)S(1)} %copy-done.1, bf16[1024,1024]{1,0:T(8,128)(2,1)S(1)} %copy-done.4, bf16[1024,128]{1,0:T(8,128)(2,1)S(1)} %get-tuple-element.12.grad, f32[1024,512]{1,0:T(8,128)S(1)} %copy-done.6), custom_call_target="tpu_custom_call" | custom-call | flops 469762048 | bytes 4000000 | tf_op jit(solution)/shard_map/pallas_call | solution.py:219
  92.8 0.7 reshape.59
  93.5 0.0 all-to-all-done.4
  93.5 16.6 %all-to-all-start.5 = ((bf16[64,12,128]{2,1,0:T(8,128)(2,1)}), bf16[64,12,128]{2,1,0:T(8,128)(2,1)S(1)}, u32[]{:S(2)}, u32[]{:S(2)}) async-start(bf16[64,12,128]{2,1,0:T(8,128)(2,1)} %reshape.59), calls=%async_computation.5 | async-start | bytes 524288 | tf_op jit(solution)/shard_map/all_to_all | solution.py:174
  110.2 1.7 %copy_bitcast_fusion = bf16[256,512]{1,0:T(8,128)(2,1)} fusion(bf16[4,256,128]{2,1,0:T(8,128)(2,1)} %copy-done.10), kind=kLoop, calls=%fused_computation.15 | loop fusion | bytes 524288 | tf_op jit(solution)/shard_map/reshape | solution.py:255
  111.9 2.0 %fusion = (bf16[256,512]{1,0:T(8,128)(2,1)}, bf16[256,512]{1,0:T(8,128)(2,1)}) fusion(bf16[256,512]{1,0:T(8,128)(2,1)} %param.8, bf16[256,512]{1,0:T(8,128)(2,1)} %param.9, bf16[4,256,128]{2,1,0:T(8,128)(2,1)} %all-to-all-done.4), kind=kLoop, calls=%fused_computation.5 | loop fusion | flops 917504 | bytes 1310720 | tf_op jit(solution)/shard_map/convert_element_type | solution.py:260
  113.9 16.2 %all-to-all-done.5 = bf16[64,12,128]{2,1,0:T(8,128)(2,1)S(1)} async-done(((bf16[64,12,128]{2,1,0:T(8,128)(2,1)}), bf16[64,12,128]{2,1,0:T(8,128)(2,1)S(1)}, u32[]{:S(2)}, u32[]{:S(2)}) %all-to-all-start.5) | async-done | bytes 196640 | tf_op jit(solution)/shard_map/all_to_all | solution.py:174
  130.0 0.1 convert_reduce_fusion
  130.1 0.6 copy.36
  (10 shorter events, 0.1 us)
Async XLA Ops:
  0.6 46.9 %copy-start = (bf16[768,512]{1,0:T(8,128)(2,1)S(1)}, bf16[768,512]{1,0:T(8,128)(2,1)}, u32[]{:S(2)}) copy-start(bf16[768,512]{1,0:T(8,128)(2,1)} %param.11) | copy-start | bytes 2359300
  2.5 15.4 %all-to-all-start.1 = ((bf16[4,256,128]{2,1,0:T(8,128)(2,1)}), bf16[4,256,128]{2,1,0:T(8,128)(2,1)S(1)}, u32[]{:S(2)}, u32[]{:S(2)}) async-start(bf16[4,256,128]{2,1,0:T(8,128)(2,1)} %bitcast_bitcast_fusion.1), calls=%async_computation.1 | async-start | bytes 524288 | tf_op jit(solution)/shard_map/all_to_all | solution.py:174
  12.8 39.4 %copy-start.1 = (bf16[1024,1024]{1,0:T(8,128)(2,1)S(1)}, bf16[1024,1024]{1,0:T(8,128)(2,1)}, u32[]{:S(2)}) copy-start(bf16[1024,1024]{1,0:T(8,128)(2,1)} %constant.24.clone.forward) | copy-start | bytes 6291460
  17.9 10.1 %all-to-all-start.3 = ((bf16[4,256,128]{2,1,0:T(8,128)(2,1)}), bf16[4,256,128]{2,1,0:T(8,128)(2,1)}, u32[]{:S(2)}, u32[]{:S(2)}) async-start(bf16[4,256,128]{2,1,0:T(8,128)(2,1)} %bitcast_bitcast_fusion), calls=%async_computation.3 | async-start | bytes 524288 | tf_op jit(solution)/shard_map/all_to_all | solution.py:174
  28.1 32.2 %all-to-all-start = ((bf16[32,32,128]{2,1,0:T(8,128)(2,1)}), bf16[32,32,128]{2,1,0:T(8,128)(2,1)S(1)}, u32[]{:S(2)}, u32[]{:S(2)}) async-start(bf16[32,32,128]{2,1,0:T(8,128)(2,1)} %bitcast.1), calls=%async_computation | async-start | bytes 524288 | tf_op jit(solution)/shard_map/all_to_all | solution.py:174
  42.0 9.2 %collective-permute-start = (bf16[768,128]{1,0:T(8,128)(2,1)}, bf16[768,128]{1,0:T(8,128)(2,1)}, u32[]{:S(2)}, u32[]{:S(2)}) collective-permute-start(bf16[768,128]{1,0:T(8,128)(2,1)} %bitcast.4), channel_id=1, source_target_pairs={{0,32},{32,64},{64,96},{96,128},{128,160},{160,192},{192,224},{224... | collective-permute-start | bytes 589832 | tf_op jit(solution)/shard_map/ppermute | solution.py:170
  52.1 1.6 %copy-start.2 = (bf16[1024,1024]{1,0:T(8,128)(2,1)S(1)}, bf16[1024,1024]{1,0:T(8,128)(2,1)}, u32[]{:S(2)}) copy-start(bf16[1024,1024]{1,0:T(8,128)(2,1)} %constant.25.clone.inverse) | copy-start | bytes 6291460
  57.3 1.3 %copy-start.5 = (f32[1024,512]{1,0:T(8,128)}, f32[1024,512]{1,0:T(8,128)S(1)}, u32[]{:S(2)}) copy-start(f32[1024,512]{1,0:T(8,128)S(1)} %get-tuple-element.9.spectrum) | copy-start | bytes 6291460
  58.7 0.8 copy-start.7
  59.5 0.8 copy-start.8
  62.9 10.9 %collective-permute-start.1 = (bf16[768,128]{1,0:T(8,128)(2,1)}, bf16[768,128]{1,0:T(8,128)(2,1)}, u32[]{:S(2)}, u32[]{:S(2)}) collective-permute-start(bf16[768,128]{1,0:T(8,128)(2,1)} %slice.13), channel_id=1, source_target_pairs={{32,0},{64,32},{96,64},{128,96},{160,128},{192,160},{224,192},{256... | collective-permute-start | bytes 589832 | tf_op jit(solution)/shard_map/ppermute | solution.py:170
  64.2 17.0 %all-to-all-start.2 = ((bf16[4,256,128]{2,1,0:T(8,128)(2,1)}), bf16[4,256,128]{2,1,0:T(8,128)(2,1)S(1)}, u32[]{:S(2)}, u32[]{:S(2)}) async-start(bf16[4,256,128]{2,1,0:T(8,128)(2,1)} %bitcast.49), calls=%async_computation.2 | async-start | bytes 524288 | tf_op jit(solution)/shard_map/all_to_all | solution.py:174
  74.7 1.6 %copy-start.3 = (bf16[1024,1024]{1,0:T(8,128)(2,1)S(1)}, bf16[1024,1024]{1,0:T(8,128)(2,1)}, u32[]{:S(2)}) copy-start(bf16[1024,1024]{1,0:T(8,128)(2,1)} %constant.25.clone.inverse) | copy-start | bytes 6291460
  76.3 1.0 copy-start.9
  81.2 5.8 %copy-start.10 = (bf16[4,256,128]{2,1,0:T(8,128)(2,1)}, bf16[4,256,128]{2,1,0:T(8,128)(2,1)S(1)}, u32[]{:S(2)}) copy-start(bf16[4,256,128]{2,1,0:T(8,128)(2,1)S(1)} %all-to-all-done.2) | copy-start | bytes 786436
  81.2 12.3 %all-to-all-start.4 = ((bf16[4,256,128]{2,1,0:T(8,128)(2,1)}), bf16[4,256,128]{2,1,0:T(8,128)(2,1)}, u32[]{:S(2)}, u32[]{:S(2)}) async-start(bf16[4,256,128]{2,1,0:T(8,128)(2,1)} %bitcast.11), calls=%async_computation.4 | async-start | bytes 524288 | tf_op jit(solution)/shard_map/all_to_all | solution.py:174
  87.0 1.6 %copy-start.4 = (bf16[1024,1024]{1,0:T(8,128)(2,1)S(1)}, bf16[1024,1024]{1,0:T(8,128)(2,1)}, u32[]{:S(2)}) copy-start(bf16[1024,1024]{1,0:T(8,128)(2,1)} %constant.25.clone.inverse) | copy-start | bytes 6291460
  88.6 1.6 %copy-start.6 = (f32[1024,512]{1,0:T(8,128)S(1)}, f32[1024,512]{1,0:T(8,128)}, u32[]{:S(2)}) copy-start(f32[1024,512]{1,0:T(8,128)} %copy-done.5) | copy-start | bytes 6291460
  93.5 36.5 %all-to-all-start.5 = ((bf16[64,12,128]{2,1,0:T(8,128)(2,1)}), bf16[64,12,128]{2,1,0:T(8,128)(2,1)S(1)}, u32[]{:S(2)}, u32[]{:S(2)}) async-start(bf16[64,12,128]{2,1,0:T(8,128)(2,1)} %reshape.59), calls=%async_computation.5 | async-start | bytes 524288 | tf_op jit(solution)/shard_map/all_to_all | solution.py:174

commit v2 on v1

v2 whole, which is shorter than its diff:
```python
import functools
import math

import jax
import jax.numpy as jnp
import ml_dtypes
import numpy as np
from jax import lax
from jax.experimental import pallas as pl
from jax.experimental.pallas import tpu as pltpu
from jax.sharding import Mesh, PartitionSpec as P

BF16 = jnp.bfloat16
F32 = jnp.float32
AXES = ("z", "yh", "yl", "c", "x", "zh")
SIZES = (8, 2, 2, 2, 4, 2)
CTX = ("z", "yh", "yl", "c")
GROUP = ("yl", "c")
RUNS = ("z", "yh")
CH = ("x", "zh")

BLOCK = 256
PERIOD = 1024
LANES = 128
BLOCKS = 4
TOKENS = BLOCKS * BLOCK
WIDE = BLOCKS * LANES
BINS = 128
STEPS = PERIOD // 2 // BINS
ROWS = 2 * BINS
SLOT = 16
MIB = 1024 * 1024


def make_tables(lags, share):
    freq = np.arange(PERIOD // 2)[:, None]
    place = np.arange(PERIOD)[None, :]
    angle = math.pi / PERIOD * ((2 * freq + 1) * place % (2 * PERIOD)).astype(np.float64)
    both = np.stack([np.cos(angle), -np.sin(angle)])
    both = both.reshape(2, STEPS, BINS, PERIOD).transpose(1, 0, 2, 3).reshape(PERIOD, PERIOD)
    by_slot = np.zeros((lags // share, SLOT, PERIOD))
    by_slot[:, :share] = both.T[:lags].reshape(lags // share, share, PERIOD)
    tables = both, both.T, by_slot.reshape(-1, PERIOD)
    return tuple(np.ascontiguousarray(t).astype(ml_dtypes.bfloat16) for t in tables)


def dot(a, b):
    return jnp.dot(a, b, preferred_element_type=F32)


def lane_block(index):
    return slice(index * LANES, (index + 1) * LANES)


def lanes_at(index):
    return pl.ds(pl.multiple_of(index * LANES, LANES), LANES)


def token_block(index):
    return slice(index * BLOCK, (index + 1) * BLOCK)


def spread(part):
    return jnp.concatenate([part] * BLOCKS, axis=1)


def accumulate(step, total, part):
    @pl.when(step == 0)
    def _():
        total[...] = part

    @pl.when(step > 0)
    def _():
        total[...] += part


def prep_kernel(place, key, value, gate, out_grad, *outs):
    ships, pieces = outs[:BLOCKS], outs[BLOCKS]
    for hop, ship in enumerate(ships):
        at = (slice(None), lanes_at(place[0] ^ hop))
        ship[:BLOCK, :] = (key[at].astype(F32) * value[at].astype(F32)).astype(BF16)
        ship[BLOCK:, :] = gate[at]
    count = pieces.shape[0]
    for piece in range(count):
        target = piece % BLOCKS * (count // BLOCKS) + piece // BLOCKS
        pieces[target] = out_grad[:, lane_block(piece)]


def join_kernel(place, *refs):
    ships, (mixed, tail, gate) = refs[:BLOCKS], refs[BLOCKS:]
    skipped = TOKENS - tail.shape[0]
    for hop, ship in enumerate(ships):
        block = place[0] ^ hop
        at = pl.multiple_of(block * BLOCK, BLOCK)
        mixed[pl.ds(at, BLOCK), :] = ship[:BLOCK, :]
        gate[pl.ds(at, BLOCK), :] = ship[BLOCK:, :]

    tail[...] = mixed[skipped:, :]


def conv_kernel(scale, forward, inverse, halo, mixed, taps, conv, spectrum, response, windows, total):
    step = pl.program_id(0)
    lags = taps.shape[0]

    @pl.when(step == 0)
    def _():
        for block in range(BLOCKS):
            early = lags - block * BLOCK
            if early:
                windows[:early, lane_block(block)] = halo[block * BLOCK :, :]
            windows[early:, lane_block(block)] = mixed[: (block + 1) * BLOCK, :]

    resp = dot(forward[:, :lags], taps[...])
    response[...] = resp
    spec = dot(forward[...], windows[...])
    spectrum[...] = spec
    f_re, f_im = spread(resp[:BINS]), spread(resp[BINS:])
    x_re, x_im = spec[:BINS], spec[BINS:]
    y = jnp.concatenate([f_re * x_re - f_im * x_im, f_re * x_im + f_im * x_re]).astype(BF16)
    accumulate(step, total, dot(inverse[...], y))

    @pl.when(step == STEPS - 1)
    def _():
        for block in range(BLOCKS):
            conv[token_block(block), :] = total[:, lane_block(block)] * scale


def cross_kernel(
    scale, forward, inverse, cotangent, gate, spectrum, grad, head, lag_grad, windows, total
):
    step = pl.program_id(0)

    @pl.when(step == 0)
    def _():
        product = (cotangent[...].astype(F32) * gate[...].astype(F32)).astype(BF16)
        grad[...] = product
        head[...] = product[: head.shape[0]]
        for block in range(BLOCKS):
            windows[:, lane_block(block)] = product[token_block(block)]

    spec = dot(forward[...], windows[...])
    g_re, g_im = spec[:BINS], spec[BINS:]
    x_re, x_im = spectrum[:BINS], spectrum[BINS:]
    re = g_re * x_re + g_im * x_im
    im = g_im * x_re - g_re * x_im
    re = sum(re[:, lane_block(b)] for b in range(BLOCKS))
    im = sum(im[:, lane_block(b)] for b in range(BLOCKS))
    accumulate(step, total, dot(inverse[...], jnp.concatenate([re, im]).astype(BF16)))

    @pl.when(step == STEPS - 1)
    def _():
        lag_grad[...] = (total[...] * scale).astype(BF16)


def back_kernel(
    scale, place, forward, inverse, grad, halo, response, conv, cotangent, *refs
):
    outs, (windows, total) = refs[:BLOCKS], refs[BLOCKS:]
    step = pl.program_id(0)

    @pl.when(step == 0)
    def _():
        for block in range(BLOCKS):
            own = min(PERIOD, TOKENS - block * BLOCK)
            windows[:own, lane_block(block)] = grad[block * BLOCK : block * BLOCK + own, :]
            if own < PERIOD:
                windows[own:, lane_block(block)] = halo[: PERIOD - own, :]
        for hop, out in enumerate(outs):
            at = pl.ds(pl.multiple_of((place[0] ^ hop) * BLOCK, BLOCK), BLOCK)
            out[:BLOCK, :] = (cotangent[at, :].astype(F32) * conv[at, :]).astype(BF16)

    spec = dot(forward[...], windows[...])
    f_re, f_im = spread(response[:BINS]), spread(response[BINS:])
    g_re, g_im = spec[:BINS], spec[BINS:]
    y = jnp.concatenate([f_re * g_re + f_im * g_im, f_re * g_im - f_im * g_re]).astype(BF16)
    accumulate(step, total, dot(inverse[...], y))

    @pl.when(step == STEPS - 1)
    def _():
        for hop, out in enumerate(outs):
            out[BLOCK:, :] = (total[:, lanes_at(place[0] ^ hop)] * scale).astype(BF16)


def final_kernel(place, *refs):
    ships, (key, value, gate_grad, key_grad, value_grad) = refs[:BLOCKS], refs[BLOCKS:]
    for hop, ship in enumerate(ships):
        at = (slice(None), lanes_at(place[0] ^ hop))
        gate_grad[at] = ship[:BLOCK, :]
        back = ship[BLOCK:, :].astype(F32)
        key_grad[at] = (back * value[at].astype(F32)).astype(BF16)
        value_grad[at] = (back * key[at].astype(F32)).astype(BF16)


def sum_kernel(parts, out):
    for block in range(BLOCKS):
        total = parts[block].astype(F32)
        for source in range(1, parts.shape[0] // BLOCKS):
            total += parts[source * BLOCKS + block].astype(F32)
        out[:, lane_block(block)] = total[: out.shape[0]]


def whole(shape):
    return pl.BlockSpec(shape, lambda *_: (0,) * len(shape))


def shaped(shape, dtype=BF16):
    return jax.ShapeDtypeStruct(shape, dtype)


def call(kernel, in_specs, out_specs, out_shape, scratch=(), steps=1, macs=0, moved=0):
    return pl.pallas_call(
        kernel,
        grid=(steps,),
        in_specs=in_specs,
        out_specs=out_specs,
        out_shape=out_shape,
        scratch_shapes=scratch,
        compiler_params=pltpu.CompilerParams(
            dimension_semantics=("arbitrary",), vmem_limit_bytes=VMEM_LIMIT
        ),
        cost_estimate=pl.CostEstimate(flops=2 * macs, bytes_accessed=moved, transcendentals=0),
    )


VMEM_LIMIT = 56 * MIB


def shift(value, steps):
    count = lax.axis_size(RUNS)
    first, last = max(0, -steps), min(count, count - steps)
    return lax.ppermute(value, RUNS, [(i, i + steps) for i in range(first, last)])


def swap(ships):
    return [ships[0]] + [
        lax.ppermute(ships[hop], GROUP, [(i, i ^ hop) for i in range(BLOCKS)])
        for hop in range(1, BLOCKS)
    ]


def exchange(value, axes):
    return lax.all_to_all(value, axes, split_axis=0, concat_axis=0, tiled=True)


def body(forward, inverse, slotted, gate_input, key_input, value_input, out_grad, filter_taps):
    lags = filter_taps.shape[0]
    held, channels = out_grad.shape
    share = lags // lax.axis_size(CTX)
    norm = 2.0 / PERIOD / lags**0.5
    local = (BLOCK, WIDE)
    ship = (2 * BLOCK, LANES)
    pieces = (channels // LANES, held, LANES)
    flat = (TOKENS, LANES)
    reach = (lags, LANES)
    scalar = pl.BlockSpec(memory_space=pltpu.SMEM)
    place = lax.axis_index(GROUP).reshape(1)

    *ships, cotangent = call(
        prep_kernel,
        [scalar] + [whole(local)] * 3 + [whole(out_grad.shape)],
        [whole(ship)] * BLOCKS + [whole(pieces)],
        [shaped(ship)] * BLOCKS + [shaped(pieces)],
    )(place, key_input, value_input, gate_input, out_grad)
    cotangent = exchange(cotangent, GROUP + CH).reshape(flat)
    mixed, tail, gate = call(
        join_kernel,
        [scalar] + [whole(ship)] * BLOCKS,
        [whole(flat), whole(reach), whole(flat)],
        [shaped(flat), shaped(reach), shaped(flat)],
    )(place, *swap(ships))
    mixed_halo = shift(tail, 1)
    taps = lax.dynamic_slice_in_dim(filter_taps, lax.axis_index(GROUP) * LANES, LANES, 1)

    table = pl.BlockSpec((ROWS, PERIOD), lambda step: (step, 0))
    bins = pl.BlockSpec((ROWS, WIDE), lambda step: (step, 0))
    narrow_bins = pl.BlockSpec((ROWS, LANES), lambda step: (step, 0))
    conv, spectrum, response = call(
        functools.partial(conv_kernel, norm),
        [
            table,
            pl.BlockSpec((BLOCK, ROWS), lambda step: (lags // BLOCK, step)),
            whole(reach),
            whole(flat),
            whole(reach),
        ],
        [whole(flat), bins, narrow_bins],
        [shaped(flat, F32), shaped((PERIOD, WIDE), F32), shaped((PERIOD, LANES), F32)],
        [pltpu.VMEM((PERIOD, WIDE), BF16), pltpu.VMEM(local, F32)],
        STEPS,
    )(forward, inverse, mixed_halo, mixed, taps)

    grad, head, lag_grad = call(
        functools.partial(cross_kernel, norm),
        [
            pl.BlockSpec((ROWS, BLOCK), lambda step: (step, lags // BLOCK)),
            pl.BlockSpec((slotted.shape[0], ROWS), lambda step: (0, step)),
            whole(flat),
            whole(flat),
            bins,
        ],
        [whole(flat), whole(reach), whole((slotted.shape[0], LANES))],
        [shaped(flat), shaped(reach), shaped((slotted.shape[0], LANES))],
        [pltpu.VMEM(local, BF16), pltpu.VMEM((slotted.shape[0], LANES), F32)],
        STEPS,
    )(forward, slotted, cotangent, gate, spectrum)
    grad_halo = shift(head, -1)
    lag_parts = exchange(lag_grad.reshape(-1, SLOT, LANES), CTX)

    ships = call(
        functools.partial(back_kernel, norm),
        [
            scalar,
            table,
            pl.BlockSpec((BLOCK, ROWS), lambda step: (0, step)),
            whole(flat),
            whole(reach),
            narrow_bins,
            whole(flat),
            whole(flat),
        ],
        [whole(ship)] * BLOCKS,
        [shaped(ship)] * BLOCKS,
        [pltpu.VMEM((PERIOD, WIDE), BF16), pltpu.VMEM(local, F32)],
        STEPS,
    )(place, forward, inverse, grad, grad_halo, response, conv, cotangent)
    gate_grad, key_grad, value_grad = call(
        final_kernel,
        [scalar] + [whole(ship)] * BLOCKS + [whole(local)] * 2,
        [whole(local)] * 3,
        [shaped(local)] * 3,
    )(place, *swap(ships), key_input, value_input)
    filter_grad = call(
        sum_kernel,
        [whole(lag_parts.shape)],
        whole((share, WIDE)),
        shaped((share, WIDE), F32),
    )(lag_parts)
    return gate_grad, key_grad, value_grad, filter_grad


def solution(mesh):
    split = Mesh(mesh.devices.reshape(SIZES), AXES)
    spans = P(CTX, CH)
    mapped = jax.shard_map(
        body,
        mesh=split,
        in_specs=(P(), P(), P(), spans, spans, spans, P(CTX + CH, None), P(None, CH)),
        out_specs=(spans, spans, spans, spans),
        check_vma=False,
    )

    def run(gate_input, key_input, value_input, out_grad, filter_taps):
        lags = filter_taps.shape[0]
        tables = make_tables(lags, lags // math.prod(SIZES[:4]))
        return mapped(*tables, gate_input, key_input, value_input, out_grad, filter_taps)

    return run
```

time: 132 us -> 115 us (0.87)
  the two profiles are of different devices: /device:TPU:1 before, /device:TPU:113 now
where the time goes in v2:
time: 115 us; the launch traced here: 114 us
  starting transfers between devices  48.6 us (42%)
  waiting for transfers between devices  34 us (30%)
  Pallas kernels  26.1 us (23%)
  local copies, waits for them, and re-layouts  4.77 us (4%)
    all_to_all x2, starting transfers between devices, exchange(): return lax.all_to_all(value, axes, split_axis=0, concat_axis=0, tiled=True)  27.5 us
    ppermute x2, waiting for transfers between devices, shift(): lax.ppermute(value, RUNS, [(i, i + steps) for i in range(first, last)])  22.8 us
    ppermute x6, starting transfers between devices, swap(): lax.ppermute(ships[hop], GROUP, [(i, i ^ hop) for i in range(BLOCKS)])  16.3 us
    ppermute x6, waiting for transfers between devices, swap(): lax.ppermute(ships[hop], GROUP, [(i, i ^ hop) for i in range(BLOCKS)])  11.2 us
    pallas_call x1, Pallas kernels, body(): call(functools.partial(conv_kernel, norm), [table, pl.BlockSpec((BLOCK, R...  6.33 us
    pallas_call x1, Pallas kernels, body(): call(functools.partial(back_kernel, norm), [scalar, table, pl.BlockSpec((...  6.01 us
    pallas_call x1, Pallas kernels, body(): call(functools.partial(cross_kernel, norm), [pl.BlockSpec((ROWS, BLOCK),...  5.69 us
    ppermute x2, starting transfers between devices, shift(): lax.ppermute(value, RUNS, [(i, i + steps) for i in range(first, last)])  4.89 us
  transfers between devices with their start and end apart: 10, of which 6 were waited for; matrix products, arithmetic and copies ran while one was open for 1% of the time, Pallas kernels for 14%

profile of v2, /device:TPU:113, one launch (start us, length us, event | category | flops | bytes accessed | tf_op | source)
XLA Modules:
  0.0 114.3 jit_solution(6529040214614403017)
XLA Ops:
  0.6 0.0 copy-start
  0.7 2.3 %shard_map.111 = (bf16[512,128]{1,0:T(8,128)(2,1)}, bf16[512,128]{1,0:T(8,128)(2,1)}, bf16[512,128]{1,0:T(8,128)(2,1)}, bf16[512,128]{1,0:T(8,128)(2,1)}, bf16[32,32,128]{2,1,0:T(8,128)(2,1)}) custom-call(s32[1]{0:T(128)} %bitcast.place, bf16[256,512]{1,0:T(8,128)(2,1)} %refs_4_.1, bf16[256,512]{1,0:T(8,128)(2,1)} %refs_5_.1, bf16[256,512]{1,0:T(8,128)(2,1)} %gate.1, ...), custom_call_target="tpu_custom_call" | custom-call | tf_op jit(solution)/shard_map/pallas_call | solution.py:258
  2.9 16.4 %all-to-all-start = ((bf16[32,32,128]{2,1,0:T(8,128)(2,1)}), bf16[32,32,128]{2,1,0:T(8,128)(2,1)S(1)}, u32[]{:S(2)}, u32[]{:S(2)}) async-start(bf16[32,32,128]{2,1,0:T(8,128)(2,1)} %get-tuple-element.25), calls=%async_computation | async-start | bytes 524288 | tf_op jit(solution)/shard_map/all_to_all | solution.py:242
  19.3 2.1 %collective-permute-start = (bf16[512,128]{1,0:T(8,128)(2,1)}, bf16[512,128]{1,0:T(8,128)(2,1)S(1)}, u32[]{:S(2)}, u32[]{:S(2)}) collective-permute-start(bf16[512,128]{1,0:T(8,128)(2,1)} %get-tuple-element.27), channel_id=1, source_target_pairs={{0,8},{8,0},{16,24},{24,16},{1,9},{9,1},{17,25},{25,17},{2,10},{10... | collective-permute-start | bytes 393224 | tf_op jit(solution)/shard_map/ppermute | solution.py:236
  21.5 3.4 %collective-permute-start.1 = (bf16[512,128]{1,0:T(8,128)(2,1)}, bf16[512,128]{1,0:T(8,128)(2,1)S(1)}, u32[]{:S(2)}, u32[]{:S(2)}) collective-permute-start(bf16[512,128]{1,0:T(8,128)(2,1)} %get-tuple-element.28), channel_id=1, source_target_pairs={{0,16},{8,24},{16,0},{24,8},{1,17},{9,25},{17,1},{25,9},{2,18},{10... | collective-permute-start | bytes 393224 | tf_op jit(solution)/shard_map/ppermute | solution.py:236
  24.9 2.3 %collective-permute-start.2 = (bf16[512,128]{1,0:T(8,128)(2,1)}, bf16[512,128]{1,0:T(8,128)(2,1)S(1)}, u32[]{:S(2)}, u32[]{:S(2)}) collective-permute-start(bf16[512,128]{1,0:T(8,128)(2,1)} %get-tuple-element.29), channel_id=1, source_target_pairs={{0,24},{8,16},{16,8},{24,0},{1,25},{9,17},{17,9},{25,1},{2,26},{10... | collective-permute-start | bytes 393224 | tf_op jit(solution)/shard_map/ppermute | solution.py:236
  27.2 0.0 collective-permute-done.refs_1_
  27.2 0.0 copy-start.5
  27.3 1.3 %collective-permute-done.1.refs_2_ = bf16[512,128]{1,0:T(8,128)(2,1)S(1)} collective-permute-done((bf16[512,128]{1,0:T(8,128)(2,1)}, bf16[512,128]{1,0:T(8,128)(2,1)S(1)}, u32[]{:S(2)}, u32[]{:S(2)}) %collective-permute-start.1) | collective-permute-done | bytes 131104 | tf_op jit(solution)/shard_map/ppermute | solution.py:236
  28.6 0.0 copy-start.6
  28.6 4.3 %collective-permute-done.2.refs_3_ = bf16[512,128]{1,0:T(8,128)(2,1)S(1)} collective-permute-done((bf16[512,128]{1,0:T(8,128)(2,1)}, bf16[512,128]{1,0:T(8,128)(2,1)S(1)}, u32[]{:S(2)}, u32[]{:S(2)}) %collective-permute-start.2) | collective-permute-done | bytes 131104 | tf_op jit(solution)/shard_map/ppermute | solution.py:236
  32.9 0.0 copy-start.7
  32.9 0.0 copy-done.5
  32.9 0.0 copy-done.6
  32.9 0.6 copy-done.7
  33.5 2.0 %shard_map.112 = (bf16[1024,128]{1,0:T(8,128)(2,1)}, bf16[768,128]{1,0:T(8,128)(2,1)}, bf16[1024,128]{1,0:T(8,128)(2,1)}) custom-call(s32[1]{0:T(128)} %bitcast.place, bf16[512,128]{1,0:T(8,128)(2,1)} %get-tuple-element.26.refs_0_, bf16[512,128]{1,0:T(8,128)(2,1)} %copy-done.5, bf16[512,128]{1,0:T(8,128)(2,1)} %copy-done.6, bf16[512,128]{1,0:T(8,128)(2,1)} %copy-done.7), custom_call_target="tpu_custom_call" | custom-call | tf_op jit(solution)/shard_map/pallas_call | solution.py:265
  35.5 2.7 %collective-permute-start.3 = (bf16[768,128]{1,0:T(8,128)(2,1)}, bf16[768,128]{1,0:T(8,128)(2,1)S(1)}, u32[]{:S(2)}, u32[]{:S(2)}) collective-permute-start(bf16[768,128]{1,0:T(8,128)(2,1)} %get-tuple-element.31), channel_id=1, source_target_pairs={{0,32},{32,64},{64,96},{96,128},{128,160},{160,192},{192,224},{224... | collective-permute-start | bytes 589832 | tf_op jit(solution)/shard_map/ppermute | solution.py:231
  38.2 0.0 copy-done
  38.2 0.7 constant_dynamic-slice_fusion.taps
  38.9 6.5 %collective-permute-done.3.halo = bf16[768,128]{1,0:T(8,128)(2,1)S(1)} collective-permute-done((bf16[768,128]{1,0:T(8,128)(2,1)}, bf16[768,128]{1,0:T(8,128)(2,1)S(1)}, u32[]{:S(2)}, u32[]{:S(2)}) %collective-permute-start.3) | collective-permute-done | bytes 196640 | tf_op jit(solution)/shard_map/ppermute | solution.py:231
  45.4 0.0 copy-start.3
  45.5 0.7 copy-done.3
  46.1 6.3 %shard_map.113 = (f32[1024,128]{1,0:T(8,128)}, f32[1024,512]{1,0:T(8,128)}, f32[1024,128]{1,0:T(8,128)}) custom-call(bf16[1024,1024]{1,0:T(8,128)(2,1)} %constant.24.clone.forward, bf16[1024,1024]{1,0:T(8,128)(2,1)} %constant.25.clone.inverse, bf16[768,128]{1,0:T(8,128)(2,1)} %copy-done.3, bf16[1024,128]{1,0:T(8,128)(2,1)} %get-tuple-element.32.mixed, ...), custom_call_target="tpu_custom_call" | custom-call | tf_op jit(solution)/shard_map/pallas_call | solution.py:277
  52.4 0.0 all-to-all-done
  52.4 0.0 copy-start.1
  52.5 0.7 copy-done.1
  53.2 5.7 %shard_map.114 = (bf16[1024,128]{1,0:T(8,128)(2,1)}, bf16[768,128]{1,0:T(8,128)(2,1)}, bf16[1024,128]{1,0:T(8,128)(2,1)}) custom-call(bf16[1024,1024]{1,0:T(8,128)(2,1)} %constant.24.clone.forward, bf16[1024,1024]{1,0:T(8,128)(2,1)} %constant.26.clone.inverse, bf16[1024,128]{1,0:T(8,128)(2,1)} %bitcast.3, bf16[1024,128]{1,0:T(8,128)(2,1)} %get-tuple-element.30.gate, ...), custom_call_target="tpu_custom_call" | custom-call | tf_op jit(solution)/shard_map/pallas_call | solution.py:292
  58.8 11.1 %all-to-all-start.1 = ((bf16[64,16,128]{2,1,0:T(8,128)(2,1)}), bf16[64,16,128]{2,1,0:T(8,128)(2,1)S(1)}, u32[]{:S(2)}, u32[]{:S(2)}) async-start(bf16[64,16,128]{2,1,0:T(8,128)(2,1)} %bitcast.5), calls=%async_computation.1 | async-start | bytes 524288 | tf_op jit(solution)/shard_map/all_to_all | solution.py:242
  70.0 2.2 %collective-permute-start.4 = (bf16[768,128]{1,0:T(8,128)(2,1)}, bf16[768,128]{1,0:T(8,128)(2,1)S(1)}, u32[]{:S(2)}, u32[]{:S(2)}) collective-permute-start(bf16[768,128]{1,0:T(8,128)(2,1)} %get-tuple-element.35), channel_id=1, source_target_pairs={{32,0},{64,32},{96,64},{128,96},{160,128},{192,160},{224,192},{256... | collective-permute-start | bytes 589832 | tf_op jit(solution)/shard_map/ppermute | solution.py:231
  72.1 16.3 %collective-permute-done.4.halo = bf16[768,128]{1,0:T(8,128)(2,1)S(1)} collective-permute-done((bf16[768,128]{1,0:T(8,128)(2,1)}, bf16[768,128]{1,0:T(8,128)(2,1)S(1)}, u32[]{:S(2)}, u32[]{:S(2)}) %collective-permute-start.4) | collective-permute-done | bytes 196640 | tf_op jit(solution)/shard_map/ppermute | solution.py:231
  88.4 0.0 copy-start.4
  88.4 0.7 copy-done.4
  89.1 6.0 %shard_map.115 = (bf16[512,128]{1,0:T(8,128)(2,1)}, bf16[512,128]{1,0:T(8,128)(2,1)}, bf16[512,128]{1,0:T(8,128)(2,1)}, bf16[512,128]{1,0:T(8,128)(2,1)}) custom-call(s32[1]{0:T(128)} %bitcast.place, bf16[1024,1024]{1,0:T(8,128)(2,1)} %constant.24.clone.forward, bf16[1024,1024]{1,0:T(8,128)(2,1)} %constant.25.clone.inverse, ...), custom_call_target="tpu_custom_call" | custom-call | tf_op jit(solution)/shard_map/pallas_call | solution.py:309
  95.1 2.8 %collective-permute-start.5 = (bf16[512,128]{1,0:T(8,128)(2,1)}, bf16[512,128]{1,0:T(8,128)(2,1)S(1)}, u32[]{:S(2)}, u32[]{:S(2)}) collective-permute-start(bf16[512,128]{1,0:T(8,128)(2,1)} %get-tuple-element.39), channel_id=1, source_target_pairs={{0,8},{8,0},{16,24},{24,16},{1,9},{9,1},{17,25},{25,17},{2,10},{10... | collective-permute-start | bytes 393224 | tf_op jit(solution)/shard_map/ppermute | solution.py:236
  97.9 3.7 %collective-permute-start.6 = (bf16[512,128]{1,0:T(8,128)(2,1)}, bf16[512,128]{1,0:T(8,128)(2,1)S(1)}, u32[]{:S(2)}, u32[]{:S(2)}) collective-permute-start(bf16[512,128]{1,0:T(8,128)(2,1)} %get-tuple-element.40), channel_id=1, source_target_pairs={{0,16},{8,24},{16,0},{24,8},{1,17},{9,25},{17,1},{25,9},{2,18},{10... | collective-permute-start | bytes 393224 | tf_op jit(solution)/shard_map/ppermute | solution.py:236
  101.6 1.9 %collective-permute-start.7 = (bf16[512,128]{1,0:T(8,128)(2,1)}, bf16[512,128]{1,0:T(8,128)(2,1)S(1)}, u32[]{:S(2)}, u32[]{:S(2)}) collective-permute-start(bf16[512,128]{1,0:T(8,128)(2,1)} %get-tuple-element.41), channel_id=1, source_target_pairs={{0,24},{8,16},{16,8},{24,0},{1,25},{9,17},{17,9},{25,1},{2,26},{10... | collective-permute-start | bytes 393224 | tf_op jit(solution)/shard_map/ppermute | solution.py:236
  103.5 0.0 collective-permute-done.5.refs_1_
  103.5 0.0 copy-start.8
  103.6 2.1 %collective-permute-done.6.refs_2_ = bf16[512,128]{1,0:T(8,128)(2,1)S(1)} collective-permute-done((bf16[512,128]{1,0:T(8,128)(2,1)}, bf16[512,128]{1,0:T(8,128)(2,1)S(1)}, u32[]{:S(2)}, u32[]{:S(2)}) %collective-permute-start.6) | collective-permute-done | bytes 131104 | tf_op jit(solution)/shard_map/ppermute | solution.py:236
  105.7 3.4 %collective-permute-done.7.refs_3_ = bf16[512,128]{1,0:T(8,128)(2,1)S(1)} collective-permute-done((bf16[512,128]{1,0:T(8,128)(2,1)}, bf16[512,128]{1,0:T(8,128)(2,1)S(1)}, u32[]{:S(2)}, u32[]{:S(2)}) %collective-permute-start.7) | collective-permute-done | bytes 131104 | tf_op jit(solution)/shard_map/ppermute | solution.py:236
  109.1 0.0 copy-start.10
  109.1 0.0 copy-done.8
  109.1 0.0 copy-done.9
  109.1 0.6 copy-done.10
  109.8 2.2 %shard_map.116 = (bf16[256,512]{1,0:T(8,128)(2,1)}, bf16[256,512]{1,0:T(8,128)(2,1)}, bf16[256,512]{1,0:T(8,128)(2,1)}) custom-call(s32[1]{0:T(128)} %bitcast.place, bf16[512,128]{1,0:T(8,128)(2,1)} %get-tuple-element.38.refs_0_, bf16[512,128]{1,0:T(8,128)(2,1)} %copy-done.8, bf16[512,128]{1,0:T(8,128)(2,1)} %copy-done.9, bf16[512,128]{1,0:T(8,128)(2,1)} %copy-done.10, ...), custom_call_target="tpu_custom_call" | custom-call | tf_op jit(solution)/shard_map/pallas_call | solution.py:326
  112.0 0.0 all-to-all-done.1.parts
  112.0 0.7 copy-done.2
  112.7 1.6 %shard_map.117 = f32[12,512]{1,0:T(8,128)} custom-call(bf16[64,16,128]{2,1,0:T(8,128)(2,1)} %copy-done.2), custom_call_target="tpu_custom_call" | custom-call | tf_op jit(solution)/shard_map/pallas_call | solution.py:332
  (2 shorter events, 0.0 us)
Async XLA Ops:
  0.6 37.6 %copy-start = (bf16[768,512]{1,0:T(8,128)(2,1)S(1)}, bf16[768,512]{1,0:T(8,128)(2,1)}, u32[]{:S(2)}) copy-start(bf16[768,512]{1,0:T(8,128)(2,1)} %param.12) | copy-start | bytes 2359300
  2.9 49.5 %all-to-all-start = ((bf16[32,32,128]{2,1,0:T(8,128)(2,1)}), bf16[32,32,128]{2,1,0:T(8,128)(2,1)S(1)}, u32[]{:S(2)}, u32[]{:S(2)}) async-start(bf16[32,32,128]{2,1,0:T(8,128)(2,1)} %get-tuple-element.25), calls=%async_computation | async-start | bytes 524288 | tf_op jit(solution)/shard_map/all_to_all | solution.py:242
  19.3 7.9 %collective-permute-start = (bf16[512,128]{1,0:T(8,128)(2,1)}, bf16[512,128]{1,0:T(8,128)(2,1)S(1)}, u32[]{:S(2)}, u32[]{:S(2)}) collective-permute-start(bf16[512,128]{1,0:T(8,128)(2,1)} %get-tuple-element.27), channel_id=1, source_target_pairs={{0,8},{8,0},{16,24},{24,16},{1,9},{9,1},{17,25},{25,17},{2,10},{10... | collective-permute-start | bytes 393224 | tf_op jit(solution)/shard_map/ppermute | solution.py:236
  21.5 7.1 %collective-permute-start.1 = (bf16[512,128]{1,0:T(8,128)(2,1)}, bf16[512,128]{1,0:T(8,128)(2,1)S(1)}, u32[]{:S(2)}, u32[]{:S(2)}) collective-permute-start(bf16[512,128]{1,0:T(8,128)(2,1)} %get-tuple-element.28), channel_id=1, source_target_pairs={{0,16},{8,24},{16,0},{24,8},{1,17},{9,25},{17,1},{25,9},{2,18},{10... | collective-permute-start | bytes 393224 | tf_op jit(solution)/shard_map/ppermute | solution.py:236
  24.9 8.0 %collective-permute-start.2 = (bf16[512,128]{1,0:T(8,128)(2,1)}, bf16[512,128]{1,0:T(8,128)(2,1)S(1)}, u32[]{:S(2)}, u32[]{:S(2)}) collective-permute-start(bf16[512,128]{1,0:T(8,128)(2,1)} %get-tuple-element.29), channel_id=1, source_target_pairs={{0,24},{8,16},{16,8},{24,0},{1,25},{9,17},{17,9},{25,1},{2,26},{10... | collective-permute-start | bytes 393224 | tf_op jit(solution)/shard_map/ppermute | solution.py:236
  27.2 5.6 %copy-start.5 = (bf16[512,128]{1,0:T(8,128)(2,1)}, bf16[512,128]{1,0:T(8,128)(2,1)S(1)}, u32[]{:S(2)}) copy-start(bf16[512,128]{1,0:T(8,128)(2,1)S(1)} %collective-permute-done.refs_1_) | copy-start | bytes 393220
  28.6 4.3 %copy-start.6 = (bf16[512,128]{1,0:T(8,128)(2,1)}, bf16[512,128]{1,0:T(8,128)(2,1)S(1)}, u32[]{:S(2)}) copy-start(bf16[512,128]{1,0:T(8,128)(2,1)S(1)} %collective-permute-done.1.refs_2_) | copy-start | bytes 393220
  32.9 0.7 copy-start.7
  35.5 9.9 %collective-permute-start.3 = (bf16[768,128]{1,0:T(8,128)(2,1)}, bf16[768,128]{1,0:T(8,128)(2,1)S(1)}, u32[]{:S(2)}, u32[]{:S(2)}) collective-permute-start(bf16[768,128]{1,0:T(8,128)(2,1)} %get-tuple-element.31), channel_id=1, source_target_pairs={{0,32},{32,64},{64,96},{96,128},{128,160},{160,192},{192,224},{224... | collective-permute-start | bytes 589832 | tf_op jit(solution)/shard_map/ppermute | solution.py:231
  45.4 0.7 copy-start.3
  52.4 0.7 copy-start.1
  58.8 53.2 %all-to-all-start.1 = ((bf16[64,16,128]{2,1,0:T(8,128)(2,1)}), bf16[64,16,128]{2,1,0:T(8,128)(2,1)S(1)}, u32[]{:S(2)}, u32[]{:S(2)}) async-start(bf16[64,16,128]{2,1,0:T(8,128)(2,1)} %bitcast.5), calls=%async_computation.1 | async-start | bytes 524288 | tf_op jit(solution)/shard_map/all_to_all | solution.py:242
  70.0 18.5 %collective-permute-start.4 = (bf16[768,128]{1,0:T(8,128)(2,1)}, bf16[768,128]{1,0:T(8,128)(2,1)S(1)}, u32[]{:S(2)}, u32[]{:S(2)}) collective-permute-start(bf16[768,128]{1,0:T(8,128)(2,1)} %get-tuple-element.35), channel_id=1, source_target_pairs={{32,0},{64,32},{96,64},{128,96},{160,128},{192,160},{224,192},{256... | collective-permute-start | bytes 589832 | tf_op jit(solution)/shard_map/ppermute | solution.py:231
  88.4 0.7 copy-start.4
  95.1 8.4 %collective-permute-start.5 = (bf16[512,128]{1,0:T(8,128)(2,1)}, bf16[512,128]{1,0:T(8,128)(2,1)S(1)}, u32[]{:S(2)}, u32[]{:S(2)}) collective-permute-start(bf16[512,128]{1,0:T(8,128)(2,1)} %get-tuple-element.39), channel_id=1, source_target_pairs={{0,8},{8,0},{16,24},{24,16},{1,9},{9,1},{17,25},{25,17},{2,10},{10... | collective-permute-start | bytes 393224 | tf_op jit(solution)/shard_map/ppermute | solution.py:236
  97.9 7.8 %collective-permute-start.6 = (bf16[512,128]{1,0:T(8,128)(2,1)}, bf16[512,128]{1,0:T(8,128)(2,1)S(1)}, u32[]{:S(2)}, u32[]{:S(2)}) collective-permute-start(bf16[512,128]{1,0:T(8,128)(2,1)} %get-tuple-element.40), channel_id=1, source_target_pairs={{0,16},{8,24},{16,0},{24,8},{1,17},{9,25},{17,1},{25,9},{2,18},{10... | collective-permute-start | bytes 393224 | tf_op jit(solution)/shard_map/ppermute | solution.py:236
  101.6 7.5 %collective-permute-start.7 = (bf16[512,128]{1,0:T(8,128)(2,1)}, bf16[512,128]{1,0:T(8,128)(2,1)S(1)}, u32[]{:S(2)}, u32[]{:S(2)}) collective-permute-start(bf16[512,128]{1,0:T(8,128)(2,1)} %get-tuple-element.41), channel_id=1, source_target_pairs={{0,24},{8,16},{16,8},{24,0},{1,25},{9,17},{17,9},{25,1},{2,26},{10... | collective-permute-start | bytes 393224 | tf_op jit(solution)/shard_map/ppermute | solution.py:236
  103.5 5.6 %copy-start.8 = (bf16[512,128]{1,0:T(8,128)(2,1)}, bf16[512,128]{1,0:T(8,128)(2,1)S(1)}, u32[]{:S(2)}) copy-start(bf16[512,128]{1,0:T(8,128)(2,1)S(1)} %collective-permute-done.5.refs_1_) | copy-start | bytes 393220
  105.7 3.5 %copy-start.9 = (bf16[512,128]{1,0:T(8,128)(2,1)}, bf16[512,128]{1,0:T(8,128)(2,1)S(1)}, u32[]{:S(2)}) copy-start(bf16[512,128]{1,0:T(8,128)(2,1)S(1)} %collective-permute-done.6.refs_2_) | copy-start | bytes 393220
  109.1 0.6 copy-start.10
  112.0 0.7 copy-start.2

commit v3 on v0

v3 whole, which is shorter than its diff:
```python
import functools
import math

import jax
import jax.numpy as jnp
import ml_dtypes
import numpy as np
from jax import lax
from jax.experimental import pallas as pl
from jax.experimental.pallas import tpu as pltpu
from jax.sharding import Mesh, PartitionSpec as P

BF16 = jnp.bfloat16
F32 = jnp.float32
AXES = ("chip", "core", "ch")
CORES = 2
CTX = ("chip", "core")

PERIOD = 1024
REACH = 3
BINS = 128
STEPS = PERIOD // 2 // BINS
ROWS = 2 * BINS
SLOT = 16
LANES = 128
MIB = 1024 * 1024


def make_tables(lags, share):
    freq = np.arange(PERIOD // 2)[:, None]
    place = np.arange(PERIOD)[None, :]
    angle = math.pi / PERIOD * ((2 * freq + 1) * place % (2 * PERIOD)).astype(np.float64)
    both = np.stack([np.cos(angle), -np.sin(angle)])
    both = both.reshape(2, STEPS, BINS, PERIOD).transpose(1, 0, 2, 3).reshape(PERIOD, PERIOD)
    by_slot = np.zeros((CORES, lags // share // CORES, SLOT, PERIOD))
    by_slot[:, :, :share] = (
        both.T[:lags].reshape(-1, CORES, share, PERIOD).transpose(1, 0, 2, 3)
    )
    tables = both, both.T, by_slot.reshape(-1, PERIOD)
    return tuple(np.ascontiguousarray(t).astype(ml_dtypes.bfloat16) for t in tables)


def dot(a, b):
    return jnp.dot(a, b, preferred_element_type=F32)


def product(a, b):
    return (a[...].astype(F32) * b[...].astype(F32)).astype(BF16)


def lane_block(index):
    return slice(index * LANES, (index + 1) * LANES)


def spectrum(table, spans):
    rows = spans[0].shape[0]
    return sum(
        dot(table[:, i * rows : (i + 1) * rows], span[...]) for i, span in enumerate(spans)
    )


def halves(spec):
    return spec[:BINS], spec[BINS:]


def accumulate(step, total, part):
    @pl.when(step == 0)
    def _():
        total[...] = part

    @pl.when(step > 0)
    def _():
        total[...] += part


def prep_kernel(key, value, out_grad, mixed, pieces):
    mixed[...] = product(key, value)
    width = pieces.shape[2]
    for piece in range(pieces.shape[0]):
        pieces[piece] = out_grad[:, piece * width : (piece + 1) * width]


def pack(slot, share):
    rest = SLOT - share
    count = share // rest
    last = slot[:share, count * LANES :]
    return jnp.concatenate(
        [
            jnp.concatenate(
                [slot[:share, lane_block(i)], last[i * rest : (i + 1) * rest]], axis=0
            )
            for i in range(count)
        ],
        axis=1,
    )


def unpack(packed, share):
    rest = SLOT - share
    count = share // rest
    last = jnp.concatenate([packed[share:, lane_block(i)] for i in range(count)], axis=0)
    return jnp.concatenate([packed[:share], last], axis=1)


def cross_kernel(scale, share, core, table, inverse, *refs):
    spans, (cotangent, gate, grad, mine, theirs, total) = refs[: REACH + 1], refs[REACH + 1 :]
    step = pl.program_id(0)

    @pl.when(step == 0)
    def _():
        grad[...] = product(cotangent, gate)

    rows = grad.shape[0]
    x_re, x_im = halves(spectrum(table, spans))
    g_re, g_im = halves(dot(table[:, REACH * rows :], grad[...]))
    y = jnp.concatenate([g_re * x_re + g_im * x_im, g_im * x_re - g_re * x_im]).astype(BF16)
    accumulate(step, total, dot(inverse[...], y))

    @pl.when(step == STEPS - 1)
    def _():
        count = mine.shape[0]
        for out, owner in ((mine, core[0]), (theirs, 1 - core[0])):

            @pl.loop(0, count)
            def _(slot):
                at = pl.multiple_of((owner * count + slot) * SLOT, SLOT)
                out[slot] = pack(total[pl.ds(at, SLOT), :] * scale, share).astype(BF16)


def add_kernel(a, b, out):
    out[...] = (a[...].astype(F32) + b[...].astype(F32)).astype(BF16)


def sum_kernel(parts, out):
    total = parts[0].astype(F32)
    for source in range(1, parts.shape[0]):
        total += parts[source].astype(F32)
    out[...] = unpack(total, out.shape[0])


def rest_kernel(scale, table, first, last, taps, *refs):
    early, late = refs[: REACH + 1], refs[REACH + 1 : 2 * REACH + 2]
    cotangent, key, value, gate_grad, key_grad, value_grad, conv, back = refs[2 * REACH + 2 :]
    step = pl.program_id(0)
    f_re, f_im = halves(dot(table[:, : taps.shape[0]], taps[...]))
    x_re, x_im = halves(spectrum(table, early))
    y = jnp.concatenate([f_re * x_re - f_im * x_im, f_re * x_im + f_im * x_re]).astype(BF16)
    accumulate(step, conv, dot(last[...], y))
    g_re, g_im = halves(spectrum(table, late))
    y = jnp.concatenate([f_re * g_re + f_im * g_im, f_re * g_im - f_im * g_re]).astype(BF16)
    accumulate(step, back, dot(first[...], y))

    @pl.when(step == STEPS - 1)
    def _():
        gate_grad[...] = (cotangent[...].astype(F32) * (conv[...] * scale)).astype(BF16)
        grad_mixed = back[...] * scale
        key_grad[...] = (grad_mixed * value[...].astype(F32)).astype(BF16)
        value_grad[...] = (grad_mixed * key[...].astype(F32)).astype(BF16)


def whole(shape):
    return pl.BlockSpec(shape, lambda *_: (0,) * len(shape))


def shaped(shape, dtype=BF16):
    return jax.ShapeDtypeStruct(shape, dtype)


def call(kernel, in_specs, out_specs, out_shape, scratch=(), steps=1):
    return pl.pallas_call(
        kernel,
        grid=(steps,),
        in_specs=in_specs,
        out_specs=out_specs,
        out_shape=out_shape,
        scratch_shapes=scratch,
        compiler_params=pltpu.CompilerParams(
            dimension_semantics=("arbitrary",), vmem_limit_bytes=VMEM_LIMIT
        ),
        cost_estimate=pl.CostEstimate(flops=0, bytes_accessed=0, transcendentals=0),
    )


VMEM_LIMIT = 56 * MIB


def shift(value, steps):
    count = lax.axis_size(CTX)
    first, last = max(0, -steps), min(count, count - steps)
    return lax.ppermute(value, CTX, [(i, i + steps) for i in range(first, last)])


def exchange(value, axes):
    return lax.all_to_all(value, axes, split_axis=0, concat_axis=0, tiled=True)


def body(forward, inverse, slotted, gate_input, key_input, value_input, out_grad, filter_taps):
    lags, width = filter_taps.shape
    held, channels = out_grad.shape
    local = gate_input.shape
    span = local[0]
    chips = lax.axis_size("chip")
    share = lags // chips // CORES
    norm = 2.0 / PERIOD / lags**0.5
    pieces = (channels // width, held, width)
    packed = (chips, SLOT, width * share // SLOT)
    scalar = pl.BlockSpec(memory_space=pltpu.SMEM)

    mixed, cotangent = call(
        prep_kernel,
        [whole(local)] * 2 + [whole(out_grad.shape)],
        [whole(local), whole(pieces)],
        [shaped(local), shaped(pieces)],
    )(key_input, value_input, out_grad)
    early = [shift(mixed, steps) for steps in range(REACH, 0, -1)] + [mixed]
    cotangent = exchange(cotangent, "ch").reshape(local)

    table = pl.BlockSpec((ROWS, PERIOD), lambda step: (step, 0))
    grad, mine, theirs = call(
        functools.partial(cross_kernel, norm, share),
        [scalar, table, pl.BlockSpec((slotted.shape[0], ROWS), lambda step: (0, step))]
        + [whole(local)] * (REACH + 3),
        [whole(local), whole(packed), whole(packed)],
        [shaped(local), shaped(packed), shaped(packed)],
        [pltpu.VMEM((slotted.shape[0], width), F32)],
        STEPS,
    )(lax.axis_index("core").reshape(1), forward, slotted, *early, cotangent, gate_input)
    theirs = lax.ppermute(theirs, "core", [(i, 1 - i) for i in range(CORES)])
    mine = call(add_kernel, [whole(packed)] * 2, whole(packed), shaped(packed))(mine, theirs)
    parts = exchange(mine, "chip")
    filter_grad = call(
        sum_kernel, [whole(packed)], whole((share, width)), shaped((share, width), F32)
    )(parts)

    late = [grad] + [shift(grad, -steps) for steps in range(1, REACH + 1)]
    gate_grad, key_grad, value_grad = call(
        functools.partial(rest_kernel, norm),
        [
            table,
            pl.BlockSpec((span, ROWS), lambda step: (0, step)),
            pl.BlockSpec((span, ROWS), lambda step: (REACH, step)),
            whole((lags, width)),
        ]
        + [whole(local)] * (2 * REACH + 5),
        [whole(local)] * 3,
        [shaped(local)] * 3,
        [pltpu.VMEM(local, F32)] * 2,
        STEPS,
    )(forward, inverse, inverse, filter_taps, *early, *late, cotangent, key_input, value_input)
    return gate_grad, key_grad, value_grad, filter_grad


def solution(mesh):
    count, groups = mesh.devices.shape
    split = Mesh(mesh.devices.reshape(count // CORES, CORES, groups), AXES)
    spans = P(CTX, "ch")
    mapped = jax.shard_map(
        body,
        mesh=split,
        in_specs=(P(), P(), P(), spans, spans, spans, P(CTX + ("ch",), None), P(None, "ch")),
        out_specs=(spans, spans, spans, spans),
        check_vma=False,
    )

    def run(gate_input, key_input, value_input, out_grad, filter_taps):
        lags = filter_taps.shape[0]
        tables = make_tables(lags, lags // count)
        return mapped(*tables, gate_input, key_input, value_input, out_grad, filter_taps)

    return run
```

time: 959 us -> 120 us (0.13)
  the two profiles are of different devices: /device:TPU:1 before, /device:TPU:115 now
where the time goes in v3:
time: 120 us; the launch traced here: 119 us
  starting transfers between devices  53.7 us (45%)
  waiting for transfers between devices  38.5 us (32%)
  Pallas kernels  23.5 us (20%)
  local copies, waits for them, and re-layouts  2.95 us (2%)
    ppermute x6, waiting for transfers between devices, shift(): lax.ppermute(value, CTX, [(i, i + steps) for i in range(first, last)])  36.7 us
    all_to_all x2, starting transfers between devices, exchange(): return lax.all_to_all(value, axes, split_axis=0, concat_axis=0, tiled=True)  30.7 us
    ppermute x6, starting transfers between devices, shift(): lax.ppermute(value, CTX, [(i, i + steps) for i in range(first, last)])  18.5 us
    pallas_call x1, Pallas kernels, body(): call(functools.partial(rest_kernel, norm), [table, pl.BlockSpec((span, RO...  10 us
    pallas_call x1, Pallas kernels, body(): call(functools.partial(cross_kernel, norm, share), [scalar, table, pl.Blo...  7.91 us
    ppermute x1, starting transfers between devices, body(): theirs = lax.ppermute(theirs, 'core', [(i, 1 - i) for i in range(CORES)])  4.56 us
    unnamed x18, local copies, waits for them, and re-layouts  2.95 us
  transfers between devices with their start and end apart: 9, of which 8 were waited for; matrix products, arithmetic and copies ran while one was open for 0% of the time, Pallas kernels for 8%

profile of v3, /device:TPU:115, one launch (start us, length us, event | category | flops | bytes accessed | tf_op | source)
XLA Modules:
  0.0 119.4 jit_solution(18289578269144284604)
XLA Ops:
  0.6 1.9 %shard_map.111 = (bf16[256,512]{1,0:T(8,128)(2,1)}, bf16[8,32,512]{2,1,0:T(8,128)(2,1)}) custom-call(bf16[256,512]{1,0:T(8,128)(2,1)} %refs_9_.1, bf16[256,512]{1,0:T(8,128)(2,1)} %refs_10_.1, bf16[32,4096]{1,0:T(8,128)(2,1)} %out_grad.1), custom_call_target="tpu_custom_call" | custom-call | tf_op jit(solution)/shard_map/pallas_call | solution.py:209
  2.6 14.8 %all-to-all-start = ((bf16[8,32,512]{2,1,0:T(8,128)(2,1)}), bf16[8,32,512]{2,1,0:T(8,128)(2,1)S(1)}, u32[]{:S(2)}, u32[]{:S(2)}) async-start(bf16[8,32,512]{2,1,0:T(8,128)(2,1)} %get-tuple-element.13), calls=%async_computation | async-start | bytes 524288 | tf_op jit(solution)/shard_map/all_to_all | solution.py:194
  17.4 3.5 %collective-permute-start = (bf16[256,512]{1,0:T(8,128)(2,1)}, bf16[256,512]{1,0:T(8,128)(2,1)S(1)}, u32[]{:S(2)}, u32[]{:S(2)}) collective-permute-start(bf16[256,512]{1,0:T(8,128)(2,1)} %get-tuple-element.12.refs_3_), channel_id=1, source_target_pairs={{0,24},{8,32},{16,40},{24,48},{32,56},{40,64},{48,72},{56,80},{64,... | collective-permute-start | bytes 786440 | tf_op jit(solution)/shard_map/ppermute | solution.py:190
  20.9 3.8 %collective-permute-start.1 = (bf16[256,512]{1,0:T(8,128)(2,1)}, bf16[256,512]{1,0:T(8,128)(2,1)S(1)}, u32[]{:S(2)}, u32[]{:S(2)}) collective-permute-start(bf16[256,512]{1,0:T(8,128)(2,1)} %get-tuple-element.12.refs_3_), channel_id=1, source_target_pairs={{0,16},{8,24},{16,32},{24,40},{32,48},{40,56},{48,64},{56,72},{64,... | collective-permute-start | bytes 786440 | tf_op jit(solution)/shard_map/ppermute | solution.py:190
  24.8 1.9 %collective-permute-start.2 = (bf16[256,512]{1,0:T(8,128)(2,1)}, bf16[256,512]{1,0:T(8,128)(2,1)S(1)}, u32[]{:S(2)}, u32[]{:S(2)}) collective-permute-start(bf16[256,512]{1,0:T(8,128)(2,1)} %get-tuple-element.12.refs_3_), channel_id=1, source_target_pairs={{0,8},{8,16},{16,24},{24,32},{32,40},{40,48},{48,56},{56,64},{64,7... | collective-permute-start | bytes 786440 | tf_op jit(solution)/shard_map/ppermute | solution.py:190
  26.7 3.9 %collective-permute-done.refs_0_ = bf16[256,512]{1,0:T(8,128)(2,1)S(1)} collective-permute-done((bf16[256,512]{1,0:T(8,128)(2,1)}, bf16[256,512]{1,0:T(8,128)(2,1)S(1)}, u32[]{:S(2)}, u32[]{:S(2)}) %collective-permute-start) | collective-permute-done | bytes 262176 | tf_op jit(solution)/shard_map/ppermute | solution.py:190
  30.6 0.0 copy-start.2
  30.6 3.4 %collective-permute-done.1.refs_1_ = bf16[256,512]{1,0:T(8,128)(2,1)S(1)} collective-permute-done((bf16[256,512]{1,0:T(8,128)(2,1)}, bf16[256,512]{1,0:T(8,128)(2,1)S(1)}, u32[]{:S(2)}, u32[]{:S(2)}) %collective-permute-start.1) | collective-permute-done | bytes 262176 | tf_op jit(solution)/shard_map/ppermute | solution.py:190
  33.9 0.0 copy-start.3
  33.9 1.8 %collective-permute-done.2.refs_2_ = bf16[256,512]{1,0:T(8,128)(2,1)S(1)} collective-permute-done((bf16[256,512]{1,0:T(8,128)(2,1)}, bf16[256,512]{1,0:T(8,128)(2,1)S(1)}, u32[]{:S(2)}, u32[]{:S(2)}) %collective-permute-start.2) | collective-permute-done | bytes 262176 | tf_op jit(solution)/shard_map/ppermute | solution.py:190
  35.7 0.0 copy-start.4
  35.7 0.2 all-to-all-done
  35.9 0.0 copy-start
  35.9 0.0 copy-done.2
  35.9 0.0 copy-done.3
  35.9 0.5 copy-done.4
  36.4 0.2 copy-done
  36.6 7.9 %shard_map.112 = (bf16[256,512]{1,0:T(8,128)(2,1)}, bf16[32,16,384]{2,1,0:T(8,128)(2,1)}, bf16[32,16,384]{2,1,0:T(8,128)(2,1)}) custom-call(s32[1]{0:T(128)} %bitcast.core, bf16[1024,1024]{1,0:T(8,128)(2,1)} %constant.12.clone.table, bf16[1024,1024]{1,0:T(8,128)(2,1)} %constant.14.clone.inverse, bf16[256,512]{1,0:T(8,128)(2,1)} %copy-done.2, ...), custom_call_target="tpu_custom_call" | custom-call | tf_op jit(solution)/shard_map/pallas_call | solution.py:219
  44.5 4.6 %collective-permute-start.6 = (bf16[32,16,384]{2,1,0:T(8,128)(2,1)}, bf16[32,16,384]{2,1,0:T(8,128)(2,1)S(1)}, u32[]{:S(2)}, u32[]{:S(2)}) collective-permute-start(bf16[32,16,384]{2,1,0:T(8,128)(2,1)} %get-tuple-element.19), channel_id=1, source_target_pairs={{0,8},{8,0},{1,9},{9,1},{2,10},{10,2},{3,11},{11,3},{4,12},{12,4},... | collective-permute-start | bytes 1179656 | tf_op jit(solution)/shard_map/ppermute | solution.py:228
  49.1 1.5 %collective-permute-done.6.b = bf16[32,16,384]{2,1,0:T(8,128)(2,1)S(1)} collective-permute-done((bf16[32,16,384]{2,1,0:T(8,128)(2,1)}, bf16[32,16,384]{2,1,0:T(8,128)(2,1)S(1)}, u32[]{:S(2)}, u32[]{:S(2)}) %collective-permute-start.6) | collective-permute-done | bytes 393248 | tf_op jit(solution)/shard_map/ppermute | solution.py:228
  50.6 0.0 copy-start.5
  50.6 0.8 copy-done.5
  51.4 2.0 %shard_map.114 = bf16[32,16,384]{2,1,0:T(8,128)(2,1)} custom-call(bf16[32,16,384]{2,1,0:T(8,128)(2,1)} %get-tuple-element.18.a, bf16[32,16,384]{2,1,0:T(8,128)(2,1)} %copy-done.5), custom_call_target="tpu_custom_call" | custom-call | tf_op jit(solution)/shard_map/pallas_call | solution.py:229
  53.4 15.9 %all-to-all-start.1 = ((bf16[32,16,384]{2,1,0:T(8,128)(2,1)}), bf16[32,16,384]{2,1,0:T(8,128)(2,1)S(1)}, u32[]{:S(2)}, u32[]{:S(2)}) async-start(bf16[32,16,384]{2,1,0:T(8,128)(2,1)} %shard_map.114), calls=%async_computation.1 | async-start | bytes 786432 | tf_op jit(solution)/shard_map/all_to_all | solution.py:194
  69.2 2.8 %collective-permute-start.3 = (bf16[256,512]{1,0:T(8,128)(2,1)}, bf16[256,512]{1,0:T(8,128)(2,1)S(1)}, u32[]{:S(2)}, u32[]{:S(2)}) collective-permute-start(bf16[256,512]{1,0:T(8,128)(2,1)} %get-tuple-element.14.refs_4_), channel_id=1, source_target_pairs={{8,0},{16,8},{24,16},{32,24},{40,32},{48,40},{56,48},{64,56},{72,6... | collective-permute-start | bytes 786440 | tf_op jit(solution)/shard_map/ppermute | solution.py:190
  72.1 2.2 %collective-permute-start.4 = (bf16[256,512]{1,0:T(8,128)(2,1)}, bf16[256,512]{1,0:T(8,128)(2,1)S(1)}, u32[]{:S(2)}, u32[]{:S(2)}) collective-permute-start(bf16[256,512]{1,0:T(8,128)(2,1)} %get-tuple-element.14.refs_4_), channel_id=1, source_target_pairs={{16,0},{24,8},{32,16},{40,24},{48,32},{56,40},{64,48},{72,56},{80,... | collective-permute-start | bytes 786440 | tf_op jit(solution)/shard_map/ppermute | solution.py:190
  74.3 4.2 %collective-permute-start.5 = (bf16[256,512]{1,0:T(8,128)(2,1)}, bf16[256,512]{1,0:T(8,128)(2,1)S(1)}, u32[]{:S(2)}, u32[]{:S(2)}) collective-permute-start(bf16[256,512]{1,0:T(8,128)(2,1)} %get-tuple-element.14.refs_4_), channel_id=1, source_target_pairs={{24,0},{32,8},{40,16},{48,24},{56,32},{64,40},{72,48},{80,56},{88,... | collective-permute-start | bytes 786440 | tf_op jit(solution)/shard_map/ppermute | solution.py:190
  78.5 1.0 collective-permute-done.3.refs_5_
  79.5 0.0 copy-start.6
  79.5 4.5 %collective-permute-done.4.refs_6_ = bf16[256,512]{1,0:T(8,128)(2,1)S(1)} collective-permute-done((bf16[256,512]{1,0:T(8,128)(2,1)}, bf16[256,512]{1,0:T(8,128)(2,1)S(1)}, u32[]{:S(2)}, u32[]{:S(2)}) %collective-permute-start.4) | collective-permute-done | bytes 262176 | tf_op jit(solution)/shard_map/ppermute | solution.py:190
  84.0 0.0 copy-start.7
  84.0 22.2 %collective-permute-done.5.refs_7_ = bf16[256,512]{1,0:T(8,128)(2,1)S(1)} collective-permute-done((bf16[256,512]{1,0:T(8,128)(2,1)}, bf16[256,512]{1,0:T(8,128)(2,1)S(1)}, u32[]{:S(2)}, u32[]{:S(2)}) %collective-permute-start.5) | collective-permute-done | bytes 262176 | tf_op jit(solution)/shard_map/ppermute | solution.py:190
  106.2 0.0 copy-done.6
  106.2 0.0 copy-done.7
  106.2 0.0 copy-start.8
  106.2 0.7 copy-done.8
  106.9 10.0 %shard_map.113 = (bf16[256,512]{1,0:T(8,128)(2,1)}, bf16[256,512]{1,0:T(8,128)(2,1)}, bf16[256,512]{1,0:T(8,128)(2,1)}) custom-call(bf16[1024,1024]{1,0:T(8,128)(2,1)} %constant.12.clone.table, bf16[1024,1024]{1,0:T(8,128)(2,1)} %constant.13.clone.first.last, bf16[1024,1024]{1,0:T(8,128)(2,1)} %constant.13.clone.first.last, bf16[768,512]{1,0:T(8,128)(2,1)} %taps.1, ...), custom_call_target="tpu_custom_call" | custom-call | tf_op jit(solution)/shard_map/pallas_call | solution.py:236
  116.9 0.0 all-to-all-done.1.parts
  116.9 0.0 copy-start.1
  116.9 0.7 copy-done.1
  117.7 1.7 %shard_map.115 = f32[12,512]{1,0:T(8,128)} custom-call(bf16[32,16,384]{2,1,0:T(8,128)(2,1)} %copy-done.1), custom_call_target="tpu_custom_call" | custom-call | tf_op jit(solution)/shard_map/pallas_call | solution.py:231
Async XLA Ops:
  2.6 33.3 %all-to-all-start = ((bf16[8,32,512]{2,1,0:T(8,128)(2,1)}), bf16[8,32,512]{2,1,0:T(8,128)(2,1)S(1)}, u32[]{:S(2)}, u32[]{:S(2)}) async-start(bf16[8,32,512]{2,1,0:T(8,128)(2,1)} %get-tuple-element.13), calls=%async_computation | async-start | bytes 524288 | tf_op jit(solution)/shard_map/all_to_all | solution.py:194
  17.4 13.2 %collective-permute-start = (bf16[256,512]{1,0:T(8,128)(2,1)}, bf16[256,512]{1,0:T(8,128)(2,1)S(1)}, u32[]{:S(2)}, u32[]{:S(2)}) collective-permute-start(bf16[256,512]{1,0:T(8,128)(2,1)} %get-tuple-element.12.refs_3_), channel_id=1, source_target_pairs={{0,24},{8,32},{16,40},{24,48},{32,56},{40,64},{48,72},{56,80},{64,... | collective-permute-start | bytes 786440 | tf_op jit(solution)/shard_map/ppermute | solution.py:190
  20.9 13.0 %collective-permute-start.1 = (bf16[256,512]{1,0:T(8,128)(2,1)}, bf16[256,512]{1,0:T(8,128)(2,1)S(1)}, u32[]{:S(2)}, u32[]{:S(2)}) collective-permute-start(bf16[256,512]{1,0:T(8,128)(2,1)} %get-tuple-element.12.refs_3_), channel_id=1, source_target_pairs={{0,16},{8,24},{16,32},{24,40},{32,48},{40,56},{48,64},{56,72},{64,... | collective-permute-start | bytes 786440 | tf_op jit(solution)/shard_map/ppermute | solution.py:190
  24.8 11.0 %collective-permute-start.2 = (bf16[256,512]{1,0:T(8,128)(2,1)}, bf16[256,512]{1,0:T(8,128)(2,1)S(1)}, u32[]{:S(2)}, u32[]{:S(2)}) collective-permute-start(bf16[256,512]{1,0:T(8,128)(2,1)} %get-tuple-element.12.refs_3_), channel_id=1, source_target_pairs={{0,8},{8,16},{16,24},{24,32},{32,40},{40,48},{48,56},{56,64},{64,7... | collective-permute-start | bytes 786440 | tf_op jit(solution)/shard_map/ppermute | solution.py:190
  30.6 5.4 %copy-start.2 = (bf16[256,512]{1,0:T(8,128)(2,1)}, bf16[256,512]{1,0:T(8,128)(2,1)S(1)}, u32[]{:S(2)}) copy-start(bf16[256,512]{1,0:T(8,128)(2,1)S(1)} %collective-permute-done.refs_0_) | copy-start | bytes 786436
  33.9 2.0 %copy-start.3 = (bf16[256,512]{1,0:T(8,128)(2,1)}, bf16[256,512]{1,0:T(8,128)(2,1)S(1)}, u32[]{:S(2)}) copy-start(bf16[256,512]{1,0:T(8,128)(2,1)S(1)} %collective-permute-done.1.refs_1_) | copy-start | bytes 786436
  35.7 0.7 copy-start.4
  35.9 0.7 copy-start
  44.5 6.1 %collective-permute-start.6 = (bf16[32,16,384]{2,1,0:T(8,128)(2,1)}, bf16[32,16,384]{2,1,0:T(8,128)(2,1)S(1)}, u32[]{:S(2)}, u32[]{:S(2)}) collective-permute-start(bf16[32,16,384]{2,1,0:T(8,128)(2,1)} %get-tuple-element.19), channel_id=1, source_target_pairs={{0,8},{8,0},{1,9},{9,1},{2,10},{10,2},{3,11},{11,3},{4,12},{12,4},... | collective-permute-start | bytes 1179656 | tf_op jit(solution)/shard_map/ppermute | solution.py:228
  50.6 0.8 copy-start.5
  53.4 63.6 %all-to-all-start.1 = ((bf16[32,16,384]{2,1,0:T(8,128)(2,1)}), bf16[32,16,384]{2,1,0:T(8,128)(2,1)S(1)}, u32[]{:S(2)}, u32[]{:S(2)}) async-start(bf16[32,16,384]{2,1,0:T(8,128)(2,1)} %shard_map.114), calls=%async_computation.1 | async-start | bytes 786432 | tf_op jit(solution)/shard_map/all_to_all | solution.py:194
  69.2 10.2 %collective-permute-start.3 = (bf16[256,512]{1,0:T(8,128)(2,1)}, bf16[256,512]{1,0:T(8,128)(2,1)S(1)}, u32[]{:S(2)}, u32[]{:S(2)}) collective-permute-start(bf16[256,512]{1,0:T(8,128)(2,1)} %get-tuple-element.14.refs_4_), channel_id=1, source_target_pairs={{8,0},{16,8},{24,16},{32,24},{40,32},{48,40},{56,48},{64,56},{72,6... | collective-permute-start | bytes 786440 | tf_op jit(solution)/shard_map/ppermute | solution.py:190
  72.1 11.9 %collective-permute-start.4 = (bf16[256,512]{1,0:T(8,128)(2,1)}, bf16[256,512]{1,0:T(8,128)(2,1)S(1)}, u32[]{:S(2)}, u32[]{:S(2)}) collective-permute-start(bf16[256,512]{1,0:T(8,128)(2,1)} %get-tuple-element.14.refs_4_), channel_id=1, source_target_pairs={{16,0},{24,8},{32,16},{40,24},{48,32},{56,40},{64,48},{72,56},{80,... | collective-permute-start | bytes 786440 | tf_op jit(solution)/shard_map/ppermute | solution.py:190
  74.3 31.9 %collective-permute-start.5 = (bf16[256,512]{1,0:T(8,128)(2,1)}, bf16[256,512]{1,0:T(8,128)(2,1)S(1)}, u32[]{:S(2)}, u32[]{:S(2)}) collective-permute-start(bf16[256,512]{1,0:T(8,128)(2,1)} %get-tuple-element.14.refs_4_), channel_id=1, source_target_pairs={{24,0},{32,8},{40,16},{48,24},{56,32},{64,40},{72,48},{80,56},{88,... | collective-permute-start | bytes 786440 | tf_op jit(solution)/shard_map/ppermute | solution.py:190
  79.5 26.7 %copy-start.6 = (bf16[256,512]{1,0:T(8,128)(2,1)}, bf16[256,512]{1,0:T(8,128)(2,1)S(1)}, u32[]{:S(2)}) copy-start(bf16[256,512]{1,0:T(8,128)(2,1)S(1)} %collective-permute-done.3.refs_5_) | copy-start | bytes 786436
  84.0 22.2 %copy-start.7 = (bf16[256,512]{1,0:T(8,128)(2,1)}, bf16[256,512]{1,0:T(8,128)(2,1)S(1)}, u32[]{:S(2)}) copy-start(bf16[256,512]{1,0:T(8,128)(2,1)S(1)} %collective-permute-done.4.refs_6_) | copy-start | bytes 786436
  106.2 0.7 copy-start.8
  116.9 0.8 copy-start.1

commit v4 on v3

--- a/solution.py
+++ b/solution.py
@@ -102,17 +102,31 @@
     return jnp.concatenate([packed[:share], last], axis=1)
 
 
-def cross_kernel(scale, share, core, table, inverse, *refs):
-    spans, (cotangent, gate, grad, mine, theirs, total) = refs[: REACH + 1], refs[REACH + 1 :]
+def conv_kernel(scale, table, last, taps, *refs):
+    spans, (conv, spec, total) = refs[: REACH + 1], refs[REACH + 1 :]
     step = pl.program_id(0)
+    f_re, f_im = halves(dot(table[:, : taps.shape[0]], taps[...]))
+    full = spectrum(table, spans)
+    spec[...] = full.astype(BF16)
+    x_re, x_im = halves(full)
+    y = jnp.concatenate([f_re * x_re - f_im * x_im, f_re * x_im + f_im * x_re]).astype(BF16)
+    accumulate(step, total, dot(last[...], y))
+
+    @pl.when(step == STEPS - 1)
+    def _():
+        conv[...] = total[...] * scale
+
+
+def cross_kernel(scale, share, core, table, inverse, spec, cotangent, gate, grad, *refs):
+    mine, theirs, total = refs
+    step = pl.program_id(0)
 
     @pl.when(step == 0)
     def _():
         grad[...] = product(cotangent, gate)
 
-    rows = grad.shape[0]
-    x_re, x_im = halves(spectrum(table, spans))
-    g_re, g_im = halves(dot(table[:, REACH * rows :], grad[...]))
+    x_re, x_im = halves(spec[...].astype(F32))
+    g_re, g_im = halves(dot(table[...], grad[...]))
     y = jnp.concatenate([g_re * x_re + g_im * x_im, g_im * x_re - g_re * x_im]).astype(BF16)
     accumulate(step, total, dot(inverse[...], y))
 
@@ -120,9 +134,7 @@
     def _():
         count = mine.shape[0]
         for out, owner in ((mine, core[0]), (theirs, 1 - core[0])):
-
-            @pl.loop(0, count)
-            def _(slot):
+            for slot in range(count):
                 at = pl.multiple_of((owner * count + slot) * SLOT, SLOT)
                 out[slot] = pack(total[pl.ds(at, SLOT), :] * scale, share).astype(BF16)
 
@@ -138,22 +150,19 @@
     out[...] = unpack(total, out.shape[0])
 
 
-def rest_kernel(scale, table, first, last, taps, *refs):
-    early, late = refs[: REACH + 1], refs[REACH + 1 : 2 * REACH + 2]
-    cotangent, key, value, gate_grad, key_grad, value_grad, conv, back = refs[2 * REACH + 2 :]
+def back_kernel(scale, table, first, taps, *refs):
+    spans = refs[: REACH + 1]
+    cotangent, conv, key, value, gate_grad, key_grad, value_grad, total = refs[REACH + 1 :]
     step = pl.program_id(0)
     f_re, f_im = halves(dot(table[:, : taps.shape[0]], taps[...]))
-    x_re, x_im = halves(spectrum(table, early))
-    y = jnp.concatenate([f_re * x_re - f_im * x_im, f_re * x_im + f_im * x_re]).astype(BF16)
-    accumulate(step, conv, dot(last[...], y))
-    g_re, g_im = halves(spectrum(table, late))
+    g_re, g_im = halves(spectrum(table, spans))
     y = jnp.concatenate([f_re * g_re + f_im * g_im, f_re * g_im - f_im * g_re]).astype(BF16)
-    accumulate(step, back, dot(first[...], y))
+    accumulate(step, total, dot(first[...], y))
 
     @pl.when(step == STEPS - 1)
     def _():
-        gate_grad[...] = (cotangent[...].astype(F32) * (conv[...] * scale)).astype(BF16)
-        grad_mixed = back[...] * scale
+        gate_grad[...] = (cotangent[...].astype(F32) * conv[...]).astype(BF16)
+        grad_mixed = total[...] * scale
         key_grad[...] = (grad_mixed * value[...].astype(F32)).astype(BF16)
         value_grad[...] = (grad_mixed * key[...].astype(F32)).astype(BF16)
 
@@ -166,7 +175,7 @@
     return jax.ShapeDtypeStruct(shape, dtype)
 
 
-def call(kernel, in_specs, out_specs, out_shape, scratch=(), steps=1):
+def call(kernel, in_specs, out_specs, out_shape, scratch=(), steps=1, flops=0):
     return pl.pallas_call(
         kernel,
         grid=(steps,),
@@ -177,11 +186,12 @@
         compiler_params=pltpu.CompilerParams(
             dimension_semantics=("arbitrary",), vmem_limit_bytes=VMEM_LIMIT
         ),
-        cost_estimate=pl.CostEstimate(flops=0, bytes_accessed=0, transcendentals=0),
+        cost_estimate=pl.CostEstimate(flops=flops, bytes_accessed=0, transcendentals=0),
     )
 
 
 VMEM_LIMIT = 56 * MIB
+FLOPS = 35_000_000_000
 
 
 def shift(value, steps):
@@ -216,15 +226,31 @@
     cotangent = exchange(cotangent, "ch").reshape(local)
 
     table = pl.BlockSpec((ROWS, PERIOD), lambda step: (step, 0))
+    bins = pl.BlockSpec((ROWS, width), lambda step: (step, 0))
+    conv, spec = call(
+        functools.partial(conv_kernel, norm),
+        [table, pl.BlockSpec((span, ROWS), lambda step: (REACH, step)), whole((lags, width))]
+        + [whole(local)] * (REACH + 1),
+        [whole(local), bins],
+        [shaped(local, F32), shaped((PERIOD, width))],
+        [pltpu.VMEM(local, F32)],
+        STEPS,
+        FLOPS,
+    )(forward, inverse, filter_taps, *early)
     grad, mine, theirs = call(
         functools.partial(cross_kernel, norm, share),
-        [scalar, table, pl.BlockSpec((slotted.shape[0], ROWS), lambda step: (0, step))]
-        + [whole(local)] * (REACH + 3),
+        [
+            scalar,
+            pl.BlockSpec((ROWS, span), lambda step: (step, REACH)),
+            pl.BlockSpec((slotted.shape[0], ROWS), lambda step: (0, step)),
+            bins,
+        ]
+        + [whole(local)] * 2,
         [whole(local), whole(packed), whole(packed)],
         [shaped(local), shaped(packed), shaped(packed)],
         [pltpu.VMEM((slotted.shape[0], width), F32)],
         STEPS,
-    )(lax.axis_index("core").reshape(1), forward, slotted, *early, cotangent, gate_input)
+    )(lax.axis_index("core").reshape(1), forward, slotted, spec, cotangent, gate_input)
     theirs = lax.ppermute(theirs, "core", [(i, 1 - i) for i in range(CORES)])
     mine = call(add_kernel, [whole(packed)] * 2, whole(packed), shaped(packed))(mine, theirs)
     parts = exchange(mine, "chip")
@@ -234,19 +260,15 @@
 
     late = [grad] + [shift(grad, -steps) for steps in range(1, REACH + 1)]
     gate_grad, key_grad, value_grad = call(
-        functools.partial(rest_kernel, norm),
-        [
-            table,
-            pl.BlockSpec((span, ROWS), lambda step: (0, step)),
-            pl.BlockSpec((span, ROWS), lambda step: (REACH, step)),
-            whole((lags, width)),
-        ]
-        + [whole(local)] * (2 * REACH + 5),
+        functools.partial(back_kernel, norm),
+        [table, pl.BlockSpec((span, ROWS), lambda step: (0, step)), whole((lags, width))]
+        + [whole(local)] * (REACH + 5),
         [whole(local)] * 3,
         [shaped(local)] * 3,
-        [pltpu.VMEM(local, F32)] * 2,
+        [pltpu.VMEM(local, F32)],
         STEPS,
-    )(forward, inverse, inverse, filter_taps, *early, *late, cotangent, key_input, value_input)
+        FLOPS,
+    )(forward, inverse, filter_taps, *late, cotangent, conv, key_input, value_input)
     return gate_grad, key_grad, value_grad, filter_grad
 
 

time: 120 us -> 110 us (0.917)
  the two profiles are of different devices: /device:TPU:115 before, /device:TPU:8 now
where the time goes in v4:
time: 110 us; the launch traced here: 109 us
  starting transfers between devices  54.1 us (49%)
  Pallas kernels  25.7 us (23%)
  waiting for transfers between devices  24.1 us (22%)
  local copies, waits for them, and re-layouts  4.48 us (4%)
    all_to_all x2, starting transfers between devices, exchange(): return lax.all_to_all(value, axes, split_axis=0, concat_axis=0, tiled=True)  35.5 us
    all_to_all x2, waiting for transfers between devices, exchange(): return lax.all_to_all(value, axes, split_axis=0, concat_axis=0, tiled=True)  24.1 us
    ppermute x6, starting transfers between devices, shift(): lax.ppermute(value, CTX, [(i, i + steps) for i in range(first, last)])  16.7 us
    pallas_call x1, Pallas kernels, body(): call(functools.partial(back_kernel, norm), [table, pl.BlockSpec((span, RO...  6.93 us
    pallas_call x1, Pallas kernels, body(): call(functools.partial(conv_kernel, norm), [table, pl.BlockSpec((span, RO...  6.6 us
    pallas_call x1, Pallas kernels, body(): call(functools.partial(cross_kernel, norm, share), [scalar, pl.BlockSpec(...  6.59 us
    unnamed x18, local copies, waits for them, and re-layouts  4.48 us
  transfers between devices with their start and end apart: 9, of which 2 were waited for; matrix products, arithmetic and copies ran while one was open for 0% of the time, Pallas kernels for 14%

profile of v4, /device:TPU:8, one launch (start us, length us, event | category | flops | bytes accessed | tf_op | source)
XLA Modules:
  0.0 109.2 jit_solution(6256294852692679669)
XLA Ops:
  0.6 1.9 %shard_map.111 = (bf16[256,512]{1,0:T(8,128)(2,1)}, bf16[8,32,512]{2,1,0:T(8,128)(2,1)}) custom-call(bf16[256,512]{1,0:T(8,128)(2,1)} %refs_6_.1, bf16[256,512]{1,0:T(8,128)(2,1)} %refs_7_.1, bf16[32,4096]{1,0:T(8,128)(2,1)} %out_grad.1), custom_call_target="tpu_custom_call" | custom-call | tf_op jit(solution)/shard_map/pallas_call | solution.py:219
  2.6 1.9 %collective-permute-start.2 = (bf16[256,512]{1,0:T(8,128)(2,1)}, bf16[256,512]{1,0:T(8,128)(2,1)S(1)}, u32[]{:S(2)}, u32[]{:S(2)}) collective-permute-start(bf16[256,512]{1,0:T(8,128)(2,1)} %get-tuple-element.14.refs_3_), channel_id=1, source_target_pairs={{0,8},{8,16},{16,24},{24,32},{32,40},{40,48},{48,56},{56,64},{64,7... | collective-permute-start | bytes 786440 | tf_op jit(solution)/shard_map/ppermute | solution.py:200
  4.5 3.5 %collective-permute-start.1 = (bf16[256,512]{1,0:T(8,128)(2,1)}, bf16[256,512]{1,0:T(8,128)(2,1)S(1)}, u32[]{:S(2)}, u32[]{:S(2)}) collective-permute-start(bf16[256,512]{1,0:T(8,128)(2,1)} %get-tuple-element.14.refs_3_), channel_id=1, source_target_pairs={{0,16},{8,24},{16,32},{24,40},{32,48},{40,56},{48,64},{56,72},{64,... | collective-permute-start | bytes 786440 | tf_op jit(solution)/shard_map/ppermute | solution.py:200
  8.0 4.2 %collective-permute-start = (bf16[256,512]{1,0:T(8,128)(2,1)}, bf16[256,512]{1,0:T(8,128)(2,1)S(1)}, u32[]{:S(2)}, u32[]{:S(2)}) collective-permute-start(bf16[256,512]{1,0:T(8,128)(2,1)} %get-tuple-element.14.refs_3_), channel_id=1, source_target_pairs={{0,24},{8,32},{16,40},{24,48},{32,56},{40,64},{48,72},{56,80},{64,... | collective-permute-start | bytes 786440 | tf_op jit(solution)/shard_map/ppermute | solution.py:200
  12.2 16.7 %all-to-all-start = ((bf16[8,32,512]{2,1,0:T(8,128)(2,1)}), bf16[8,32,512]{2,1,0:T(8,128)(2,1)S(1)}, u32[]{:S(2)}, u32[]{:S(2)}) async-start(bf16[8,32,512]{2,1,0:T(8,128)(2,1)} %get-tuple-element.16), calls=%async_computation | async-start | bytes 524288 | tf_op jit(solution)/shard_map/all_to_all | solution.py:204
  28.9 0.0 collective-permute-done.2.refs_2_
  28.9 0.0 copy-start.5
  28.9 0.0 collective-permute-done.1.refs_1_
  28.9 0.0 copy-start.7
  28.9 0.0 collective-permute-done.refs_0_
  28.9 0.7 copy-done.5
  29.6 0.1 copy-done.7
  29.6 0.0 copy-start.8
  29.7 0.7 copy-done.8
  30.4 6.6 %shard_map.112 = (f32[256,512]{1,0:T(8,128)}, bf16[1024,512]{1,0:T(8,128)(2,1)}) custom-call(bf16[1024,1024]{1,0:T(8,128)(2,1)} %constant.12.clone.table, bf16[1024,1024]{1,0:T(8,128)(2,1)} %constant.13.clone.last.first, bf16[768,512]{1,0:T(8,128)(2,1)} %taps.3, bf16[256,512]{1,0:T(8,128)(2,1)} %copy-done.8, bf16[256,512]{1,0:T(8,128)(2,1)} %copy-done.7, ...), custom_call_target="tpu_custom_call" | custom-call | flops 35000000512 | tf_op jit(solution)/shard_map/pallas_call | solution.py:230
  36.9 8.7 %all-to-all-done = bf16[8,32,512]{2,1,0:T(8,128)(2,1)S(1)} async-done(((bf16[8,32,512]{2,1,0:T(8,128)(2,1)}), bf16[8,32,512]{2,1,0:T(8,128)(2,1)S(1)}, u32[]{:S(2)}, u32[]{:S(2)}) %all-to-all-start) | async-done | bytes 262176 | tf_op jit(solution)/shard_map/all_to_all | solution.py:204
  45.7 0.0 copy-start.1
  45.7 0.7 copy-done.1
  46.4 6.6 %shard_map.113 = (bf16[256,512]{1,0:T(8,128)(2,1)}, bf16[32,16,384]{2,1,0:T(8,128)(2,1)}, bf16[32,16,384]{2,1,0:T(8,128)(2,1)}) custom-call(s32[1]{0:T(128)} %bitcast.core, bf16[1024,1024]{1,0:T(8,128)(2,1)} %constant.12.clone.table, bf16[1024,1024]{1,0:T(8,128)(2,1)} %constant.14.clone.inverse, bf16[1024,512]{1,0:T(8,128)(2,1)} %get-tuple-element.15.spec, ...), custom_call_target="tpu_custom_call" | custom-call | tf_op jit(solution)/shard_map/pallas_call | solution.py:240
  53.0 1.9 %collective-permute-start.6 = (bf16[32,16,384]{2,1,0:T(8,128)(2,1)}, bf16[32,16,384]{2,1,0:T(8,128)(2,1)S(1)}, u32[]{:S(2)}, u32[]{:S(2)}) collective-permute-start(bf16[32,16,384]{2,1,0:T(8,128)(2,1)} %get-tuple-element.23), channel_id=1, source_target_pairs={{0,8},{8,0},{1,9},{9,1},{2,10},{10,2},{3,11},{11,3},{4,12},{12,4},... | collective-permute-start | bytes 1179656 | tf_op jit(solution)/shard_map/ppermute | solution.py:254
  54.9 1.3 %collective-permute-start.5 = (bf16[256,512]{1,0:T(8,128)(2,1)}, bf16[256,512]{1,0:T(8,128)(2,1)S(1)}, u32[]{:S(2)}, u32[]{:S(2)}) collective-permute-start(bf16[256,512]{1,0:T(8,128)(2,1)} %get-tuple-element.17.refs_0_), channel_id=1, source_target_pairs={{24,0},{32,8},{40,16},{48,24},{56,32},{64,40},{72,48},{80,56},{88,... | collective-permute-start | bytes 786440 | tf_op jit(solution)/shard_map/ppermute | solution.py:200
  56.2 3.9 %collective-permute-start.4 = (bf16[256,512]{1,0:T(8,128)(2,1)}, bf16[256,512]{1,0:T(8,128)(2,1)S(1)}, u32[]{:S(2)}, u32[]{:S(2)}) collective-permute-start(bf16[256,512]{1,0:T(8,128)(2,1)} %get-tuple-element.17.refs_0_), channel_id=1, source_target_pairs={{16,0},{24,8},{32,16},{40,24},{48,32},{56,40},{64,48},{72,56},{80,... | collective-permute-start | bytes 786440 | tf_op jit(solution)/shard_map/ppermute | solution.py:200
  60.1 1.9 %collective-permute-start.3 = (bf16[256,512]{1,0:T(8,128)(2,1)}, bf16[256,512]{1,0:T(8,128)(2,1)S(1)}, u32[]{:S(2)}, u32[]{:S(2)}) collective-permute-start(bf16[256,512]{1,0:T(8,128)(2,1)} %get-tuple-element.17.refs_0_), channel_id=1, source_target_pairs={{8,0},{16,8},{24,16},{32,24},{40,32},{48,40},{56,48},{64,56},{72,6... | collective-permute-start | bytes 786440 | tf_op jit(solution)/shard_map/ppermute | solution.py:200
  62.0 0.0 collective-permute-done.6.b
  62.0 0.0 copy-start.2
  62.0 0.7 copy-done.2
  62.7 2.0 %shard_map.115 = bf16[32,16,384]{2,1,0:T(8,128)(2,1)} custom-call(bf16[32,16,384]{2,1,0:T(8,128)(2,1)} %get-tuple-element.22.a, bf16[32,16,384]{2,1,0:T(8,128)(2,1)} %copy-done.2), custom_call_target="tpu_custom_call" | custom-call | tf_op jit(solution)/shard_map/pallas_call | solution.py:255
  64.7 18.9 %all-to-all-start.1 = ((bf16[32,16,384]{2,1,0:T(8,128)(2,1)}), bf16[32,16,384]{2,1,0:T(8,128)(2,1)S(1)}, u32[]{:S(2)}, u32[]{:S(2)}) async-start(bf16[32,16,384]{2,1,0:T(8,128)(2,1)} %shard_map.115), calls=%async_computation.1 | async-start | bytes 786432 | tf_op jit(solution)/shard_map/all_to_all | solution.py:204
  83.6 0.0 collective-permute-done.5.refs_3_
  83.6 0.0 copy-start.3
  83.6 0.0 collective-permute-done.4.refs_2_
  83.6 0.0 copy-start.4
  83.6 0.0 collective-permute-done.3.refs_1_
  83.6 0.0 copy-start.6
  83.6 0.6 copy-done.3
  84.3 0.1 copy-done.4
  84.4 0.1 copy-done.6
  84.5 6.9 %shard_map.114 = (bf16[256,512]{1,0:T(8,128)(2,1)}, bf16[256,512]{1,0:T(8,128)(2,1)}, bf16[256,512]{1,0:T(8,128)(2,1)}) custom-call(bf16[1024,1024]{1,0:T(8,128)(2,1)} %constant.12.clone.table, bf16[1024,1024]{1,0:T(8,128)(2,1)} %constant.13.clone.last.first, bf16[768,512]{1,0:T(8,128)(2,1)} %taps.3, bf16[256,512]{1,0:T(8,128)(2,1)} %get-tuple-element.17.refs_0_, ...), custom_call_target="tpu_custom_call" | custom-call | flops 35000000512 | tf_op jit(solution)/shard_map/pallas_call | solution.py:262
  91.4 15.4 %all-to-all-done.1.parts = bf16[32,16,384]{2,1,0:T(8,128)(2,1)S(1)} async-done(((bf16[32,16,384]{2,1,0:T(8,128)(2,1)}), bf16[32,16,384]{2,1,0:T(8,128)(2,1)S(1)}, u32[]{:S(2)}, u32[]{:S(2)}) %all-to-all-start.1) | async-done | bytes 393248 | tf_op jit(solution)/shard_map/all_to_all | solution.py:204
  106.8 0.0 copy-start
  106.8 0.7 copy-done
  107.5 1.7 %shard_map.116 = f32[12,512]{1,0:T(8,128)} custom-call(bf16[32,16,384]{2,1,0:T(8,128)(2,1)} %copy-done), custom_call_target="tpu_custom_call" | custom-call | tf_op jit(solution)/shard_map/pallas_call | solution.py:257
Async XLA Ops:
  2.6 26.3 %collective-permute-start.2 = (bf16[256,512]{1,0:T(8,128)(2,1)}, bf16[256,512]{1,0:T(8,128)(2,1)S(1)}, u32[]{:S(2)}, u32[]{:S(2)}) collective-permute-start(bf16[256,512]{1,0:T(8,128)(2,1)} %get-tuple-element.14.refs_3_), channel_id=1, source_target_pairs={{0,8},{8,16},{16,24},{24,32},{32,40},{40,48},{48,56},{56,64},{64,7... | collective-permute-start | bytes 786440 | tf_op jit(solution)/shard_map/ppermute | solution.py:200
  4.5 24.4 %collective-permute-start.1 = (bf16[256,512]{1,0:T(8,128)(2,1)}, bf16[256,512]{1,0:T(8,128)(2,1)S(1)}, u32[]{:S(2)}, u32[]{:S(2)}) collective-permute-start(bf16[256,512]{1,0:T(8,128)(2,1)} %get-tuple-element.14.refs_3_), channel_id=1, source_target_pairs={{0,16},{8,24},{16,32},{24,40},{32,48},{40,56},{48,64},{56,72},{64,... | collective-permute-start | bytes 786440 | tf_op jit(solution)/shard_map/ppermute | solution.py:200
  8.0 20.9 %collective-permute-start = (bf16[256,512]{1,0:T(8,128)(2,1)}, bf16[256,512]{1,0:T(8,128)(2,1)S(1)}, u32[]{:S(2)}, u32[]{:S(2)}) collective-permute-start(bf16[256,512]{1,0:T(8,128)(2,1)} %get-tuple-element.14.refs_3_), channel_id=1, source_target_pairs={{0,24},{8,32},{16,40},{24,48},{32,56},{40,64},{48,72},{56,80},{64,... | collective-permute-start | bytes 786440 | tf_op jit(solution)/shard_map/ppermute | solution.py:200
  12.2 33.5 %all-to-all-start = ((bf16[8,32,512]{2,1,0:T(8,128)(2,1)}), bf16[8,32,512]{2,1,0:T(8,128)(2,1)S(1)}, u32[]{:S(2)}, u32[]{:S(2)}) async-start(bf16[8,32,512]{2,1,0:T(8,128)(2,1)} %get-tuple-element.16), calls=%async_computation | async-start | bytes 524288 | tf_op jit(solution)/shard_map/all_to_all | solution.py:204
  28.9 0.7 copy-start.5
  28.9 0.8 copy-start.7
  29.6 0.7 copy-start.8
  45.7 0.7 copy-start.1
  53.0 9.0 %collective-permute-start.6 = (bf16[32,16,384]{2,1,0:T(8,128)(2,1)}, bf16[32,16,384]{2,1,0:T(8,128)(2,1)S(1)}, u32[]{:S(2)}, u32[]{:S(2)}) collective-permute-start(bf16[32,16,384]{2,1,0:T(8,128)(2,1)} %get-tuple-element.23), channel_id=1, source_target_pairs={{0,8},{8,0},{1,9},{9,1},{2,10},{10,2},{3,11},{11,3},{4,12},{12,4},... | collective-permute-start | bytes 1179656 | tf_op jit(solution)/shard_map/ppermute | solution.py:254
  54.9 28.7 %collective-permute-start.5 = (bf16[256,512]{1,0:T(8,128)(2,1)}, bf16[256,512]{1,0:T(8,128)(2,1)S(1)}, u32[]{:S(2)}, u32[]{:S(2)}) collective-permute-start(bf16[256,512]{1,0:T(8,128)(2,1)} %get-tuple-element.17.refs_0_), channel_id=1, source_target_pairs={{24,0},{32,8},{40,16},{48,24},{56,32},{64,40},{72,48},{80,56},{88,... | collective-permute-start | bytes 786440 | tf_op jit(solution)/shard_map/ppermute | solution.py:200
  56.2 27.4 %collective-permute-start.4 = (bf16[256,512]{1,0:T(8,128)(2,1)}, bf16[256,512]{1,0:T(8,128)(2,1)S(1)}, u32[]{:S(2)}, u32[]{:S(2)}) collective-permute-start(bf16[256,512]{1,0:T(8,128)(2,1)} %get-tuple-element.17.refs_0_), channel_id=1, source_target_pairs={{16,0},{24,8},{32,16},{40,24},{48,32},{56,40},{64,48},{72,56},{80,... | collective-permute-start | bytes 786440 | tf_op jit(solution)/shard_map/ppermute | solution.py:200
  60.1 23.6 %collective-permute-start.3 = (bf16[256,512]{1,0:T(8,128)(2,1)}, bf16[256,512]{1,0:T(8,128)(2,1)S(1)}, u32[]{:S(2)}, u32[]{:S(2)}) collective-permute-start(bf16[256,512]{1,0:T(8,128)(2,1)} %get-tuple-element.17.refs_0_), channel_id=1, source_target_pairs={{8,0},{16,8},{24,16},{32,24},{40,32},{48,40},{56,48},{64,56},{72,6... | collective-permute-start | bytes 786440 | tf_op jit(solution)/shard_map/ppermute | solution.py:200
  62.0 0.7 copy-start.2
  64.7 42.1 %all-to-all-start.1 = ((bf16[32,16,384]{2,1,0:T(8,128)(2,1)}), bf16[32,16,384]{2,1,0:T(8,128)(2,1)S(1)}, u32[]{:S(2)}, u32[]{:S(2)}) async-start(bf16[32,16,384]{2,1,0:T(8,128)(2,1)} %shard_map.115), calls=%async_computation.1 | async-start | bytes 786432 | tf_op jit(solution)/shard_map/all_to_all | solution.py:204
  83.6 0.7 copy-start.3
  83.6 0.8 copy-start.4
  83.6 0.8 copy-start.6
  106.8 0.7 copy-start

commit v5 on v2

--- a/solution.py
+++ b/solution.py
@@ -25,22 +25,21 @@
 BLOCKS = 4
 TOKENS = BLOCKS * BLOCK
 WIDE = BLOCKS * LANES
-BINS = 128
+BINS = 512
 STEPS = PERIOD // 2 // BINS
 ROWS = 2 * BINS
 SLOT = 16
 MIB = 1024 * 1024
 
 
-def make_tables(lags, share):
+def make_tables(lags):
     freq = np.arange(PERIOD // 2)[:, None]
     place = np.arange(PERIOD)[None, :]
     angle = math.pi / PERIOD * ((2 * freq + 1) * place % (2 * PERIOD)).astype(np.float64)
     both = np.stack([np.cos(angle), -np.sin(angle)])
-    both = both.reshape(2, STEPS, BINS, PERIOD).transpose(1, 0, 2, 3).reshape(PERIOD, PERIOD)
-    by_slot = np.zeros((lags // share, SLOT, PERIOD))
-    by_slot[:, :share] = both.T[:lags].reshape(lags // share, share, PERIOD)
-    tables = both, both.T, by_slot.reshape(-1, PERIOD)
+    both = both.reshape(2, STEPS, BINS, PERIOD).transpose(1, 0, 2, 3).reshape(STEPS, ROWS, PERIOD)
+    back = both.transpose(0, 2, 1)
+    tables = both, both[:, :, lags:], back[:, :BLOCK], back[:, :lags], back[:, lags:]
     return tuple(np.ascontiguousarray(t).astype(ml_dtypes.bfloat16) for t in tables)
 
 
@@ -111,9 +110,9 @@
             windows[early:, lane_block(block)] = mixed[: (block + 1) * BLOCK, :]
 
     resp = dot(forward[:, :lags], taps[...])
-    response[...] = resp
+    response[...] = resp.astype(BF16)
     spec = dot(forward[...], windows[...])
-    spectrum[...] = spec
+    spectrum[...] = spec.astype(BF16)
     f_re, f_im = spread(resp[:BINS]), spread(resp[BINS:])
     x_re, x_im = spec[:BINS], spec[BINS:]
     y = jnp.concatenate([f_re * x_re - f_im * x_im, f_re * x_im + f_im * x_re]).astype(BF16)
@@ -140,16 +139,31 @@
 
     spec = dot(forward[...], windows[...])
     g_re, g_im = spec[:BINS], spec[BINS:]
-    x_re, x_im = spectrum[:BINS], spectrum[BINS:]
+    full = spectrum[...].astype(F32)
+    x_re, x_im = full[:BINS], full[BINS:]
     re = g_re * x_re + g_im * x_im
     im = g_im * x_re - g_re * x_im
     re = sum(re[:, lane_block(b)] for b in range(BLOCKS))
     im = sum(im[:, lane_block(b)] for b in range(BLOCKS))
-    accumulate(step, total, dot(inverse[...], jnp.concatenate([re, im]).astype(BF16)))
+    lags = inverse.shape[0]
+    part = dot(inverse[...], jnp.concatenate([re, im]).astype(BF16))
+
+    @pl.when(step == 0)
+    def _():
+        total[:lags, :] = part
+        total[lags:, :] = jnp.zeros_like(total[lags:, :])
+
+    @pl.when(step > 0)
+    def _():
+        total[:lags, :] += part
 
     @pl.when(step == STEPS - 1)
     def _():
-        lag_grad[...] = (total[...] * scale).astype(BF16)
+        count = lag_grad.shape[0]
+        share = lags // count
+        for slot in range(count):
+            rows = total[slot * share : slot * share + SLOT, :] * scale
+            lag_grad[slot] = rows.astype(BF16)
 
 
 def back_kernel(
@@ -170,7 +184,8 @@
             out[:BLOCK, :] = (cotangent[at, :].astype(F32) * conv[at, :]).astype(BF16)
 
     spec = dot(forward[...], windows[...])
-    f_re, f_im = spread(response[:BINS]), spread(response[BINS:])
+    resp = response[...].astype(F32)
+    f_re, f_im = spread(resp[:BINS]), spread(resp[BINS:])
     g_re, g_im = spec[:BINS], spec[BINS:]
     y = jnp.concatenate([f_re * g_re + f_im * g_im, f_re * g_im - f_im * g_re]).astype(BF16)
     accumulate(step, total, dot(inverse[...], y))
@@ -207,7 +222,7 @@
     return jax.ShapeDtypeStruct(shape, dtype)
 
 
-def call(kernel, in_specs, out_specs, out_shape, scratch=(), steps=1, macs=0, moved=0):
+def call(kernel, in_specs, out_specs, out_shape, scratch=(), steps=1, flops=0):
     return pl.pallas_call(
         kernel,
         grid=(steps,),
@@ -218,11 +233,15 @@
         compiler_params=pltpu.CompilerParams(
             dimension_semantics=("arbitrary",), vmem_limit_bytes=VMEM_LIMIT
         ),
-        cost_estimate=pl.CostEstimate(flops=2 * macs, bytes_accessed=moved, transcendentals=0),
+        cost_estimate=pl.CostEstimate(flops=flops, bytes_accessed=0, transcendentals=0),
     )
 
 
 VMEM_LIMIT = 56 * MIB
+CONV_FLOPS = 6_000_000_000
+CROSS_FLOPS = 0
+JOIN_FLOPS = 8_000_000_000
+BACK_FLOPS = 35_000_000_000
 
 
 def shift(value, steps):
@@ -242,7 +261,7 @@
     return lax.all_to_all(value, axes, split_axis=0, concat_axis=0, tiled=True)
 
 
-def body(forward, inverse, slotted, gate_input, key_input, value_input, out_grad, filter_taps):
+def body(forward, own, first, lagged, last, gate_input, key_input, value_input, out_grad, filter_taps):
     lags = filter_taps.shape[0]
     held, channels = out_grad.shape
     share = lags // lax.axis_size(CTX)
@@ -252,6 +271,7 @@
     pieces = (channels // LANES, held, LANES)
     flat = (TOKENS, LANES)
     reach = (lags, LANES)
+    slots = (lags // share, SLOT, LANES)
     scalar = pl.BlockSpec(memory_space=pltpu.SMEM)
     place = lax.axis_index(GROUP).reshape(1)
 
@@ -267,51 +287,57 @@
         [scalar] + [whole(ship)] * BLOCKS,
         [whole(flat), whole(reach), whole(flat)],
         [shaped(flat), shaped(reach), shaped(flat)],
+        flops=JOIN_FLOPS,
     )(place, *swap(ships))
     mixed_halo = shift(tail, 1)
     taps = lax.dynamic_slice_in_dim(filter_taps, lax.axis_index(GROUP) * LANES, LANES, 1)
 
-    table = pl.BlockSpec((ROWS, PERIOD), lambda step: (step, 0))
+    def stepped(*shape):
+        return pl.BlockSpec((None,) + shape, lambda step: (step, 0, 0))
+
+    table = stepped(ROWS, PERIOD)
     bins = pl.BlockSpec((ROWS, WIDE), lambda step: (step, 0))
     narrow_bins = pl.BlockSpec((ROWS, LANES), lambda step: (step, 0))
     conv, spectrum, response = call(
         functools.partial(conv_kernel, norm),
         [
             table,
-            pl.BlockSpec((BLOCK, ROWS), lambda step: (lags // BLOCK, step)),
+            stepped(BLOCK, ROWS),
             whole(reach),
             whole(flat),
             whole(reach),
         ],
         [whole(flat), bins, narrow_bins],
-        [shaped(flat, F32), shaped((PERIOD, WIDE), F32), shaped((PERIOD, LANES), F32)],
+        [shaped(flat, F32), shaped((PERIOD, WIDE)), shaped((PERIOD, LANES))],
         [pltpu.VMEM((PERIOD, WIDE), BF16), pltpu.VMEM(local, F32)],
         STEPS,
-    )(forward, inverse, mixed_halo, mixed, taps)
+        CONV_FLOPS,
+    )(forward, last, mixed_halo, mixed, taps)
 
     grad, head, lag_grad = call(
         functools.partial(cross_kernel, norm),
         [
-            pl.BlockSpec((ROWS, BLOCK), lambda step: (step, lags // BLOCK)),
-            pl.BlockSpec((slotted.shape[0], ROWS), lambda step: (0, step)),
+            stepped(ROWS, BLOCK),
+            stepped(lags, ROWS),
             whole(flat),
             whole(flat),
             bins,
         ],
-        [whole(flat), whole(reach), whole((slotted.shape[0], LANES))],
-        [shaped(flat), shaped(reach), shaped((slotted.shape[0], LANES))],
-        [pltpu.VMEM(local, BF16), pltpu.VMEM((slotted.shape[0], LANES), F32)],
+        [whole(flat), whole(reach), whole(slots)],
+        [shaped(flat), shaped(reach), shaped(slots)],
+        [pltpu.VMEM(local, BF16), pltpu.VMEM((lags + SLOT, LANES), F32)],
         STEPS,
-    )(forward, slotted, cotangent, gate, spectrum)
+        CROSS_FLOPS,
+    )(own, lagged, cotangent, gate, spectrum)
     grad_halo = shift(head, -1)
-    lag_parts = exchange(lag_grad.reshape(-1, SLOT, LANES), CTX)
+    lag_parts = exchange(lag_grad, CTX)
 
     ships = call(
         functools.partial(back_kernel, norm),
         [
             scalar,
             table,
-            pl.BlockSpec((BLOCK, ROWS), lambda step: (0, step)),
+            stepped(BLOCK, ROWS),
             whole(flat),
             whole(reach),
             narrow_bins,
@@ -322,7 +348,8 @@
         [shaped(ship)] * BLOCKS,
         [pltpu.VMEM((PERIOD, WIDE), BF16), pltpu.VMEM(local, F32)],
         STEPS,
-    )(place, forward, inverse, grad, grad_halo, response, conv, cotangent)
+        BACK_FLOPS,
+    )(place, forward, first, grad, grad_halo, response, conv, cotangent)
     gate_grad, key_grad, value_grad = call(
         final_kernel,
         [scalar] + [whole(ship)] * BLOCKS + [whole(local)] * 2,
@@ -344,14 +371,14 @@
     mapped = jax.shard_map(
         body,
         mesh=split,
-        in_specs=(P(), P(), P(), spans, spans, spans, P(CTX + CH, None), P(None, CH)),
+        in_specs=(P(), P(), P(), P(), P(), spans, spans, spans, P(CTX + CH, None), P(None, CH)),
         out_specs=(spans, spans, spans, spans),
         check_vma=False,
     )
 
     def run(gate_input, key_input, value_input, out_grad, filter_taps):
         lags = filter_taps.shape[0]
-        tables = make_tables(lags, lags // math.prod(SIZES[:4]))
+        tables = make_tables(lags)
         return mapped(*tables, gate_input, key_input, value_input, out_grad, filter_taps)
 
     return run

time: 115 us -> 98.9 us (0.86)
  the two profiles are of different devices: /device:TPU:113 before, /device:TPU:1 now
where the time goes in v5:
time: 98.9 us; the launch traced here: 98.3 us
  starting transfers between devices  60.7 us (61%)
  Pallas kernels  22.5 us (23%)
  waiting for transfers between devices  9.49 us (10%)
  local copies, waits for them, and re-layouts  4.84 us (5%)
    all_to_all x2, starting transfers between devices, exchange(): return lax.all_to_all(value, axes, split_axis=0, concat_axis=0, tiled=True)  32.8 us
    ppermute x6, starting transfers between devices, swap(): lax.ppermute(ships[hop], GROUP, [(i, i ^ hop) for i in range(BLOCKS)])  22.1 us
    ppermute x6, waiting for transfers between devices, swap(): lax.ppermute(ships[hop], GROUP, [(i, i ^ hop) for i in range(BLOCKS)])  5.88 us
    ppermute x2, starting transfers between devices, shift(): lax.ppermute(value, RUNS, [(i, i + steps) for i in range(first, last)])  5.8 us
    pallas_call x1, Pallas kernels, body(): call(functools.partial(conv_kernel, norm), [table, stepped(BLOCK, ROWS),...  5.18 us
    pallas_call x1, Pallas kernels, body(): call(functools.partial(back_kernel, norm), [scalar, table, stepped(BLOCK,...  4.82 us
    pallas_call x1, Pallas kernels, body(): call(functools.partial(cross_kernel, norm), [stepped(ROWS, BLOCK), steppe...  4.37 us
    unnamed x22, local copies, waits for them, and re-layouts  4.11 us
  transfers between devices with their start and end apart: 10, of which 3 were waited for; matrix products, arithmetic and copies ran while one was open for 1% of the time, Pallas kernels for 14%

profile of v5, /device:TPU:1, one launch (start us, length us, event | category | flops | bytes accessed | tf_op | source)
XLA Modules:
  0.0 98.3 jit_solution(10177394335829163053)
XLA Ops:
  0.6 0.0 copy-start
  0.7 2.3 %shard_map.129 = (bf16[512,128]{1,0:T(8,128)(2,1)}, bf16[512,128]{1,0:T(8,128)(2,1)}, bf16[512,128]{1,0:T(8,128)(2,1)}, bf16[512,128]{1,0:T(8,128)(2,1)}, bf16[32,32,128]{2,1,0:T(8,128)(2,1)}) custom-call(s32[1]{0:T(128)} %bitcast.place, bf16[256,512]{1,0:T(8,128)(2,1)} %refs_4_.1, bf16[256,512]{1,0:T(8,128)(2,1)} %refs_5_.1, bf16[256,512]{1,0:T(8,128)(2,1)} %gate.1, ...), custom_call_target="tpu_custom_call" | custom-call | tf_op jit(solution)/shard_map/pallas_call | solution.py:278
  2.9 8.8 %collective-permute-start = (bf16[512,128]{1,0:T(8,128)(2,1)}, bf16[512,128]{1,0:T(8,128)(2,1)S(1)}, u32[]{:S(2)}, u32[]{:S(2)}) collective-permute-start(bf16[512,128]{1,0:T(8,128)(2,1)} %get-tuple-element.27), channel_id=1, source_target_pairs={{0,8},{8,0},{16,24},{24,16},{1,9},{9,1},{17,25},{25,17},{2,10},{10... | collective-permute-start | bytes 393224 | tf_op jit(solution)/shard_map/ppermute | solution.py:255
  11.7 1.9 %collective-permute-start.1 = (bf16[512,128]{1,0:T(8,128)(2,1)}, bf16[512,128]{1,0:T(8,128)(2,1)S(1)}, u32[]{:S(2)}, u32[]{:S(2)}) collective-permute-start(bf16[512,128]{1,0:T(8,128)(2,1)} %get-tuple-element.28), channel_id=1, source_target_pairs={{0,16},{8,24},{16,0},{24,8},{1,17},{9,25},{17,1},{25,9},{2,18},{10... | collective-permute-start | bytes 393224 | tf_op jit(solution)/shard_map/ppermute | solution.py:255
  13.6 3.5 %collective-permute-start.2 = (bf16[512,128]{1,0:T(8,128)(2,1)}, bf16[512,128]{1,0:T(8,128)(2,1)S(1)}, u32[]{:S(2)}, u32[]{:S(2)}) collective-permute-start(bf16[512,128]{1,0:T(8,128)(2,1)} %get-tuple-element.29), channel_id=1, source_target_pairs={{0,24},{8,16},{16,8},{24,0},{1,25},{9,17},{17,9},{25,1},{2,26},{10... | collective-permute-start | bytes 393224 | tf_op jit(solution)/shard_map/ppermute | solution.py:255
  17.2 13.6 %all-to-all-start = ((bf16[32,32,128]{2,1,0:T(8,128)(2,1)}), bf16[32,32,128]{2,1,0:T(8,128)(2,1)S(1)}, u32[]{:S(2)}, u32[]{:S(2)}) async-start(bf16[32,32,128]{2,1,0:T(8,128)(2,1)} %get-tuple-element.25), calls=%async_computation | async-start | bytes 524288 | tf_op jit(solution)/shard_map/all_to_all | solution.py:261
  30.8 0.0 collective-permute-done.refs_1_
  30.8 0.0 copy-start.8
  30.8 0.0 collective-permute-done.1.refs_2_
  30.8 0.0 copy-start.9
  30.8 0.0 collective-permute-done.2.refs_3_
  30.8 0.0 copy-start.10
  30.8 0.6 copy-done.8
  31.5 0.0 copy-done.9
  31.5 0.0 copy-done.10
  31.5 2.0 %shard_map.130 = (bf16[1024,128]{1,0:T(8,128)(2,1)}, bf16[768,128]{1,0:T(8,128)(2,1)}, bf16[1024,128]{1,0:T(8,128)(2,1)}) custom-call(s32[1]{0:T(128)} %bitcast.place, bf16[512,128]{1,0:T(8,128)(2,1)} %get-tuple-element.26.refs_0_, bf16[512,128]{1,0:T(8,128)(2,1)} %copy-done.8, bf16[512,128]{1,0:T(8,128)(2,1)} %copy-done.9, bf16[512,128]{1,0:T(8,128)(2,1)} %copy-done.10), custom_call_target="tpu_custom_call" | custom-call | flops 8000000000 | tf_op jit(solution)/shard_map/pallas_call | solution.py:285
  33.5 4.5 %collective-permute-start.3 = (bf16[768,128]{1,0:T(8,128)(2,1)}, bf16[768,128]{1,0:T(8,128)(2,1)S(1)}, u32[]{:S(2)}, u32[]{:S(2)}) collective-permute-start(bf16[768,128]{1,0:T(8,128)(2,1)} %get-tuple-element.31), channel_id=1, source_target_pairs={{0,32},{32,64},{64,96},{96,128},{128,160},{160,192},{192,224},{224... | collective-permute-start | bytes 589832 | tf_op jit(solution)/shard_map/ppermute | solution.py:250
  38.0 0.0 copy-done
  38.0 0.7 constant_dynamic-slice_fusion.taps
  38.8 3.6 %collective-permute-done.3.halo = bf16[768,128]{1,0:T(8,128)(2,1)S(1)} collective-permute-done((bf16[768,128]{1,0:T(8,128)(2,1)}, bf16[768,128]{1,0:T(8,128)(2,1)S(1)}, u32[]{:S(2)}, u32[]{:S(2)}) %collective-permute-start.3) | collective-permute-done | bytes 196640 | tf_op jit(solution)/shard_map/ppermute | solution.py:250
  42.4 0.0 copy-start.6
  42.4 0.7 copy-done.6
  43.0 5.2 %shard_map.131 = (f32[1024,128]{1,0:T(8,128)}, bf16[1024,512]{1,0:T(8,128)(2,1)}, bf16[1024,128]{1,0:T(8,128)(2,1)}) custom-call(bf16[1,1024,1024]{2,1,0:T(8,128)(2,1)} %constant.28.clone.forward, bf16[1,256,1024]{2,1,0:T(8,128)(2,1)} %constant.32.clone.inverse, bf16[768,128]{1,0:T(8,128)(2,1)} %copy-done.6, bf16[1024,128]{1,0:T(8,128)(2,1)} %get-tuple-element.32.mixed, ...), custom_call_target="tpu_custom_call" | custom-call | flops 6000000000 | tf_op jit(solution)/shard_map/pallas_call | solution.py:301
  48.2 0.0 all-to-all-done
  48.2 0.0 copy-start.1
  48.2 0.7 copy-done.1
  48.9 4.4 %shard_map.132 = (bf16[1024,128]{1,0:T(8,128)(2,1)}, bf16[768,128]{1,0:T(8,128)(2,1)}, bf16[64,16,128]{2,1,0:T(8,128)(2,1)}) custom-call(bf16[1,1024,256]{2,1,0:T(8,128)(2,1)} %constant.29.clone.forward, bf16[1,768,1024]{2,1,0:T(8,128)(2,1)} %constant.31.clone.inverse, bf16[1024,128]{1,0:T(8,128)(2,1)} %bitcast.2, bf16[1024,128]{1,0:T(8,128)(2,1)} %get-tuple-element.30.gate, ...), custom_call_target="tpu_custom_call" | custom-call | tf_op jit(solution)/shard_map/pallas_call | solution.py:317
  53.3 1.3 %collective-permute-start.4 = (bf16[768,128]{1,0:T(8,128)(2,1)}, bf16[768,128]{1,0:T(8,128)(2,1)S(1)}, u32[]{:S(2)}, u32[]{:S(2)}) collective-permute-start(bf16[768,128]{1,0:T(8,128)(2,1)} %get-tuple-element.35), channel_id=1, source_target_pairs={{32,0},{64,32},{96,64},{128,96},{160,128},{192,160},{224,192},{256... | collective-permute-start | bytes 589832 | tf_op jit(solution)/shard_map/ppermute | solution.py:250
  54.6 19.2 %all-to-all-start.1 = ((bf16[64,16,128]{2,1,0:T(8,128)(2,1)}), bf16[64,16,128]{2,1,0:T(8,128)(2,1)S(1)}, u32[]{:S(2)}, u32[]{:S(2)}) async-start(bf16[64,16,128]{2,1,0:T(8,128)(2,1)} %get-tuple-element.45), calls=%async_computation.1 | async-start | bytes 524288 | tf_op jit(solution)/shard_map/all_to_all | solution.py:261
  73.8 0.0 collective-permute-done.4.halo
  73.8 0.0 copy-start.7
  73.8 0.7 copy-done.7
  74.5 4.8 %shard_map.133 = (bf16[512,128]{1,0:T(8,128)(2,1)}, bf16[512,128]{1,0:T(8,128)(2,1)}, bf16[512,128]{1,0:T(8,128)(2,1)}, bf16[512,128]{1,0:T(8,128)(2,1)}) custom-call(s32[1]{0:T(128)} %bitcast.place, bf16[1,1024,1024]{2,1,0:T(8,128)(2,1)} %constant.28.clone.forward, bf16[1,256,1024]{2,1,0:T(8,128)(2,1)} %constant.30.clone.inverse, ...), custom_call_target="tpu_custom_call" | custom-call | flops 35000000512 | tf_op jit(solution)/shard_map/pallas_call | solution.py:335
  79.3 2.4 %collective-permute-start.5 = (bf16[512,128]{1,0:T(8,128)(2,1)}, bf16[512,128]{1,0:T(8,128)(2,1)S(1)}, u32[]{:S(2)}, u32[]{:S(2)}) collective-permute-start(bf16[512,128]{1,0:T(8,128)(2,1)} %get-tuple-element.39), channel_id=1, source_target_pairs={{0,8},{8,0},{16,24},{24,16},{1,9},{9,1},{17,25},{25,17},{2,10},{10... | collective-permute-start | bytes 393224 | tf_op jit(solution)/shard_map/ppermute | solution.py:255
  81.7 3.2 %collective-permute-start.6 = (bf16[512,128]{1,0:T(8,128)(2,1)}, bf16[512,128]{1,0:T(8,128)(2,1)S(1)}, u32[]{:S(2)}, u32[]{:S(2)}) collective-permute-start(bf16[512,128]{1,0:T(8,128)(2,1)} %get-tuple-element.40), channel_id=1, source_target_pairs={{0,16},{8,24},{16,0},{24,8},{1,17},{9,25},{17,1},{25,9},{2,18},{10... | collective-permute-start | bytes 393224 | tf_op jit(solution)/shard_map/ppermute | solution.py:255
  84.9 2.3 %collective-permute-start.7 = (bf16[512,128]{1,0:T(8,128)(2,1)}, bf16[512,128]{1,0:T(8,128)(2,1)S(1)}, u32[]{:S(2)}, u32[]{:S(2)}) collective-permute-start(bf16[512,128]{1,0:T(8,128)(2,1)} %get-tuple-element.41), channel_id=1, source_target_pairs={{0,24},{8,16},{16,8},{24,0},{1,25},{9,17},{17,9},{25,1},{2,26},{10... | collective-permute-start | bytes 393224 | tf_op jit(solution)/shard_map/ppermute | solution.py:255
  87.2 0.0 collective-permute-done.5.refs_1_
  87.2 0.0 copy-start.3
  87.2 2.1 %collective-permute-done.6.refs_2_ = bf16[512,128]{1,0:T(8,128)(2,1)S(1)} collective-permute-done((bf16[512,128]{1,0:T(8,128)(2,1)}, bf16[512,128]{1,0:T(8,128)(2,1)S(1)}, u32[]{:S(2)}, u32[]{:S(2)}) %collective-permute-start.6) | collective-permute-done | bytes 131104 | tf_op jit(solution)/shard_map/ppermute | solution.py:255
  89.3 0.0 copy-start.4
  89.3 3.8 %collective-permute-done.7.refs_3_ = bf16[512,128]{1,0:T(8,128)(2,1)S(1)} collective-permute-done((bf16[512,128]{1,0:T(8,128)(2,1)}, bf16[512,128]{1,0:T(8,128)(2,1)S(1)}, u32[]{:S(2)}, u32[]{:S(2)}) %collective-permute-start.7) | collective-permute-done | bytes 131104 | tf_op jit(solution)/shard_map/ppermute | solution.py:255
  93.1 0.0 copy-done.3
  93.1 0.0 copy-done.4
  93.1 0.6 copy-done.5
  93.7 2.2 %shard_map.134 = (bf16[256,512]{1,0:T(8,128)(2,1)}, bf16[256,512]{1,0:T(8,128)(2,1)}, bf16[256,512]{1,0:T(8,128)(2,1)}) custom-call(s32[1]{0:T(128)} %bitcast.place, bf16[512,128]{1,0:T(8,128)(2,1)} %get-tuple-element.38.refs_0_, bf16[512,128]{1,0:T(8,128)(2,1)} %copy-done.3, bf16[512,128]{1,0:T(8,128)(2,1)} %copy-done.4, bf16[512,128]{1,0:T(8,128)(2,1)} %copy-done.5, ...), custom_call_target="tpu_custom_call" | custom-call | tf_op jit(solution)/shard_map/pallas_call | solution.py:353
  96.0 0.0 all-to-all-done.1.parts
  96.0 0.7 copy-done.2
  96.7 1.6 %shard_map.135 = f32[12,512]{1,0:T(8,128)} custom-call(bf16[64,16,128]{2,1,0:T(8,128)(2,1)} %copy-done.2), custom_call_target="tpu_custom_call" | custom-call | tf_op jit(solution)/shard_map/pallas_call | solution.py:359
  (2 shorter events, 0.0 us)
Async XLA Ops:
  0.6 37.4 %copy-start = (bf16[768,512]{1,0:T(8,128)(2,1)S(1)}, bf16[768,512]{1,0:T(8,128)(2,1)}, u32[]{:S(2)}) copy-start(bf16[768,512]{1,0:T(8,128)(2,1)} %param.14) | copy-start | bytes 2359300
  2.9 27.8 %collective-permute-start = (bf16[512,128]{1,0:T(8,128)(2,1)}, bf16[512,128]{1,0:T(8,128)(2,1)S(1)}, u32[]{:S(2)}, u32[]{:S(2)}) collective-permute-start(bf16[512,128]{1,0:T(8,128)(2,1)} %get-tuple-element.27), channel_id=1, source_target_pairs={{0,8},{8,0},{16,24},{24,16},{1,9},{9,1},{17,25},{25,17},{2,10},{10... | collective-permute-start | bytes 393224 | tf_op jit(solution)/shard_map/ppermute | solution.py:255
  11.7 19.1 %collective-permute-start.1 = (bf16[512,128]{1,0:T(8,128)(2,1)}, bf16[512,128]{1,0:T(8,128)(2,1)S(1)}, u32[]{:S(2)}, u32[]{:S(2)}) collective-permute-start(bf16[512,128]{1,0:T(8,128)(2,1)} %get-tuple-element.28), channel_id=1, source_target_pairs={{0,16},{8,24},{16,0},{24,8},{1,17},{9,25},{17,1},{25,9},{2,18},{10... | collective-permute-start | bytes 393224 | tf_op jit(solution)/shard_map/ppermute | solution.py:255
  13.6 17.2 %collective-permute-start.2 = (bf16[512,128]{1,0:T(8,128)(2,1)}, bf16[512,128]{1,0:T(8,128)(2,1)S(1)}, u32[]{:S(2)}, u32[]{:S(2)}) collective-permute-start(bf16[512,128]{1,0:T(8,128)(2,1)} %get-tuple-element.29), channel_id=1, source_target_pairs={{0,24},{8,16},{16,8},{24,0},{1,25},{9,17},{17,9},{25,1},{2,26},{10... | collective-permute-start | bytes 393224 | tf_op jit(solution)/shard_map/ppermute | solution.py:255
  17.2 31.0 %all-to-all-start = ((bf16[32,32,128]{2,1,0:T(8,128)(2,1)}), bf16[32,32,128]{2,1,0:T(8,128)(2,1)S(1)}, u32[]{:S(2)}, u32[]{:S(2)}) async-start(bf16[32,32,128]{2,1,0:T(8,128)(2,1)} %get-tuple-element.25), calls=%async_computation | async-start | bytes 524288 | tf_op jit(solution)/shard_map/all_to_all | solution.py:261
  30.8 0.7 copy-start.8
  30.8 0.7 copy-start.9
  30.8 0.7 copy-start.10
  33.5 8.9 %collective-permute-start.3 = (bf16[768,128]{1,0:T(8,128)(2,1)}, bf16[768,128]{1,0:T(8,128)(2,1)S(1)}, u32[]{:S(2)}, u32[]{:S(2)}) collective-permute-start(bf16[768,128]{1,0:T(8,128)(2,1)} %get-tuple-element.31), channel_id=1, source_target_pairs={{0,32},{32,64},{64,96},{96,128},{128,160},{160,192},{192,224},{224... | collective-permute-start | bytes 589832 | tf_op jit(solution)/shard_map/ppermute | solution.py:250
  42.4 0.7 copy-start.6
  48.2 0.7 copy-start.1
  53.3 20.5 %collective-permute-start.4 = (bf16[768,128]{1,0:T(8,128)(2,1)}, bf16[768,128]{1,0:T(8,128)(2,1)S(1)}, u32[]{:S(2)}, u32[]{:S(2)}) collective-permute-start(bf16[768,128]{1,0:T(8,128)(2,1)} %get-tuple-element.35), channel_id=1, source_target_pairs={{32,0},{64,32},{96,64},{128,96},{160,128},{192,160},{224,192},{256... | collective-permute-start | bytes 589832 | tf_op jit(solution)/shard_map/ppermute | solution.py:250
  54.6 41.4 %all-to-all-start.1 = ((bf16[64,16,128]{2,1,0:T(8,128)(2,1)}), bf16[64,16,128]{2,1,0:T(8,128)(2,1)S(1)}, u32[]{:S(2)}, u32[]{:S(2)}) async-start(bf16[64,16,128]{2,1,0:T(8,128)(2,1)} %get-tuple-element.45), calls=%async_computation.1 | async-start | bytes 524288 | tf_op jit(solution)/shard_map/all_to_all | solution.py:261
  73.8 0.7 copy-start.7
  79.3 7.9 %collective-permute-start.5 = (bf16[512,128]{1,0:T(8,128)(2,1)}, bf16[512,128]{1,0:T(8,128)(2,1)S(1)}, u32[]{:S(2)}, u32[]{:S(2)}) collective-permute-start(bf16[512,128]{1,0:T(8,128)(2,1)} %get-tuple-element.39), channel_id=1, source_target_pairs={{0,8},{8,0},{16,24},{24,16},{1,9},{9,1},{17,25},{25,17},{2,10},{10... | collective-permute-start | bytes 393224 | tf_op jit(solution)/shard_map/ppermute | solution.py:255
  81.7 7.6 %collective-permute-start.6 = (bf16[512,128]{1,0:T(8,128)(2,1)}, bf16[512,128]{1,0:T(8,128)(2,1)S(1)}, u32[]{:S(2)}, u32[]{:S(2)}) collective-permute-start(bf16[512,128]{1,0:T(8,128)(2,1)} %get-tuple-element.40), channel_id=1, source_target_pairs={{0,16},{8,24},{16,0},{24,8},{1,17},{9,25},{17,1},{25,9},{2,18},{10... | collective-permute-start | bytes 393224 | tf_op jit(solution)/shard_map/ppermute | solution.py:255
  84.9 8.2 %collective-permute-start.7 = (bf16[512,128]{1,0:T(8,128)(2,1)}, bf16[512,128]{1,0:T(8,128)(2,1)S(1)}, u32[]{:S(2)}, u32[]{:S(2)}) collective-permute-start(bf16[512,128]{1,0:T(8,128)(2,1)} %get-tuple-element.41), channel_id=1, source_target_pairs={{0,24},{8,16},{16,8},{24,0},{1,25},{9,17},{17,9},{25,1},{2,26},{10... | collective-permute-start | bytes 393224 | tf_op jit(solution)/shard_map/ppermute | solution.py:255
  87.2 5.9 %copy-start.3 = (bf16[512,128]{1,0:T(8,128)(2,1)}, bf16[512,128]{1,0:T(8,128)(2,1)S(1)}, u32[]{:S(2)}) copy-start(bf16[512,128]{1,0:T(8,128)(2,1)S(1)} %collective-permute-done.5.refs_1_) | copy-start | bytes 393220
  89.3 3.8 %copy-start.4 = (bf16[512,128]{1,0:T(8,128)(2,1)}, bf16[512,128]{1,0:T(8,128)(2,1)S(1)}, u32[]{:S(2)}) copy-start(bf16[512,128]{1,0:T(8,128)(2,1)S(1)} %collective-permute-done.6.refs_2_) | copy-start | bytes 393220
  93.1 0.6 copy-start.5
  96.0 0.7 copy-start.2

commit v6 on v5

--- a/solution.py
+++ b/solution.py
@@ -55,6 +55,10 @@
     return pl.ds(pl.multiple_of(index * LANES, LANES), LANES)
 
 
+def rows_at(index):
+    return pl.ds(pl.multiple_of(index * BLOCK, BLOCK), BLOCK)
+
+
 def token_block(index):
     return slice(index * BLOCK, (index + 1) * BLOCK)
 
@@ -73,28 +77,17 @@
         total[...] += part
 
 
-def prep_kernel(place, key, value, gate, out_grad, *outs):
+def prep_kernel(place, key, value, gate, out_grad, mixed, *outs):
     ships, pieces = outs[:BLOCKS], outs[BLOCKS]
+    product = (key[...].astype(F32) * value[...].astype(F32)).astype(BF16)
+    for block in range(BLOCKS):
+        mixed[block] = product[:, lane_block(block)]
     for hop, ship in enumerate(ships):
-        at = (slice(None), lanes_at(place[0] ^ hop))
-        ship[:BLOCK, :] = (key[at].astype(F32) * value[at].astype(F32)).astype(BF16)
-        ship[BLOCK:, :] = gate[at]
+        ship[...] = gate[:, lanes_at(place[0] ^ hop)]
     count = pieces.shape[0]
     for piece in range(count):
         target = piece % BLOCKS * (count // BLOCKS) + piece // BLOCKS
         pieces[target] = out_grad[:, lane_block(piece)]
-
-
-def join_kernel(place, *refs):
-    ships, (mixed, tail, gate) = refs[:BLOCKS], refs[BLOCKS:]
-    skipped = TOKENS - tail.shape[0]
-    for hop, ship in enumerate(ships):
-        block = place[0] ^ hop
-        at = pl.multiple_of(block * BLOCK, BLOCK)
-        mixed[pl.ds(at, BLOCK), :] = ship[:BLOCK, :]
-        gate[pl.ds(at, BLOCK), :] = ship[BLOCK:, :]
-
-    tail[...] = mixed[skipped:, :]
 
 
 def conv_kernel(scale, forward, inverse, halo, mixed, taps, conv, spectrum, response, windows, total):
@@ -124,18 +117,19 @@
             conv[token_block(block), :] = total[:, lane_block(block)] * scale
 
 
-def cross_kernel(
-    scale, forward, inverse, cotangent, gate, spectrum, grad, head, lag_grad, windows, total
-):
+def cross_kernel(scale, place, forward, inverse, cotangent, spectrum, *refs):
+    gates, (grad, head, lag_grad, windows, total) = refs[:BLOCKS], refs[BLOCKS:]
     step = pl.program_id(0)
 
     @pl.when(step == 0)
     def _():
-        product = (cotangent[...].astype(F32) * gate[...].astype(F32)).astype(BF16)
-        grad[...] = product
-        head[...] = product[: head.shape[0]]
-        for block in range(BLOCKS):
-            windows[:, lane_block(block)] = product[token_block(block)]
+        for hop, gate in enumerate(gates):
+            block = place[0] ^ hop
+            at = rows_at(block)
+            product = (cotangent[at, :].astype(F32) * gate[...].astype(F32)).astype(BF16)
+            grad[at, :] = product
+            windows[:, lanes_at(block)] = product
+        head[...] = grad[: head.shape[0], :]
 
     spec = dot(forward[...], windows[...])
     g_re, g_im = spec[:BINS], spec[BINS:]
@@ -180,7 +174,7 @@
             if own < PERIOD:
                 windows[own:, lane_block(block)] = halo[: PERIOD - own, :]
         for hop, out in enumerate(outs):
-            at = pl.ds(pl.multiple_of((place[0] ^ hop) * BLOCK, BLOCK), BLOCK)
+            at = rows_at(place[0] ^ hop)
             out[:BLOCK, :] = (cotangent[at, :].astype(F32) * conv[at, :]).astype(BF16)
 
     spec = dot(forward[...], windows[...])
@@ -197,21 +191,21 @@
 
 
 def final_kernel(place, *refs):
-    ships, (key, value, gate_grad, key_grad, value_grad) = refs[:BLOCKS], refs[BLOCKS:]
+    ships, (key, value, parts, gate_grad, key_grad, value_grad, lag_grad) = (
+        refs[:BLOCKS],
+        refs[BLOCKS:],
+    )
     for hop, ship in enumerate(ships):
         at = (slice(None), lanes_at(place[0] ^ hop))
         gate_grad[at] = ship[:BLOCK, :]
         back = ship[BLOCK:, :].astype(F32)
         key_grad[at] = (back * value[at].astype(F32)).astype(BF16)
         value_grad[at] = (back * key[at].astype(F32)).astype(BF16)
-
-
-def sum_kernel(parts, out):
     for block in range(BLOCKS):
         total = parts[block].astype(F32)
         for source in range(1, parts.shape[0] // BLOCKS):
             total += parts[source * BLOCKS + block].astype(F32)
-        out[:, lane_block(block)] = total[: out.shape[0]]
+        lag_grad[:, lane_block(block)] = total[: lag_grad.shape[0]]
 
 
 def whole(shape):
@@ -222,7 +216,7 @@
     return jax.ShapeDtypeStruct(shape, dtype)
 
 
-def call(kernel, in_specs, out_specs, out_shape, scratch=(), steps=1, flops=0):
+def call(kernel, in_specs, out_specs, out_shape, scratch=(), steps=1, flops=0, limit=None):
     return pl.pallas_call(
         kernel,
         grid=(steps,),
@@ -231,16 +225,16 @@
         out_shape=out_shape,
         scratch_shapes=scratch,
         compiler_params=pltpu.CompilerParams(
-            dimension_semantics=("arbitrary",), vmem_limit_bytes=VMEM_LIMIT
+            dimension_semantics=("arbitrary",), vmem_limit_bytes=limit or VMEM_LIMIT
         ),
         cost_estimate=pl.CostEstimate(flops=flops, bytes_accessed=0, transcendentals=0),
     )
 
 
 VMEM_LIMIT = 56 * MIB
-CONV_FLOPS = 6_000_000_000
+FINAL_LIMIT = 16 * MIB
+CONV_FLOPS = 24_000_000_000
 CROSS_FLOPS = 0
-JOIN_FLOPS = 8_000_000_000
 BACK_FLOPS = 35_000_000_000
 
 
@@ -275,21 +269,18 @@
     scalar = pl.BlockSpec(memory_space=pltpu.SMEM)
     place = lax.axis_index(GROUP).reshape(1)
 
-    *ships, cotangent = call(
+    part = (BLOCK, LANES)
+    by_block = (BLOCKS, BLOCK, LANES)
+    mixed, *gates, cotangent = call(
         prep_kernel,
         [scalar] + [whole(local)] * 3 + [whole(out_grad.shape)],
-        [whole(ship)] * BLOCKS + [whole(pieces)],
-        [shaped(ship)] * BLOCKS + [shaped(pieces)],
+        [whole(by_block)] + [whole(part)] * BLOCKS + [whole(pieces)],
+        [shaped(by_block)] + [shaped(part)] * BLOCKS + [shaped(pieces)],
     )(place, key_input, value_input, gate_input, out_grad)
+    mixed = exchange(mixed, GROUP).reshape(flat)
+    mixed_halo = shift(mixed[TOKENS - lags :], 1)
     cotangent = exchange(cotangent, GROUP + CH).reshape(flat)
-    mixed, tail, gate = call(
-        join_kernel,
-        [scalar] + [whole(ship)] * BLOCKS,
-        [whole(flat), whole(reach), whole(flat)],
-        [shaped(flat), shaped(reach), shaped(flat)],
-        flops=JOIN_FLOPS,
-    )(place, *swap(ships))
-    mixed_halo = shift(tail, 1)
+    gates = swap(gates)
     taps = lax.dynamic_slice_in_dim(filter_taps, lax.axis_index(GROUP) * LANES, LANES, 1)
 
     def stepped(*shape):
@@ -317,18 +308,19 @@
     grad, head, lag_grad = call(
         functools.partial(cross_kernel, norm),
         [
+            scalar,
             stepped(ROWS, BLOCK),
             stepped(lags, ROWS),
             whole(flat),
-            whole(flat),
             bins,
-        ],
+        ]
+        + [whole(part)] * BLOCKS,
         [whole(flat), whole(reach), whole(slots)],
         [shaped(flat), shaped(reach), shaped(slots)],
         [pltpu.VMEM(local, BF16), pltpu.VMEM((lags + SLOT, LANES), F32)],
         STEPS,
         CROSS_FLOPS,
-    )(own, lagged, cotangent, gate, spectrum)
+    )(place, own, lagged, cotangent, spectrum, *gates)
     grad_halo = shift(head, -1)
     lag_parts = exchange(lag_grad, CTX)
 
@@ -350,18 +342,13 @@
         STEPS,
         BACK_FLOPS,
     )(place, forward, first, grad, grad_halo, response, conv, cotangent)
-    gate_grad, key_grad, value_grad = call(
+    gate_grad, key_grad, value_grad, filter_grad = call(
         final_kernel,
-        [scalar] + [whole(ship)] * BLOCKS + [whole(local)] * 2,
-        [whole(local)] * 3,
-        [shaped(local)] * 3,
-    )(place, *swap(ships), key_input, value_input)
-    filter_grad = call(
-        sum_kernel,
-        [whole(lag_parts.shape)],
-        whole((share, WIDE)),
-        shaped((share, WIDE), F32),
-    )(lag_parts)
+        [scalar] + [whole(ship)] * BLOCKS + [whole(local)] * 2 + [whole(slots)],
+        [whole(local)] * 3 + [whole((share, WIDE))],
+        [shaped(local)] * 3 + [shaped((share, WIDE), F32)],
+        limit=FINAL_LIMIT,
+    )(place, *swap(ships), key_input, value_input, lag_parts)
     return gate_grad, key_grad, value_grad, filter_grad
 
 

time: 98.9 us -> 100 us (1.011)
  blocking collectives: 0 us -> 15.2 us
  starting transfers between devices: 60.7 us -> 53.3 us
  Pallas kernels: 22.5 us -> 17.6 us
  local copies, waits for them, and re-layouts: 4.84 us -> 3.7 us
    all_to_all x0 -> x1, blocking collectives: none -> 15.2 us  [exchange(): return lax.all_to_all(value, axes, split_axis=0, concat_axis=0, tiled=True)]
    ppermute x6, starting transfers between devices: 22.1 us -> 15.7 us  [swap(): lax.ppermute(ships[hop], GROUP, [(i, i ^ hop) for i in range(BLOCKS)])]
    pallas_call x3 -> x1, Pallas kernels: 7.95 us -> 4.33 us  [body(): call(functools.partial(cross_kernel, norm), [scalar, stepped(ROWS, BLOCK)...]
    ppermute x2, waiting for transfers between devices: 3.61 us -> 0.01 us  [shift(): lax.ppermute(value, RUNS, [(i, i + steps) for i in range(first, last)])]
    ppermute x2, starting transfers between devices: 5.8 us -> 2.58 us  [shift(): lax.ppermute(value, RUNS, [(i, i + steps) for i in range(first, last)])]
    all_to_all x2, waiting for transfers between devices: 0.01 us -> 2.95 us  [exchange(): return lax.all_to_all(value, axes, split_axis=0, concat_axis=0, tiled=True)]
    all_to_all x2, starting transfers between devices: 32.8 us -> 35 us  [exchange(): return lax.all_to_all(value, axes, split_axis=0, concat_axis=0, tiled=True)]
    pallas_call x1, Pallas kernels: 2.25 us -> 1 us  [body(): call(final_kernel, [scalar] + [whole(ship)] * BLOCKS + [whole(local)] * 2...]
  transfers between devices with their start and end apart: 10 -> 10, of which waited for: 3 -> 4; matrix products, arithmetic and copies ran while one was open for 1% -> 1% of each run, Pallas kernels for 14% -> 10%
where the time goes in v6:
time: 100 us; the launch traced here: 99.4 us
  starting transfers between devices  53.3 us (53%)
  Pallas kernels  17.6 us (18%)
  blocking collectives  15.2 us (15%)
  waiting for transfers between devices  8.82 us (9%)
  local copies, waits for them, and re-layouts  3.7 us (4%)
    all_to_all x2, starting transfers between devices, exchange(): return lax.all_to_all(value, axes, split_axis=0, concat_axis=0, tiled=True)  35 us
    ppermute x6, starting transfers between devices, swap(): lax.ppermute(ships[hop], GROUP, [(i, i ^ hop) for i in range(BLOCKS)])  15.7 us
    all_to_all x1, blocking collectives, exchange(): return lax.all_to_all(value, axes, split_axis=0, concat_axis=0, tiled=True)  15.2 us
    ppermute x6, waiting for transfers between devices, swap(): lax.ppermute(ships[hop], GROUP, [(i, i ^ hop) for i in range(BLOCKS)])  5.86 us
    pallas_call x1, Pallas kernels, body(): call(functools.partial(conv_kernel, norm), [table, stepped(BLOCK, ROWS),...  5.17 us
    pallas_call x1, Pallas kernels, body(): call(functools.partial(back_kernel, norm), [scalar, table, stepped(BLOCK,...  4.86 us
    pallas_call x1, Pallas kernels, body(): call(functools.partial(cross_kernel, norm), [scalar, stepped(ROWS, BLOCK)...  4.33 us
    unnamed x22, local copies, waits for them, and re-layouts  2.98 us
  transfers between devices with their start and end apart: 10, of which 4 were waited for; matrix products, arithmetic and copies ran while one was open for 1% of the time, Pallas kernels for 10%

profile of v6, /device:TPU:1, one launch (start us, length us, event | category | flops | bytes accessed | tf_op | source)
XLA Modules:
  0.0 99.4 jit_solution(12724304413721449489)
XLA Ops:
  0.6 0.0 copy-start
  0.7 2.2 %shard_map.129 = (bf16[4,256,128]{2,1,0:T(8,128)(2,1)}, bf16[256,128]{1,0:T(8,128)(2,1)}, bf16[256,128]{1,0:T(8,128)(2,1)}, bf16[256,128]{1,0:T(8,128)(2,1)}, bf...) custom-call(s32[1]{0:T(128)} %bitcast.place, bf16[256,512]{1,0:T(8,128)(2,1)} %refs_4_.1, bf16[256,512]{1,0:T(8,128)(2,1)} %refs_5_.1, ...), custom_call_target="tpu_custom_call" | custom-call | tf_op jit(solution)/shard_map/pallas_call | solution.py:274
  2.9 15.2 %all_to_all.15 = bf16[4,256,128]{2,1,0:T(8,128)(2,1)S(1)} all-to-all(bf16[4,256,128]{2,1,0:T(8,128)(2,1)} %get-tuple-element.21), channel_id=1, replica_groups=mesh['z'=8,'yh'=2,'yl'=2,'c'=2,'x'=4,'zh'=2] {'yl','c'}, dimensions={0} | all-to-all | bytes 524288 | tf_op jit(solution)/shard_map/all_to_all | solution.py:255
  18.1 0.0 copy-start.5
  18.1 1.3 %collective-permute-start = (bf16[768,128]{1,0:T(8,128)(2,1)S(1)}, bf16[768,128]{1,0:T(8,128)(2,1)S(1)}, u32[]{:S(2)}, u32[]{:S(2)}) collective-permute-start(bf16[768,128]{1,0:T(8,128)(2,1)S(1)} %bitcast.7), channel_id=1, source_target_pairs={{0,32},{32,64},{64,96},{96,128},{128,160},{160,192},{192,224},{224... | collective-permute-start | bytes 589832 | tf_op jit(solution)/shard_map/ppermute | solution.py:244
  19.5 17.2 %all-to-all-start = ((bf16[32,32,128]{2,1,0:T(8,128)(2,1)}), bf16[32,32,128]{2,1,0:T(8,128)(2,1)S(1)}, u32[]{:S(2)}, u32[]{:S(2)}) async-start(bf16[32,32,128]{2,1,0:T(8,128)(2,1)} %get-tuple-element.20), calls=%async_computation | async-start | bytes 524288 | tf_op jit(solution)/shard_map/all_to_all | solution.py:255
  36.7 2.1 %collective-permute-start.1 = (bf16[256,128]{1,0:T(8,128)(2,1)}, bf16[256,128]{1,0:T(8,128)(2,1)S(1)}, u32[]{:S(2)}, u32[]{:S(2)}) collective-permute-start(bf16[256,128]{1,0:T(8,128)(2,1)} %get-tuple-element.24), channel_id=1, source_target_pairs={{0,8},{8,0},{16,24},{24,16},{1,9},{9,1},{17,25},{25,17},{2,10},{10... | collective-permute-start | bytes 196616 | tf_op jit(solution)/shard_map/ppermute | solution.py:249
  38.8 3.4 %collective-permute-start.2 = (bf16[256,128]{1,0:T(8,128)(2,1)}, bf16[256,128]{1,0:T(8,128)(2,1)S(1)}, u32[]{:S(2)}, u32[]{:S(2)}) collective-permute-start(bf16[256,128]{1,0:T(8,128)(2,1)} %get-tuple-element.25), channel_id=1, source_target_pairs={{0,16},{8,24},{16,0},{24,8},{1,17},{9,25},{17,1},{25,9},{2,18},{10... | collective-permute-start | bytes 196616 | tf_op jit(solution)/shard_map/ppermute | solution.py:249
  42.2 2.3 %collective-permute-start.3 = (bf16[256,128]{1,0:T(8,128)(2,1)}, bf16[256,128]{1,0:T(8,128)(2,1)S(1)}, u32[]{:S(2)}, u32[]{:S(2)}) collective-permute-start(bf16[256,128]{1,0:T(8,128)(2,1)} %get-tuple-element.26), channel_id=1, source_target_pairs={{0,24},{8,16},{16,8},{24,0},{1,25},{9,17},{17,9},{25,1},{2,26},{10... | collective-permute-start | bytes 196616 | tf_op jit(solution)/shard_map/ppermute | solution.py:249
  44.6 0.0 copy-done
  44.6 0.7 constant_dynamic-slice_fusion.taps
  45.3 0.0 collective-permute-done.halo
  45.3 0.0 copy-start.9
  45.3 0.0 copy-done.5
  45.3 0.7 copy-done.9
  46.0 5.2 %shard_map.130 = (f32[1024,128]{1,0:T(8,128)}, bf16[1024,512]{1,0:T(8,128)(2,1)}, bf16[1024,128]{1,0:T(8,128)(2,1)}) custom-call(bf16[1,1024,1024]{2,1,0:T(8,128)(2,1)} %constant.28.clone.forward, bf16[1,256,1024]{2,1,0:T(8,128)(2,1)} %constant.32.clone.inverse, bf16[768,128]{1,0:T(8,128)(2,1)} %copy-done.9, bf16[1024,128]{1,0:T(8,128)(2,1)} %bitcast.6, ...), custom_call_target="tpu_custom_call" | custom-call | flops 24000000000 | tf_op jit(solution)/shard_map/pallas_call | solution.py:292
  51.1 0.0 collective-permute-done.1.refs_1_
  51.1 0.0 copy-start.6
  51.1 0.0 collective-permute-done.2.refs_2_
  51.1 0.0 copy-start.7
  51.1 0.0 collective-permute-done.3.refs_3_
  51.2 0.0 copy-start.8
  51.2 2.4 %all-to-all-done = bf16[32,32,128]{2,1,0:T(8,128)(2,1)S(1)} async-done(((bf16[32,32,128]{2,1,0:T(8,128)(2,1)}), bf16[32,32,128]{2,1,0:T(8,128)(2,1)S(1)}, u32[]{:S(2)}, u32[]{:S(2)}) %all-to-all-start) | async-done | bytes 262176 | tf_op jit(solution)/shard_map/all_to_all | solution.py:255
  53.6 0.0 copy-start.4
  53.6 0.0 copy-done.6
  53.6 0.0 copy-done.7
  53.6 0.0 copy-done.8
  53.6 0.7 copy-done.4
  54.3 4.3 %shard_map.131 = (bf16[1024,128]{1,0:T(8,128)(2,1)}, bf16[768,128]{1,0:T(8,128)(2,1)}, bf16[64,16,128]{2,1,0:T(8,128)(2,1)}) custom-call(s32[1]{0:T(128)} %bitcast.place, bf16[1,1024,256]{2,1,0:T(8,128)(2,1)} %constant.29.clone.forward, bf16[1,768,1024]{2,1,0:T(8,128)(2,1)} %constant.31.clone.inverse, bf16[1024,128]{1,0:T(8,128)(2,1)} %bitcast.4, ...), custom_call_target="tpu_custom_call" | custom-call | tf_op jit(solution)/shard_map/pallas_call | solution.py:308
  58.6 1.3 %collective-permute-start.4 = (bf16[768,128]{1,0:T(8,128)(2,1)}, bf16[768,128]{1,0:T(8,128)(2,1)S(1)}, u32[]{:S(2)}, u32[]{:S(2)}) collective-permute-start(bf16[768,128]{1,0:T(8,128)(2,1)} %get-tuple-element.28), channel_id=1, source_target_pairs={{32,0},{64,32},{96,64},{128,96},{160,128},{192,160},{224,192},{256... | collective-permute-start | bytes 589832 | tf_op jit(solution)/shard_map/ppermute | solution.py:244
  59.9 17.8 %all-to-all-start.2 = ((bf16[64,16,128]{2,1,0:T(8,128)(2,1)}), bf16[64,16,128]{2,1,0:T(8,128)(2,1)S(1)}, u32[]{:S(2)}, u32[]{:S(2)}) async-start(bf16[64,16,128]{2,1,0:T(8,128)(2,1)} %get-tuple-element.35), calls=%async_computation.2 | async-start | bytes 524288 | tf_op jit(solution)/shard_map/all_to_all | solution.py:255
  77.7 0.0 collective-permute-done.4.halo
  77.7 0.0 copy-start.10
  77.7 0.7 copy-done.10
  78.3 0.0 copy-start.1
  78.4 0.0 copy-start.2
  78.4 4.9 %shard_map.132 = (bf16[512,128]{1,0:T(8,128)(2,1)}, bf16[512,128]{1,0:T(8,128)(2,1)}, bf16[512,128]{1,0:T(8,128)(2,1)}, bf16[512,128]{1,0:T(8,128)(2,1)}) custom-call(s32[1]{0:T(128)} %bitcast.place, bf16[1,1024,1024]{2,1,0:T(8,128)(2,1)} %constant.28.clone.forward, bf16[1,256,1024]{2,1,0:T(8,128)(2,1)} %constant.30.clone.inverse, ...), custom_call_target="tpu_custom_call" | custom-call | flops 35000000512 | tf_op jit(solution)/shard_map/pallas_call | solution.py:327
  83.2 2.3 %collective-permute-start.5 = (bf16[512,128]{1,0:T(8,128)(2,1)}, bf16[512,128]{1,0:T(8,128)(2,1)S(1)}, u32[]{:S(2)}, u32[]{:S(2)}) collective-permute-start(bf16[512,128]{1,0:T(8,128)(2,1)} %get-tuple-element.32), channel_id=1, source_target_pairs={{0,8},{8,0},{16,24},{24,16},{1,9},{9,1},{17,25},{25,17},{2,10},{10... | collective-permute-start | bytes 393224 | tf_op jit(solution)/shard_map/ppermute | solution.py:249
  85.6 3.2 %collective-permute-start.6 = (bf16[512,128]{1,0:T(8,128)(2,1)}, bf16[512,128]{1,0:T(8,128)(2,1)S(1)}, u32[]{:S(2)}, u32[]{:S(2)}) collective-permute-start(bf16[512,128]{1,0:T(8,128)(2,1)} %get-tuple-element.33), channel_id=1, source_target_pairs={{0,16},{8,24},{16,0},{24,8},{1,17},{9,25},{17,1},{25,9},{2,18},{10... | collective-permute-start | bytes 393224 | tf_op jit(solution)/shard_map/ppermute | solution.py:249
  88.8 2.3 %collective-permute-start.7 = (bf16[512,128]{1,0:T(8,128)(2,1)}, bf16[512,128]{1,0:T(8,128)(2,1)S(1)}, u32[]{:S(2)}, u32[]{:S(2)}) collective-permute-start(bf16[512,128]{1,0:T(8,128)(2,1)} %get-tuple-element.34), channel_id=1, source_target_pairs={{0,24},{8,16},{16,8},{24,0},{1,25},{9,17},{17,9},{25,1},{2,26},{10... | collective-permute-start | bytes 393224 | tf_op jit(solution)/shard_map/ppermute | solution.py:249
  91.1 0.0 collective-permute-done.5.refs_1_
  91.1 2.1 %collective-permute-done.6.refs_2_ = bf16[512,128]{1,0:T(8,128)(2,1)S(1)} collective-permute-done((bf16[512,128]{1,0:T(8,128)(2,1)}, bf16[512,128]{1,0:T(8,128)(2,1)S(1)}, u32[]{:S(2)}, u32[]{:S(2)}) %collective-permute-start.6) | collective-permute-done | bytes 131104 | tf_op jit(solution)/shard_map/ppermute | solution.py:249
  93.2 3.7 %collective-permute-done.7.refs_3_ = bf16[512,128]{1,0:T(8,128)(2,1)S(1)} collective-permute-done((bf16[512,128]{1,0:T(8,128)(2,1)}, bf16[512,128]{1,0:T(8,128)(2,1)S(1)}, u32[]{:S(2)}, u32[]{:S(2)}) %collective-permute-start.7) | collective-permute-done | bytes 131104 | tf_op jit(solution)/shard_map/ppermute | solution.py:249
  97.0 0.6 all-to-all-done.2.refs_6_
  97.5 0.0 copy-done.1
  97.5 0.0 copy-done.2
  97.5 0.9 copy-done.3
  98.4 1.0 %shard_map.133 = (bf16[256,512]{1,0:T(8,128)(2,1)}, bf16[256,512]{1,0:T(8,128)(2,1)}, bf16[256,512]{1,0:T(8,128)(2,1)}, f32[12,512]{1,0:T(8,128)}) custom-call(s32[1]{0:T(128)} %bitcast.place, bf16[512,128]{1,0:T(8,128)(2,1)S(1)} %copy-done.3, bf16[512,128]{1,0:T(8,128)(2,1)S(1)} %collective-permute-done.5.refs_1_, ...), custom_call_target="tpu_custom_call" | custom-call | tf_op jit(solution)/shard_map/pallas_call | solution.py:345
  (2 shorter events, 0.0 us)
Async XLA Ops:
  0.6 43.9 %copy-start = (bf16[768,512]{1,0:T(8,128)(2,1)S(1)}, bf16[768,512]{1,0:T(8,128)(2,1)}, u32[]{:S(2)}) copy-start(bf16[768,512]{1,0:T(8,128)(2,1)} %param.14) | copy-start | bytes 2359300
  18.1 27.1 %copy-start.5 = (bf16[4,256,128]{2,1,0:T(8,128)(2,1)}, bf16[4,256,128]{2,1,0:T(8,128)(2,1)S(1)}, u32[]{:S(2)}) copy-start(bf16[4,256,128]{2,1,0:T(8,128)(2,1)S(1)} %all_to_all.15) | copy-start | bytes 786436
  18.1 27.1 %collective-permute-start = (bf16[768,128]{1,0:T(8,128)(2,1)S(1)}, bf16[768,128]{1,0:T(8,128)(2,1)S(1)}, u32[]{:S(2)}, u32[]{:S(2)}) collective-permute-start(bf16[768,128]{1,0:T(8,128)(2,1)S(1)} %bitcast.7), channel_id=1, source_target_pairs={{0,32},{32,64},{64,96},{96,128},{128,160},{160,192},{192,224},{224... | collective-permute-start | bytes 589832 | tf_op jit(solution)/shard_map/ppermute | solution.py:244
  19.5 34.1 %all-to-all-start = ((bf16[32,32,128]{2,1,0:T(8,128)(2,1)}), bf16[32,32,128]{2,1,0:T(8,128)(2,1)S(1)}, u32[]{:S(2)}, u32[]{:S(2)}) async-start(bf16[32,32,128]{2,1,0:T(8,128)(2,1)} %get-tuple-element.20), calls=%async_computation | async-start | bytes 524288 | tf_op jit(solution)/shard_map/all_to_all | solution.py:255
  36.7 14.5 %collective-permute-start.1 = (bf16[256,128]{1,0:T(8,128)(2,1)}, bf16[256,128]{1,0:T(8,128)(2,1)S(1)}, u32[]{:S(2)}, u32[]{:S(2)}) collective-permute-start(bf16[256,128]{1,0:T(8,128)(2,1)} %get-tuple-element.24), channel_id=1, source_target_pairs={{0,8},{8,0},{16,24},{24,16},{1,9},{9,1},{17,25},{25,17},{2,10},{10... | collective-permute-start | bytes 196616 | tf_op jit(solution)/shard_map/ppermute | solution.py:249
  38.8 12.3 %collective-permute-start.2 = (bf16[256,128]{1,0:T(8,128)(2,1)}, bf16[256,128]{1,0:T(8,128)(2,1)S(1)}, u32[]{:S(2)}, u32[]{:S(2)}) collective-permute-start(bf16[256,128]{1,0:T(8,128)(2,1)} %get-tuple-element.25), channel_id=1, source_target_pairs={{0,16},{8,24},{16,0},{24,8},{1,17},{9,25},{17,1},{25,9},{2,18},{10... | collective-permute-start | bytes 196616 | tf_op jit(solution)/shard_map/ppermute | solution.py:249
  42.2 8.9 %collective-permute-start.3 = (bf16[256,128]{1,0:T(8,128)(2,1)}, bf16[256,128]{1,0:T(8,128)(2,1)S(1)}, u32[]{:S(2)}, u32[]{:S(2)}) collective-permute-start(bf16[256,128]{1,0:T(8,128)(2,1)} %get-tuple-element.26), channel_id=1, source_target_pairs={{0,24},{8,16},{16,8},{24,0},{1,25},{9,17},{17,9},{25,1},{2,26},{10... | collective-permute-start | bytes 196616 | tf_op jit(solution)/shard_map/ppermute | solution.py:249
  45.3 0.7 copy-start.9
  51.1 2.4 %copy-start.6 = (bf16[256,128]{1,0:T(8,128)(2,1)}, bf16[256,128]{1,0:T(8,128)(2,1)S(1)}, u32[]{:S(2)}) copy-start(bf16[256,128]{1,0:T(8,128)(2,1)S(1)} %collective-permute-done.1.refs_1_) | copy-start | bytes 196612
  51.1 2.4 %copy-start.7 = (bf16[256,128]{1,0:T(8,128)(2,1)}, bf16[256,128]{1,0:T(8,128)(2,1)S(1)}, u32[]{:S(2)}) copy-start(bf16[256,128]{1,0:T(8,128)(2,1)S(1)} %collective-permute-done.2.refs_2_) | copy-start | bytes 196612
  51.2 2.4 %copy-start.8 = (bf16[256,128]{1,0:T(8,128)(2,1)}, bf16[256,128]{1,0:T(8,128)(2,1)S(1)}, u32[]{:S(2)}) copy-start(bf16[256,128]{1,0:T(8,128)(2,1)S(1)} %collective-permute-done.3.refs_3_) | copy-start | bytes 196612
  53.6 0.7 copy-start.4
  58.6 19.1 %collective-permute-start.4 = (bf16[768,128]{1,0:T(8,128)(2,1)}, bf16[768,128]{1,0:T(8,128)(2,1)S(1)}, u32[]{:S(2)}, u32[]{:S(2)}) collective-permute-start(bf16[768,128]{1,0:T(8,128)(2,1)} %get-tuple-element.28), channel_id=1, source_target_pairs={{32,0},{64,32},{96,64},{128,96},{160,128},{192,160},{224,192},{256... | collective-permute-start | bytes 589832 | tf_op jit(solution)/shard_map/ppermute | solution.py:244
  59.9 37.6 %all-to-all-start.2 = ((bf16[64,16,128]{2,1,0:T(8,128)(2,1)}), bf16[64,16,128]{2,1,0:T(8,128)(2,1)S(1)}, u32[]{:S(2)}, u32[]{:S(2)}) async-start(bf16[64,16,128]{2,1,0:T(8,128)(2,1)} %get-tuple-element.35), calls=%async_computation.2 | async-start | bytes 524288 | tf_op jit(solution)/shard_map/all_to_all | solution.py:255
  77.7 0.7 copy-start.10
  78.3 19.2 %copy-start.1 = (bf16[256,512]{1,0:T(8,128)(2,1)S(1)}, bf16[256,512]{1,0:T(8,128)(2,1)}, u32[]{:S(2)}) copy-start(bf16[256,512]{1,0:T(8,128)(2,1)} %refs_4_.1) | copy-start | bytes 786436
  78.4 19.2 %copy-start.2 = (bf16[256,512]{1,0:T(8,128)(2,1)S(1)}, bf16[256,512]{1,0:T(8,128)(2,1)}, u32[]{:S(2)}) copy-start(bf16[256,512]{1,0:T(8,128)(2,1)} %refs_5_.1) | copy-start | bytes 786436
  83.2 7.9 %collective-permute-start.5 = (bf16[512,128]{1,0:T(8,128)(2,1)}, bf16[512,128]{1,0:T(8,128)(2,1)S(1)}, u32[]{:S(2)}, u32[]{:S(2)}) collective-permute-start(bf16[512,128]{1,0:T(8,128)(2,1)} %get-tuple-element.32), channel_id=1, source_target_pairs={{0,8},{8,0},{16,24},{24,16},{1,9},{9,1},{17,25},{25,17},{2,10},{10... | collective-permute-start | bytes 393224 | tf_op jit(solution)/shard_map/ppermute | solution.py:249
  85.6 7.7 %collective-permute-start.6 = (bf16[512,128]{1,0:T(8,128)(2,1)}, bf16[512,128]{1,0:T(8,128)(2,1)S(1)}, u32[]{:S(2)}, u32[]{:S(2)}) collective-permute-start(bf16[512,128]{1,0:T(8,128)(2,1)} %get-tuple-element.33), channel_id=1, source_target_pairs={{0,16},{8,24},{16,0},{24,8},{1,17},{9,25},{17,1},{25,9},{2,18},{10... | collective-permute-start | bytes 393224 | tf_op jit(solution)/shard_map/ppermute | solution.py:249
  88.8 8.2 %collective-permute-start.7 = (bf16[512,128]{1,0:T(8,128)(2,1)}, bf16[512,128]{1,0:T(8,128)(2,1)S(1)}, u32[]{:S(2)}, u32[]{:S(2)}) collective-permute-start(bf16[512,128]{1,0:T(8,128)(2,1)} %get-tuple-element.34), channel_id=1, source_target_pairs={{0,24},{8,16},{16,8},{24,0},{1,25},{9,17},{17,9},{25,1},{2,26},{10... | collective-permute-start | bytes 393224 | tf_op jit(solution)/shard_map/ppermute | solution.py:249
  97.5 0.9 copy-start.3

commit v7 on v6

--- a/solution.py
+++ b/solution.py
@@ -77,20 +77,31 @@
         total[...] += part
 
 
-def prep_kernel(place, key, value, gate, out_grad, mixed, *outs):
+def prep_kernel(place, key, value, out_grad, *outs):
     ships, pieces = outs[:BLOCKS], outs[BLOCKS]
-    product = (key[...].astype(F32) * value[...].astype(F32)).astype(BF16)
+    for hop, ship in enumerate(ships):
+        at = (slice(None), lanes_at(place[0] ^ hop))
+        ship[...] = (key[at].astype(F32) * value[at].astype(F32)).astype(BF16)
+    for piece in range(pieces.shape[0]):
+        pieces[piece] = out_grad[:, piece * WIDE : (piece + 1) * WIDE]
+
+
+def join_kernel(place, *refs):
+    ships, (mixed, tail) = refs[:BLOCKS], refs[BLOCKS:]
+    for hop, ship in enumerate(ships):
+        mixed[rows_at(place[0] ^ hop), :] = ship[...]
+    tail[...] = mixed[TOKENS - tail.shape[0] :, :]
+
+
+def grad_kernel(cotangent, gate, grad):
+    product = (cotangent[...].astype(F32) * gate[...].astype(F32)).astype(BF16)
     for block in range(BLOCKS):
-        mixed[block] = product[:, lane_block(block)]
-    for hop, ship in enumerate(ships):
-        ship[...] = gate[:, lanes_at(place[0] ^ hop)]
-    count = pieces.shape[0]
-    for piece in range(count):
-        target = piece % BLOCKS * (count // BLOCKS) + piece // BLOCKS
-        pieces[target] = out_grad[:, lane_block(piece)]
-
-
-def conv_kernel(scale, forward, inverse, halo, mixed, taps, conv, spectrum, response, windows, total):
+        grad[block] = product[:, lane_block(block)]
+
+
+def conv_kernel(
+    scale, place, forward, inverse, halo, mixed, taps, conv, spectrum, response, windows, total
+):
     step = pl.program_id(0)
     lags = taps.shape[0]
 
@@ -114,22 +125,17 @@
     @pl.when(step == STEPS - 1)
     def _():
         for block in range(BLOCKS):
-            conv[token_block(block), :] = total[:, lane_block(block)] * scale
-
-
-def cross_kernel(scale, place, forward, inverse, cotangent, spectrum, *refs):
-    gates, (grad, head, lag_grad, windows, total) = refs[:BLOCKS], refs[BLOCKS:]
+            conv[token_block(block), :] = (total[:, lane_block(block)] * scale).astype(BF16)
+
+
+def cross_kernel(scale, forward, inverse, grad, spectrum, head, lag_grad, windows, total):
     step = pl.program_id(0)
 
     @pl.when(step == 0)
     def _():
-        for hop, gate in enumerate(gates):
-            block = place[0] ^ hop
-            at = rows_at(block)
-            product = (cotangent[at, :].astype(F32) * gate[...].astype(F32)).astype(BF16)
-            grad[at, :] = product
-            windows[:, lanes_at(block)] = product
         head[...] = grad[: head.shape[0], :]
+        for block in range(BLOCKS):
+            windows[:, lane_block(block)] = grad[token_block(block), :]
 
     spec = dot(forward[...], windows[...])
     g_re, g_im = spec[:BINS], spec[BINS:]
@@ -160,9 +166,7 @@
             lag_grad[slot] = rows.astype(BF16)
 
 
-def back_kernel(
-    scale, place, forward, inverse, grad, halo, response, conv, cotangent, *refs
-):
+def back_kernel(scale, place, forward, inverse, grad, halo, response, conv, *refs):
     outs, (windows, total) = refs[:BLOCKS], refs[BLOCKS:]
     step = pl.program_id(0)
 
@@ -174,8 +178,7 @@
             if own < PERIOD:
                 windows[own:, lane_block(block)] = halo[: PERIOD - own, :]
         for hop, out in enumerate(outs):
-            at = rows_at(place[0] ^ hop)
-            out[:BLOCK, :] = (cotangent[at, :].astype(F32) * conv[at, :]).astype(BF16)
+            out[:BLOCK, :] = conv[rows_at(place[0] ^ hop), :]
 
     spec = dot(forward[...], windows[...])
     resp = response[...].astype(F32)
@@ -191,14 +194,12 @@
 
 
 def final_kernel(place, *refs):
-    ships, (key, value, parts, gate_grad, key_grad, value_grad, lag_grad) = (
-        refs[:BLOCKS],
-        refs[BLOCKS:],
-    )
+    ships, refs = refs[:BLOCKS], refs[BLOCKS:]
+    cotangent, key, value, parts, gate_grad, key_grad, value_grad, lag_grad = refs
     for hop, ship in enumerate(ships):
         at = (slice(None), lanes_at(place[0] ^ hop))
-        gate_grad[at] = ship[:BLOCK, :]
-        back = ship[BLOCK:, :].astype(F32)
+        conv, back = ship[:BLOCK, :].astype(F32), ship[BLOCK:, :].astype(F32)
+        gate_grad[at] = (cotangent[at].astype(F32) * conv).astype(BF16)
         key_grad[at] = (back * value[at].astype(F32)).astype(BF16)
         value_grad[at] = (back * key[at].astype(F32)).astype(BF16)
     for block in range(BLOCKS):
@@ -216,14 +217,17 @@
     return jax.ShapeDtypeStruct(shape, dtype)
 
 
-def call(kernel, in_specs, out_specs, out_shape, scratch=(), steps=1, flops=0, limit=None):
+def call(kernel, in_specs, out_specs, out_shape, scratch=(), steps=1, flops=0, limit=None, scalars=0):
     return pl.pallas_call(
         kernel,
-        grid=(steps,),
-        in_specs=in_specs,
-        out_specs=out_specs,
+        grid_spec=pltpu.PrefetchScalarGridSpec(
+            num_scalar_prefetch=scalars,
+            grid=(steps,),
+            in_specs=in_specs,
+            out_specs=out_specs,
+            scratch_shapes=scratch,
+        ),
         out_shape=out_shape,
-        scratch_shapes=scratch,
         compiler_params=pltpu.CompilerParams(
             dimension_semantics=("arbitrary",), vmem_limit_bytes=limit or VMEM_LIMIT
         ),
@@ -235,6 +239,7 @@
 FINAL_LIMIT = 16 * MIB
 CONV_FLOPS = 24_000_000_000
 CROSS_FLOPS = 0
+JOIN_FLOPS = 0
 BACK_FLOPS = 35_000_000_000
 
 
@@ -262,7 +267,7 @@
     norm = 2.0 / PERIOD / lags**0.5
     local = (BLOCK, WIDE)
     ship = (2 * BLOCK, LANES)
-    pieces = (channels // LANES, held, LANES)
+    pieces = (channels // WIDE, held, WIDE)
     flat = (TOKENS, LANES)
     reach = (lags, LANES)
     slots = (lags // share, SLOT, LANES)
@@ -271,24 +276,32 @@
 
     part = (BLOCK, LANES)
     by_block = (BLOCKS, BLOCK, LANES)
-    mixed, *gates, cotangent = call(
+    *ships, cotangent = call(
         prep_kernel,
-        [scalar] + [whole(local)] * 3 + [whole(out_grad.shape)],
-        [whole(by_block)] + [whole(part)] * BLOCKS + [whole(pieces)],
-        [shaped(by_block)] + [shaped(part)] * BLOCKS + [shaped(pieces)],
-    )(place, key_input, value_input, gate_input, out_grad)
-    mixed = exchange(mixed, GROUP).reshape(flat)
-    mixed_halo = shift(mixed[TOKENS - lags :], 1)
-    cotangent = exchange(cotangent, GROUP + CH).reshape(flat)
-    gates = swap(gates)
-    taps = lax.dynamic_slice_in_dim(filter_taps, lax.axis_index(GROUP) * LANES, LANES, 1)
+        [scalar] + [whole(local)] * 2 + [whole(out_grad.shape)],
+        [whole(part)] * BLOCKS + [whole(pieces)],
+        [shaped(part)] * BLOCKS + [shaped(pieces)],
+    )(place, key_input, value_input, out_grad)
+    cotangent = exchange(cotangent, CH).reshape(local)
+    mixed, tail = call(
+        join_kernel,
+        [scalar] + [whole(part)] * BLOCKS,
+        [whole(flat), whole(reach)],
+        [shaped(flat), shaped(reach)],
+        flops=JOIN_FLOPS,
+    )(place, *swap(ships))
+    mixed_halo = shift(tail, 1)
+    grad = call(grad_kernel, [whole(local)] * 2, whole(by_block), shaped(by_block))(
+        cotangent, gate_input
+    )
+    grad = exchange(grad, GROUP).reshape(flat)
 
     def stepped(*shape):
-        return pl.BlockSpec((None,) + shape, lambda step: (step, 0, 0))
+        return pl.BlockSpec((None,) + shape, lambda step, *_: (step, 0, 0))
 
     table = stepped(ROWS, PERIOD)
-    bins = pl.BlockSpec((ROWS, WIDE), lambda step: (step, 0))
-    narrow_bins = pl.BlockSpec((ROWS, LANES), lambda step: (step, 0))
+    bins = pl.BlockSpec((ROWS, WIDE), lambda step, *_: (step, 0))
+    narrow_bins = pl.BlockSpec((ROWS, LANES), lambda step, *_: (step, 0))
     conv, spectrum, response = call(
         functools.partial(conv_kernel, norm),
         [
@@ -296,31 +309,25 @@
             stepped(BLOCK, ROWS),
             whole(reach),
             whole(flat),
-            whole(reach),
+            pl.BlockSpec(reach, lambda step, place: (0, place[0])),
         ],
         [whole(flat), bins, narrow_bins],
-        [shaped(flat, F32), shaped((PERIOD, WIDE)), shaped((PERIOD, LANES))],
+        [shaped(flat), shaped((PERIOD, WIDE)), shaped((PERIOD, LANES))],
         [pltpu.VMEM((PERIOD, WIDE), BF16), pltpu.VMEM(local, F32)],
         STEPS,
         CONV_FLOPS,
-    )(forward, last, mixed_halo, mixed, taps)
-
-    grad, head, lag_grad = call(
+        scalars=1,
+    )(place, forward, last, mixed_halo, mixed, filter_taps)
+
+    head, lag_grad = call(
         functools.partial(cross_kernel, norm),
-        [
-            scalar,
-            stepped(ROWS, BLOCK),
-            stepped(lags, ROWS),
-            whole(flat),
-            bins,
-        ]
-        + [whole(part)] * BLOCKS,
-        [whole(flat), whole(reach), whole(slots)],
-        [shaped(flat), shaped(reach), shaped(slots)],
+        [stepped(ROWS, BLOCK), stepped(lags, ROWS), whole(flat), bins],
+        [whole(reach), whole(slots)],
+        [shaped(reach), shaped(slots)],
         [pltpu.VMEM(local, BF16), pltpu.VMEM((lags + SLOT, LANES), F32)],
         STEPS,
         CROSS_FLOPS,
-    )(place, own, lagged, cotangent, spectrum, *gates)
+    )(own, lagged, grad, spectrum)
     grad_halo = shift(head, -1)
     lag_parts = exchange(lag_grad, CTX)
 
@@ -334,21 +341,20 @@
             whole(reach),
             narrow_bins,
             whole(flat),
-            whole(flat),
         ],
         [whole(ship)] * BLOCKS,
         [shaped(ship)] * BLOCKS,
         [pltpu.VMEM((PERIOD, WIDE), BF16), pltpu.VMEM(local, F32)],
         STEPS,
         BACK_FLOPS,
-    )(place, forward, first, grad, grad_halo, response, conv, cotangent)
+    )(place, forward, first, grad, grad_halo, response, conv)
     gate_grad, key_grad, value_grad, filter_grad = call(
         final_kernel,
-        [scalar] + [whole(ship)] * BLOCKS + [whole(local)] * 2 + [whole(slots)],
+        [scalar] + [whole(ship)] * BLOCKS + [whole(local)] * 3 + [whole(slots)],
         [whole(local)] * 3 + [whole((share, WIDE))],
         [shaped(local)] * 3 + [shaped((share, WIDE), F32)],
         limit=FINAL_LIMIT,
-    )(place, *swap(ships), key_input, value_input, lag_parts)
+    )(place, *swap(ships), cotangent, key_input, value_input, lag_parts)
     return gate_grad, key_grad, value_grad, filter_grad
 
 

time: 100 us -> 97.3 us (0.973)
  blocking collectives: 15.2 us -> 0 us
  starting transfers between devices: 53.3 us -> 60.3 us
  Pallas kernels: 17.6 us -> 20.5 us
  waiting for transfers between devices: 8.82 us -> 10.7 us
    all_to_all x1 -> x0, blocking collectives: 15.2 us -> none  [exchange(): return lax.all_to_all(value, axes, split_axis=0, concat_axis=0, tiled=True)]
    ppermute x6, waiting for transfers between devices: 5.86 us -> 10 us  [swap(): lax.ppermute(ships[hop], GROUP, [(i, i ^ hop) for i in range(BLOCKS)])]
    all_to_all x2 -> x3, starting transfers between devices: 35 us -> 38.3 us  [exchange(): return lax.all_to_all(value, axes, split_axis=0, concat_axis=0, tiled=True)]
    ppermute x2, starting transfers between devices: 2.58 us -> 5.82 us  [shift(): lax.ppermute(value, RUNS, [(i, i + steps) for i in range(first, last)])]
    pallas_call x3 -> x5, Pallas kernels: 7.55 us -> 10.7 us  [the longest x1 4.25 us: body(): call(functools.partial(cross_kernel, norm), [stepped(ROWS, BLOCK), steppe...]
    all_to_all x2 -> x3, waiting for transfers between devices: 2.95 us -> 0.68 us  [exchange(): return lax.all_to_all(value, axes, split_axis=0, concat_axis=0, tiled=True)]
    unnamed x22, local copies, waits for them, and re-layouts: 2.98 us -> 4.29 us
  transfers between devices with their start and end apart: 10 -> 11, of which waited for: 4 -> 5; matrix products, arithmetic and copies ran while one was open for 1% -> 0% of each run, Pallas kernels for 10% -> 14%
where the time goes in v7:
time: 97.3 us; the launch traced here: 96.6 us
  starting transfers between devices  60.3 us (62%)
  Pallas kernels  20.5 us (21%)
  waiting for transfers between devices  10.7 us (11%)
  local copies, waits for them, and re-layouts  4.29 us (4%)
    all_to_all x3, starting transfers between devices, exchange(): return lax.all_to_all(value, axes, split_axis=0, concat_axis=0, tiled=True)  38.3 us
    ppermute x6, starting transfers between devices, swap(): lax.ppermute(ships[hop], GROUP, [(i, i ^ hop) for i in range(BLOCKS)])  16.2 us
    ppermute x6, waiting for transfers between devices, swap(): lax.ppermute(ships[hop], GROUP, [(i, i ^ hop) for i in range(BLOCKS)])  10 us
    ppermute x2, starting transfers between devices, shift(): lax.ppermute(value, RUNS, [(i, i + steps) for i in range(first, last)])  5.82 us
    pallas_call x1, Pallas kernels, body(): call(functools.partial(conv_kernel, norm), [table, stepped(BLOCK, ROWS),...  5.1 us
    pallas_call x1, Pallas kernels, body(): call(functools.partial(back_kernel, norm), [scalar, table, stepped(BLOCK,...  4.69 us
    unnamed x22, local copies, waits for them, and re-layouts  4.29 us
    pallas_call x1, Pallas kernels, body(): call(functools.partial(cross_kernel, norm), [stepped(ROWS, BLOCK), steppe...  4.25 us
  transfers between devices with their start and end apart: 11, of which 5 were waited for; matrix products, arithmetic and copies ran while one was open for 0% of the time, Pallas kernels for 14%

profile of v7, /device:TPU:1, one launch (start us, length us, event | category | flops | bytes accessed | tf_op | source)
XLA Modules:
  0.0 96.6 jit_solution(11021270158119081846)
XLA Ops:
  0.6 1.9 %shard_map.129 = (bf16[256,128]{1,0:T(8,128)(2,1)}, bf16[256,128]{1,0:T(8,128)(2,1)}, bf16[256,128]{1,0:T(8,128)(2,1)}, bf16[256,128]{1,0:T(8,128)(2,1)}, bf16[8,32,512]{2,1,0:T(8,128)(2,1)}) custom-call(s32[1]{0:T(128)} %bitcast.place, bf16[256,512]{1,0:T(8,128)(2,1)} %refs_5_.1, bf16[256,512]{1,0:T(8,128)(2,1)} %refs_6_.1, bf16[32,4096]{1,0:T(8,128)(2,1)} %out_grad.1), custom_call_target="tpu_custom_call" | custom-call | tf_op jit(solution)/shard_map/pallas_call | solution.py:279
  2.6 18.1 %all-to-all-start = ((bf16[8,32,512]{2,1,0:T(8,128)(2,1)}), bf16[8,32,512]{2,1,0:T(8,128)(2,1)S(1)}, u32[]{:S(2)}, u32[]{:S(2)}) async-start(bf16[8,32,512]{2,1,0:T(8,128)(2,1)} %get-tuple-element.20), calls=%async_computation | async-start | bytes 524288 | tf_op jit(solution)/shard_map/all_to_all | solution.py:260
  20.7 2.9 %collective-permute-start = (bf16[256,128]{1,0:T(8,128)(2,1)}, bf16[256,128]{1,0:T(8,128)(2,1)S(1)}, u32[]{:S(2)}, u32[]{:S(2)}) collective-permute-start(bf16[256,128]{1,0:T(8,128)(2,1)} %get-tuple-element.22), channel_id=1, source_target_pairs={{0,8},{8,0},{16,24},{24,16},{1,9},{9,1},{17,25},{25,17},{2,10},{10... | collective-permute-start | bytes 196616 | tf_op jit(solution)/shard_map/ppermute | solution.py:254
  23.5 3.2 %collective-permute-start.1 = (bf16[256,128]{1,0:T(8,128)(2,1)}, bf16[256,128]{1,0:T(8,128)(2,1)S(1)}, u32[]{:S(2)}, u32[]{:S(2)}) collective-permute-start(bf16[256,128]{1,0:T(8,128)(2,1)} %get-tuple-element.23), channel_id=1, source_target_pairs={{0,16},{8,24},{16,0},{24,8},{1,17},{9,25},{17,1},{25,9},{2,18},{10... | collective-permute-start | bytes 196616 | tf_op jit(solution)/shard_map/ppermute | solution.py:254
  26.7 2.3 %collective-permute-start.2 = (bf16[256,128]{1,0:T(8,128)(2,1)}, bf16[256,128]{1,0:T(8,128)(2,1)S(1)}, u32[]{:S(2)}, u32[]{:S(2)}) collective-permute-start(bf16[256,128]{1,0:T(8,128)(2,1)} %get-tuple-element.24), channel_id=1, source_target_pairs={{0,24},{8,16},{16,8},{24,0},{1,25},{9,17},{17,9},{25,1},{2,26},{10... | collective-permute-start | bytes 196616 | tf_op jit(solution)/shard_map/ppermute | solution.py:254
  29.0 0.0 collective-permute-done.refs_1_
  29.0 0.0 copy-start.6
  29.0 0.3 collective-permute-done.1.refs_2_
  29.3 0.0 copy-start.7
  29.3 3.8 %collective-permute-done.2.refs_3_ = bf16[256,128]{1,0:T(8,128)(2,1)S(1)} collective-permute-done((bf16[256,128]{1,0:T(8,128)(2,1)}, bf16[256,128]{1,0:T(8,128)(2,1)S(1)}, u32[]{:S(2)}, u32[]{:S(2)}) %collective-permute-start.2) | collective-permute-done | bytes 65568 | tf_op jit(solution)/shard_map/ppermute | solution.py:254
  33.1 0.0 copy-start.8
  33.1 0.0 copy-done.6
  33.1 0.0 copy-done.7
  33.1 0.6 copy-done.8
  33.7 1.7 %shard_map.131 = (bf16[1024,128]{1,0:T(8,128)(2,1)}, bf16[768,128]{1,0:T(8,128)(2,1)}) custom-call(s32[1]{0:T(128)} %bitcast.place, bf16[256,128]{1,0:T(8,128)(2,1)} %get-tuple-element.21.refs_0_, bf16[256,128]{1,0:T(8,128)(2,1)} %copy-done.6, bf16[256,128]{1,0:T(8,128)(2,1)} %copy-done.7, bf16[256,128]{1,0:T(8,128)(2,1)} %copy-done.8), custom_call_target="tpu_custom_call" | custom-call | tf_op jit(solution)/shard_map/pallas_call | solution.py:286
  35.5 4.5 %collective-permute-start.3 = (bf16[768,128]{1,0:T(8,128)(2,1)}, bf16[768,128]{1,0:T(8,128)(2,1)S(1)}, u32[]{:S(2)}, u32[]{:S(2)}) collective-permute-start(bf16[768,128]{1,0:T(8,128)(2,1)} %get-tuple-element.25), channel_id=1, source_target_pairs={{0,32},{32,64},{64,96},{96,128},{128,160},{160,192},{192,224},{224... | collective-permute-start | bytes 589832 | tf_op jit(solution)/shard_map/ppermute | solution.py:249
  40.0 0.0 all-to-all-done
  40.0 0.0 copy-start
  40.0 0.7 copy-done
  40.7 1.8 %shard_map.130 = bf16[4,256,128]{2,1,0:T(8,128)(2,1)} custom-call(bf16[256,512]{1,0:T(8,128)(2,1)} %bitcast.3, bf16[256,512]{1,0:T(8,128)(2,1)} %gate.1), custom_call_target="tpu_custom_call" | custom-call | tf_op jit(solution)/shard_map/pallas_call | solution.py:294
  42.5 3.7 %all-to-all-start.1 = ((bf16[4,256,128]{2,1,0:T(8,128)(2,1)}), bf16[4,256,128]{2,1,0:T(8,128)(2,1)S(1)}, u32[]{:S(2)}, u32[]{:S(2)}) async-start(bf16[4,256,128]{2,1,0:T(8,128)(2,1)} %shard_map.130), calls=%async_computation.1 | async-start | bytes 524288 | tf_op jit(solution)/shard_map/all_to_all | solution.py:260
  46.2 0.0 collective-permute-done.3.halo
  46.2 0.0 copy-start.9
  46.2 0.7 copy-done.9
  46.9 5.1 %shard_map.132 = (bf16[1024,128]{1,0:T(8,128)(2,1)}, bf16[1024,512]{1,0:T(8,128)(2,1)}, bf16[1024,128]{1,0:T(8,128)(2,1)}) custom-call(s32[1]{0:T(128)} %bitcast.place, bf16[1,1024,1024]{2,1,0:T(8,128)(2,1)} %constant.22.clone.forward, bf16[1,256,1024]{2,1,0:T(8,128)(2,1)} %constant.26.clone.inverse, bf16[768,128]{1,0:T(8,128)(2,1)} %copy-done.9, ...), custom_call_target="tpu_custom_call" | custom-call | flops 24000000000 | tf_op jit(solution)/shard_map/pallas_call | solution.py:305
  52.0 0.0 all-to-all-done.1
  52.0 0.0 copy-start.5
  52.0 0.7 copy-done.5
  52.7 4.2 %shard_map.133 = (bf16[768,128]{1,0:T(8,128)(2,1)}, bf16[64,16,128]{2,1,0:T(8,128)(2,1)}) custom-call(bf16[1,1024,256]{2,1,0:T(8,128)(2,1)} %constant.23.clone.forward, bf16[1,768,1024]{2,1,0:T(8,128)(2,1)} %constant.25.clone.inverse, bf16[1024,128]{1,0:T(8,128)(2,1)} %bitcast.5, bf16[1024,512]{1,0:T(8,128)(2,1)} %get-tuple-element.27.spectrum), custom_call_target="tpu_custom_call" | custom-call | tf_op jit(solution)/shard_map/pallas_call | solution.py:322
  57.0 1.3 %collective-permute-start.4 = (bf16[768,128]{1,0:T(8,128)(2,1)}, bf16[768,128]{1,0:T(8,128)(2,1)S(1)}, u32[]{:S(2)}, u32[]{:S(2)}) collective-permute-start(bf16[768,128]{1,0:T(8,128)(2,1)} %get-tuple-element.28), channel_id=1, source_target_pairs={{32,0},{64,32},{96,64},{128,96},{160,128},{192,160},{224,192},{256... | collective-permute-start | bytes 589832 | tf_op jit(solution)/shard_map/ppermute | solution.py:249
  58.3 16.5 %all-to-all-start.2 = ((bf16[64,16,128]{2,1,0:T(8,128)(2,1)}), bf16[64,16,128]{2,1,0:T(8,128)(2,1)S(1)}, u32[]{:S(2)}, u32[]{:S(2)}) async-start(bf16[64,16,128]{2,1,0:T(8,128)(2,1)} %get-tuple-element.35), calls=%async_computation.2 | async-start | bytes 524288 | tf_op jit(solution)/shard_map/all_to_all | solution.py:260
  74.8 0.0 collective-permute-done.4.halo
  74.8 0.0 copy-start.10
  74.8 0.7 copy-done.10
  75.5 4.7 %shard_map.134 = (bf16[512,128]{1,0:T(8,128)(2,1)}, bf16[512,128]{1,0:T(8,128)(2,1)}, bf16[512,128]{1,0:T(8,128)(2,1)}, bf16[512,128]{1,0:T(8,128)(2,1)}) custom-call(s32[1]{0:T(128)} %bitcast.place, bf16[1,1024,1024]{2,1,0:T(8,128)(2,1)} %constant.22.clone.forward, bf16[1,256,1024]{2,1,0:T(8,128)(2,1)} %constant.24.clone.inverse, ...), custom_call_target="tpu_custom_call" | custom-call | flops 35000000512 | tf_op jit(solution)/shard_map/pallas_call | solution.py:334
  80.2 2.4 %collective-permute-start.5 = (bf16[512,128]{1,0:T(8,128)(2,1)}, bf16[512,128]{1,0:T(8,128)(2,1)S(1)}, u32[]{:S(2)}, u32[]{:S(2)}) collective-permute-start(bf16[512,128]{1,0:T(8,128)(2,1)} %get-tuple-element.32), channel_id=1, source_target_pairs={{0,8},{8,0},{16,24},{24,16},{1,9},{9,1},{17,25},{25,17},{2,10},{10... | collective-permute-start | bytes 393224 | tf_op jit(solution)/shard_map/ppermute | solution.py:254
  82.5 3.2 %collective-permute-start.6 = (bf16[512,128]{1,0:T(8,128)(2,1)}, bf16[512,128]{1,0:T(8,128)(2,1)S(1)}, u32[]{:S(2)}, u32[]{:S(2)}) collective-permute-start(bf16[512,128]{1,0:T(8,128)(2,1)} %get-tuple-element.33), channel_id=1, source_target_pairs={{0,16},{8,24},{16,0},{24,8},{1,17},{9,25},{17,1},{25,9},{2,18},{10... | collective-permute-start | bytes 393224 | tf_op jit(solution)/shard_map/ppermute | solution.py:254
  85.7 2.3 %collective-permute-start.7 = (bf16[512,128]{1,0:T(8,128)(2,1)}, bf16[512,128]{1,0:T(8,128)(2,1)S(1)}, u32[]{:S(2)}, u32[]{:S(2)}) collective-permute-start(bf16[512,128]{1,0:T(8,128)(2,1)} %get-tuple-element.34), channel_id=1, source_target_pairs={{0,24},{8,16},{16,8},{24,0},{1,25},{9,17},{17,9},{25,1},{2,26},{10... | collective-permute-start | bytes 393224 | tf_op jit(solution)/shard_map/ppermute | solution.py:254
  88.0 0.0 collective-permute-done.5.refs_1_
  88.0 2.2 %collective-permute-done.6.refs_2_ = bf16[512,128]{1,0:T(8,128)(2,1)S(1)} collective-permute-done((bf16[512,128]{1,0:T(8,128)(2,1)}, bf16[512,128]{1,0:T(8,128)(2,1)S(1)}, u32[]{:S(2)}, u32[]{:S(2)}) %collective-permute-start.6) | collective-permute-done | bytes 131104 | tf_op jit(solution)/shard_map/ppermute | solution.py:254
  90.2 3.7 %collective-permute-done.7.refs_3_ = bf16[512,128]{1,0:T(8,128)(2,1)S(1)} collective-permute-done((bf16[512,128]{1,0:T(8,128)(2,1)}, bf16[512,128]{1,0:T(8,128)(2,1)S(1)}, u32[]{:S(2)}, u32[]{:S(2)}) %collective-permute-start.7) | collective-permute-done | bytes 131104 | tf_op jit(solution)/shard_map/ppermute | solution.py:254
  93.9 0.7 all-to-all-done.2.refs_7_
  94.6 0.0 copy-done.1
  94.6 0.0 copy-done.2
  94.6 0.0 copy-done.3
  94.6 0.0 copy-start.4
  94.6 0.9 copy-done.4
  95.5 1.0 %shard_map.135 = (bf16[256,512]{1,0:T(8,128)(2,1)}, bf16[256,512]{1,0:T(8,128)(2,1)}, bf16[256,512]{1,0:T(8,128)(2,1)}, f32[12,512]{1,0:T(8,128)}) custom-call(s32[1]{0:T(128)} %bitcast.place, bf16[512,128]{1,0:T(8,128)(2,1)S(1)} %copy-done.4, bf16[512,128]{1,0:T(8,128)(2,1)S(1)} %collective-permute-done.5.refs_1_, ...), custom_call_target="tpu_custom_call" | custom-call | tf_op jit(solution)/shard_map/pallas_call | solution.py:351
  (3 shorter events, 0.0 us)
Async XLA Ops:
  2.6 37.5 %all-to-all-start = ((bf16[8,32,512]{2,1,0:T(8,128)(2,1)}), bf16[8,32,512]{2,1,0:T(8,128)(2,1)S(1)}, u32[]{:S(2)}, u32[]{:S(2)}) async-start(bf16[8,32,512]{2,1,0:T(8,128)(2,1)} %get-tuple-element.20), calls=%async_computation | async-start | bytes 524288 | tf_op jit(solution)/shard_map/all_to_all | solution.py:260
  20.7 8.3 %collective-permute-start = (bf16[256,128]{1,0:T(8,128)(2,1)}, bf16[256,128]{1,0:T(8,128)(2,1)S(1)}, u32[]{:S(2)}, u32[]{:S(2)}) collective-permute-start(bf16[256,128]{1,0:T(8,128)(2,1)} %get-tuple-element.22), channel_id=1, source_target_pairs={{0,8},{8,0},{16,24},{24,16},{1,9},{9,1},{17,25},{25,17},{2,10},{10... | collective-permute-start | bytes 196616 | tf_op jit(solution)/shard_map/ppermute | solution.py:254
  23.5 5.8 %collective-permute-start.1 = (bf16[256,128]{1,0:T(8,128)(2,1)}, bf16[256,128]{1,0:T(8,128)(2,1)S(1)}, u32[]{:S(2)}, u32[]{:S(2)}) collective-permute-start(bf16[256,128]{1,0:T(8,128)(2,1)} %get-tuple-element.23), channel_id=1, source_target_pairs={{0,16},{8,24},{16,0},{24,8},{1,17},{9,25},{17,1},{25,9},{2,18},{10... | collective-permute-start | bytes 196616 | tf_op jit(solution)/shard_map/ppermute | solution.py:254
  26.7 6.4 %collective-permute-start.2 = (bf16[256,128]{1,0:T(8,128)(2,1)}, bf16[256,128]{1,0:T(8,128)(2,1)S(1)}, u32[]{:S(2)}, u32[]{:S(2)}) collective-permute-start(bf16[256,128]{1,0:T(8,128)(2,1)} %get-tuple-element.24), channel_id=1, source_target_pairs={{0,24},{8,16},{16,8},{24,0},{1,25},{9,17},{17,9},{25,1},{2,26},{10... | collective-permute-start | bytes 196616 | tf_op jit(solution)/shard_map/ppermute | solution.py:254
  29.0 4.1 %copy-start.6 = (bf16[256,128]{1,0:T(8,128)(2,1)}, bf16[256,128]{1,0:T(8,128)(2,1)S(1)}, u32[]{:S(2)}) copy-start(bf16[256,128]{1,0:T(8,128)(2,1)S(1)} %collective-permute-done.refs_1_) | copy-start | bytes 196612
  29.3 3.8 %copy-start.7 = (bf16[256,128]{1,0:T(8,128)(2,1)}, bf16[256,128]{1,0:T(8,128)(2,1)S(1)}, u32[]{:S(2)}) copy-start(bf16[256,128]{1,0:T(8,128)(2,1)S(1)} %collective-permute-done.1.refs_2_) | copy-start | bytes 196612
  33.1 0.6 copy-start.8
  35.5 10.8 %collective-permute-start.3 = (bf16[768,128]{1,0:T(8,128)(2,1)}, bf16[768,128]{1,0:T(8,128)(2,1)S(1)}, u32[]{:S(2)}, u32[]{:S(2)}) collective-permute-start(bf16[768,128]{1,0:T(8,128)(2,1)} %get-tuple-element.25), channel_id=1, source_target_pairs={{0,32},{32,64},{64,96},{96,128},{128,160},{160,192},{192,224},{224... | collective-permute-start | bytes 589832 | tf_op jit(solution)/shard_map/ppermute | solution.py:249
  40.0 0.7 copy-start
  42.5 9.5 %all-to-all-start.1 = ((bf16[4,256,128]{2,1,0:T(8,128)(2,1)}), bf16[4,256,128]{2,1,0:T(8,128)(2,1)S(1)}, u32[]{:S(2)}, u32[]{:S(2)}) async-start(bf16[4,256,128]{2,1,0:T(8,128)(2,1)} %shard_map.130), calls=%async_computation.1 | async-start | bytes 524288 | tf_op jit(solution)/shard_map/all_to_all | solution.py:260
  46.2 0.7 copy-start.9
  52.0 0.7 copy-start.5
  57.0 17.8 %collective-permute-start.4 = (bf16[768,128]{1,0:T(8,128)(2,1)}, bf16[768,128]{1,0:T(8,128)(2,1)S(1)}, u32[]{:S(2)}, u32[]{:S(2)}) collective-permute-start(bf16[768,128]{1,0:T(8,128)(2,1)} %get-tuple-element.28), channel_id=1, source_target_pairs={{32,0},{64,32},{96,64},{128,96},{160,128},{192,160},{224,192},{256... | collective-permute-start | bytes 589832 | tf_op jit(solution)/shard_map/ppermute | solution.py:249
  58.3 36.3 %all-to-all-start.2 = ((bf16[64,16,128]{2,1,0:T(8,128)(2,1)}), bf16[64,16,128]{2,1,0:T(8,128)(2,1)S(1)}, u32[]{:S(2)}, u32[]{:S(2)}) async-start(bf16[64,16,128]{2,1,0:T(8,128)(2,1)} %get-tuple-element.35), calls=%async_computation.2 | async-start | bytes 524288 | tf_op jit(solution)/shard_map/all_to_all | solution.py:260
  74.8 0.7 copy-start.10
  75.4 19.2 %copy-start.1 = (bf16[8,32,512]{2,1,0:T(8,128)(2,1)S(1)}, bf16[8,32,512]{2,1,0:T(8,128)(2,1)}, u32[]{:S(2)}) copy-start(bf16[8,32,512]{2,1,0:T(8,128)(2,1)} %copy-done) | copy-start | bytes 786436
  75.5 19.2 %copy-start.2 = (bf16[256,512]{1,0:T(8,128)(2,1)S(1)}, bf16[256,512]{1,0:T(8,128)(2,1)}, u32[]{:S(2)}) copy-start(bf16[256,512]{1,0:T(8,128)(2,1)} %refs_5_.1) | copy-start | bytes 786436
  75.5 19.2 %copy-start.3 = (bf16[256,512]{1,0:T(8,128)(2,1)S(1)}, bf16[256,512]{1,0:T(8,128)(2,1)}, u32[]{:S(2)}) copy-start(bf16[256,512]{1,0:T(8,128)(2,1)} %refs_6_.1) | copy-start | bytes 786436
  80.2 7.9 %collective-permute-start.5 = (bf16[512,128]{1,0:T(8,128)(2,1)}, bf16[512,128]{1,0:T(8,128)(2,1)S(1)}, u32[]{:S(2)}, u32[]{:S(2)}) collective-permute-start(bf16[512,128]{1,0:T(8,128)(2,1)} %get-tuple-element.32), channel_id=1, source_target_pairs={{0,8},{8,0},{16,24},{24,16},{1,9},{9,1},{17,25},{25,17},{2,10},{10... | collective-permute-start | bytes 393224 | tf_op jit(solution)/shard_map/ppermute | solution.py:254
  82.5 7.7 %collective-permute-start.6 = (bf16[512,128]{1,0:T(8,128)(2,1)}, bf16[512,128]{1,0:T(8,128)(2,1)S(1)}, u32[]{:S(2)}, u32[]{:S(2)}) collective-permute-start(bf16[512,128]{1,0:T(8,128)(2,1)} %get-tuple-element.33), channel_id=1, source_target_pairs={{0,16},{8,24},{16,0},{24,8},{1,17},{9,25},{17,1},{25,9},{2,18},{10... | collective-permute-start | bytes 393224 | tf_op jit(solution)/shard_map/ppermute | solution.py:254
  85.7 8.2 %collective-permute-start.7 = (bf16[512,128]{1,0:T(8,128)(2,1)}, bf16[512,128]{1,0:T(8,128)(2,1)S(1)}, u32[]{:S(2)}, u32[]{:S(2)}) collective-permute-start(bf16[512,128]{1,0:T(8,128)(2,1)} %get-tuple-element.34), channel_id=1, source_target_pairs={{0,24},{8,16},{16,8},{24,0},{1,25},{9,17},{17,9},{25,1},{2,26},{10... | collective-permute-start | bytes 393224 | tf_op jit(solution)/shard_map/ppermute | solution.py:254
  94.6 0.9 copy-start.4

commit v8 on v7

--- a/solution.py
+++ b/solution.py
@@ -25,7 +25,7 @@
 BLOCKS = 4
 TOKENS = BLOCKS * BLOCK
 WIDE = BLOCKS * LANES
-BINS = 512
+BINS = 128
 STEPS = PERIOD // 2 // BINS
 ROWS = 2 * BINS
 SLOT = 16
@@ -67,14 +67,25 @@
     return jnp.concatenate([part] * BLOCKS, axis=1)
 
 
-def accumulate(step, total, part):
-    @pl.when(step == 0)
-    def _():
-        total[...] = part
-
-    @pl.when(step > 0)
-    def _():
-        total[...] += part
+def start(source, target, sem):
+    copy = pltpu.make_async_copy(source, target, sem)
+    copy.start()
+    return copy
+
+
+def wait(copies):
+    for copy in copies:
+        copy.wait()
+
+
+def start_chunks(sources, targets, sems):
+    return [
+        [
+            start(source.at[chunk], target.at[chunk], sems.at[number, chunk])
+            for number, (source, target) in enumerate(zip(sources, targets))
+        ]
+        for chunk in range(STEPS)
+    ]
 
 
 def prep_kernel(place, key, value, out_grad, *outs):
@@ -93,104 +104,133 @@
     tail[...] = mixed[TOKENS - tail.shape[0] :, :]
 
 
-def grad_kernel(cotangent, gate, grad):
-    product = (cotangent[...].astype(F32) * gate[...].astype(F32)).astype(BF16)
+def conv_kernel(
+    scale,
+    place,
+    forward,
+    inverse,
+    halo,
+    mixed,
+    taps,
+    conv,
+    spectrum,
+    response,
+    table,
+    back,
+    windows,
+    filt,
+    spec_out,
+    sems,
+    small_sems,
+    out_sems,
+):
+    lags = halo.shape[0]
+    copies = [start(taps.at[:, lanes_at(place[0])], filt, small_sems.at[0])]
     for block in range(BLOCKS):
-        grad[block] = product[:, lane_block(block)]
-
-
-def conv_kernel(
-    scale, place, forward, inverse, halo, mixed, taps, conv, spectrum, response, windows, total
+        early = lags - block * BLOCK
+        target = windows.at[early:, lane_block(block)]
+        copies.append(start(mixed.at[: (block + 1) * BLOCK], target, small_sems.at[1 + block]))
+    for block in range(BLOCKS - 1):
+        early = lags - block * BLOCK
+        target = windows.at[:early, lane_block(block)]
+        sem = small_sems.at[1 + BLOCKS + block]
+        copies.append(start(halo.at[block * BLOCK :], target, sem))
+    chunks = start_chunks((forward, inverse), (table, back), sems)
+    wait(copies)
+    outs = []
+    for chunk in range(STEPS):
+        wait(chunks[chunk])
+        resp = dot(table[chunk, :, :lags], filt[...])
+        response[chunk] = resp.astype(BF16)
+        spec = dot(table[chunk], windows[...])
+        spec_out[chunk] = spec.astype(BF16)
+        outs.append(start(spec_out.at[chunk], spectrum.at[chunk], out_sems.at[chunk]))
+        f_re, f_im = spread(resp[:BINS]), spread(resp[BINS:])
+        x_re, x_im = spec[:BINS], spec[BINS:]
+        y = jnp.concatenate([f_re * x_re - f_im * x_im, f_re * x_im + f_im * x_re])
+        part = dot(back[chunk], y.astype(BF16))
+        total = total + part if chunk else part
+    for block in range(BLOCKS):
+        conv[token_block(block), :] = (total[:, lane_block(block)] * scale).astype(BF16)
+    wait(outs)
+
+
+def cross_kernel(
+    scale,
+    forward,
+    inverse,
+    grad,
+    spectrum,
+    head,
+    lag_grad,
+    table,
+    back,
+    spec_in,
+    windows,
+    total,
+    sems,
+    small_sems,
 ):
-    step = pl.program_id(0)
-    lags = taps.shape[0]
-
-    @pl.when(step == 0)
-    def _():
-        for block in range(BLOCKS):
-            early = lags - block * BLOCK
-            if early:
-                windows[:early, lane_block(block)] = halo[block * BLOCK :, :]
-            windows[early:, lane_block(block)] = mixed[: (block + 1) * BLOCK, :]
-
-    resp = dot(forward[:, :lags], taps[...])
-    response[...] = resp.astype(BF16)
-    spec = dot(forward[...], windows[...])
-    spectrum[...] = spec.astype(BF16)
-    f_re, f_im = spread(resp[:BINS]), spread(resp[BINS:])
-    x_re, x_im = spec[:BINS], spec[BINS:]
-    y = jnp.concatenate([f_re * x_re - f_im * x_im, f_re * x_im + f_im * x_re]).astype(BF16)
-    accumulate(step, total, dot(inverse[...], y))
-
-    @pl.when(step == STEPS - 1)
-    def _():
-        for block in range(BLOCKS):
-            conv[token_block(block), :] = (total[:, lane_block(block)] * scale).astype(BF16)
-
-
-def cross_kernel(scale, forward, inverse, grad, spectrum, head, lag_grad, windows, total):
-    step = pl.program_id(0)
-
-    @pl.when(step == 0)
-    def _():
-        head[...] = grad[: head.shape[0], :]
-        for block in range(BLOCKS):
-            windows[:, lane_block(block)] = grad[token_block(block), :]
-
-    spec = dot(forward[...], windows[...])
-    g_re, g_im = spec[:BINS], spec[BINS:]
-    full = spectrum[...].astype(F32)
-    x_re, x_im = full[:BINS], full[BINS:]
-    re = g_re * x_re + g_im * x_im
-    im = g_im * x_re - g_re * x_im
-    re = sum(re[:, lane_block(b)] for b in range(BLOCKS))
-    im = sum(im[:, lane_block(b)] for b in range(BLOCKS))
-    lags = inverse.shape[0]
-    part = dot(inverse[...], jnp.concatenate([re, im]).astype(BF16))
-
-    @pl.when(step == 0)
-    def _():
-        total[:lags, :] = part
-        total[lags:, :] = jnp.zeros_like(total[lags:, :])
-
-    @pl.when(step > 0)
-    def _():
-        total[:lags, :] += part
-
-    @pl.when(step == STEPS - 1)
-    def _():
-        count = lag_grad.shape[0]
-        share = lags // count
-        for slot in range(count):
-            rows = total[slot * share : slot * share + SLOT, :] * scale
-            lag_grad[slot] = rows.astype(BF16)
+    lags = head.shape[0]
+    copies = [
+        start(grad.at[token_block(b)], windows.at[:, lane_block(b)], small_sems.at[b])
+        for b in range(BLOCKS)
+    ]
+    chunks = start_chunks((forward, spectrum, inverse), (table, spec_in, back), sems)
+    wait(copies)
+    for block in range(lags // BLOCK):
+        head[token_block(block), :] = windows[:, lane_block(block)]
+    for chunk in range(STEPS):
+        wait(chunks[chunk])
+        spec = dot(table[chunk], windows[...])
+        g_re, g_im = spec[:BINS], spec[BINS:]
+        full = spec_in[chunk].astype(F32)
+        x_re, x_im = full[:BINS], full[BINS:]
+        re = g_re * x_re + g_im * x_im
+        im = g_im * x_re - g_re * x_im
+        re = sum(re[:, lane_block(b)] for b in range(BLOCKS))
+        im = sum(im[:, lane_block(b)] for b in range(BLOCKS))
+        part = dot(back[chunk], jnp.concatenate([re, im]).astype(BF16))
+        whole_part = whole_part + part if chunk else part
+    total[:lags, :] = whole_part * scale
+    total[lags:, :] = jnp.zeros_like(total[lags:, :])
+    count = lag_grad.shape[0]
+    share = lags // count
+    for slot in range(count):
+        lag_grad[slot] = total[slot * share : slot * share + SLOT, :].astype(BF16)
 
 
 def back_kernel(scale, place, forward, inverse, grad, halo, response, conv, *refs):
-    outs, (windows, total) = refs[:BLOCKS], refs[BLOCKS:]
-    step = pl.program_id(0)
-
-    @pl.when(step == 0)
-    def _():
-        for block in range(BLOCKS):
-            own = min(PERIOD, TOKENS - block * BLOCK)
-            windows[:own, lane_block(block)] = grad[block * BLOCK : block * BLOCK + own, :]
-            if own < PERIOD:
-                windows[own:, lane_block(block)] = halo[: PERIOD - own, :]
-        for hop, out in enumerate(outs):
-            out[:BLOCK, :] = conv[rows_at(place[0] ^ hop), :]
-
-    spec = dot(forward[...], windows[...])
-    resp = response[...].astype(F32)
-    f_re, f_im = spread(resp[:BINS]), spread(resp[BINS:])
-    g_re, g_im = spec[:BINS], spec[BINS:]
-    y = jnp.concatenate([f_re * g_re + f_im * g_im, f_re * g_im - f_im * g_re]).astype(BF16)
-    accumulate(step, total, dot(inverse[...], y))
-
-    @pl.when(step == STEPS - 1)
-    def _():
-        for hop, out in enumerate(outs):
-            out[BLOCK:, :] = (total[:, lanes_at(place[0] ^ hop)] * scale).astype(BF16)
+    outs, (table, back, filt, windows, sems, small_sems) = refs[:BLOCKS], refs[BLOCKS:]
+    copies = []
+    for block in range(BLOCKS):
+        own = min(PERIOD, TOKENS - block * BLOCK)
+        source = grad.at[block * BLOCK : block * BLOCK + own]
+        target = windows.at[:own, lane_block(block)]
+        copies.append(start(source, target, small_sems.at[block]))
+        if own < PERIOD:
+            target = windows.at[own:, lane_block(block)]
+            sem = small_sems.at[BLOCKS + block]
+            copies.append(start(halo.at[: PERIOD - own], target, sem))
+    chunks = start_chunks((forward, response, inverse), (table, filt, back), sems)
+    moved = [
+        start(conv.at[rows_at(place[0] ^ hop)], out.at[:BLOCK], small_sems.at[2 * BLOCKS + hop])
+        for hop, out in enumerate(outs)
+    ]
+    wait(copies)
+    for chunk in range(STEPS):
+        wait(chunks[chunk])
+        spec = dot(table[chunk], windows[...])
+        resp = filt[chunk].astype(F32)
+        f_re, f_im = spread(resp[:BINS]), spread(resp[BINS:])
+        g_re, g_im = spec[:BINS], spec[BINS:]
+        y = jnp.concatenate([f_re * g_re + f_im * g_im, f_re * g_im - f_im * g_re])
+        part = dot(back[chunk], y.astype(BF16))
+        total = total + part if chunk else part
+    windows[:BLOCK, :] = (total * scale).astype(BF16)
+    for hop, out in enumerate(outs):
+        out[BLOCK:, :] = windows[:BLOCK, lanes_at(place[0] ^ hop)]
+    wait(moved)
 
 
 def final_kernel(place, *refs):
@@ -217,12 +257,12 @@
     return jax.ShapeDtypeStruct(shape, dtype)
 
 
-def call(kernel, in_specs, out_specs, out_shape, scratch=(), steps=1, flops=0, limit=None, scalars=0):
+def call(kernel, in_specs, out_specs, out_shape, scratch=(), flops=0, limit=None, scalars=0):
     return pl.pallas_call(
         kernel,
         grid_spec=pltpu.PrefetchScalarGridSpec(
             num_scalar_prefetch=scalars,
-            grid=(steps,),
+            grid=(1,),
             in_specs=in_specs,
             out_specs=out_specs,
             scratch_shapes=scratch,
@@ -272,6 +312,7 @@
     reach = (lags, LANES)
     slots = (lags // share, SLOT, LANES)
     scalar = pl.BlockSpec(memory_space=pltpu.SMEM)
+    anywhere = pl.BlockSpec(memory_space=pl.ANY)
     place = lax.axis_index(GROUP).reshape(1)
 
     part = (BLOCK, LANES)
@@ -291,41 +332,47 @@
         flops=JOIN_FLOPS,
     )(place, *swap(ships))
     mixed_halo = shift(tail, 1)
-    grad = call(grad_kernel, [whole(local)] * 2, whole(by_block), shaped(by_block))(
-        cotangent, gate_input
-    )
-    grad = exchange(grad, GROUP).reshape(flat)
-
-    def stepped(*shape):
-        return pl.BlockSpec((None,) + shape, lambda step, *_: (step, 0, 0))
-
-    table = stepped(ROWS, PERIOD)
-    bins = pl.BlockSpec((ROWS, WIDE), lambda step, *_: (step, 0))
-    narrow_bins = pl.BlockSpec((ROWS, LANES), lambda step, *_: (step, 0))
+    grad = (cotangent.astype(F32) * gate_input.astype(F32)).astype(BF16)
+    grad = exchange(grad.reshape(BLOCK, BLOCKS, LANES).transpose(1, 0, 2), GROUP).reshape(flat)
+
+    table = pltpu.VMEM((STEPS, ROWS, PERIOD), BF16)
+    narrow = pltpu.VMEM((STEPS, ROWS, BLOCK), BF16)
+    by_bins = (STEPS, ROWS, WIDE)
+    filt_bins = (STEPS, ROWS, LANES)
+    windows = pltpu.VMEM((PERIOD, WIDE), BF16)
+    dma = pltpu.SemaphoreType.DMA
     conv, spectrum, response = call(
         functools.partial(conv_kernel, norm),
+        [anywhere] * 5,
+        [whole(flat), anywhere, whole(filt_bins)],
+        [shaped(flat), shaped(by_bins), shaped(filt_bins)],
         [
             table,
-            stepped(BLOCK, ROWS),
-            whole(reach),
-            whole(flat),
-            pl.BlockSpec(reach, lambda step, place: (0, place[0])),
+            narrow,
+            windows,
+            pltpu.VMEM(reach, BF16),
+            pltpu.VMEM(by_bins, BF16),
+            dma((2, STEPS)),
+            dma((2 * BLOCKS,)),
+            dma((STEPS,)),
         ],
-        [whole(flat), bins, narrow_bins],
-        [shaped(flat), shaped((PERIOD, WIDE)), shaped((PERIOD, LANES))],
-        [pltpu.VMEM((PERIOD, WIDE), BF16), pltpu.VMEM(local, F32)],
-        STEPS,
         CONV_FLOPS,
         scalars=1,
     )(place, forward, last, mixed_halo, mixed, filter_taps)
-
     head, lag_grad = call(
         functools.partial(cross_kernel, norm),
-        [stepped(ROWS, BLOCK), stepped(lags, ROWS), whole(flat), bins],
+        [anywhere] * 4,
         [whole(reach), whole(slots)],
         [shaped(reach), shaped(slots)],
-        [pltpu.VMEM(local, BF16), pltpu.VMEM((lags + SLOT, LANES), F32)],
-        STEPS,
+        [
+            narrow,
+            pltpu.VMEM((STEPS, lags, ROWS), BF16),
+            pltpu.VMEM(by_bins, BF16),
+            pltpu.VMEM(local, BF16),
+            pltpu.VMEM((lags + SLOT, LANES), F32),
+            dma((3, STEPS)),
+            dma((BLOCKS,)),
+        ],
         CROSS_FLOPS,
     )(own, lagged, grad, spectrum)
     grad_halo = shift(head, -1)
@@ -333,19 +380,17 @@
 
     ships = call(
         functools.partial(back_kernel, norm),
-        [
-            scalar,
-            table,
-            stepped(BLOCK, ROWS),
-            whole(flat),
-            whole(reach),
-            narrow_bins,
-            whole(flat),
-        ],
+        [scalar] + [anywhere] * 6,
         [whole(ship)] * BLOCKS,
         [shaped(ship)] * BLOCKS,
-        [pltpu.VMEM((PERIOD, WIDE), BF16), pltpu.VMEM(local, F32)],
-        STEPS,
+        [
+            table,
+            narrow,
+            pltpu.VMEM(filt_bins, BF16),
+            windows,
+            dma((3, STEPS)),
+            dma((3 * BLOCKS,)),
+        ],
         BACK_FLOPS,
     )(place, forward, first, grad, grad_halo, response, conv)
     gate_grad, key_grad, value_grad, filter_grad = call(

time: 97.3 us -> 98.1 us (level)
  other arithmetic: 0 us -> 1.72 us
    transpose x0 -> x1, other arithmetic: none -> 1.72 us  [body(): grad.reshape(BLOCK, BLOCKS, LANES).transpose(1, 0, 2)]
    unnamed x22 -> x18, local copies, waits for them, and re-layouts: 4.29 us -> 3.56 us
    pallas_call x4 -> x3, Pallas kernels: 15.8 us -> 16.2 us  [the longest x1 6.14 us: body(): call(functools.partial(conv_kernel, norm), [anywhere] * 5, [whole(flat),...]
  transfers between devices with their start and end apart: 11 -> 11, of which waited for: 5 -> 5; matrix products, arithmetic and copies ran while one was open for 0% -> 2% of each run, Pallas kernels for 14% -> 14%
where the time goes in v8:
time: 98.1 us; the launch traced here: 97.3 us
  starting transfers between devices  60.3 us (61%)
  Pallas kernels  20.9 us (21%)
  waiting for transfers between devices  10 us (10%)
  local copies, waits for them, and re-layouts  3.56 us (4%)
  other arithmetic  1.72 us (2%)
    all_to_all x3, starting transfers between devices, exchange(): return lax.all_to_all(value, axes, split_axis=0, concat_axis=0, tiled=True)  38.3 us
    ppermute x6, starting transfers between devices, swap(): lax.ppermute(ships[hop], GROUP, [(i, i ^ hop) for i in range(BLOCKS)])  16.2 us
    ppermute x6, waiting for transfers between devices, swap(): lax.ppermute(ships[hop], GROUP, [(i, i ^ hop) for i in range(BLOCKS)])  9.87 us
    pallas_call x1, Pallas kernels, body(): call(functools.partial(conv_kernel, norm), [anywhere] * 5, [whole(flat),...  6.14 us
    ppermute x2, starting transfers between devices, shift(): lax.ppermute(value, RUNS, [(i, i + steps) for i in range(first, last)])  5.83 us
    pallas_call x1, Pallas kernels, body(): call(functools.partial(back_kernel, norm), [scalar] + [anywhere] * 6, [wh...  5.36 us
    pallas_call x1, Pallas kernels, body(): call(functools.partial(cross_kernel, norm), [anywhere] * 4, [whole(reach)...  4.75 us
    unnamed x18, local copies, waits for them, and re-layouts  3.56 us
  transfers between devices with their start and end apart: 11, of which 5 were waited for; matrix products, arithmetic and copies ran while one was open for 2% of the time, Pallas kernels for 14%

profile of v8, /device:TPU:1, one launch (start us, length us, event | category | flops | bytes accessed | tf_op | source)
XLA Modules:
  0.0 97.3 jit_solution(6321605873081188665)
XLA Ops:
  0.6 1.9 %shard_map.129 = (bf16[256,128]{1,0:T(8,128)(2,1)}, bf16[256,128]{1,0:T(8,128)(2,1)}, bf16[256,128]{1,0:T(8,128)(2,1)}, bf16[256,128]{1,0:T(8,128)(2,1)}, bf16[8,32,512]{2,1,0:T(8,128)(2,1)}) custom-call(s32[1]{0:T(128)} %bitcast.place, bf16[256,512]{1,0:T(8,128)(2,1)} %refs_5_.1, bf16[256,512]{1,0:T(8,128)(2,1)} %refs_6_.1, bf16[32,4096]{1,0:T(8,128)(2,1)} %out_grad.1), custom_call_target="tpu_custom_call" | custom-call | tf_op jit(solution)/shard_map/pallas_call | solution.py:320
  2.6 18.1 %all-to-all-start = ((bf16[8,32,512]{2,1,0:T(8,128)(2,1)}), bf16[8,32,512]{2,1,0:T(8,128)(2,1)S(1)}, u32[]{:S(2)}, u32[]{:S(2)}) async-start(bf16[8,32,512]{2,1,0:T(8,128)(2,1)} %get-tuple-element.20), calls=%async_computation | async-start | bytes 524288 | tf_op jit(solution)/shard_map/all_to_all | solution.py:300
  20.7 2.9 %collective-permute-start = (bf16[256,128]{1,0:T(8,128)(2,1)}, bf16[256,128]{1,0:T(8,128)(2,1)S(1)}, u32[]{:S(2)}, u32[]{:S(2)}) collective-permute-start(bf16[256,128]{1,0:T(8,128)(2,1)} %get-tuple-element.22), channel_id=1, source_target_pairs={{0,8},{8,0},{16,24},{24,16},{1,9},{9,1},{17,25},{25,17},{2,10},{10... | collective-permute-start | bytes 196616 | tf_op jit(solution)/shard_map/ppermute | solution.py:294
  23.5 3.2 %collective-permute-start.1 = (bf16[256,128]{1,0:T(8,128)(2,1)}, bf16[256,128]{1,0:T(8,128)(2,1)S(1)}, u32[]{:S(2)}, u32[]{:S(2)}) collective-permute-start(bf16[256,128]{1,0:T(8,128)(2,1)} %get-tuple-element.23), channel_id=1, source_target_pairs={{0,16},{8,24},{16,0},{24,8},{1,17},{9,25},{17,1},{25,9},{2,18},{10... | collective-permute-start | bytes 196616 | tf_op jit(solution)/shard_map/ppermute | solution.py:294
  26.7 2.3 %collective-permute-start.2 = (bf16[256,128]{1,0:T(8,128)(2,1)}, bf16[256,128]{1,0:T(8,128)(2,1)S(1)}, u32[]{:S(2)}, u32[]{:S(2)}) collective-permute-start(bf16[256,128]{1,0:T(8,128)(2,1)} %get-tuple-element.24), channel_id=1, source_target_pairs={{0,24},{8,16},{16,8},{24,0},{1,25},{9,17},{17,9},{25,1},{2,26},{10... | collective-permute-start | bytes 196616 | tf_op jit(solution)/shard_map/ppermute | solution.py:294
  29.0 0.0 collective-permute-done.refs_1_
  29.0 0.0 copy-start.4
  29.0 0.3 collective-permute-done.1.refs_2_
  29.3 0.0 copy-start.5
  29.4 3.8 %collective-permute-done.2.refs_3_ = bf16[256,128]{1,0:T(8,128)(2,1)S(1)} collective-permute-done((bf16[256,128]{1,0:T(8,128)(2,1)}, bf16[256,128]{1,0:T(8,128)(2,1)S(1)}, u32[]{:S(2)}, u32[]{:S(2)}) %collective-permute-start.2) | collective-permute-done | bytes 65568 | tf_op jit(solution)/shard_map/ppermute | solution.py:294
  33.1 0.0 copy-start.6
  33.1 0.0 copy-done.4
  33.1 0.0 copy-done.5
  33.1 0.6 copy-done.6
  33.8 1.7 %shard_map.130 = (bf16[1024,128]{1,0:T(8,128)(2,1)}, bf16[768,128]{1,0:T(8,128)(2,1)}) custom-call(s32[1]{0:T(128)} %bitcast.place, bf16[256,128]{1,0:T(8,128)(2,1)} %get-tuple-element.21.refs_0_, bf16[256,128]{1,0:T(8,128)(2,1)} %copy-done.4, bf16[256,128]{1,0:T(8,128)(2,1)} %copy-done.5, bf16[256,128]{1,0:T(8,128)(2,1)} %copy-done.6), custom_call_target="tpu_custom_call" | custom-call | tf_op jit(solution)/shard_map/pallas_call | solution.py:327
  35.5 4.5 %collective-permute-start.3 = (bf16[768,128]{1,0:T(8,128)(2,1)}, bf16[768,128]{1,0:T(8,128)(2,1)S(1)}, u32[]{:S(2)}, u32[]{:S(2)}) collective-permute-start(bf16[768,128]{1,0:T(8,128)(2,1)} %get-tuple-element.25), channel_id=1, source_target_pairs={{0,32},{32,64},{64,96},{96,128},{128,160},{160,192},{192,224},{224... | collective-permute-start | bytes 589832 | tf_op jit(solution)/shard_map/ppermute | solution.py:289
  40.0 0.0 all-to-all-done
  40.0 1.7 %bitcast_bitcast_fusion = bf16[4,256,128]{2,1,0:T(8,128)(2,1)} fusion(bf16[256,512]{1,0:T(8,128)(2,1)} %param.10, bf16[8,32,512]{2,1,0:T(8,128)(2,1)S(1)} %all-to-all-done), kind=kLoop, calls=%fused_computation.2 | loop fusion | flops 524288 | bytes 786432 | tf_op jit(solution)/shard_map/transpose | solution.py:336
  41.8 3.7 %all-to-all-start.1 = ((bf16[4,256,128]{2,1,0:T(8,128)(2,1)}), bf16[4,256,128]{2,1,0:T(8,128)(2,1)S(1)}, u32[]{:S(2)}, u32[]{:S(2)}) async-start(bf16[4,256,128]{2,1,0:T(8,128)(2,1)} %bitcast_bitcast_fusion), calls=%async_computation.1 | async-start | bytes 524288 | tf_op jit(solution)/shard_map/all_to_all | solution.py:300
  45.5 0.0 collective-permute-done.3.halo
  45.5 0.0 copy-start.7
  45.5 0.7 copy-done.7
  46.1 6.1 %shard_map.131 = (bf16[1024,128]{1,0:T(8,128)(2,1)}, bf16[4,256,512]{2,1,0:T(8,128)(2,1)}, bf16[4,256,128]{2,1,0:T(8,128)(2,1)}) custom-call(s32[1]{0:T(128)} %bitcast.place, bf16[4,256,1024]{2,1,0:T(8,128)(2,1)} %constant.22.clone.forward, bf16[4,256,256]{2,1,0:T(8,128)(2,1)} %constant.26.clone.inverse, bf16[768,128]{1,0:T(8,128)(2,1)} %copy-done.7, ...), custom_call_target="tpu_custom_call" | custom-call | flops 24000000000 | tf_op jit(solution)/shard_map/pallas_call | solution.py:344
  52.3 0.0 all-to-all-done.1
  52.3 0.0 copy-start.3
  52.3 0.7 copy-done.3
  53.0 4.7 %shard_map.132 = (bf16[768,128]{1,0:T(8,128)(2,1)}, bf16[64,16,128]{2,1,0:T(8,128)(2,1)}) custom-call(bf16[4,256,256]{2,1,0:T(8,128)(2,1)} %constant.23.clone.forward, bf16[4,768,256]{2,1,0:T(8,128)(2,1)} %constant.25.clone.inverse, bf16[1024,128]{1,0:T(8,128)(2,1)} %bitcast.13, bf16[4,256,512]{2,1,0:T(8,128)(2,1)} %get-tuple-element.27.spectrum), custom_call_target="tpu_custom_call" | custom-call | tf_op jit(solution)/shard_map/pallas_call | solution.py:362
  57.8 1.3 %collective-permute-start.4 = (bf16[768,128]{1,0:T(8,128)(2,1)}, bf16[768,128]{1,0:T(8,128)(2,1)S(1)}, u32[]{:S(2)}, u32[]{:S(2)}) collective-permute-start(bf16[768,128]{1,0:T(8,128)(2,1)} %get-tuple-element.28), channel_id=1, source_target_pairs={{32,0},{64,32},{96,64},{128,96},{160,128},{192,160},{224,192},{256... | collective-permute-start | bytes 589832 | tf_op jit(solution)/shard_map/ppermute | solution.py:289
  59.1 16.5 %all-to-all-start.2 = ((bf16[64,16,128]{2,1,0:T(8,128)(2,1)}), bf16[64,16,128]{2,1,0:T(8,128)(2,1)S(1)}, u32[]{:S(2)}, u32[]{:S(2)}) async-start(bf16[64,16,128]{2,1,0:T(8,128)(2,1)} %get-tuple-element.35), calls=%async_computation.2 | async-start | bytes 524288 | tf_op jit(solution)/shard_map/all_to_all | solution.py:300
  75.5 0.0 collective-permute-done.4.halo
  75.5 0.0 copy-start.8
  75.6 0.7 copy-done.8
  76.2 0.0 copy-start
  76.2 0.0 copy-start.1
  76.2 5.4 %shard_map.133 = (bf16[512,128]{1,0:T(8,128)(2,1)}, bf16[512,128]{1,0:T(8,128)(2,1)}, bf16[512,128]{1,0:T(8,128)(2,1)}, bf16[512,128]{1,0:T(8,128)(2,1)}) custom-call(s32[1]{0:T(128)} %bitcast.place, bf16[4,256,1024]{2,1,0:T(8,128)(2,1)} %constant.22.clone.forward, bf16[4,256,256]{2,1,0:T(8,128)(2,1)} %constant.24.clone.inverse, bf16[1024,128]{1,0:T(8,128)(2,1)} %bitcast.14, ...), custom_call_target="tpu_custom_call" | custom-call | flops 35000000512 | tf_op jit(solution)/shard_map/pallas_call | solution.py:381
  81.6 2.4 %collective-permute-start.5 = (bf16[512,128]{1,0:T(8,128)(2,1)}, bf16[512,128]{1,0:T(8,128)(2,1)S(1)}, u32[]{:S(2)}, u32[]{:S(2)}) collective-permute-start(bf16[512,128]{1,0:T(8,128)(2,1)} %get-tuple-element.32), channel_id=1, source_target_pairs={{0,8},{8,0},{16,24},{24,16},{1,9},{9,1},{17,25},{25,17},{2,10},{10... | collective-permute-start | bytes 393224 | tf_op jit(solution)/shard_map/ppermute | solution.py:294
  84.0 3.2 %collective-permute-start.6 = (bf16[512,128]{1,0:T(8,128)(2,1)}, bf16[512,128]{1,0:T(8,128)(2,1)S(1)}, u32[]{:S(2)}, u32[]{:S(2)}) collective-permute-start(bf16[512,128]{1,0:T(8,128)(2,1)} %get-tuple-element.33), channel_id=1, source_target_pairs={{0,16},{8,24},{16,0},{24,8},{1,17},{9,25},{17,1},{25,9},{2,18},{10... | collective-permute-start | bytes 393224 | tf_op jit(solution)/shard_map/ppermute | solution.py:294
  87.2 2.3 %collective-permute-start.7 = (bf16[512,128]{1,0:T(8,128)(2,1)}, bf16[512,128]{1,0:T(8,128)(2,1)S(1)}, u32[]{:S(2)}, u32[]{:S(2)}) collective-permute-start(bf16[512,128]{1,0:T(8,128)(2,1)} %get-tuple-element.34), channel_id=1, source_target_pairs={{0,24},{8,16},{16,8},{24,0},{1,25},{9,17},{17,9},{25,1},{2,26},{10... | collective-permute-start | bytes 393224 | tf_op jit(solution)/shard_map/ppermute | solution.py:294
  89.5 0.0 collective-permute-done.5.refs_1_
  89.5 2.0 %collective-permute-done.6.refs_2_ = bf16[512,128]{1,0:T(8,128)(2,1)S(1)} collective-permute-done((bf16[512,128]{1,0:T(8,128)(2,1)}, bf16[512,128]{1,0:T(8,128)(2,1)S(1)}, u32[]{:S(2)}, u32[]{:S(2)}) %collective-permute-start.6) | collective-permute-done | bytes 131104 | tf_op jit(solution)/shard_map/ppermute | solution.py:294
  91.5 3.8 %collective-permute-done.7.refs_3_ = bf16[512,128]{1,0:T(8,128)(2,1)S(1)} collective-permute-done((bf16[512,128]{1,0:T(8,128)(2,1)}, bf16[512,128]{1,0:T(8,128)(2,1)S(1)}, u32[]{:S(2)}, u32[]{:S(2)}) %collective-permute-start.7) | collective-permute-done | bytes 131104 | tf_op jit(solution)/shard_map/ppermute | solution.py:294
  95.3 0.1 all-to-all-done.2.refs_7_
  95.4 0.0 copy-done
  95.4 0.0 copy-done.1
  95.4 0.0 copy-start.2
  95.4 0.9 copy-done.2
  96.3 1.0 %shard_map.134 = (bf16[256,512]{1,0:T(8,128)(2,1)}, bf16[256,512]{1,0:T(8,128)(2,1)}, bf16[256,512]{1,0:T(8,128)(2,1)}, f32[12,512]{1,0:T(8,128)}) custom-call(s32[1]{0:T(128)} %bitcast.place, bf16[512,128]{1,0:T(8,128)(2,1)S(1)} %copy-done.2, bf16[512,128]{1,0:T(8,128)(2,1)S(1)} %collective-permute-done.5.refs_1_, ...), custom_call_target="tpu_custom_call" | custom-call | tf_op jit(solution)/shard_map/pallas_call | solution.py:396
Async XLA Ops:
  2.6 37.4 %all-to-all-start = ((bf16[8,32,512]{2,1,0:T(8,128)(2,1)}), bf16[8,32,512]{2,1,0:T(8,128)(2,1)S(1)}, u32[]{:S(2)}, u32[]{:S(2)}) async-start(bf16[8,32,512]{2,1,0:T(8,128)(2,1)} %get-tuple-element.20), calls=%async_computation | async-start | bytes 524288 | tf_op jit(solution)/shard_map/all_to_all | solution.py:300
  20.7 8.3 %collective-permute-start = (bf16[256,128]{1,0:T(8,128)(2,1)}, bf16[256,128]{1,0:T(8,128)(2,1)S(1)}, u32[]{:S(2)}, u32[]{:S(2)}) collective-permute-start(bf16[256,128]{1,0:T(8,128)(2,1)} %get-tuple-element.22), channel_id=1, source_target_pairs={{0,8},{8,0},{16,24},{24,16},{1,9},{9,1},{17,25},{25,17},{2,10},{10... | collective-permute-start | bytes 196616 | tf_op jit(solution)/shard_map/ppermute | solution.py:294
  23.5 5.8 %collective-permute-start.1 = (bf16[256,128]{1,0:T(8,128)(2,1)}, bf16[256,128]{1,0:T(8,128)(2,1)S(1)}, u32[]{:S(2)}, u32[]{:S(2)}) collective-permute-start(bf16[256,128]{1,0:T(8,128)(2,1)} %get-tuple-element.23), channel_id=1, source_target_pairs={{0,16},{8,24},{16,0},{24,8},{1,17},{9,25},{17,1},{25,9},{2,18},{10... | collective-permute-start | bytes 196616 | tf_op jit(solution)/shard_map/ppermute | solution.py:294
  26.7 6.4 %collective-permute-start.2 = (bf16[256,128]{1,0:T(8,128)(2,1)}, bf16[256,128]{1,0:T(8,128)(2,1)S(1)}, u32[]{:S(2)}, u32[]{:S(2)}) collective-permute-start(bf16[256,128]{1,0:T(8,128)(2,1)} %get-tuple-element.24), channel_id=1, source_target_pairs={{0,24},{8,16},{16,8},{24,0},{1,25},{9,17},{17,9},{25,1},{2,26},{10... | collective-permute-start | bytes 196616 | tf_op jit(solution)/shard_map/ppermute | solution.py:294
  29.0 4.1 %copy-start.4 = (bf16[256,128]{1,0:T(8,128)(2,1)}, bf16[256,128]{1,0:T(8,128)(2,1)S(1)}, u32[]{:S(2)}) copy-start(bf16[256,128]{1,0:T(8,128)(2,1)S(1)} %collective-permute-done.refs_1_) | copy-start | bytes 196612
  29.3 3.8 %copy-start.5 = (bf16[256,128]{1,0:T(8,128)(2,1)}, bf16[256,128]{1,0:T(8,128)(2,1)S(1)}, u32[]{:S(2)}) copy-start(bf16[256,128]{1,0:T(8,128)(2,1)S(1)} %collective-permute-done.1.refs_2_) | copy-start | bytes 196612
  33.1 0.6 copy-start.6
  35.5 10.0 %collective-permute-start.3 = (bf16[768,128]{1,0:T(8,128)(2,1)}, bf16[768,128]{1,0:T(8,128)(2,1)S(1)}, u32[]{:S(2)}, u32[]{:S(2)}) collective-permute-start(bf16[768,128]{1,0:T(8,128)(2,1)} %get-tuple-element.25), channel_id=1, source_target_pairs={{0,32},{32,64},{64,96},{96,128},{128,160},{160,192},{192,224},{224... | collective-permute-start | bytes 589832 | tf_op jit(solution)/shard_map/ppermute | solution.py:289
  41.8 10.5 %all-to-all-start.1 = ((bf16[4,256,128]{2,1,0:T(8,128)(2,1)}), bf16[4,256,128]{2,1,0:T(8,128)(2,1)S(1)}, u32[]{:S(2)}, u32[]{:S(2)}) async-start(bf16[4,256,128]{2,1,0:T(8,128)(2,1)} %bitcast_bitcast_fusion), calls=%async_computation.1 | async-start | bytes 524288 | tf_op jit(solution)/shard_map/all_to_all | solution.py:300
  45.5 0.7 copy-start.7
  52.3 0.7 copy-start.3
  57.8 17.8 %collective-permute-start.4 = (bf16[768,128]{1,0:T(8,128)(2,1)}, bf16[768,128]{1,0:T(8,128)(2,1)S(1)}, u32[]{:S(2)}, u32[]{:S(2)}) collective-permute-start(bf16[768,128]{1,0:T(8,128)(2,1)} %get-tuple-element.28), channel_id=1, source_target_pairs={{32,0},{64,32},{96,64},{128,96},{160,128},{192,160},{224,192},{256... | collective-permute-start | bytes 589832 | tf_op jit(solution)/shard_map/ppermute | solution.py:289
  59.1 36.3 %all-to-all-start.2 = ((bf16[64,16,128]{2,1,0:T(8,128)(2,1)}), bf16[64,16,128]{2,1,0:T(8,128)(2,1)S(1)}, u32[]{:S(2)}, u32[]{:S(2)}) async-start(bf16[64,16,128]{2,1,0:T(8,128)(2,1)} %get-tuple-element.35), calls=%async_computation.2 | async-start | bytes 524288 | tf_op jit(solution)/shard_map/all_to_all | solution.py:300
  75.5 0.7 copy-start.8
  76.2 19.2 %copy-start = (bf16[256,512]{1,0:T(8,128)(2,1)S(1)}, bf16[256,512]{1,0:T(8,128)(2,1)}, u32[]{:S(2)}) copy-start(bf16[256,512]{1,0:T(8,128)(2,1)} %refs_5_.1) | copy-start | bytes 786436
  76.2 19.2 %copy-start.1 = (bf16[256,512]{1,0:T(8,128)(2,1)S(1)}, bf16[256,512]{1,0:T(8,128)(2,1)}, u32[]{:S(2)}) copy-start(bf16[256,512]{1,0:T(8,128)(2,1)} %refs_6_.1) | copy-start | bytes 786436
  81.6 7.9 %collective-permute-start.5 = (bf16[512,128]{1,0:T(8,128)(2,1)}, bf16[512,128]{1,0:T(8,128)(2,1)S(1)}, u32[]{:S(2)}, u32[]{:S(2)}) collective-permute-start(bf16[512,128]{1,0:T(8,128)(2,1)} %get-tuple-element.32), channel_id=1, source_target_pairs={{0,8},{8,0},{16,24},{24,16},{1,9},{9,1},{17,25},{25,17},{2,10},{10... | collective-permute-start | bytes 393224 | tf_op jit(solution)/shard_map/ppermute | solution.py:294
  84.0 7.5 %collective-permute-start.6 = (bf16[512,128]{1,0:T(8,128)(2,1)}, bf16[512,128]{1,0:T(8,128)(2,1)S(1)}, u32[]{:S(2)}, u32[]{:S(2)}) collective-permute-start(bf16[512,128]{1,0:T(8,128)(2,1)} %get-tuple-element.33), channel_id=1, source_target_pairs={{0,16},{8,24},{16,0},{24,8},{1,17},{9,25},{17,1},{25,9},{2,18},{10... | collective-permute-start | bytes 393224 | tf_op jit(solution)/shard_map/ppermute | solution.py:294
  87.2 8.1 %collective-permute-start.7 = (bf16[512,128]{1,0:T(8,128)(2,1)}, bf16[512,128]{1,0:T(8,128)(2,1)S(1)}, u32[]{:S(2)}, u32[]{:S(2)}) collective-permute-start(bf16[512,128]{1,0:T(8,128)(2,1)} %get-tuple-element.34), channel_id=1, source_target_pairs={{0,24},{8,16},{16,8},{24,0},{1,25},{9,17},{17,9},{25,1},{2,26},{10... | collective-permute-start | bytes 393224 | tf_op jit(solution)/shard_map/ppermute | solution.py:294
  95.4 0.9 copy-start.2

commit v9 on v7

--- a/solution.py
+++ b/solution.py
@@ -91,12 +91,6 @@
     for hop, ship in enumerate(ships):
         mixed[rows_at(place[0] ^ hop), :] = ship[...]
     tail[...] = mixed[TOKENS - tail.shape[0] :, :]
-
-
-def grad_kernel(cotangent, gate, grad):
-    product = (cotangent[...].astype(F32) * gate[...].astype(F32)).astype(BF16)
-    for block in range(BLOCKS):
-        grad[block] = product[:, lane_block(block)]
 
 
 def conv_kernel(
@@ -235,8 +229,9 @@
     )
 
 
-VMEM_LIMIT = 56 * MIB
+VMEM_LIMIT = 52 * MIB
 FINAL_LIMIT = 16 * MIB
+PREP_LIMIT = 56 * MIB
 CONV_FLOPS = 24_000_000_000
 CROSS_FLOPS = 0
 JOIN_FLOPS = 0
@@ -281,6 +276,7 @@
         [scalar] + [whole(local)] * 2 + [whole(out_grad.shape)],
         [whole(part)] * BLOCKS + [whole(pieces)],
         [shaped(part)] * BLOCKS + [shaped(pieces)],
+        limit=PREP_LIMIT,
     )(place, key_input, value_input, out_grad)
     cotangent = exchange(cotangent, CH).reshape(local)
     mixed, tail = call(
@@ -291,10 +287,8 @@
         flops=JOIN_FLOPS,
     )(place, *swap(ships))
     mixed_halo = shift(tail, 1)
-    grad = call(grad_kernel, [whole(local)] * 2, whole(by_block), shaped(by_block))(
-        cotangent, gate_input
-    )
-    grad = exchange(grad, GROUP).reshape(flat)
+    grad = (cotangent.astype(F32) * gate_input.astype(F32)).astype(BF16)
+    grad = exchange(grad.reshape(BLOCK, BLOCKS, LANES).transpose(1, 0, 2), GROUP).reshape(flat)
 
     def stepped(*shape):
         return pl.BlockSpec((None,) + shape, lambda step, *_: (step, 0, 0))

time: 97.3 us -> 94.3 us (0.969)
  Pallas kernels: 20.5 us -> 15.5 us
  local copies, waits for them, and re-layouts: 4.29 us -> 0.86 us
  waiting for transfers between devices: 10.7 us -> 12.8 us
  other arithmetic: 0 us -> 1.72 us
  starting transfers between devices: 60.3 us -> 61.9 us
    unnamed x22 -> x10, local copies, waits for them, and re-layouts: 4.29 us -> 0.86 us
    all_to_all x3, waiting for transfers between devices: 0.68 us -> 2.88 us  [exchange(): return lax.all_to_all(value, axes, split_axis=0, concat_axis=0, tiled=True)]
    pallas_call x1 -> x0, Pallas kernels: 1.8 us -> none  [body(): call(grad_kernel, [whole(local)] * 2, whole(by_block), shaped(by_block))]
    transpose x0 -> x1, other arithmetic: none -> 1.72 us  [body(): grad.reshape(BLOCK, BLOCKS, LANES).transpose(1, 0, 2)]
    pallas_call x1, Pallas kernels: 1.72 us -> 0.03 us  [body(): call(join_kernel, [scalar] + [whole(part)] * BLOCKS, [whole(flat), whole(...]
    all_to_all x3, starting transfers between devices: 38.3 us -> 39.9 us  [exchange(): return lax.all_to_all(value, axes, split_axis=0, concat_axis=0, tiled=True)]
    pallas_call x1, Pallas kernels: 4.69 us -> 3.7 us  [body(): call(functools.partial(back_kernel, norm), [scalar, table, stepped(BLOCK,...]
  transfers between devices with their start and end apart: 11 -> 11, of which waited for: 5 -> 6; matrix products, arithmetic and copies ran while one was open for 0% -> 2% of each run, Pallas kernels for 14% -> 9%
where the time goes in v9:
time: 94.3 us; the launch traced here: 93.5 us
  starting transfers between devices  61.9 us (66%)
  Pallas kernels  15.5 us (16%)
  waiting for transfers between devices  12.8 us (14%)
  other arithmetic  1.72 us (2%)
    all_to_all x3, starting transfers between devices, exchange(): return lax.all_to_all(value, axes, split_axis=0, concat_axis=0, tiled=True)  39.9 us
    ppermute x6, starting transfers between devices, swap(): lax.ppermute(ships[hop], GROUP, [(i, i ^ hop) for i in range(BLOCKS)])  16.2 us
    ppermute x6, waiting for transfers between devices, swap(): lax.ppermute(ships[hop], GROUP, [(i, i ^ hop) for i in range(BLOCKS)])  9.92 us
    ppermute x2, starting transfers between devices, shift(): lax.ppermute(value, RUNS, [(i, i + steps) for i in range(first, last)])  5.83 us
    pallas_call x1, Pallas kernels, body(): call(functools.partial(conv_kernel, norm), [table, stepped(BLOCK, ROWS),...  4.69 us
    pallas_call x1, Pallas kernels, body(): call(functools.partial(cross_kernel, norm), [stepped(ROWS, BLOCK), steppe...  4.05 us
    pallas_call x1, Pallas kernels, body(): call(functools.partial(back_kernel, norm), [scalar, table, stepped(BLOCK,...  3.7 us
    all_to_all x3, waiting for transfers between devices, exchange(): return lax.all_to_all(value, axes, split_axis=0, concat_axis=0, tiled=True)  2.88 us
  transfers between devices with their start and end apart: 11, of which 6 were waited for; matrix products, arithmetic and copies ran while one was open for 2% of the time, Pallas kernels for 9%

profile of v9, /device:TPU:1, one launch (start us, length us, event | category | flops | bytes accessed | tf_op | source)
XLA Modules:
  0.0 93.5 jit_solution(1017413929702073605)
XLA Ops:
  0.6 0.0 copy-start.4
  0.6 2.0 %shard_map.129 = (bf16[256,128]{1,0:T(8,128)(2,1)}, bf16[256,128]{1,0:T(8,128)(2,1)}, bf16[256,128]{1,0:T(8,128)(2,1)}, bf16[256,128]{1,0:T(8,128)(2,1)}, bf16[8,32,512]{2,1,0:T(8,128)(2,1)}) custom-call(s32[1]{0:T(128)} %bitcast.place, bf16[256,512]{1,0:T(8,128)(2,1)} %refs_5_.1, bf16[256,512]{1,0:T(8,128)(2,1)} %refs_6_.1, bf16[32,4096]{1,0:T(8,128)(2,1)} %out_grad.1), custom_call_target="tpu_custom_call" | custom-call | tf_op jit(solution)/shard_map/pallas_call | solution.py:274
  2.6 18.1 %all-to-all-start = ((bf16[8,32,512]{2,1,0:T(8,128)(2,1)}), bf16[8,32,512]{2,1,0:T(8,128)(2,1)S(1)}, u32[]{:S(2)}, u32[]{:S(2)}) async-start(bf16[8,32,512]{2,1,0:T(8,128)(2,1)} %get-tuple-element.20), calls=%async_computation | async-start | bytes 524288 | tf_op jit(solution)/shard_map/all_to_all | solution.py:255
  20.7 2.9 %collective-permute-start = (bf16[256,128]{1,0:T(8,128)(2,1)}, bf16[256,128]{1,0:T(8,128)(2,1)S(1)}, u32[]{:S(2)}, u32[]{:S(2)}) collective-permute-start(bf16[256,128]{1,0:T(8,128)(2,1)} %get-tuple-element.22), channel_id=1, source_target_pairs={{0,8},{8,0},{16,24},{24,16},{1,9},{9,1},{17,25},{25,17},{2,10},{10... | collective-permute-start | bytes 196616 | tf_op jit(solution)/shard_map/ppermute | solution.py:249
  23.6 3.2 %collective-permute-start.1 = (bf16[256,128]{1,0:T(8,128)(2,1)}, bf16[256,128]{1,0:T(8,128)(2,1)S(1)}, u32[]{:S(2)}, u32[]{:S(2)}) collective-permute-start(bf16[256,128]{1,0:T(8,128)(2,1)} %get-tuple-element.23), channel_id=1, source_target_pairs={{0,16},{8,24},{16,0},{24,8},{1,17},{9,25},{17,1},{25,9},{2,18},{10... | collective-permute-start | bytes 196616 | tf_op jit(solution)/shard_map/ppermute | solution.py:249
  26.8 2.3 %collective-permute-start.2 = (bf16[256,128]{1,0:T(8,128)(2,1)}, bf16[256,128]{1,0:T(8,128)(2,1)S(1)}, u32[]{:S(2)}, u32[]{:S(2)}) collective-permute-start(bf16[256,128]{1,0:T(8,128)(2,1)} %get-tuple-element.24), channel_id=1, source_target_pairs={{0,24},{8,16},{16,8},{24,0},{1,25},{9,17},{17,9},{25,1},{2,26},{10... | collective-permute-start | bytes 196616 | tf_op jit(solution)/shard_map/ppermute | solution.py:249
  29.1 0.0 collective-permute-done.refs_1_
  29.1 0.3 collective-permute-done.1.refs_2_
  29.4 3.8 %collective-permute-done.2.refs_3_ = bf16[256,128]{1,0:T(8,128)(2,1)S(1)} collective-permute-done((bf16[256,128]{1,0:T(8,128)(2,1)}, bf16[256,128]{1,0:T(8,128)(2,1)S(1)}, u32[]{:S(2)}, u32[]{:S(2)}) %collective-permute-start.2) | collective-permute-done | bytes 65568 | tf_op jit(solution)/shard_map/ppermute | solution.py:249
  33.2 0.0 copy-start.3
  33.2 0.8 copy-done.3
  34.1 4.6 %collective-permute-start.3 = (bf16[768,128]{1,0:T(8,128)(2,1)S(1)}, bf16[768,128]{1,0:T(8,128)(2,1)S(1)}, u32[]{:S(2)}, u32[]{:S(2)}) collective-permute-start(bf16[768,128]{1,0:T(8,128)(2,1)S(1)} %get-tuple-element.25), channel_id=1, source_target_pairs={{0,32},{32,64},{64,96},{96,128},{128,160},{160,192},{192,224},{224... | collective-permute-start | bytes 589832 | tf_op jit(solution)/shard_map/ppermute | solution.py:244
  38.6 0.0 all-to-all-done
  38.6 1.7 %bitcast_bitcast_fusion = bf16[4,256,128]{2,1,0:T(8,128)(2,1)} fusion(bf16[256,512]{1,0:T(8,128)(2,1)} %param.10, bf16[8,32,512]{2,1,0:T(8,128)(2,1)S(1)} %all-to-all-done), kind=kLoop, calls=%fused_computation.2 | loop fusion | flops 524288 | bytes 786432 | tf_op jit(solution)/shard_map/transpose | solution.py:291
  40.4 3.7 %all-to-all-start.1 = ((bf16[4,256,128]{2,1,0:T(8,128)(2,1)}), bf16[4,256,128]{2,1,0:T(8,128)(2,1)S(1)}, u32[]{:S(2)}, u32[]{:S(2)}) async-start(bf16[4,256,128]{2,1,0:T(8,128)(2,1)} %bitcast_bitcast_fusion), calls=%async_computation.1 | async-start | bytes 524288 | tf_op jit(solution)/shard_map/all_to_all | solution.py:255
  44.1 0.0 collective-permute-done.3.halo
  44.1 0.0 copy-done.4
  44.1 0.0 copy-start.2
  44.1 4.7 %shard_map.131 = (bf16[1024,128]{1,0:T(8,128)(2,1)S(1)}, bf16[1024,512]{1,0:T(8,128)(2,1)}, bf16[1024,128]{1,0:T(8,128)(2,1)S(1)}) custom-call(s32[1]{0:T(128)} %bitcast.place, bf16[1,1024,1024]{2,1,0:T(8,128)(2,1)} %constant.22.clone.forward, bf16[1,256,1024]{2,1,0:T(8,128)(2,1)S(1)} %copy-done.4, bf16[768,128]{1,0:T(8,128)(2,1)S(1)} %collective-permute-done.3.halo, ...), custom_call_target="tpu_custom_call" | custom-call | flops 24000000000 | tf_op jit(solution)/shard_map/pallas_call | solution.py:299
  48.8 0.5 all-to-all-done.1
  49.3 0.0 copy-done.2
  49.3 4.0 %shard_map.132 = (bf16[768,128]{1,0:T(8,128)(2,1)S(1)}, bf16[64,16,128]{2,1,0:T(8,128)(2,1)}) custom-call(bf16[1,1024,256]{2,1,0:T(8,128)(2,1)S(1)} %copy-done.2, bf16[1,768,1024]{2,1,0:T(8,128)(2,1)} %constant.25.clone.inverse, bf16[1024,128]{1,0:T(8,128)(2,1)S(1)} %bitcast.13, bf16[1024,512]{1,0:T(8,128)(2,1)} %get-tuple-element.27.spectrum), custom_call_target="tpu_custom_call" | custom-call | tf_op jit(solution)/shard_map/pallas_call | solution.py:316
  53.3 1.3 %collective-permute-start.4 = (bf16[768,128]{1,0:T(8,128)(2,1)S(1)}, bf16[768,128]{1,0:T(8,128)(2,1)S(1)}, u32[]{:S(2)}, u32[]{:S(2)}) collective-permute-start(bf16[768,128]{1,0:T(8,128)(2,1)S(1)} %get-tuple-element.28), channel_id=1, source_target_pairs={{32,0},{64,32},{96,64},{128,96},{160,128},{192,160},{224,192},{256... | collective-permute-start | bytes 589832 | tf_op jit(solution)/shard_map/ppermute | solution.py:244
  54.6 18.0 %all-to-all-start.2 = ((bf16[64,16,128]{2,1,0:T(8,128)(2,1)}), bf16[64,16,128]{2,1,0:T(8,128)(2,1)S(1)}, u32[]{:S(2)}, u32[]{:S(2)}) async-start(bf16[64,16,128]{2,1,0:T(8,128)(2,1)} %get-tuple-element.35), calls=%async_computation.2 | async-start | bytes 524288 | tf_op jit(solution)/shard_map/all_to_all | solution.py:255
  72.6 0.0 collective-permute-done.4.halo
  72.6 0.0 copy-start
  72.7 0.0 copy-start.1
  72.7 3.7 %shard_map.133 = (bf16[512,128]{1,0:T(8,128)(2,1)S(1)}, bf16[512,128]{1,0:T(8,128)(2,1)S(1)}, bf16[512,128]{1,0:T(8,128)(2,1)S(1)}, bf16[512,128]{1,0:T(8,128)(2,1)S(1)}) custom-call(s32[1]{0:T(128)} %bitcast.place, bf16[1,1024,1024]{2,1,0:T(8,128)(2,1)} %constant.22.clone.forward, bf16[1,256,1024]{2,1,0:T(8,128)(2,1)} %constant.24.clone.inverse, ...), custom_call_target="tpu_custom_call" | custom-call | flops 35000000512 | tf_op jit(solution)/shard_map/pallas_call | solution.py:328
  76.4 2.4 %collective-permute-start.5 = (bf16[512,128]{1,0:T(8,128)(2,1)S(1)}, bf16[512,128]{1,0:T(8,128)(2,1)S(1)}, u32[]{:S(2)}, u32[]{:S(2)}) collective-permute-start(bf16[512,128]{1,0:T(8,128)(2,1)S(1)} %get-tuple-element.32), channel_id=1, source_target_pairs={{0,8},{8,0},{16,24},{24,16},{1,9},{9,1},{17,25},{25,17},{2,10},{10... | collective-permute-start | bytes 393224 | tf_op jit(solution)/shard_map/ppermute | solution.py:249
  78.8 3.2 %collective-permute-start.6 = (bf16[512,128]{1,0:T(8,128)(2,1)S(1)}, bf16[512,128]{1,0:T(8,128)(2,1)S(1)}, u32[]{:S(2)}, u32[]{:S(2)}) collective-permute-start(bf16[512,128]{1,0:T(8,128)(2,1)S(1)} %get-tuple-element.33), channel_id=1, source_target_pairs={{0,16},{8,24},{16,0},{24,8},{1,17},{9,25},{17,1},{25,9},{2,18},{10... | collective-permute-start | bytes 393224 | tf_op jit(solution)/shard_map/ppermute | solution.py:249
  81.9 2.3 %collective-permute-start.7 = (bf16[512,128]{1,0:T(8,128)(2,1)S(1)}, bf16[512,128]{1,0:T(8,128)(2,1)S(1)}, u32[]{:S(2)}, u32[]{:S(2)}) collective-permute-start(bf16[512,128]{1,0:T(8,128)(2,1)S(1)} %get-tuple-element.34), channel_id=1, source_target_pairs={{0,24},{8,16},{16,8},{24,0},{1,25},{9,17},{17,9},{25,1},{2,26},{10... | collective-permute-start | bytes 393224 | tf_op jit(solution)/shard_map/ppermute | solution.py:249
  84.3 0.0 collective-permute-done.5.refs_1_
  84.3 2.0 %collective-permute-done.6.refs_2_ = bf16[512,128]{1,0:T(8,128)(2,1)S(1)} collective-permute-done((bf16[512,128]{1,0:T(8,128)(2,1)S(1)}, bf16[512,128]{1,0:T(8,128)(2,1)S(1)}, u32[]{:S(2)}, u32[]{:S(2)}) %collective-permute-start.6) | collective-permute-done | bytes 131104 | tf_op jit(solution)/shard_map/ppermute | solution.py:249
  86.3 3.8 %collective-permute-done.7.refs_3_ = bf16[512,128]{1,0:T(8,128)(2,1)S(1)} collective-permute-done((bf16[512,128]{1,0:T(8,128)(2,1)S(1)}, bf16[512,128]{1,0:T(8,128)(2,1)S(1)}, u32[]{:S(2)}, u32[]{:S(2)}) %collective-permute-start.7) | collective-permute-done | bytes 131104 | tf_op jit(solution)/shard_map/ppermute | solution.py:249
  90.1 2.4 %all-to-all-done.2.refs_7_ = bf16[64,16,128]{2,1,0:T(8,128)(2,1)S(1)} async-done(((bf16[64,16,128]{2,1,0:T(8,128)(2,1)}), bf16[64,16,128]{2,1,0:T(8,128)(2,1)S(1)}, u32[]{:S(2)}, u32[]{:S(2)}) %all-to-all-start.2) | async-done | bytes 262176 | tf_op jit(solution)/shard_map/all_to_all | solution.py:255
  92.5 0.0 copy-done
  92.5 0.0 copy-done.1
  92.5 1.1 %shard_map.134 = (bf16[256,512]{1,0:T(8,128)(2,1)}, bf16[256,512]{1,0:T(8,128)(2,1)}, bf16[256,512]{1,0:T(8,128)(2,1)}, f32[12,512]{1,0:T(8,128)}) custom-call(s32[1]{0:T(128)} %bitcast.place, bf16[512,128]{1,0:T(8,128)(2,1)S(1)} %get-tuple-element.31.refs_0_, bf16[512,128]{1,0:T(8,128)(2,1)S(1)} %collective-permute-done.5.refs_1_, ...), custom_call_target="tpu_custom_call" | custom-call | tf_op jit(solution)/shard_map/pallas_call | solution.py:345
  (1 shorter events, 0.0 us)
Async XLA Ops:
  0.6 43.5 %copy-start.4 = (bf16[1,256,1024]{2,1,0:T(8,128)(2,1)S(1)}, bf16[1,256,1024]{2,1,0:T(8,128)(2,1)}, u32[]{:S(2)}) copy-start(bf16[1,256,1024]{2,1,0:T(8,128)(2,1)} %constant.26.clone.inverse) | copy-start | bytes 1572868
  2.6 36.0 %all-to-all-start = ((bf16[8,32,512]{2,1,0:T(8,128)(2,1)}), bf16[8,32,512]{2,1,0:T(8,128)(2,1)S(1)}, u32[]{:S(2)}, u32[]{:S(2)}) async-start(bf16[8,32,512]{2,1,0:T(8,128)(2,1)} %get-tuple-element.20), calls=%async_computation | async-start | bytes 524288 | tf_op jit(solution)/shard_map/all_to_all | solution.py:255
  20.7 8.3 %collective-permute-start = (bf16[256,128]{1,0:T(8,128)(2,1)}, bf16[256,128]{1,0:T(8,128)(2,1)S(1)}, u32[]{:S(2)}, u32[]{:S(2)}) collective-permute-start(bf16[256,128]{1,0:T(8,128)(2,1)} %get-tuple-element.22), channel_id=1, source_target_pairs={{0,8},{8,0},{16,24},{24,16},{1,9},{9,1},{17,25},{25,17},{2,10},{10... | collective-permute-start | bytes 196616 | tf_op jit(solution)/shard_map/ppermute | solution.py:249
  23.6 5.8 %collective-permute-start.1 = (bf16[256,128]{1,0:T(8,128)(2,1)}, bf16[256,128]{1,0:T(8,128)(2,1)S(1)}, u32[]{:S(2)}, u32[]{:S(2)}) collective-permute-start(bf16[256,128]{1,0:T(8,128)(2,1)} %get-tuple-element.23), channel_id=1, source_target_pairs={{0,16},{8,24},{16,0},{24,8},{1,17},{9,25},{17,1},{25,9},{2,18},{10... | collective-permute-start | bytes 196616 | tf_op jit(solution)/shard_map/ppermute | solution.py:249
  26.8 6.4 %collective-permute-start.2 = (bf16[256,128]{1,0:T(8,128)(2,1)}, bf16[256,128]{1,0:T(8,128)(2,1)S(1)}, u32[]{:S(2)}, u32[]{:S(2)}) collective-permute-start(bf16[256,128]{1,0:T(8,128)(2,1)} %get-tuple-element.24), channel_id=1, source_target_pairs={{0,24},{8,16},{16,8},{24,0},{1,25},{9,17},{17,9},{25,1},{2,26},{10... | collective-permute-start | bytes 196616 | tf_op jit(solution)/shard_map/ppermute | solution.py:249
  33.2 0.8 copy-start.3
  34.1 10.0 %collective-permute-start.3 = (bf16[768,128]{1,0:T(8,128)(2,1)S(1)}, bf16[768,128]{1,0:T(8,128)(2,1)S(1)}, u32[]{:S(2)}, u32[]{:S(2)}) collective-permute-start(bf16[768,128]{1,0:T(8,128)(2,1)S(1)} %get-tuple-element.25), channel_id=1, source_target_pairs={{0,32},{32,64},{64,96},{96,128},{128,160},{160,192},{192,224},{224... | collective-permute-start | bytes 589832 | tf_op jit(solution)/shard_map/ppermute | solution.py:244
  40.4 8.9 %all-to-all-start.1 = ((bf16[4,256,128]{2,1,0:T(8,128)(2,1)}), bf16[4,256,128]{2,1,0:T(8,128)(2,1)S(1)}, u32[]{:S(2)}, u32[]{:S(2)}) async-start(bf16[4,256,128]{2,1,0:T(8,128)(2,1)} %bitcast_bitcast_fusion), calls=%async_computation.1 | async-start | bytes 524288 | tf_op jit(solution)/shard_map/all_to_all | solution.py:255
  44.1 5.2 %copy-start.2 = (bf16[1,1024,256]{2,1,0:T(8,128)(2,1)S(1)}, bf16[1,1024,256]{2,1,0:T(8,128)(2,1)}, u32[]{:S(2)}) copy-start(bf16[1,1024,256]{2,1,0:T(8,128)(2,1)} %constant.23.clone.forward) | copy-start | bytes 1572868
  53.3 19.3 %collective-permute-start.4 = (bf16[768,128]{1,0:T(8,128)(2,1)S(1)}, bf16[768,128]{1,0:T(8,128)(2,1)S(1)}, u32[]{:S(2)}, u32[]{:S(2)}) collective-permute-start(bf16[768,128]{1,0:T(8,128)(2,1)S(1)} %get-tuple-element.28), channel_id=1, source_target_pairs={{32,0},{64,32},{96,64},{128,96},{160,128},{192,160},{224,192},{256... | collective-permute-start | bytes 589832 | tf_op jit(solution)/shard_map/ppermute | solution.py:244
  54.6 37.9 %all-to-all-start.2 = ((bf16[64,16,128]{2,1,0:T(8,128)(2,1)}), bf16[64,16,128]{2,1,0:T(8,128)(2,1)S(1)}, u32[]{:S(2)}, u32[]{:S(2)}) async-start(bf16[64,16,128]{2,1,0:T(8,128)(2,1)} %get-tuple-element.35), calls=%async_computation.2 | async-start | bytes 524288 | tf_op jit(solution)/shard_map/all_to_all | solution.py:255
  72.6 19.8 %copy-start = (bf16[256,512]{1,0:T(8,128)(2,1)S(1)}, bf16[256,512]{1,0:T(8,128)(2,1)}, u32[]{:S(2)}) copy-start(bf16[256,512]{1,0:T(8,128)(2,1)} %refs_5_.1) | copy-start | bytes 786436
  72.7 19.8 %copy-start.1 = (bf16[256,512]{1,0:T(8,128)(2,1)S(1)}, bf16[256,512]{1,0:T(8,128)(2,1)}, u32[]{:S(2)}) copy-start(bf16[256,512]{1,0:T(8,128)(2,1)} %refs_6_.1) | copy-start | bytes 786436
  76.4 7.9 %collective-permute-start.5 = (bf16[512,128]{1,0:T(8,128)(2,1)S(1)}, bf16[512,128]{1,0:T(8,128)(2,1)S(1)}, u32[]{:S(2)}, u32[]{:S(2)}) collective-permute-start(bf16[512,128]{1,0:T(8,128)(2,1)S(1)} %get-tuple-element.32), channel_id=1, source_target_pairs={{0,8},{8,0},{16,24},{24,16},{1,9},{9,1},{17,25},{25,17},{2,10},{10... | collective-permute-start | bytes 393224 | tf_op jit(solution)/shard_map/ppermute | solution.py:249
  78.8 7.5 %collective-permute-start.6 = (bf16[512,128]{1,0:T(8,128)(2,1)S(1)}, bf16[512,128]{1,0:T(8,128)(2,1)S(1)}, u32[]{:S(2)}, u32[]{:S(2)}) collective-permute-start(bf16[512,128]{1,0:T(8,128)(2,1)S(1)} %get-tuple-element.33), channel_id=1, source_target_pairs={{0,16},{8,24},{16,0},{24,8},{1,17},{9,25},{17,1},{25,9},{2,18},{10... | collective-permute-start | bytes 393224 | tf_op jit(solution)/shard_map/ppermute | solution.py:249
  81.9 8.1 %collective-permute-start.7 = (bf16[512,128]{1,0:T(8,128)(2,1)S(1)}, bf16[512,128]{1,0:T(8,128)(2,1)S(1)}, u32[]{:S(2)}, u32[]{:S(2)}) collective-permute-start(bf16[512,128]{1,0:T(8,128)(2,1)S(1)} %get-tuple-element.34), channel_id=1, source_target_pairs={{0,24},{8,16},{16,8},{24,0},{1,25},{9,17},{17,9},{25,1},{2,26},{10... | collective-permute-start | bytes 393224 | tf_op jit(solution)/shard_map/ppermute | solution.py:249

commit v10 on v9

v10 whole, which is shorter than its diff:
```python
import functools
import math

import jax
import jax.numpy as jnp
import ml_dtypes
import numpy as np
from jax import lax
from jax.experimental import pallas as pl
from jax.experimental.pallas import tpu as pltpu
from jax.sharding import Mesh, PartitionSpec as P

BF16 = jnp.bfloat16
F32 = jnp.float32
AXES = ("z", "yh", "yl", "c", "x", "zh")
SIZES = (8, 2, 2, 2, 4, 2)
CTX = ("z", "yh", "yl", "c")
GROUP = ("yl", "c")
RUNS = ("z", "yh")
CH = ("x", "zh")

BLOCK = 256
PERIOD = 1024
LANES = 128
BLOCKS = 4
TOKENS = BLOCKS * BLOCK
WIDE = BLOCKS * LANES
BINS = 128
STEPS = 4
ROWS = 2 * BINS
SLOT = 16
MIB = 1024 * 1024


def make_tables():
    freq = np.arange(PERIOD // 2)[:, None]
    place = np.arange(BLOCK)[None, :]
    angle = math.pi / PERIOD * ((2 * freq + 1) * place % (2 * PERIOD)).astype(np.float64)
    both = np.stack([np.cos(angle), -np.sin(angle)]).reshape(2, BINS, STEPS, BLOCK)
    both = both.transpose(2, 0, 1, 3).reshape(STEPS, ROWS, BLOCK)
    tables = both, both.transpose(0, 2, 1)
    return tuple(np.ascontiguousarray(t).astype(ml_dtypes.bfloat16) for t in tables)


def turn(spec, chunk, block):
    re, im = spec
    eighths = (2 * chunk + 1) * block % 8
    half = math.sqrt(0.5)
    if eighths == 0:
        return re, im
    if eighths == 1:
        return (re + im) * half, (im - re) * half
    if eighths == 2:
        return im, -re
    if eighths == 3:
        return (im - re) * half, (re + im) * -half
    if eighths == 4:
        return -re, -im
    if eighths == 5:
        return (re + im) * -half, (re - im) * half
    if eighths == 6:
        return -im, re
    return (re - im) * half, (re + im) * half


def add(specs):
    return sum(re for re, _ in specs), sum(im for _, im in specs)


def times(a, b):
    return a[0] * b[0] - a[1] * b[1], a[0] * b[1] + a[1] * b[0]


def times_conj(a, b):
    return a[0] * b[0] + a[1] * b[1], a[1] * b[0] - a[0] * b[1]


def transform(table, blocks, chunk, first=0):
    flat = dot(table, blocks)
    count = blocks.shape[1] // LANES
    parts = [flat[:, lane_block(i)] for i in range(count)]
    return [turn((p[:BINS], p[BINS:]), chunk, first + i) for i, p in enumerate(parts)]


def stacked(specs):
    return jnp.concatenate([jnp.concatenate(spec, axis=0) for spec in specs], axis=1).astype(BF16)


def fill(blocks, *sources):
    at = 0
    for source in sources:
        for block in range(source.shape[0] // BLOCK):
            blocks[:, lane_block(at)] = source[token_block(block), :]
            at += 1


def dot(a, b):
    return jnp.dot(a, b, preferred_element_type=F32)


def lane_block(index):
    return slice(index * LANES, (index + 1) * LANES)


def lanes_at(index):
    return pl.ds(pl.multiple_of(index * LANES, LANES), LANES)


def rows_at(index):
    return pl.ds(pl.multiple_of(index * BLOCK, BLOCK), BLOCK)


def token_block(index):
    return slice(index * BLOCK, (index + 1) * BLOCK)


def prep_kernel(place, key, value, out_grad, *outs):
    ships, pieces = outs[:BLOCKS], outs[BLOCKS]
    for hop, ship in enumerate(ships):
        at = (slice(None), lanes_at(place[0] ^ hop))
        ship[...] = (key[at].astype(F32) * value[at].astype(F32)).astype(BF16)
    for piece in range(pieces.shape[0]):
        pieces[piece] = out_grad[:, piece * WIDE : (piece + 1) * WIDE]


def join_kernel(place, *refs):
    ships, (mixed, tail) = refs[:BLOCKS], refs[BLOCKS:]
    for hop, ship in enumerate(ships):
        mixed[rows_at(place[0] ^ hop), :] = ship[...]
    tail[...] = mixed[TOKENS - tail.shape[0] :, :]


def conv_kernel(scale, place, table, back, halo, mixed, taps, conv, spectrum, response, blocks, filt):
    reach = taps.shape[0] // BLOCK
    fill(blocks, halo, mixed)
    fill(filt, taps)
    for chunk in range(STEPS):
        resp = add(transform(table[chunk], filt[...], chunk))
        response[chunk] = stacked([resp])
        specs = transform(table[chunk], blocks[...], chunk)
        specs = [add(specs[b : b + reach + 1]) for b in range(BLOCKS)]
        spectrum[chunk] = stacked(specs)
        y = [turn(times(resp, spec), chunk, -(b + reach)) for b, spec in enumerate(specs)]
        part = dot(back[chunk], stacked(y))
        total = total + part if chunk else part
    for block in range(BLOCKS):
        conv[token_block(block), :] = (total[:, lane_block(block)] * scale).astype(BF16)


def cross_kernel(scale, table, back, grad, spectrum, head, lag_grad, blocks, total):
    lags = head.shape[0]
    reach = lags // BLOCK
    head[...] = grad[:lags, :]
    fill(blocks, grad)
    for chunk in range(STEPS):
        specs = transform(table[chunk], blocks[...], chunk, reach)
        terms = []
        for block, spec in enumerate(specs):
            held = spectrum[chunk, :, lane_block(block)].astype(F32)
            terms.append(times_conj(spec, (held[:BINS], held[BINS:])))
        term = add(terms)
        part = dot(back[chunk], stacked([turn(term, chunk, -j) for j in range(reach)]))
        summed = summed + part if chunk else part
    for j in range(reach):
        total[token_block(j), :] = summed[:, lane_block(j)] * scale
    total[lags:, :] = jnp.zeros_like(total[lags:, :])
    count = lag_grad.shape[0]
    share = lags // count
    for slot in range(count):
        lag_grad[slot] = total[slot * share : slot * share + SLOT, :].astype(BF16)


def back_kernel(scale, place, table, back, grad, halo, response, conv, *refs):
    outs, (blocks,) = refs[:BLOCKS], refs[BLOCKS:]
    reach = halo.shape[0] // BLOCK
    fill(blocks, grad, halo)
    for chunk in range(STEPS):
        held = response[chunk].astype(F32)
        resp = held[:BINS], held[BINS:]
        specs = transform(table[chunk], blocks[...], chunk)
        specs = [add(specs[b : b + reach + 1]) for b in range(BLOCKS)]
        y = [turn(times_conj(spec, resp), chunk, -b) for b, spec in enumerate(specs)]
        part = dot(back[chunk], stacked(y))
        total = total + part if chunk else part
    blocks[:, :WIDE] = (total * scale).astype(BF16)
    for hop, out in enumerate(outs):
        out[:BLOCK, :] = conv[rows_at(place[0] ^ hop), :]
        out[BLOCK:, :] = blocks[:, lanes_at(place[0] ^ hop)]


def final_kernel(place, *refs):
    ships, refs = refs[:BLOCKS], refs[BLOCKS:]
    cotangent, key, value, parts, gate_grad, key_grad, value_grad, lag_grad = refs
    for hop, ship in enumerate(ships):
        at = (slice(None), lanes_at(place[0] ^ hop))
        conv, back = ship[:BLOCK, :].astype(F32), ship[BLOCK:, :].astype(F32)
        gate_grad[at] = (cotangent[at].astype(F32) * conv).astype(BF16)
        key_grad[at] = (back * value[at].astype(F32)).astype(BF16)
        value_grad[at] = (back * key[at].astype(F32)).astype(BF16)
    for block in range(BLOCKS):
        total = parts[block].astype(F32)
        for source in range(1, parts.shape[0] // BLOCKS):
            total += parts[source * BLOCKS + block].astype(F32)
        lag_grad[:, lane_block(block)] = total[: lag_grad.shape[0]]


def whole(shape):
    return pl.BlockSpec(shape, lambda *_: (0,) * len(shape))


def shaped(shape, dtype=BF16):
    return jax.ShapeDtypeStruct(shape, dtype)


def call(kernel, in_specs, out_specs, out_shape, scratch=(), flops=0, limit=None, scalars=0):
    return pl.pallas_call(
        kernel,
        grid_spec=pltpu.PrefetchScalarGridSpec(
            num_scalar_prefetch=scalars,
            grid=(1,),
            in_specs=in_specs,
            out_specs=out_specs,
            scratch_shapes=scratch,
        ),
        out_shape=out_shape,
        compiler_params=pltpu.CompilerParams(
            dimension_semantics=("arbitrary",), vmem_limit_bytes=limit or VMEM_LIMIT
        ),
        cost_estimate=pl.CostEstimate(flops=flops, bytes_accessed=0, transcendentals=0),
    )


VMEM_LIMIT = 52 * MIB
FINAL_LIMIT = 16 * MIB
PREP_LIMIT = 56 * MIB
CONV_FLOPS = 24_000_000_000
CROSS_FLOPS = 0
JOIN_FLOPS = 0
BACK_FLOPS = 35_000_000_000


def shift(value, steps):
    count = lax.axis_size(RUNS)
    first, last = max(0, -steps), min(count, count - steps)
    return lax.ppermute(value, RUNS, [(i, i + steps) for i in range(first, last)])


def swap(ships):
    return [ships[0]] + [
        lax.ppermute(ships[hop], GROUP, [(i, i ^ hop) for i in range(BLOCKS)])
        for hop in range(1, BLOCKS)
    ]


def exchange(value, axes):
    return lax.all_to_all(value, axes, split_axis=0, concat_axis=0, tiled=True)


def body(forward, inverse, gate_input, key_input, value_input, out_grad, filter_taps):
    lags = filter_taps.shape[0]
    held, channels = out_grad.shape
    share = lags // lax.axis_size(CTX)
    norm = 2.0 / PERIOD / lags**0.5
    local = (BLOCK, WIDE)
    ship = (2 * BLOCK, LANES)
    pieces = (channels // WIDE, held, WIDE)
    flat = (TOKENS, LANES)
    reach = (lags, LANES)
    slots = (lags // share, SLOT, LANES)
    scalar = pl.BlockSpec(memory_space=pltpu.SMEM)
    place = lax.axis_index(GROUP).reshape(1)

    part = (BLOCK, LANES)
    by_block = (BLOCKS, BLOCK, LANES)
    *ships, cotangent = call(
        prep_kernel,
        [scalar] + [whole(local)] * 2 + [whole(out_grad.shape)],
        [whole(part)] * BLOCKS + [whole(pieces)],
        [shaped(part)] * BLOCKS + [shaped(pieces)],
        limit=PREP_LIMIT,
    )(place, key_input, value_input, out_grad)
    cotangent = exchange(cotangent, CH).reshape(local)
    mixed, tail = call(
        join_kernel,
        [scalar] + [whole(part)] * BLOCKS,
        [whole(flat), whole(reach)],
        [shaped(flat), shaped(reach)],
        flops=JOIN_FLOPS,
    )(place, *swap(ships))
    mixed_halo = shift(tail, 1)
    grad = (cotangent.astype(F32) * gate_input.astype(F32)).astype(BF16)
    grad = exchange(grad.reshape(BLOCK, BLOCKS, LANES).transpose(1, 0, 2), GROUP).reshape(flat)

    table = whole(forward.shape)
    by_bins = (STEPS, ROWS, WIDE)
    filt_bins = (STEPS, ROWS, LANES)
    seven = pltpu.VMEM((BLOCK, WIDE + lags // BLOCK * LANES), BF16)
    conv, spectrum, response = call(
        functools.partial(conv_kernel, norm),
        [
            table,
            table,
            whole(reach),
            whole(flat),
            pl.BlockSpec(reach, lambda step, place: (0, place[0])),
        ],
        [whole(flat), whole(by_bins), whole(filt_bins)],
        [shaped(flat), shaped(by_bins), shaped(filt_bins)],
        [seven, pltpu.VMEM((BLOCK, lags // BLOCK * LANES), BF16)],
        CONV_FLOPS,
        scalars=1,
    )(place, forward, inverse, mixed_halo, mixed, filter_taps)
    head, lag_grad = call(
        functools.partial(cross_kernel, norm),
        [table, table, whole(flat), whole(by_bins)],
        [whole(reach), whole(slots)],
        [shaped(reach), shaped(slots)],
        [pltpu.VMEM(local, BF16), pltpu.VMEM((lags + SLOT, LANES), F32)],
        CROSS_FLOPS,
    )(forward, inverse, grad, spectrum)
    grad_halo = shift(head, -1)
    lag_parts = exchange(lag_grad, CTX)

    ships = call(
        functools.partial(back_kernel, norm),
        [
            scalar,
            table,
            table,
            whole(flat),
            whole(reach),
            whole(filt_bins),
            whole(flat),
        ],
        [whole(ship)] * BLOCKS,
        [shaped(ship)] * BLOCKS,
        [seven],
        BACK_FLOPS,
    )(place, forward, inverse, grad, grad_halo, response, conv)
    gate_grad, key_grad, value_grad, filter_grad = call(
        final_kernel,
        [scalar] + [whole(ship)] * BLOCKS + [whole(local)] * 3 + [whole(slots)],
        [whole(local)] * 3 + [whole((share, WIDE))],
        [shaped(local)] * 3 + [shaped((share, WIDE), F32)],
        limit=FINAL_LIMIT,
    )(place, *swap(ships), cotangent, key_input, value_input, lag_parts)
    return gate_grad, key_grad, value_grad, filter_grad


def solution(mesh):
    split = Mesh(mesh.devices.reshape(SIZES), AXES)
    spans = P(CTX, CH)
    mapped = jax.shard_map(
        body,
        mesh=split,
        in_specs=(P(), P(), spans, spans, spans, P(CTX + CH, None), P(None, CH)),
        out_specs=(spans, spans, spans, spans),
        check_vma=False,
    )

    def run(gate_input, key_input, value_input, out_grad, filter_taps):
        return mapped(*make_tables(), gate_input, key_input, value_input, out_grad, filter_taps)

    return run
```

time: 94.3 us -> 92.8 us (0.984)
  Pallas kernels: 15.5 us -> 13.4 us
  waiting for transfers between devices: 12.8 us -> 14 us
  starting transfers between devices: 61.9 us -> 63 us
    pallas_call x3, Pallas kernels: 12.4 us -> 10.4 us  [the longest x1 3.93 us: body(): call(functools.partial(conv_kernel, norm), [table, table, whole(reach), w...]
    all_to_all x3, waiting for transfers between devices: 2.88 us -> 4.2 us  [exchange(): return lax.all_to_all(value, axes, split_axis=0, concat_axis=0, tiled=True)]
  transfers between devices with their start and end apart: 11 -> 11, of which waited for: 6 -> 6; matrix products, arithmetic and copies ran while one was open for 2% -> 1% of each run, Pallas kernels for 9% -> 8%
where the time goes in v10:
time: 92.8 us; the launch traced here: 92.1 us
  starting transfers between devices  63 us (68%)
  waiting for transfers between devices  14 us (15%)
  Pallas kernels  13.4 us (14%)
    all_to_all x3, starting transfers between devices, exchange(): return lax.all_to_all(value, axes, split_axis=0, concat_axis=0, tiled=True)  40.7 us
    ppermute x6, starting transfers between devices, swap(): lax.ppermute(ships[hop], GROUP, [(i, i ^ hop) for i in range(BLOCKS)])  16.3 us
    ppermute x6, waiting for transfers between devices, swap(): lax.ppermute(ships[hop], GROUP, [(i, i ^ hop) for i in range(BLOCKS)])  9.77 us
    ppermute x2, starting transfers between devices, shift(): lax.ppermute(value, RUNS, [(i, i + steps) for i in range(first, last)])  5.96 us
    all_to_all x3, waiting for transfers between devices, exchange(): return lax.all_to_all(value, axes, split_axis=0, concat_axis=0, tiled=True)  4.2 us
    pallas_call x1, Pallas kernels, body(): call(functools.partial(conv_kernel, norm), [table, table, whole(reach), w...  3.93 us
    pallas_call x1, Pallas kernels, body(): call(functools.partial(cross_kernel, norm), [table, table, whole(flat), w...  3.43 us
    pallas_call x1, Pallas kernels, body(): call(functools.partial(back_kernel, norm), [scalar, table, table, whole(f...  3.08 us
  transfers between devices with their start and end apart: 11, of which 6 were waited for; matrix products, arithmetic and copies ran while one was open for 1% of the time, Pallas kernels for 8%

profile of v10, /device:TPU:1, one launch (start us, length us, event | category | flops | bytes accessed | tf_op | source)
XLA Modules:
  0.0 92.1 jit_solution(2486990487268416606)
XLA Ops:
  0.6 1.9 %shard_map.102 = (bf16[256,128]{1,0:T(8,128)(2,1)}, bf16[256,128]{1,0:T(8,128)(2,1)}, bf16[256,128]{1,0:T(8,128)(2,1)}, bf16[256,128]{1,0:T(8,128)(2,1)}, bf16[8,32,512]{2,1,0:T(8,128)(2,1)}) custom-call(s32[1]{0:T(128)} %bitcast.place, bf16[256,512]{1,0:T(8,128)(2,1)} %refs_5_.1, bf16[256,512]{1,0:T(8,128)(2,1)} %refs_6_.1, bf16[32,4096]{1,0:T(8,128)(2,1)} %out_grad.1), custom_call_target="tpu_custom_call" | custom-call | tf_op jit(solution)/shard_map/pallas_call | solution.py:275
  2.6 0.0 copy-start.8
  2.6 0.0 copy-start.7
  2.6 0.0 copy-start.6
  2.6 0.0 copy-start.4
  2.6 18.2 %all-to-all-start = ((bf16[8,32,512]{2,1,0:T(8,128)(2,1)}), bf16[8,32,512]{2,1,0:T(8,128)(2,1)S(1)}, u32[]{:S(2)}, u32[]{:S(2)}) async-start(bf16[8,32,512]{2,1,0:T(8,128)(2,1)} %get-tuple-element.20), calls=%async_computation | async-start | bytes 524288 | tf_op jit(solution)/shard_map/all_to_all | solution.py:256
  20.8 0.0 copy-start.5
  20.8 0.0 copy-done.8
  20.8 3.0 %collective-permute-start = (bf16[256,128]{1,0:T(8,128)(2,1)S(1)}, bf16[256,128]{1,0:T(8,128)(2,1)S(1)}, u32[]{:S(2)}, u32[]{:S(2)}) collective-permute-start(bf16[256,128]{1,0:T(8,128)(2,1)S(1)} %copy-done.8), channel_id=1, source_target_pairs={{0,8},{8,0},{16,24},{24,16},{1,9},{9,1},{17,25},{25,17},{2,10},{10... | collective-permute-start | bytes 196616 | tf_op jit(solution)/shard_map/ppermute | solution.py:250
  23.8 0.0 copy-done.7
  23.9 3.2 %collective-permute-start.1 = (bf16[256,128]{1,0:T(8,128)(2,1)S(1)}, bf16[256,128]{1,0:T(8,128)(2,1)S(1)}, u32[]{:S(2)}, u32[]{:S(2)}) collective-permute-start(bf16[256,128]{1,0:T(8,128)(2,1)S(1)} %copy-done.7), channel_id=1, source_target_pairs={{0,16},{8,24},{16,0},{24,8},{1,17},{9,25},{17,1},{25,9},{2,18},{10... | collective-permute-start | bytes 196616 | tf_op jit(solution)/shard_map/ppermute | solution.py:250
  27.1 0.0 copy-done.6
  27.1 2.3 %collective-permute-start.2 = (bf16[256,128]{1,0:T(8,128)(2,1)S(1)}, bf16[256,128]{1,0:T(8,128)(2,1)S(1)}, u32[]{:S(2)}, u32[]{:S(2)}) collective-permute-start(bf16[256,128]{1,0:T(8,128)(2,1)S(1)} %copy-done.6), channel_id=1, source_target_pairs={{0,24},{8,16},{16,8},{24,0},{1,25},{9,17},{17,9},{25,1},{2,26},{10... | collective-permute-start | bytes 196616 | tf_op jit(solution)/shard_map/ppermute | solution.py:250
  29.3 0.0 collective-permute-done.refs_1_
  29.3 0.1 collective-permute-done.1.refs_2_
  29.5 3.8 %collective-permute-done.2.refs_3_ = bf16[256,128]{1,0:T(8,128)(2,1)S(1)} collective-permute-done((bf16[256,128]{1,0:T(8,128)(2,1)S(1)}, bf16[256,128]{1,0:T(8,128)(2,1)S(1)}, u32[]{:S(2)}, u32[]{:S(2)}) %collective-permute-start.2) | collective-permute-done | bytes 65568 | tf_op jit(solution)/shard_map/ppermute | solution.py:250
  33.3 0.0 copy-done.4
  33.3 0.0 copy-start.3
  33.3 4.7 %collective-permute-start.3 = (bf16[768,128]{1,0:T(8,128)(2,1)S(1)}, bf16[768,128]{1,0:T(8,128)(2,1)S(1)}, u32[]{:S(2)}, u32[]{:S(2)}) collective-permute-start(bf16[768,128]{1,0:T(8,128)(2,1)S(1)} %get-tuple-element.25), channel_id=1, source_target_pairs={{0,32},{32,64},{64,96},{96,128},{128,160},{160,192},{192,224},{224... | collective-permute-start | bytes 589832 | tf_op jit(solution)/shard_map/ppermute | solution.py:245
  38.0 0.0 all-to-all-done
  38.0 0.0 copy-done.5
  38.0 0.8 bitcast_bitcast_fusion
  38.8 3.7 %all-to-all-start.1 = ((bf16[4,256,128]{2,1,0:T(8,128)(2,1)}), bf16[4,256,128]{2,1,0:T(8,128)(2,1)S(1)}, u32[]{:S(2)}, u32[]{:S(2)}) async-start(bf16[4,256,128]{2,1,0:T(8,128)(2,1)} %bitcast_bitcast_fusion), calls=%async_computation.1 | async-start | bytes 524288 | tf_op jit(solution)/shard_map/all_to_all | solution.py:256
  42.5 0.0 collective-permute-done.3.halo
  42.5 0.0 copy-done.3
  42.5 0.0 copy-start.2
  42.5 3.9 %shard_map.104 = (bf16[1024,128]{1,0:T(8,128)(2,1)S(1)}, bf16[4,256,512]{2,1,0:T(8,128)(2,1)}, bf16[4,256,128]{2,1,0:T(8,128)(2,1)S(1)}) custom-call(s32[1]{0:T(128)} %bitcast.place, bf16[4,256,256]{2,1,0:T(8,128)(2,1)S(1)} %copy-done.3, bf16[4,256,256]{2,1,0:T(8,128)(2,1)} %constant.17.clone.back, bf16[768,128]{1,0:T(8,128)(2,1)S(1)} %collective-permute-done.3.halo, ...), custom_call_target="tpu_custom_call" | custom-call | flops 24000000000 | tf_op jit(solution)/shard_map/pallas_call | solution.py:298
  46.5 1.2 %all-to-all-done.1 = bf16[4,256,128]{2,1,0:T(8,128)(2,1)S(1)} async-done(((bf16[4,256,128]{2,1,0:T(8,128)(2,1)}), bf16[4,256,128]{2,1,0:T(8,128)(2,1)S(1)}, u32[]{:S(2)}, u32[]{:S(2)}) %all-to-all-start.1) | async-done | bytes 262176 | tf_op jit(solution)/shard_map/all_to_all | solution.py:256
  47.7 0.0 copy-done.2
  47.7 3.4 %shard_map.105 = (bf16[768,128]{1,0:T(8,128)(2,1)S(1)}, bf16[64,16,128]{2,1,0:T(8,128)(2,1)}) custom-call(bf16[4,256,256]{2,1,0:T(8,128)(2,1)S(1)} %copy-done.3, bf16[4,256,256]{2,1,0:T(8,128)(2,1)S(1)} %copy-done.2, bf16[1024,128]{1,0:T(8,128)(2,1)S(1)} %bitcast.13, bf16[4,256,512]{2,1,0:T(8,128)(2,1)} %get-tuple-element.27.spectrum), custom_call_target="tpu_custom_call" | custom-call | tf_op jit(solution)/shard_map/pallas_call | solution.py:313
  51.1 1.3 %collective-permute-start.4 = (bf16[768,128]{1,0:T(8,128)(2,1)S(1)}, bf16[768,128]{1,0:T(8,128)(2,1)S(1)}, u32[]{:S(2)}, u32[]{:S(2)}) collective-permute-start(bf16[768,128]{1,0:T(8,128)(2,1)S(1)} %get-tuple-element.28), channel_id=1, source_target_pairs={{32,0},{64,32},{96,64},{128,96},{160,128},{192,160},{224,192},{256... | collective-permute-start | bytes 589832 | tf_op jit(solution)/shard_map/ppermute | solution.py:245
  52.4 18.7 %all-to-all-start.2 = ((bf16[64,16,128]{2,1,0:T(8,128)(2,1)}), bf16[64,16,128]{2,1,0:T(8,128)(2,1)S(1)}, u32[]{:S(2)}, u32[]{:S(2)}) async-start(bf16[64,16,128]{2,1,0:T(8,128)(2,1)} %get-tuple-element.35), calls=%async_computation.2 | async-start | bytes 524288 | tf_op jit(solution)/shard_map/all_to_all | solution.py:256
  71.2 0.0 collective-permute-done.4.halo
  71.2 0.0 copy-start
  71.2 0.0 copy-start.1
  71.2 3.1 %shard_map.106 = (bf16[512,128]{1,0:T(8,128)(2,1)S(1)}, bf16[512,128]{1,0:T(8,128)(2,1)S(1)}, bf16[512,128]{1,0:T(8,128)(2,1)S(1)}, bf16[512,128]{1,0:T(8,128)(2,1)S(1)}) custom-call(s32[1]{0:T(128)} %bitcast.place, bf16[4,256,256]{2,1,0:T(8,128)(2,1)} %constant.16.clone.table, bf16[4,256,256]{2,1,0:T(8,128)(2,1)} %constant.17.clone.back, ...), custom_call_target="tpu_custom_call" | custom-call | flops 35000000512 | tf_op jit(solution)/shard_map/pallas_call | solution.py:324
  74.3 2.4 %collective-permute-start.5 = (bf16[512,128]{1,0:T(8,128)(2,1)S(1)}, bf16[512,128]{1,0:T(8,128)(2,1)S(1)}, u32[]{:S(2)}, u32[]{:S(2)}) collective-permute-start(bf16[512,128]{1,0:T(8,128)(2,1)S(1)} %get-tuple-element.32), channel_id=1, source_target_pairs={{0,8},{8,0},{16,24},{24,16},{1,9},{9,1},{17,25},{25,17},{2,10},{10... | collective-permute-start | bytes 393224 | tf_op jit(solution)/shard_map/ppermute | solution.py:250
  76.7 3.2 %collective-permute-start.6 = (bf16[512,128]{1,0:T(8,128)(2,1)S(1)}, bf16[512,128]{1,0:T(8,128)(2,1)S(1)}, u32[]{:S(2)}, u32[]{:S(2)}) collective-permute-start(bf16[512,128]{1,0:T(8,128)(2,1)S(1)} %get-tuple-element.33), channel_id=1, source_target_pairs={{0,16},{8,24},{16,0},{24,8},{1,17},{9,25},{17,1},{25,9},{2,18},{10... | collective-permute-start | bytes 393224 | tf_op jit(solution)/shard_map/ppermute | solution.py:250
  79.9 2.3 %collective-permute-start.7 = (bf16[512,128]{1,0:T(8,128)(2,1)S(1)}, bf16[512,128]{1,0:T(8,128)(2,1)S(1)}, u32[]{:S(2)}, u32[]{:S(2)}) collective-permute-start(bf16[512,128]{1,0:T(8,128)(2,1)S(1)} %get-tuple-element.34), channel_id=1, source_target_pairs={{0,24},{8,16},{16,8},{24,0},{1,25},{9,17},{17,9},{25,1},{2,26},{10... | collective-permute-start | bytes 393224 | tf_op jit(solution)/shard_map/ppermute | solution.py:250
  82.2 0.0 collective-permute-done.5.refs_1_
  82.2 2.0 %collective-permute-done.6.refs_2_ = bf16[512,128]{1,0:T(8,128)(2,1)S(1)} collective-permute-done((bf16[512,128]{1,0:T(8,128)(2,1)S(1)}, bf16[512,128]{1,0:T(8,128)(2,1)S(1)}, u32[]{:S(2)}, u32[]{:S(2)}) %collective-permute-start.6) | collective-permute-done | bytes 131104 | tf_op jit(solution)/shard_map/ppermute | solution.py:250
  84.2 3.8 %collective-permute-done.7.refs_3_ = bf16[512,128]{1,0:T(8,128)(2,1)S(1)} collective-permute-done((bf16[512,128]{1,0:T(8,128)(2,1)S(1)}, bf16[512,128]{1,0:T(8,128)(2,1)S(1)}, u32[]{:S(2)}, u32[]{:S(2)}) %collective-permute-start.7) | collective-permute-done | bytes 131104 | tf_op jit(solution)/shard_map/ppermute | solution.py:250
  88.1 3.0 %all-to-all-done.2.refs_7_ = bf16[64,16,128]{2,1,0:T(8,128)(2,1)S(1)} async-done(((bf16[64,16,128]{2,1,0:T(8,128)(2,1)}), bf16[64,16,128]{2,1,0:T(8,128)(2,1)S(1)}, u32[]{:S(2)}, u32[]{:S(2)}) %all-to-all-start.2) | async-done | bytes 262176 | tf_op jit(solution)/shard_map/all_to_all | solution.py:256
  91.0 0.0 copy-done
  91.0 0.0 copy-done.1
  91.0 1.1 %shard_map.107 = (bf16[256,512]{1,0:T(8,128)(2,1)}, bf16[256,512]{1,0:T(8,128)(2,1)}, bf16[256,512]{1,0:T(8,128)(2,1)}, f32[12,512]{1,0:T(8,128)}) custom-call(s32[1]{0:T(128)} %bitcast.place, bf16[512,128]{1,0:T(8,128)(2,1)S(1)} %get-tuple-element.31.refs_0_, bf16[512,128]{1,0:T(8,128)(2,1)S(1)} %collective-permute-done.5.refs_1_, ...), custom_call_target="tpu_custom_call" | custom-call | tf_op jit(solution)/shard_map/pallas_call | solution.py:340
  (1 shorter events, 0.0 us)
Async XLA Ops:
  2.6 18.3 %copy-start.8 = (bf16[256,128]{1,0:T(8,128)(2,1)S(1)}, bf16[256,128]{1,0:T(8,128)(2,1)}, u32[]{:S(2)}) copy-start(bf16[256,128]{1,0:T(8,128)(2,1)} %get-tuple-element.22) | copy-start | bytes 196612
  2.6 21.3 %copy-start.7 = (bf16[256,128]{1,0:T(8,128)(2,1)S(1)}, bf16[256,128]{1,0:T(8,128)(2,1)}, u32[]{:S(2)}) copy-start(bf16[256,128]{1,0:T(8,128)(2,1)} %get-tuple-element.23) | copy-start | bytes 196612
  2.6 24.5 %copy-start.6 = (bf16[256,128]{1,0:T(8,128)(2,1)S(1)}, bf16[256,128]{1,0:T(8,128)(2,1)}, u32[]{:S(2)}) copy-start(bf16[256,128]{1,0:T(8,128)(2,1)} %get-tuple-element.24) | copy-start | bytes 196612
  2.6 30.7 %copy-start.4 = (bf16[256,128]{1,0:T(8,128)(2,1)S(1)}, bf16[256,128]{1,0:T(8,128)(2,1)}, u32[]{:S(2)}) copy-start(bf16[256,128]{1,0:T(8,128)(2,1)} %get-tuple-element.21.refs_0_) | copy-start | bytes 196612
  2.6 35.4 %all-to-all-start = ((bf16[8,32,512]{2,1,0:T(8,128)(2,1)}), bf16[8,32,512]{2,1,0:T(8,128)(2,1)S(1)}, u32[]{:S(2)}, u32[]{:S(2)}) async-start(bf16[8,32,512]{2,1,0:T(8,128)(2,1)} %get-tuple-element.20), calls=%async_computation | async-start | bytes 524288 | tf_op jit(solution)/shard_map/all_to_all | solution.py:256
  20.8 17.2 %copy-start.5 = (bf16[256,512]{1,0:T(8,128)(2,1)S(1)}, bf16[256,512]{1,0:T(8,128)(2,1)}, u32[]{:S(2)}) copy-start(bf16[256,512]{1,0:T(8,128)(2,1)} %param.7) | copy-start | bytes 786436
  20.8 8.5 %collective-permute-start = (bf16[256,128]{1,0:T(8,128)(2,1)S(1)}, bf16[256,128]{1,0:T(8,128)(2,1)S(1)}, u32[]{:S(2)}, u32[]{:S(2)}) collective-permute-start(bf16[256,128]{1,0:T(8,128)(2,1)S(1)} %copy-done.8), channel_id=1, source_target_pairs={{0,8},{8,0},{16,24},{24,16},{1,9},{9,1},{17,25},{25,17},{2,10},{10... | collective-permute-start | bytes 196616 | tf_op jit(solution)/shard_map/ppermute | solution.py:250
  23.9 5.6 %collective-permute-start.1 = (bf16[256,128]{1,0:T(8,128)(2,1)S(1)}, bf16[256,128]{1,0:T(8,128)(2,1)S(1)}, u32[]{:S(2)}, u32[]{:S(2)}) collective-permute-start(bf16[256,128]{1,0:T(8,128)(2,1)S(1)} %copy-done.7), channel_id=1, source_target_pairs={{0,16},{8,24},{16,0},{24,8},{1,17},{9,25},{17,1},{25,9},{2,18},{10... | collective-permute-start | bytes 196616 | tf_op jit(solution)/shard_map/ppermute | solution.py:250
  27.1 6.2 %collective-permute-start.2 = (bf16[256,128]{1,0:T(8,128)(2,1)S(1)}, bf16[256,128]{1,0:T(8,128)(2,1)S(1)}, u32[]{:S(2)}, u32[]{:S(2)}) collective-permute-start(bf16[256,128]{1,0:T(8,128)(2,1)S(1)} %copy-done.6), channel_id=1, source_target_pairs={{0,24},{8,16},{16,8},{24,0},{1,25},{9,17},{17,9},{25,1},{2,26},{10... | collective-permute-start | bytes 196616 | tf_op jit(solution)/shard_map/ppermute | solution.py:250
  33.3 9.2 %copy-start.3 = (bf16[4,256,256]{2,1,0:T(8,128)(2,1)S(1)}, bf16[4,256,256]{2,1,0:T(8,128)(2,1)}, u32[]{:S(2)}) copy-start(bf16[4,256,256]{2,1,0:T(8,128)(2,1)} %constant.16.clone.table) | copy-start | bytes 1572868
  33.3 9.2 %collective-permute-start.3 = (bf16[768,128]{1,0:T(8,128)(2,1)S(1)}, bf16[768,128]{1,0:T(8,128)(2,1)S(1)}, u32[]{:S(2)}, u32[]{:S(2)}) collective-permute-start(bf16[768,128]{1,0:T(8,128)(2,1)S(1)} %get-tuple-element.25), channel_id=1, source_target_pairs={{0,32},{32,64},{64,96},{96,128},{128,160},{160,192},{192,224},{224... | collective-permute-start | bytes 589832 | tf_op jit(solution)/shard_map/ppermute | solution.py:245
  38.8 8.9 %all-to-all-start.1 = ((bf16[4,256,128]{2,1,0:T(8,128)(2,1)}), bf16[4,256,128]{2,1,0:T(8,128)(2,1)S(1)}, u32[]{:S(2)}, u32[]{:S(2)}) async-start(bf16[4,256,128]{2,1,0:T(8,128)(2,1)} %bitcast_bitcast_fusion), calls=%async_computation.1 | async-start | bytes 524288 | tf_op jit(solution)/shard_map/all_to_all | solution.py:256
  42.5 5.2 %copy-start.2 = (bf16[4,256,256]{2,1,0:T(8,128)(2,1)S(1)}, bf16[4,256,256]{2,1,0:T(8,128)(2,1)}, u32[]{:S(2)}) copy-start(bf16[4,256,256]{2,1,0:T(8,128)(2,1)} %constant.17.clone.back) | copy-start | bytes 1572868
  51.1 20.0 %collective-permute-start.4 = (bf16[768,128]{1,0:T(8,128)(2,1)S(1)}, bf16[768,128]{1,0:T(8,128)(2,1)S(1)}, u32[]{:S(2)}, u32[]{:S(2)}) collective-permute-start(bf16[768,128]{1,0:T(8,128)(2,1)S(1)} %get-tuple-element.28), channel_id=1, source_target_pairs={{32,0},{64,32},{96,64},{128,96},{160,128},{192,160},{224,192},{256... | collective-permute-start | bytes 589832 | tf_op jit(solution)/shard_map/ppermute | solution.py:245
  52.4 38.6 %all-to-all-start.2 = ((bf16[64,16,128]{2,1,0:T(8,128)(2,1)}), bf16[64,16,128]{2,1,0:T(8,128)(2,1)S(1)}, u32[]{:S(2)}, u32[]{:S(2)}) async-start(bf16[64,16,128]{2,1,0:T(8,128)(2,1)} %get-tuple-element.35), calls=%async_computation.2 | async-start | bytes 524288 | tf_op jit(solution)/shard_map/all_to_all | solution.py:256
  71.2 19.8 %copy-start = (bf16[256,512]{1,0:T(8,128)(2,1)S(1)}, bf16[256,512]{1,0:T(8,128)(2,1)}, u32[]{:S(2)}) copy-start(bf16[256,512]{1,0:T(8,128)(2,1)} %refs_5_.1) | copy-start | bytes 786436
  71.2 19.8 %copy-start.1 = (bf16[256,512]{1,0:T(8,128)(2,1)S(1)}, bf16[256,512]{1,0:T(8,128)(2,1)}, u32[]{:S(2)}) copy-start(bf16[256,512]{1,0:T(8,128)(2,1)} %refs_6_.1) | copy-start | bytes 786436
  74.3 7.9 %collective-permute-start.5 = (bf16[512,128]{1,0:T(8,128)(2,1)S(1)}, bf16[512,128]{1,0:T(8,128)(2,1)S(1)}, u32[]{:S(2)}, u32[]{:S(2)}) collective-permute-start(bf16[512,128]{1,0:T(8,128)(2,1)S(1)} %get-tuple-element.32), channel_id=1, source_target_pairs={{0,8},{8,0},{16,24},{24,16},{1,9},{9,1},{17,25},{25,17},{2,10},{10... | collective-permute-start | bytes 393224 | tf_op jit(solution)/shard_map/ppermute | solution.py:250
  76.7 7.6 %collective-permute-start.6 = (bf16[512,128]{1,0:T(8,128)(2,1)S(1)}, bf16[512,128]{1,0:T(8,128)(2,1)S(1)}, u32[]{:S(2)}, u32[]{:S(2)}) collective-permute-start(bf16[512,128]{1,0:T(8,128)(2,1)S(1)} %get-tuple-element.33), channel_id=1, source_target_pairs={{0,16},{8,24},{16,0},{24,8},{1,17},{9,25},{17,1},{25,9},{2,18},{10... | collective-permute-start | bytes 393224 | tf_op jit(solution)/shard_map/ppermute | solution.py:250
  79.9 8.2 %collective-permute-start.7 = (bf16[512,128]{1,0:T(8,128)(2,1)S(1)}, bf16[512,128]{1,0:T(8,128)(2,1)S(1)}, u32[]{:S(2)}, u32[]{:S(2)}) collective-permute-start(bf16[512,128]{1,0:T(8,128)(2,1)S(1)} %get-tuple-element.34), channel_id=1, source_target_pairs={{0,24},{8,16},{16,8},{24,0},{1,25},{9,17},{17,9},{25,1},{2,26},{10... | collective-permute-start | bytes 393224 | tf_op jit(solution)/shard_map/ppermute | solution.py:250

commit v11 on v10

--- a/solution.py
+++ b/solution.py
@@ -114,18 +114,29 @@
     return slice(index * BLOCK, (index + 1) * BLOCK)
 
 
-def prep_kernel(place, key, value, out_grad, *outs):
-    ships, pieces = outs[:BLOCKS], outs[BLOCKS]
-    for hop, ship in enumerate(ships):
+def at_hops(kept, near, far):
+    return [kept, near.at[0], far.at[0], far.at[1]]
+
+
+def out_hops(kept, near, far):
+    return [kept, near.at[0], far, near.at[1]]
+
+
+def prep_kernel(place, key, value, out_grad, kept, near, far, pieces):
+    for hop, ship in enumerate(out_hops(kept, near, far)):
         at = (slice(None), lanes_at(place[0] ^ hop))
         ship[...] = (key[at].astype(F32) * value[at].astype(F32)).astype(BF16)
     for piece in range(pieces.shape[0]):
         pieces[piece] = out_grad[:, piece * WIDE : (piece + 1) * WIDE]
 
 
-def join_kernel(place, *refs):
-    ships, (mixed, tail) = refs[:BLOCKS], refs[BLOCKS:]
-    for hop, ship in enumerate(ships):
+def pick_kernel(far, near, out):
+    out[0] = far[...]
+    out[1] = near[1]
+
+
+def join_kernel(place, kept, near, far, mixed, tail):
+    for hop, ship in enumerate(at_hops(kept, near, far)):
         mixed[rows_at(place[0] ^ hop), :] = ship[...]
     tail[...] = mixed[TOKENS - tail.shape[0] :, :]
 
@@ -170,8 +181,9 @@
         lag_grad[slot] = total[slot * share : slot * share + SLOT, :].astype(BF16)
 
 
-def back_kernel(scale, place, table, back, grad, halo, response, conv, *refs):
-    outs, (blocks,) = refs[:BLOCKS], refs[BLOCKS:]
+def back_kernel(
+    scale, place, table, back, grad, halo, response, conv, kept, near, far, blocks
+):
     reach = halo.shape[0] // BLOCK
     fill(blocks, grad, halo)
     for chunk in range(STEPS):
@@ -183,15 +195,26 @@
         part = dot(back[chunk], stacked(y))
         total = total + part if chunk else part
     blocks[:, :WIDE] = (total * scale).astype(BF16)
-    for hop, out in enumerate(outs):
+    for hop, out in enumerate(out_hops(kept, near, far)):
         out[:BLOCK, :] = conv[rows_at(place[0] ^ hop), :]
         out[BLOCK:, :] = blocks[:, lanes_at(place[0] ^ hop)]
 
 
-def final_kernel(place, *refs):
-    ships, refs = refs[:BLOCKS], refs[BLOCKS:]
-    cotangent, key, value, parts, gate_grad, key_grad, value_grad, lag_grad = refs
-    for hop, ship in enumerate(ships):
+def final_kernel(
+    place,
+    kept,
+    near,
+    far,
+    cotangent,
+    key,
+    value,
+    parts,
+    gate_grad,
+    key_grad,
+    value_grad,
+    lag_grad,
+):
+    for hop, ship in enumerate(at_hops(kept, near, far)):
         at = (slice(None), lanes_at(place[0] ^ hop))
         conv, back = ship[:BLOCK, :].astype(F32), ship[BLOCK:, :].astype(F32)
         gate_grad[at] = (cotangent[at].astype(F32) * conv).astype(BF16)
@@ -245,11 +268,18 @@
     return lax.ppermute(value, RUNS, [(i, i + steps) for i in range(first, last)])
 
 
-def swap(ships):
-    return [ships[0]] + [
-        lax.ppermute(ships[hop], GROUP, [(i, i ^ hop) for i in range(BLOCKS)])
-        for hop in range(1, BLOCKS)
-    ]
+def swap(kept, near, far):
+    def flip(value, axis):
+        return lax.ppermute(value, axis, [(0, 1), (1, 0)])
+
+    near = flip(near, "c")
+    far = call(
+        pick_kernel,
+        [whole(far.shape), whole(near.shape)],
+        whole(near.shape),
+        shaped(near.shape),
+    )(far, near)
+    return kept, near, flip(far, "yl")
 
 
 def exchange(value, axes):
@@ -264,6 +294,7 @@
     local = (BLOCK, WIDE)
     ship = (2 * BLOCK, LANES)
     pieces = (channels // WIDE, held, WIDE)
+    ships_pair = (2,) + ship
     flat = (TOKENS, LANES)
     reach = (lags, LANES)
     slots = (lags // share, SLOT, LANES)
@@ -272,21 +303,22 @@
 
     part = (BLOCK, LANES)
     by_block = (BLOCKS, BLOCK, LANES)
+    pair = (2,) + part
     *ships, cotangent = call(
         prep_kernel,
         [scalar] + [whole(local)] * 2 + [whole(out_grad.shape)],
-        [whole(part)] * BLOCKS + [whole(pieces)],
-        [shaped(part)] * BLOCKS + [shaped(pieces)],
+        [whole(part), whole(pair), whole(part), whole(pieces)],
+        [shaped(part), shaped(pair), shaped(part), shaped(pieces)],
         limit=PREP_LIMIT,
     )(place, key_input, value_input, out_grad)
     cotangent = exchange(cotangent, CH).reshape(local)
     mixed, tail = call(
         join_kernel,
-        [scalar] + [whole(part)] * BLOCKS,
+        [scalar, whole(part), whole(pair), whole(pair)],
         [whole(flat), whole(reach)],
         [shaped(flat), shaped(reach)],
         flops=JOIN_FLOPS,
-    )(place, *swap(ships))
+    )(place, *swap(*ships))
     mixed_halo = shift(tail, 1)
     grad = (cotangent.astype(F32) * gate_input.astype(F32)).astype(BF16)
     grad = exchange(grad.reshape(BLOCK, BLOCKS, LANES).transpose(1, 0, 2), GROUP).reshape(flat)
@@ -332,18 +364,20 @@
             whole(filt_bins),
             whole(flat),
         ],
-        [whole(ship)] * BLOCKS,
-        [shaped(ship)] * BLOCKS,
+        [whole(ship), whole(ships_pair), whole(ship)],
+        [shaped(ship), shaped(ships_pair), shaped(ship)],
         [seven],
         BACK_FLOPS,
     )(place, forward, inverse, grad, grad_halo, response, conv)
     gate_grad, key_grad, value_grad, filter_grad = call(
         final_kernel,
-        [scalar] + [whole(ship)] * BLOCKS + [whole(local)] * 3 + [whole(slots)],
+        [scalar, whole(ship), whole(ships_pair), whole(ships_pair)]
+        + [whole(local)] * 3
+        + [whole(slots)],
         [whole(local)] * 3 + [whole((share, WIDE))],
         [shaped(local)] * 3 + [shaped((share, WIDE), F32)],
         limit=FINAL_LIMIT,
-    )(place, *swap(ships), cotangent, key_input, value_input, lag_parts)
+    )(place, *swap(*ships), cotangent, key_input, value_input, lag_parts)
     return gate_grad, key_grad, value_grad, filter_grad
 
 

time: 92.8 us -> 92.7 us (level)
  waiting for transfers between devices: 14 us -> 16.7 us
  starting transfers between devices: 63 us -> 60.4 us
    ppermute x6 -> x4, starting transfers between devices: 16.3 us -> 11.9 us  [flip(): return lax.ppermute(value, axis, [(0, 1), (1, 0)])]
    ppermute x6 -> x4, waiting for transfers between devices: 9.77 us -> 12.7 us  [flip(): return lax.ppermute(value, axis, [(0, 1), (1, 0)])]
    all_to_all x3, starting transfers between devices: 40.7 us -> 42.2 us  [exchange(): return lax.all_to_all(value, axes, split_axis=0, concat_axis=0, tiled=True)]
  transfers between devices with their start and end apart: 11 -> 9, of which waited for: 6 -> 6; matrix products, arithmetic and copies ran while one was open for 1% -> 1% of each run, Pallas kernels for 8% -> 8%
where the time goes in v11:
time: 92.7 us; the launch traced here: 92.1 us
  starting transfers between devices  60.4 us (65%)
  waiting for transfers between devices  16.7 us (18%)
  Pallas kernels  13.4 us (14%)
    all_to_all x3, starting transfers between devices, exchange(): return lax.all_to_all(value, axes, split_axis=0, concat_axis=0, tiled=True)  42.2 us
    ppermute x4, waiting for transfers between devices, flip(): return lax.ppermute(value, axis, [(0, 1), (1, 0)])  12.7 us
    ppermute x4, starting transfers between devices, flip(): return lax.ppermute(value, axis, [(0, 1), (1, 0)])  11.9 us
    ppermute x2, starting transfers between devices, shift(): lax.ppermute(value, RUNS, [(i, i + steps) for i in range(first, last)])  6.24 us
    all_to_all x3, waiting for transfers between devices, exchange(): return lax.all_to_all(value, axes, split_axis=0, concat_axis=0, tiled=True)  4 us
    pallas_call x1, Pallas kernels, body(): call(functools.partial(conv_kernel, norm), [table, table, whole(reach), w...  3.91 us
    pallas_call x1, Pallas kernels, body(): call(functools.partial(cross_kernel, norm), [table, table, whole(flat), w...  3.43 us
    pallas_call x1, Pallas kernels, body(): call(functools.partial(back_kernel, norm), [scalar, table, table, whole(f...  3.03 us
  transfers between devices with their start and end apart: 9, of which 6 were waited for; matrix products, arithmetic and copies ran while one was open for 1% of the time, Pallas kernels for 8%

profile of v11, /device:TPU:1, one launch (start us, length us, event | category | flops | bytes accessed | tf_op | source)
XLA Modules:
  0.0 92.1 jit_solution(18262630578956665294)
XLA Ops:
  0.6 1.9 %shard_map.102 = (bf16[256,128]{1,0:T(8,128)(2,1)}, bf16[2,256,128]{2,1,0:T(8,128)(2,1)}, bf16[256,128]{1,0:T(8,128)(2,1)}, bf16[8,32,512]{2,1,0:T(8,128)(2,1)}) custom-call(s32[1]{0:T(128)} %bitcast.place, bf16[256,512]{1,0:T(8,128)(2,1)} %key.3, bf16[256,512]{1,0:T(8,128)(2,1)} %value.3, bf16[32,4096]{1,0:T(8,128)(2,1)} %out_grad.1), custom_call_target="tpu_custom_call" | custom-call | tf_op jit(solution)/shard_map/pallas_call | solution.py:307
  2.6 0.0 copy-start.7
  2.6 0.0 copy-start.5
  2.6 18.2 %all-to-all-start = ((bf16[8,32,512]{2,1,0:T(8,128)(2,1)}), bf16[8,32,512]{2,1,0:T(8,128)(2,1)S(1)}, u32[]{:S(2)}, u32[]{:S(2)}) async-start(bf16[8,32,512]{2,1,0:T(8,128)(2,1)} %get-tuple-element.18), calls=%async_computation | async-start | bytes 524288 | tf_op jit(solution)/shard_map/all_to_all | solution.py:286
  20.8 0.0 copy-done.7
  20.8 2.9 %collective-permute-start = (bf16[2,256,128]{2,1,0:T(8,128)(2,1)S(1)}, bf16[2,256,128]{2,1,0:T(8,128)(2,1)S(1)}, u32[]{:S(2)}, u32[]{:S(2)}) collective-permute-start(bf16[2,256,128]{2,1,0:T(8,128)(2,1)S(1)} %copy-done.7), channel_id=1, source_target_pairs={{0,8},{8,0},{1,9},{9,1},{2,10},{10,2},{3,11},{11,3},{4,12},{12,4},... | collective-permute-start | bytes 393224 | tf_op jit(solution)/shard_map/ppermute | solution.py:273
  23.7 1.0 %collective-permute-done.near = bf16[2,256,128]{2,1,0:T(8,128)(2,1)S(1)} collective-permute-done((bf16[2,256,128]{2,1,0:T(8,128)(2,1)S(1)}, bf16[2,256,128]{2,1,0:T(8,128)(2,1)S(1)}, u32[]{:S(2)}, u32[]{:S(2)}) %collective-permute-start) | collective-permute-done | bytes 131104 | tf_op jit(solution)/shard_map/ppermute | solution.py:273
  24.7 0.0 copy-done.5
  24.7 0.0 copy-start.4
  24.7 0.0 copy-start.6
  24.7 3.3 %collective-permute-start.1 = (bf16[2,256,128]{2,1,0:T(8,128)(2,1)S(1)}, bf16[2,256,128]{2,1,0:T(8,128)(2,1)S(1)}, u32[]{:S(2)}, u32[]{:S(2)}) collective-permute-start(bf16[2,256,128]{2,1,0:T(8,128)(2,1)S(1)} %shard_map.103), channel_id=1, source_target_pairs={{0,16},{16,0},{1,17},{17,1},{2,18},{18,2},{3,19},{19,3},{4,20},{20... | collective-permute-start | bytes 393224 | tf_op jit(solution)/shard_map/ppermute | solution.py:273
  28.0 3.4 %collective-permute-done.1.far = bf16[2,256,128]{2,1,0:T(8,128)(2,1)S(1)} collective-permute-done((bf16[2,256,128]{2,1,0:T(8,128)(2,1)S(1)}, bf16[2,256,128]{2,1,0:T(8,128)(2,1)S(1)}, u32[]{:S(2)}, u32[]{:S(2)}) %collective-permute-start.1) | collective-permute-done | bytes 131104 | tf_op jit(solution)/shard_map/ppermute | solution.py:273
  31.4 0.0 copy-done.4
  31.5 0.0 copy-start.3
  31.5 5.0 %collective-permute-start.2 = (bf16[768,128]{1,0:T(8,128)(2,1)S(1)}, bf16[768,128]{1,0:T(8,128)(2,1)S(1)}, u32[]{:S(2)}, u32[]{:S(2)}) collective-permute-start(bf16[768,128]{1,0:T(8,128)(2,1)S(1)} %get-tuple-element.22), channel_id=1, source_target_pairs={{0,32},{32,64},{64,96},{96,128},{128,160},{160,192},{192,224},{224... | collective-permute-start | bytes 589832 | tf_op jit(solution)/shard_map/ppermute | solution.py:268
  36.4 0.0 all-to-all-done
  36.5 0.0 copy-done.6
  36.5 0.8 bitcast_bitcast_fusion
  37.3 5.2 %all-to-all-start.1 = ((bf16[4,256,128]{2,1,0:T(8,128)(2,1)}), bf16[4,256,128]{2,1,0:T(8,128)(2,1)S(1)}, u32[]{:S(2)}, u32[]{:S(2)}) async-start(bf16[4,256,128]{2,1,0:T(8,128)(2,1)} %bitcast_bitcast_fusion), calls=%async_computation.1 | async-start | bytes 524288 | tf_op jit(solution)/shard_map/all_to_all | solution.py:286
  42.4 0.0 collective-permute-done.2.halo
  42.5 0.0 copy-done.3
  42.5 0.0 copy-start.2
  42.5 3.9 %shard_map.105 = (bf16[1024,128]{1,0:T(8,128)(2,1)S(1)}, bf16[4,256,512]{2,1,0:T(8,128)(2,1)}, bf16[4,256,128]{2,1,0:T(8,128)(2,1)S(1)}) custom-call(s32[1]{0:T(128)} %bitcast.place, bf16[4,256,256]{2,1,0:T(8,128)(2,1)S(1)} %copy-done.3, bf16[4,256,256]{2,1,0:T(8,128)(2,1)} %constant.17.clone.back, bf16[768,128]{1,0:T(8,128)(2,1)S(1)} %collective-permute-done.2.halo, ...), custom_call_target="tpu_custom_call" | custom-call | flops 24000000000 | tf_op jit(solution)/shard_map/pallas_call | solution.py:330
  46.4 1.2 %all-to-all-done.1 = bf16[4,256,128]{2,1,0:T(8,128)(2,1)S(1)} async-done(((bf16[4,256,128]{2,1,0:T(8,128)(2,1)}), bf16[4,256,128]{2,1,0:T(8,128)(2,1)S(1)}, u32[]{:S(2)}, u32[]{:S(2)}) %all-to-all-start.1) | async-done | bytes 262176 | tf_op jit(solution)/shard_map/all_to_all | solution.py:286
  47.6 0.0 copy-done.2
  47.6 3.4 %shard_map.106 = (bf16[768,128]{1,0:T(8,128)(2,1)S(1)}, bf16[64,16,128]{2,1,0:T(8,128)(2,1)}) custom-call(bf16[4,256,256]{2,1,0:T(8,128)(2,1)S(1)} %copy-done.3, bf16[4,256,256]{2,1,0:T(8,128)(2,1)S(1)} %copy-done.2, bf16[1024,128]{1,0:T(8,128)(2,1)S(1)} %bitcast.13, bf16[4,256,512]{2,1,0:T(8,128)(2,1)} %get-tuple-element.24.spectrum), custom_call_target="tpu_custom_call" | custom-call | tf_op jit(solution)/shard_map/pallas_call | solution.py:345
  51.1 1.3 %collective-permute-start.3 = (bf16[768,128]{1,0:T(8,128)(2,1)S(1)}, bf16[768,128]{1,0:T(8,128)(2,1)S(1)}, u32[]{:S(2)}, u32[]{:S(2)}) collective-permute-start(bf16[768,128]{1,0:T(8,128)(2,1)S(1)} %get-tuple-element.25), channel_id=1, source_target_pairs={{32,0},{64,32},{96,64},{128,96},{160,128},{192,160},{224,192},{256... | collective-permute-start | bytes 589832 | tf_op jit(solution)/shard_map/ppermute | solution.py:268
  52.3 18.8 %all-to-all-start.2 = ((bf16[64,16,128]{2,1,0:T(8,128)(2,1)}), bf16[64,16,128]{2,1,0:T(8,128)(2,1)S(1)}, u32[]{:S(2)}, u32[]{:S(2)}) async-start(bf16[64,16,128]{2,1,0:T(8,128)(2,1)} %get-tuple-element.31), calls=%async_computation.2 | async-start | bytes 524288 | tf_op jit(solution)/shard_map/all_to_all | solution.py:286
  71.2 0.0 collective-permute-done.3.halo
  71.2 3.0 %shard_map.107 = (bf16[512,128]{1,0:T(8,128)(2,1)S(1)}, bf16[2,512,128]{2,1,0:T(8,128)(2,1)S(1)}, bf16[512,128]{1,0:T(8,128)(2,1)S(1)}) custom-call(s32[1]{0:T(128)} %bitcast.place, bf16[4,256,256]{2,1,0:T(8,128)(2,1)} %constant.16.clone.table, bf16[4,256,256]{2,1,0:T(8,128)(2,1)} %constant.17.clone.back, bf16[1024,128]{1,0:T(8,128)(2,1)S(1)} %bitcast.14, ...), custom_call_target="tpu_custom_call" | custom-call | flops 35000000512 | tf_op jit(solution)/shard_map/pallas_call | solution.py:356
  74.2 2.4 %collective-permute-start.4 = (bf16[2,512,128]{2,1,0:T(8,128)(2,1)S(1)}, bf16[2,512,128]{2,1,0:T(8,128)(2,1)S(1)}, u32[]{:S(2)}, u32[]{:S(2)}) collective-permute-start(bf16[2,512,128]{2,1,0:T(8,128)(2,1)S(1)} %get-tuple-element.29), channel_id=1, source_target_pairs={{0,8},{8,0},{1,9},{9,1},{2,10},{10,2},{3,11},{11,3},{4,12},{12,4},... | collective-permute-start | bytes 786440 | tf_op jit(solution)/shard_map/ppermute | solution.py:273
  76.6 1.1 %collective-permute-done.4.near = bf16[2,512,128]{2,1,0:T(8,128)(2,1)S(1)} collective-permute-done((bf16[2,512,128]{2,1,0:T(8,128)(2,1)S(1)}, bf16[2,512,128]{2,1,0:T(8,128)(2,1)S(1)}, u32[]{:S(2)}, u32[]{:S(2)}) %collective-permute-start.4) | collective-permute-done | bytes 262176 | tf_op jit(solution)/shard_map/ppermute | solution.py:273
  77.7 0.0 copy-start
  77.7 0.0 copy-start.1
  77.8 3.3 %collective-permute-start.5 = (bf16[2,512,128]{2,1,0:T(8,128)(2,1)S(1)}, bf16[2,512,128]{2,1,0:T(8,128)(2,1)S(1)}, u32[]{:S(2)}, u32[]{:S(2)}) collective-permute-start(bf16[2,512,128]{2,1,0:T(8,128)(2,1)S(1)} %shard_map.108), channel_id=1, source_target_pairs={{0,16},{16,0},{1,17},{17,1},{2,18},{18,2},{3,19},{19,3},{4,20},{20... | collective-permute-start | bytes 786440 | tf_op jit(solution)/shard_map/ppermute | solution.py:273
  81.1 7.2 %collective-permute-done.5.far = bf16[2,512,128]{2,1,0:T(8,128)(2,1)S(1)} collective-permute-done((bf16[2,512,128]{2,1,0:T(8,128)(2,1)S(1)}, bf16[2,512,128]{2,1,0:T(8,128)(2,1)S(1)}, u32[]{:S(2)}, u32[]{:S(2)}) %collective-permute-start.5) | collective-permute-done | bytes 262176 | tf_op jit(solution)/shard_map/ppermute | solution.py:273
  88.3 2.7 %all-to-all-done.2.parts = bf16[64,16,128]{2,1,0:T(8,128)(2,1)S(1)} async-done(((bf16[64,16,128]{2,1,0:T(8,128)(2,1)}), bf16[64,16,128]{2,1,0:T(8,128)(2,1)S(1)}, u32[]{:S(2)}, u32[]{:S(2)}) %all-to-all-start.2) | async-done | bytes 262176 | tf_op jit(solution)/shard_map/all_to_all | solution.py:286
  91.0 0.0 copy-done
  91.0 0.0 copy-done.1
  91.0 1.1 %shard_map.109 = (bf16[256,512]{1,0:T(8,128)(2,1)}, bf16[256,512]{1,0:T(8,128)(2,1)}, bf16[256,512]{1,0:T(8,128)(2,1)}, f32[12,512]{1,0:T(8,128)}) custom-call(s32[1]{0:T(128)} %bitcast.place, bf16[512,128]{1,0:T(8,128)(2,1)S(1)} %get-tuple-element.28.kept, bf16[2,512,128]{2,1,0:T(8,128)(2,1)S(1)} %collective-permute-done.4.near, ...), custom_call_target="tpu_custom_call" | custom-call | tf_op jit(solution)/shard_map/pallas_call | solution.py:372
  (3 shorter events, 0.1 us)
Async XLA Ops:
  2.6 18.2 %copy-start.7 = (bf16[2,256,128]{2,1,0:T(8,128)(2,1)S(1)}, bf16[2,256,128]{2,1,0:T(8,128)(2,1)}, u32[]{:S(2)}) copy-start(bf16[2,256,128]{2,1,0:T(8,128)(2,1)} %get-tuple-element.20) | copy-start | bytes 393220
  2.6 22.1 %copy-start.5 = (bf16[256,128]{1,0:T(8,128)(2,1)S(1)}, bf16[256,128]{1,0:T(8,128)(2,1)}, u32[]{:S(2)}) copy-start(bf16[256,128]{1,0:T(8,128)(2,1)} %get-tuple-element.21.far) | copy-start | bytes 196612
  2.6 33.9 %all-to-all-start = ((bf16[8,32,512]{2,1,0:T(8,128)(2,1)}), bf16[8,32,512]{2,1,0:T(8,128)(2,1)S(1)}, u32[]{:S(2)}, u32[]{:S(2)}) async-start(bf16[8,32,512]{2,1,0:T(8,128)(2,1)} %get-tuple-element.18), calls=%async_computation | async-start | bytes 524288 | tf_op jit(solution)/shard_map/all_to_all | solution.py:286
  20.8 3.8 %collective-permute-start = (bf16[2,256,128]{2,1,0:T(8,128)(2,1)S(1)}, bf16[2,256,128]{2,1,0:T(8,128)(2,1)S(1)}, u32[]{:S(2)}, u32[]{:S(2)}) collective-permute-start(bf16[2,256,128]{2,1,0:T(8,128)(2,1)S(1)} %copy-done.7), channel_id=1, source_target_pairs={{0,8},{8,0},{1,9},{9,1},{2,10},{10,2},{3,11},{11,3},{4,12},{12,4},... | collective-permute-start | bytes 393224 | tf_op jit(solution)/shard_map/ppermute | solution.py:273
  24.7 6.8 %copy-start.4 = (bf16[256,128]{1,0:T(8,128)(2,1)S(1)}, bf16[256,128]{1,0:T(8,128)(2,1)}, u32[]{:S(2)}) copy-start(bf16[256,128]{1,0:T(8,128)(2,1)} %get-tuple-element.19.kept) | copy-start | bytes 196612
  24.7 11.8 %copy-start.6 = (bf16[256,512]{1,0:T(8,128)(2,1)S(1)}, bf16[256,512]{1,0:T(8,128)(2,1)}, u32[]{:S(2)}) copy-start(bf16[256,512]{1,0:T(8,128)(2,1)} %param.7) | copy-start | bytes 786436
  24.7 6.7 %collective-permute-start.1 = (bf16[2,256,128]{2,1,0:T(8,128)(2,1)S(1)}, bf16[2,256,128]{2,1,0:T(8,128)(2,1)S(1)}, u32[]{:S(2)}, u32[]{:S(2)}) collective-permute-start(bf16[2,256,128]{2,1,0:T(8,128)(2,1)S(1)} %shard_map.103), channel_id=1, source_target_pairs={{0,16},{16,0},{1,17},{17,1},{2,18},{18,2},{3,19},{19,3},{4,20},{20... | collective-permute-start | bytes 393224 | tf_op jit(solution)/shard_map/ppermute | solution.py:273
  31.5 11.0 %copy-start.3 = (bf16[4,256,256]{2,1,0:T(8,128)(2,1)S(1)}, bf16[4,256,256]{2,1,0:T(8,128)(2,1)}, u32[]{:S(2)}) copy-start(bf16[4,256,256]{2,1,0:T(8,128)(2,1)} %constant.16.clone.table) | copy-start | bytes 1572868
  31.5 11.0 %collective-permute-start.2 = (bf16[768,128]{1,0:T(8,128)(2,1)S(1)}, bf16[768,128]{1,0:T(8,128)(2,1)S(1)}, u32[]{:S(2)}, u32[]{:S(2)}) collective-permute-start(bf16[768,128]{1,0:T(8,128)(2,1)S(1)} %get-tuple-element.22), channel_id=1, source_target_pairs={{0,32},{32,64},{64,96},{96,128},{128,160},{160,192},{192,224},{224... | collective-permute-start | bytes 589832 | tf_op jit(solution)/shard_map/ppermute | solution.py:268
  37.3 10.4 %all-to-all-start.1 = ((bf16[4,256,128]{2,1,0:T(8,128)(2,1)}), bf16[4,256,128]{2,1,0:T(8,128)(2,1)S(1)}, u32[]{:S(2)}, u32[]{:S(2)}) async-start(bf16[4,256,128]{2,1,0:T(8,128)(2,1)} %bitcast_bitcast_fusion), calls=%async_computation.1 | async-start | bytes 524288 | tf_op jit(solution)/shard_map/all_to_all | solution.py:286
  42.5 5.2 %copy-start.2 = (bf16[4,256,256]{2,1,0:T(8,128)(2,1)S(1)}, bf16[4,256,256]{2,1,0:T(8,128)(2,1)}, u32[]{:S(2)}) copy-start(bf16[4,256,256]{2,1,0:T(8,128)(2,1)} %constant.17.clone.back) | copy-start | bytes 1572868
  51.1 20.1 %collective-permute-start.3 = (bf16[768,128]{1,0:T(8,128)(2,1)S(1)}, bf16[768,128]{1,0:T(8,128)(2,1)S(1)}, u32[]{:S(2)}, u32[]{:S(2)}) collective-permute-start(bf16[768,128]{1,0:T(8,128)(2,1)S(1)} %get-tuple-element.25), channel_id=1, source_target_pairs={{32,0},{64,32},{96,64},{128,96},{160,128},{192,160},{224,192},{256... | collective-permute-start | bytes 589832 | tf_op jit(solution)/shard_map/ppermute | solution.py:268
  52.3 38.7 %all-to-all-start.2 = ((bf16[64,16,128]{2,1,0:T(8,128)(2,1)}), bf16[64,16,128]{2,1,0:T(8,128)(2,1)S(1)}, u32[]{:S(2)}, u32[]{:S(2)}) async-start(bf16[64,16,128]{2,1,0:T(8,128)(2,1)} %get-tuple-element.31), calls=%async_computation.2 | async-start | bytes 524288 | tf_op jit(solution)/shard_map/all_to_all | solution.py:286
  74.2 3.5 %collective-permute-start.4 = (bf16[2,512,128]{2,1,0:T(8,128)(2,1)S(1)}, bf16[2,512,128]{2,1,0:T(8,128)(2,1)S(1)}, u32[]{:S(2)}, u32[]{:S(2)}) collective-permute-start(bf16[2,512,128]{2,1,0:T(8,128)(2,1)S(1)} %get-tuple-element.29), channel_id=1, source_target_pairs={{0,8},{8,0},{1,9},{9,1},{2,10},{10,2},{3,11},{11,3},{4,12},{12,4},... | collective-permute-start | bytes 786440 | tf_op jit(solution)/shard_map/ppermute | solution.py:273
  77.7 13.3 %copy-start = (bf16[256,512]{1,0:T(8,128)(2,1)S(1)}, bf16[256,512]{1,0:T(8,128)(2,1)}, u32[]{:S(2)}) copy-start(bf16[256,512]{1,0:T(8,128)(2,1)} %key.3) | copy-start | bytes 786436
  77.7 13.3 %copy-start.1 = (bf16[256,512]{1,0:T(8,128)(2,1)S(1)}, bf16[256,512]{1,0:T(8,128)(2,1)}, u32[]{:S(2)}) copy-start(bf16[256,512]{1,0:T(8,128)(2,1)} %value.3) | copy-start | bytes 786436
  77.8 10.5 %collective-permute-start.5 = (bf16[2,512,128]{2,1,0:T(8,128)(2,1)S(1)}, bf16[2,512,128]{2,1,0:T(8,128)(2,1)S(1)}, u32[]{:S(2)}, u32[]{:S(2)}) collective-permute-start(bf16[2,512,128]{2,1,0:T(8,128)(2,1)S(1)} %shard_map.108), channel_id=1, source_target_pairs={{0,16},{16,0},{1,17},{17,1},{2,18},{18,2},{3,19},{19,3},{4,20},{20... | collective-permute-start | bytes 786440 | tf_op jit(solution)/shard_map/ppermute | solution.py:273

commit v12 on v10

--- a/solution.py
+++ b/solution.py
@@ -114,49 +114,90 @@
     return slice(index * BLOCK, (index + 1) * BLOCK)
 
 
-def prep_kernel(place, key, value, out_grad, *outs):
-    ships, pieces = outs[:BLOCKS], outs[BLOCKS]
-    for hop, ship in enumerate(ships):
+def at_hops(kept, near, far):
+    return [kept, near.at[0], far.at[0], far.at[1]]
+
+
+def out_hops(kept, near, far):
+    return [kept, near.at[0], far, near.at[1]]
+
+
+def prep_kernel(place, key, value, out_grad, kept, near, far, pieces):
+    for hop, ship in enumerate(out_hops(kept, near, far)):
         at = (slice(None), lanes_at(place[0] ^ hop))
         ship[...] = (key[at].astype(F32) * value[at].astype(F32)).astype(BF16)
     for piece in range(pieces.shape[0]):
         pieces[piece] = out_grad[:, piece * WIDE : (piece + 1) * WIDE]
 
 
-def join_kernel(place, *refs):
-    ships, (mixed, tail) = refs[:BLOCKS], refs[BLOCKS:]
-    for hop, ship in enumerate(ships):
+def pick_kernel(far, near, out):
+    out[0] = far[...]
+    out[1] = near[1]
+
+
+def join_kernel(place, kept, near, far, mixed, tail):
+    for hop, ship in enumerate(at_hops(kept, near, far)):
         mixed[rows_at(place[0] ^ hop), :] = ship[...]
     tail[...] = mixed[TOKENS - tail.shape[0] :, :]
 
 
-def conv_kernel(scale, place, table, back, halo, mixed, taps, conv, spectrum, response, blocks, filt):
-    reach = taps.shape[0] // BLOCK
+def conv_kernel(
+    scale, place, table, back, halo, mixed, taps, conv, spectrum, response, blocks, filt, held, sems
+):
+    lags = halo.shape[0]
+    reach = lags // BLOCK
+    taps_copies = [
+        pltpu.make_async_copy(
+            taps.at[token_block(j), lanes_at(place[0])],
+            filt.at[:, lane_block(j)],
+            sems.at[STEPS + j],
+        )
+        for j in range(reach)
+    ]
+    for copy in taps_copies:
+        copy.start()
     fill(blocks, halo, mixed)
-    fill(filt, taps)
+    copies = []
     for chunk in range(STEPS):
+        specs = transform(table[chunk], blocks[...], chunk)
+        specs = [add(specs[b : b + reach + 1]) for b in range(BLOCKS)]
+        held[chunk] = stacked(specs)
+        copy = pltpu.make_async_copy(held.at[chunk], spectrum.at[chunk], sems.at[chunk])
+        copy.start()
+        copies.append(copy)
+        if chunk == 0:
+            for copy in taps_copies:
+                copy.wait()
         resp = add(transform(table[chunk], filt[...], chunk))
         response[chunk] = stacked([resp])
-        specs = transform(table[chunk], blocks[...], chunk)
-        specs = [add(specs[b : b + reach + 1]) for b in range(BLOCKS)]
-        spectrum[chunk] = stacked(specs)
         y = [turn(times(resp, spec), chunk, -(b + reach)) for b, spec in enumerate(specs)]
         part = dot(back[chunk], stacked(y))
         total = total + part if chunk else part
     for block in range(BLOCKS):
         conv[token_block(block), :] = (total[:, lane_block(block)] * scale).astype(BF16)
-
-
-def cross_kernel(scale, table, back, grad, spectrum, head, lag_grad, blocks, total):
+    for copy in copies:
+        copy.wait()
+
+
+def cross_kernel(
+    scale, table, back, grad, spectrum, head, lag_grad, blocks, total, arrived, sems
+):
+    copies = [
+        pltpu.make_async_copy(spectrum.at[chunk], arrived.at[chunk], sems.at[chunk])
+        for chunk in range(STEPS)
+    ]
+    for copy in copies:
+        copy.start()
     lags = head.shape[0]
     reach = lags // BLOCK
     head[...] = grad[:lags, :]
     fill(blocks, grad)
     for chunk in range(STEPS):
         specs = transform(table[chunk], blocks[...], chunk, reach)
+        copies[chunk].wait()
         terms = []
         for block, spec in enumerate(specs):
-            held = spectrum[chunk, :, lane_block(block)].astype(F32)
+            held = arrived[chunk, :, lane_block(block)].astype(F32)
             terms.append(times_conj(spec, (held[:BINS], held[BINS:])))
         term = add(terms)
         part = dot(back[chunk], stacked([turn(term, chunk, -j) for j in range(reach)]))
@@ -230,7 +271,7 @@
     )
 
 
-VMEM_LIMIT = 52 * MIB
+VMEM_LIMIT = 103 * MIB // 2
 FINAL_LIMIT = 16 * MIB
 PREP_LIMIT = 56 * MIB
 CONV_FLOPS = 24_000_000_000
@@ -245,7 +286,21 @@
     return lax.ppermute(value, RUNS, [(i, i + steps) for i in range(first, last)])
 
 
-def swap(ships):
+def swap(kept, near, far):
+    def flip(value, axis):
+        return lax.ppermute(value, axis, [(0, 1), (1, 0)])
+
+    near = flip(near, "c")
+    far = call(
+        pick_kernel,
+        [whole(far.shape), whole(near.shape)],
+        whole(near.shape),
+        shaped(near.shape),
+    )(far, near)
+    return kept, near, flip(far, "yl")
+
+
+def swap_direct(ships):
     return [ships[0]] + [
         lax.ppermute(ships[hop], GROUP, [(i, i ^ hop) for i in range(BLOCKS)])
         for hop in range(1, BLOCKS)
@@ -268,25 +323,27 @@
     reach = (lags, LANES)
     slots = (lags // share, SLOT, LANES)
     scalar = pl.BlockSpec(memory_space=pltpu.SMEM)
+    anywhere = pl.BlockSpec(memory_space=pl.ANY)
     place = lax.axis_index(GROUP).reshape(1)
 
     part = (BLOCK, LANES)
     by_block = (BLOCKS, BLOCK, LANES)
+    pair = (2,) + part
     *ships, cotangent = call(
         prep_kernel,
         [scalar] + [whole(local)] * 2 + [whole(out_grad.shape)],
-        [whole(part)] * BLOCKS + [whole(pieces)],
-        [shaped(part)] * BLOCKS + [shaped(pieces)],
+        [whole(part), whole(pair), whole(part), whole(pieces)],
+        [shaped(part), shaped(pair), shaped(part), shaped(pieces)],
         limit=PREP_LIMIT,
     )(place, key_input, value_input, out_grad)
     cotangent = exchange(cotangent, CH).reshape(local)
     mixed, tail = call(
         join_kernel,
-        [scalar] + [whole(part)] * BLOCKS,
+        [scalar, whole(part), whole(pair), whole(pair)],
         [whole(flat), whole(reach)],
         [shaped(flat), shaped(reach)],
         flops=JOIN_FLOPS,
-    )(place, *swap(ships))
+    )(place, *swap(*ships))
     mixed_halo = shift(tail, 1)
     grad = (cotangent.astype(F32) * gate_input.astype(F32)).astype(BF16)
     grad = exchange(grad.reshape(BLOCK, BLOCKS, LANES).transpose(1, 0, 2), GROUP).reshape(flat)
@@ -302,20 +359,30 @@
             table,
             whole(reach),
             whole(flat),
-            pl.BlockSpec(reach, lambda step, place: (0, place[0])),
+            anywhere,
         ],
-        [whole(flat), whole(by_bins), whole(filt_bins)],
+        [whole(flat), anywhere, whole(filt_bins)],
         [shaped(flat), shaped(by_bins), shaped(filt_bins)],
-        [seven, pltpu.VMEM((BLOCK, lags // BLOCK * LANES), BF16)],
+        [
+            seven,
+            pltpu.VMEM((BLOCK, lags // BLOCK * LANES), BF16),
+            pltpu.VMEM(by_bins, BF16),
+            pltpu.SemaphoreType.DMA((STEPS + lags // BLOCK,)),
+        ],
         CONV_FLOPS,
         scalars=1,
     )(place, forward, inverse, mixed_halo, mixed, filter_taps)
     head, lag_grad = call(
         functools.partial(cross_kernel, norm),
-        [table, table, whole(flat), whole(by_bins)],
+        [table, table, whole(flat), anywhere],
         [whole(reach), whole(slots)],
         [shaped(reach), shaped(slots)],
-        [pltpu.VMEM(local, BF16), pltpu.VMEM((lags + SLOT, LANES), F32)],
+        [
+            pltpu.VMEM(local, BF16),
+            pltpu.VMEM((lags + SLOT, LANES), F32),
+            pltpu.VMEM(by_bins, BF16),
+            pltpu.SemaphoreType.DMA((STEPS,)),
+        ],
         CROSS_FLOPS,
     )(forward, inverse, grad, spectrum)
     grad_halo = shift(head, -1)
@@ -343,7 +410,7 @@
         [whole(local)] * 3 + [whole((share, WIDE))],
         [shaped(local)] * 3 + [shaped((share, WIDE), F32)],
         limit=FINAL_LIMIT,
-    )(place, *swap(ships), cotangent, key_input, value_input, lag_parts)
+    )(place, *swap_direct(ships), cotangent, key_input, value_input, lag_parts)
     return gate_grad, key_grad, value_grad, filter_grad
 
 

time: 92.8 us -> 92.6 us (level)
  waiting for transfers between devices: 14 us -> 15.2 us
    ppermute x6 -> x5, starting transfers between devices: 16.3 us -> 14.1 us  [the longest x3 7.87 us: swap_direct(): lax.ppermute(ships[hop], GROUP, [(i, i ^ hop) for i in range(BLOCKS)])]
    all_to_all x3, starting transfers between devices: 40.7 us -> 42.2 us  [exchange(): return lax.all_to_all(value, axes, split_axis=0, concat_axis=0, tiled=True)]
    ppermute x6 -> x5, waiting for transfers between devices: 9.77 us -> 10.2 us  [the longest x3 5.86 us: swap_direct(): lax.ppermute(ships[hop], GROUP, [(i, i ^ hop) for i in range(BLOCKS)])]
    pallas_call x2 -> x3, Pallas kernels: 3.46 us -> 3.36 us  [the longest x1 3.32 us: body(): call(functools.partial(cross_kernel, norm), [table, table, whole(flat), a...]
  transfers between devices with their start and end apart: 11 -> 10, of which waited for: 6 -> 6; matrix products, arithmetic and copies ran while one was open for 1% -> 1% of each run, Pallas kernels for 8% -> 7%
where the time goes in v12:
time: 92.6 us; the launch traced here: 92 us
  starting transfers between devices  62.6 us (68%)
  waiting for transfers between devices  15.2 us (16%)
  Pallas kernels  12.5 us (13%)
    all_to_all x3, starting transfers between devices, exchange(): return lax.all_to_all(value, axes, split_axis=0, concat_axis=0, tiled=True)  42.2 us
    ppermute x3, starting transfers between devices, swap_direct(): lax.ppermute(ships[hop], GROUP, [(i, i ^ hop) for i in range(BLOCKS)])  7.87 us
    ppermute x2, starting transfers between devices, shift(): lax.ppermute(value, RUNS, [(i, i + steps) for i in range(first, last)])  6.25 us
    ppermute x2, starting transfers between devices, flip(): return lax.ppermute(value, axis, [(0, 1), (1, 0)])  6.2 us
    ppermute x3, waiting for transfers between devices, swap_direct(): lax.ppermute(ships[hop], GROUP, [(i, i ^ hop) for i in range(BLOCKS)])  5.86 us
    all_to_all x3, waiting for transfers between devices, exchange(): return lax.all_to_all(value, axes, split_axis=0, concat_axis=0, tiled=True)  5.01 us
    ppermute x2, waiting for transfers between devices, flip(): return lax.ppermute(value, axis, [(0, 1), (1, 0)])  4.37 us
    pallas_call x1, Pallas kernels, body(): call(functools.partial(cross_kernel, norm), [table, table, whole(flat), a...  3.32 us
  transfers between devices with their start and end apart: 10, of which 6 were waited for; matrix products, arithmetic and copies ran while one was open for 1% of the time, Pallas kernels for 7%

profile of v12, /device:TPU:1, one launch (start us, length us, event | category | flops | bytes accessed | tf_op | source)
XLA Modules:
  0.0 92.0 jit_solution(1706621547280950236)
XLA Ops:
  0.6 1.9 %shard_map.102 = (bf16[256,128]{1,0:T(8,128)(2,1)}, bf16[2,256,128]{2,1,0:T(8,128)(2,1)}, bf16[256,128]{1,0:T(8,128)(2,1)}, bf16[8,32,512]{2,1,0:T(8,128)(2,1)}) custom-call(s32[1]{0:T(128)} %bitcast.place, bf16[256,512]{1,0:T(8,128)(2,1)} %refs_5_.1, bf16[256,512]{1,0:T(8,128)(2,1)} %refs_6_.1, bf16[32,4096]{1,0:T(8,128)(2,1)} %out_grad.1), custom_call_target="tpu_custom_call" | custom-call | tf_op jit(solution)/shard_map/pallas_call | solution.py:332
  2.6 0.0 copy-start.7
  2.6 0.0 copy-start.5
  2.6 18.2 %all-to-all-start = ((bf16[8,32,512]{2,1,0:T(8,128)(2,1)}), bf16[8,32,512]{2,1,0:T(8,128)(2,1)S(1)}, u32[]{:S(2)}, u32[]{:S(2)}) async-start(bf16[8,32,512]{2,1,0:T(8,128)(2,1)} %get-tuple-element.19), calls=%async_computation | async-start | bytes 524288 | tf_op jit(solution)/shard_map/all_to_all | solution.py:311
  20.8 0.0 copy-done.7
  20.8 2.9 %collective-permute-start = (bf16[2,256,128]{2,1,0:T(8,128)(2,1)S(1)}, bf16[2,256,128]{2,1,0:T(8,128)(2,1)S(1)}, u32[]{:S(2)}, u32[]{:S(2)}) collective-permute-start(bf16[2,256,128]{2,1,0:T(8,128)(2,1)S(1)} %copy-done.7), channel_id=1, source_target_pairs={{0,8},{8,0},{1,9},{9,1},{2,10},{10,2},{3,11},{11,3},{4,12},{12,4},... | collective-permute-start | bytes 393224 | tf_op jit(solution)/shard_map/ppermute | solution.py:291
  23.7 1.0 %collective-permute-done.near = bf16[2,256,128]{2,1,0:T(8,128)(2,1)S(1)} collective-permute-done((bf16[2,256,128]{2,1,0:T(8,128)(2,1)S(1)}, bf16[2,256,128]{2,1,0:T(8,128)(2,1)S(1)}, u32[]{:S(2)}, u32[]{:S(2)}) %collective-permute-start) | collective-permute-done | bytes 131104 | tf_op jit(solution)/shard_map/ppermute | solution.py:291
  24.7 0.0 copy-done.5
  24.7 0.0 copy-start.4
  24.7 0.0 copy-start.6
  24.7 3.3 %collective-permute-start.1 = (bf16[2,256,128]{2,1,0:T(8,128)(2,1)S(1)}, bf16[2,256,128]{2,1,0:T(8,128)(2,1)S(1)}, u32[]{:S(2)}, u32[]{:S(2)}) collective-permute-start(bf16[2,256,128]{2,1,0:T(8,128)(2,1)S(1)} %shard_map.103), channel_id=1, source_target_pairs={{0,16},{16,0},{1,17},{17,1},{2,18},{18,2},{3,19},{19,3},{4,20},{20... | collective-permute-start | bytes 393224 | tf_op jit(solution)/shard_map/ppermute | solution.py:291
  28.0 3.4 %collective-permute-done.1.far = bf16[2,256,128]{2,1,0:T(8,128)(2,1)S(1)} collective-permute-done((bf16[2,256,128]{2,1,0:T(8,128)(2,1)S(1)}, bf16[2,256,128]{2,1,0:T(8,128)(2,1)S(1)}, u32[]{:S(2)}, u32[]{:S(2)}) %collective-permute-start.1) | collective-permute-done | bytes 131104 | tf_op jit(solution)/shard_map/ppermute | solution.py:291
  31.4 0.0 copy-done.4
  31.5 0.0 copy-start.2
  31.5 0.0 copy-start.3
  31.5 5.0 %collective-permute-start.2 = (bf16[768,128]{1,0:T(8,128)(2,1)S(1)}, bf16[768,128]{1,0:T(8,128)(2,1)S(1)}, u32[]{:S(2)}, u32[]{:S(2)}) collective-permute-start(bf16[768,128]{1,0:T(8,128)(2,1)S(1)} %get-tuple-element.23), channel_id=1, source_target_pairs={{0,32},{32,64},{64,96},{96,128},{128,160},{160,192},{192,224},{224... | collective-permute-start | bytes 589832 | tf_op jit(solution)/shard_map/ppermute | solution.py:286
  36.5 0.0 all-to-all-done
  36.5 0.0 copy-done.6
  36.5 0.8 bitcast_bitcast_fusion
  37.3 5.2 %all-to-all-start.1 = ((bf16[4,256,128]{2,1,0:T(8,128)(2,1)}), bf16[4,256,128]{2,1,0:T(8,128)(2,1)S(1)}, u32[]{:S(2)}, u32[]{:S(2)}) async-start(bf16[4,256,128]{2,1,0:T(8,128)(2,1)} %bitcast_bitcast_fusion), calls=%async_computation.1 | async-start | bytes 524288 | tf_op jit(solution)/shard_map/all_to_all | solution.py:311
  42.4 0.0 collective-permute-done.2.halo
  42.4 0.0 copy-done.2
  42.5 0.0 copy-done.3
  42.5 3.3 %shard_map.105 = (bf16[1024,128]{1,0:T(8,128)(2,1)S(1)}, bf16[4,256,512]{2,1,0:T(8,128)(2,1)}, bf16[4,256,128]{2,1,0:T(8,128)(2,1)S(1)}) custom-call(s32[1]{0:T(128)} %bitcast.place, bf16[4,256,256]{2,1,0:T(8,128)(2,1)S(1)} %copy-done.3, bf16[4,256,256]{2,1,0:T(8,128)(2,1)S(1)} %copy-done.2, bf16[768,128]{1,0:T(8,128)(2,1)S(1)} %collective-permute-done.2.halo, ...), custom_call_target="tpu_custom_call" | custom-call | flops 24000000000 | tf_op jit(solution)/shard_map/pallas_call | solution.py:355
  45.7 1.9 %all-to-all-done.1 = bf16[4,256,128]{2,1,0:T(8,128)(2,1)S(1)} async-done(((bf16[4,256,128]{2,1,0:T(8,128)(2,1)}), bf16[4,256,128]{2,1,0:T(8,128)(2,1)S(1)}, u32[]{:S(2)}, u32[]{:S(2)}) %all-to-all-start.1) | async-done | bytes 262176 | tf_op jit(solution)/shard_map/all_to_all | solution.py:311
  47.6 3.3 %shard_map.106 = (bf16[768,128]{1,0:T(8,128)(2,1)S(1)}, bf16[64,16,128]{2,1,0:T(8,128)(2,1)}) custom-call(bf16[4,256,256]{2,1,0:T(8,128)(2,1)S(1)} %copy-done.3, bf16[4,256,256]{2,1,0:T(8,128)(2,1)S(1)} %copy-done.2, bf16[1024,128]{1,0:T(8,128)(2,1)S(1)} %bitcast.13, bf16[4,256,512]{2,1,0:T(8,128)(2,1)} %get-tuple-element.25.spectrum), custom_call_target="tpu_custom_call" | custom-call | tf_op jit(solution)/shard_map/pallas_call | solution.py:375
  50.9 1.3 %collective-permute-start.3 = (bf16[768,128]{1,0:T(8,128)(2,1)S(1)}, bf16[768,128]{1,0:T(8,128)(2,1)S(1)}, u32[]{:S(2)}, u32[]{:S(2)}) collective-permute-start(bf16[768,128]{1,0:T(8,128)(2,1)S(1)} %get-tuple-element.26), channel_id=1, source_target_pairs={{32,0},{64,32},{96,64},{128,96},{160,128},{192,160},{224,192},{256... | collective-permute-start | bytes 589832 | tf_op jit(solution)/shard_map/ppermute | solution.py:286
  52.2 18.8 %all-to-all-start.2 = ((bf16[64,16,128]{2,1,0:T(8,128)(2,1)}), bf16[64,16,128]{2,1,0:T(8,128)(2,1)S(1)}, u32[]{:S(2)}, u32[]{:S(2)}) async-start(bf16[64,16,128]{2,1,0:T(8,128)(2,1)} %get-tuple-element.33), calls=%async_computation.2 | async-start | bytes 524288 | tf_op jit(solution)/shard_map/all_to_all | solution.py:311
  71.1 0.0 collective-permute-done.3.halo
  71.1 0.0 copy-start
  71.1 0.0 copy-start.1
  71.1 2.9 %shard_map.107 = (bf16[512,128]{1,0:T(8,128)(2,1)S(1)}, bf16[512,128]{1,0:T(8,128)(2,1)S(1)}, bf16[512,128]{1,0:T(8,128)(2,1)S(1)}, bf16[512,128]{1,0:T(8,128)(2,1)S(1)}) custom-call(s32[1]{0:T(128)} %bitcast.place, bf16[4,256,256]{2,1,0:T(8,128)(2,1)S(1)} %copy-done.3, bf16[4,256,256]{2,1,0:T(8,128)(2,1)} %constant.17.clone.back, ...), custom_call_target="tpu_custom_call" | custom-call | flops 35000000512 | tf_op jit(solution)/shard_map/pallas_call | solution.py:391
  74.0 2.4 %collective-permute-start.4 = (bf16[512,128]{1,0:T(8,128)(2,1)S(1)}, bf16[512,128]{1,0:T(8,128)(2,1)S(1)}, u32[]{:S(2)}, u32[]{:S(2)}) collective-permute-start(bf16[512,128]{1,0:T(8,128)(2,1)S(1)} %get-tuple-element.30), channel_id=1, source_target_pairs={{0,8},{8,0},{16,24},{24,16},{1,9},{9,1},{17,25},{25,17},{2,10},{10... | collective-permute-start | bytes 393224 | tf_op jit(solution)/shard_map/ppermute | solution.py:305
  76.4 3.2 %collective-permute-start.5 = (bf16[512,128]{1,0:T(8,128)(2,1)S(1)}, bf16[512,128]{1,0:T(8,128)(2,1)S(1)}, u32[]{:S(2)}, u32[]{:S(2)}) collective-permute-start(bf16[512,128]{1,0:T(8,128)(2,1)S(1)} %get-tuple-element.31), channel_id=1, source_target_pairs={{0,16},{8,24},{16,0},{24,8},{1,17},{9,25},{17,1},{25,9},{2,18},{10... | collective-permute-start | bytes 393224 | tf_op jit(solution)/shard_map/ppermute | solution.py:305
  79.6 2.3 %collective-permute-start.6 = (bf16[512,128]{1,0:T(8,128)(2,1)S(1)}, bf16[512,128]{1,0:T(8,128)(2,1)S(1)}, u32[]{:S(2)}, u32[]{:S(2)}) collective-permute-start(bf16[512,128]{1,0:T(8,128)(2,1)S(1)} %get-tuple-element.32), channel_id=1, source_target_pairs={{0,24},{8,16},{16,8},{24,0},{1,25},{9,17},{17,9},{25,1},{2,26},{10... | collective-permute-start | bytes 393224 | tf_op jit(solution)/shard_map/ppermute | solution.py:305
  81.9 0.0 collective-permute-done.4.refs_1_
  81.9 2.1 %collective-permute-done.5.refs_2_ = bf16[512,128]{1,0:T(8,128)(2,1)S(1)} collective-permute-done((bf16[512,128]{1,0:T(8,128)(2,1)S(1)}, bf16[512,128]{1,0:T(8,128)(2,1)S(1)}, u32[]{:S(2)}, u32[]{:S(2)}) %collective-permute-start.5) | collective-permute-done | bytes 131104 | tf_op jit(solution)/shard_map/ppermute | solution.py:305
  84.0 3.8 %collective-permute-done.6.refs_3_ = bf16[512,128]{1,0:T(8,128)(2,1)S(1)} collective-permute-done((bf16[512,128]{1,0:T(8,128)(2,1)S(1)}, bf16[512,128]{1,0:T(8,128)(2,1)S(1)}, u32[]{:S(2)}, u32[]{:S(2)}) %collective-permute-start.6) | collective-permute-done | bytes 131104 | tf_op jit(solution)/shard_map/ppermute | solution.py:305
  87.8 3.1 %all-to-all-done.2.refs_7_ = bf16[64,16,128]{2,1,0:T(8,128)(2,1)S(1)} async-done(((bf16[64,16,128]{2,1,0:T(8,128)(2,1)}), bf16[64,16,128]{2,1,0:T(8,128)(2,1)S(1)}, u32[]{:S(2)}, u32[]{:S(2)}) %all-to-all-start.2) | async-done | bytes 262176 | tf_op jit(solution)/shard_map/all_to_all | solution.py:311
  90.9 0.0 copy-done
  90.9 0.0 copy-done.1
  90.9 1.1 %shard_map.108 = (bf16[256,512]{1,0:T(8,128)(2,1)}, bf16[256,512]{1,0:T(8,128)(2,1)}, bf16[256,512]{1,0:T(8,128)(2,1)}, f32[12,512]{1,0:T(8,128)}) custom-call(s32[1]{0:T(128)} %bitcast.place, bf16[512,128]{1,0:T(8,128)(2,1)S(1)} %get-tuple-element.29.refs_0_, bf16[512,128]{1,0:T(8,128)(2,1)S(1)} %collective-permute-done.4.refs_1_, ...), custom_call_target="tpu_custom_call" | custom-call | tf_op jit(solution)/shard_map/pallas_call | solution.py:407
  (2 shorter events, 0.0 us)
Async XLA Ops:
  2.6 18.2 %copy-start.7 = (bf16[2,256,128]{2,1,0:T(8,128)(2,1)S(1)}, bf16[2,256,128]{2,1,0:T(8,128)(2,1)}, u32[]{:S(2)}) copy-start(bf16[2,256,128]{2,1,0:T(8,128)(2,1)} %get-tuple-element.21) | copy-start | bytes 393220
  2.6 22.1 %copy-start.5 = (bf16[256,128]{1,0:T(8,128)(2,1)S(1)}, bf16[256,128]{1,0:T(8,128)(2,1)}, u32[]{:S(2)}) copy-start(bf16[256,128]{1,0:T(8,128)(2,1)} %get-tuple-element.22.far) | copy-start | bytes 196612
  2.6 33.9 %all-to-all-start = ((bf16[8,32,512]{2,1,0:T(8,128)(2,1)}), bf16[8,32,512]{2,1,0:T(8,128)(2,1)S(1)}, u32[]{:S(2)}, u32[]{:S(2)}) async-start(bf16[8,32,512]{2,1,0:T(8,128)(2,1)} %get-tuple-element.19), calls=%async_computation | async-start | bytes 524288 | tf_op jit(solution)/shard_map/all_to_all | solution.py:311
  20.8 3.8 %collective-permute-start = (bf16[2,256,128]{2,1,0:T(8,128)(2,1)S(1)}, bf16[2,256,128]{2,1,0:T(8,128)(2,1)S(1)}, u32[]{:S(2)}, u32[]{:S(2)}) collective-permute-start(bf16[2,256,128]{2,1,0:T(8,128)(2,1)S(1)} %copy-done.7), channel_id=1, source_target_pairs={{0,8},{8,0},{1,9},{9,1},{2,10},{10,2},{3,11},{11,3},{4,12},{12,4},... | collective-permute-start | bytes 393224 | tf_op jit(solution)/shard_map/ppermute | solution.py:291
  24.7 6.8 %copy-start.4 = (bf16[256,128]{1,0:T(8,128)(2,1)S(1)}, bf16[256,128]{1,0:T(8,128)(2,1)}, u32[]{:S(2)}) copy-start(bf16[256,128]{1,0:T(8,128)(2,1)} %get-tuple-element.20.kept) | copy-start | bytes 196612
  24.7 11.8 %copy-start.6 = (bf16[256,512]{1,0:T(8,128)(2,1)S(1)}, bf16[256,512]{1,0:T(8,128)(2,1)}, u32[]{:S(2)}) copy-start(bf16[256,512]{1,0:T(8,128)(2,1)} %param.7) | copy-start | bytes 786436
  24.7 6.7 %collective-permute-start.1 = (bf16[2,256,128]{2,1,0:T(8,128)(2,1)S(1)}, bf16[2,256,128]{2,1,0:T(8,128)(2,1)S(1)}, u32[]{:S(2)}, u32[]{:S(2)}) collective-permute-start(bf16[2,256,128]{2,1,0:T(8,128)(2,1)S(1)} %shard_map.103), channel_id=1, source_target_pairs={{0,16},{16,0},{1,17},{17,1},{2,18},{18,2},{3,19},{19,3},{4,20},{20... | collective-permute-start | bytes 393224 | tf_op jit(solution)/shard_map/ppermute | solution.py:291
  31.5 11.0 %copy-start.2 = (bf16[4,256,256]{2,1,0:T(8,128)(2,1)S(1)}, bf16[4,256,256]{2,1,0:T(8,128)(2,1)}, u32[]{:S(2)}) copy-start(bf16[4,256,256]{2,1,0:T(8,128)(2,1)} %constant.17.clone.back) | copy-start | bytes 1572868
  31.5 11.0 %copy-start.3 = (bf16[4,256,256]{2,1,0:T(8,128)(2,1)S(1)}, bf16[4,256,256]{2,1,0:T(8,128)(2,1)}, u32[]{:S(2)}) copy-start(bf16[4,256,256]{2,1,0:T(8,128)(2,1)} %constant.16.clone.table) | copy-start | bytes 1572868
  31.5 11.0 %collective-permute-start.2 = (bf16[768,128]{1,0:T(8,128)(2,1)S(1)}, bf16[768,128]{1,0:T(8,128)(2,1)S(1)}, u32[]{:S(2)}, u32[]{:S(2)}) collective-permute-start(bf16[768,128]{1,0:T(8,128)(2,1)S(1)} %get-tuple-element.23), channel_id=1, source_target_pairs={{0,32},{32,64},{64,96},{96,128},{128,160},{160,192},{192,224},{224... | collective-permute-start | bytes 589832 | tf_op jit(solution)/shard_map/ppermute | solution.py:286
  37.3 10.3 %all-to-all-start.1 = ((bf16[4,256,128]{2,1,0:T(8,128)(2,1)}), bf16[4,256,128]{2,1,0:T(8,128)(2,1)S(1)}, u32[]{:S(2)}, u32[]{:S(2)}) async-start(bf16[4,256,128]{2,1,0:T(8,128)(2,1)} %bitcast_bitcast_fusion), calls=%async_computation.1 | async-start | bytes 524288 | tf_op jit(solution)/shard_map/all_to_all | solution.py:311
  50.9 20.1 %collective-permute-start.3 = (bf16[768,128]{1,0:T(8,128)(2,1)S(1)}, bf16[768,128]{1,0:T(8,128)(2,1)S(1)}, u32[]{:S(2)}, u32[]{:S(2)}) collective-permute-start(bf16[768,128]{1,0:T(8,128)(2,1)S(1)} %get-tuple-element.26), channel_id=1, source_target_pairs={{32,0},{64,32},{96,64},{128,96},{160,128},{192,160},{224,192},{256... | collective-permute-start | bytes 589832 | tf_op jit(solution)/shard_map/ppermute | solution.py:286
  52.2 38.7 %all-to-all-start.2 = ((bf16[64,16,128]{2,1,0:T(8,128)(2,1)}), bf16[64,16,128]{2,1,0:T(8,128)(2,1)S(1)}, u32[]{:S(2)}, u32[]{:S(2)}) async-start(bf16[64,16,128]{2,1,0:T(8,128)(2,1)} %get-tuple-element.33), calls=%async_computation.2 | async-start | bytes 524288 | tf_op jit(solution)/shard_map/all_to_all | solution.py:311
  71.1 19.8 %copy-start = (bf16[256,512]{1,0:T(8,128)(2,1)S(1)}, bf16[256,512]{1,0:T(8,128)(2,1)}, u32[]{:S(2)}) copy-start(bf16[256,512]{1,0:T(8,128)(2,1)} %refs_5_.1) | copy-start | bytes 786436
  71.1 19.8 %copy-start.1 = (bf16[256,512]{1,0:T(8,128)(2,1)S(1)}, bf16[256,512]{1,0:T(8,128)(2,1)}, u32[]{:S(2)}) copy-start(bf16[256,512]{1,0:T(8,128)(2,1)} %refs_6_.1) | copy-start | bytes 786436
  74.0 7.9 %collective-permute-start.4 = (bf16[512,128]{1,0:T(8,128)(2,1)S(1)}, bf16[512,128]{1,0:T(8,128)(2,1)S(1)}, u32[]{:S(2)}, u32[]{:S(2)}) collective-permute-start(bf16[512,128]{1,0:T(8,128)(2,1)S(1)} %get-tuple-element.30), channel_id=1, source_target_pairs={{0,8},{8,0},{16,24},{24,16},{1,9},{9,1},{17,25},{25,17},{2,10},{10... | collective-permute-start | bytes 393224 | tf_op jit(solution)/shard_map/ppermute | solution.py:305
  76.4 7.6 %collective-permute-start.5 = (bf16[512,128]{1,0:T(8,128)(2,1)S(1)}, bf16[512,128]{1,0:T(8,128)(2,1)S(1)}, u32[]{:S(2)}, u32[]{:S(2)}) collective-permute-start(bf16[512,128]{1,0:T(8,128)(2,1)S(1)} %get-tuple-element.31), channel_id=1, source_target_pairs={{0,16},{8,24},{16,0},{24,8},{1,17},{9,25},{17,1},{25,9},{2,18},{10... | collective-permute-start | bytes 393224 | tf_op jit(solution)/shard_map/ppermute | solution.py:305
  79.6 8.2 %collective-permute-start.6 = (bf16[512,128]{1,0:T(8,128)(2,1)S(1)}, bf16[512,128]{1,0:T(8,128)(2,1)S(1)}, u32[]{:S(2)}, u32[]{:S(2)}) collective-permute-start(bf16[512,128]{1,0:T(8,128)(2,1)S(1)} %get-tuple-element.32), channel_id=1, source_target_pairs={{0,24},{8,16},{16,8},{24,0},{1,25},{9,17},{17,9},{25,1},{2,26},{10... | collective-permute-start | bytes 393224 | tf_op jit(solution)/shard_map/ppermute | solution.py:305

commit v13 on v12

--- a/solution.py
+++ b/solution.py
@@ -28,7 +28,7 @@
 BINS = 128
 STEPS = 4
 ROWS = 2 * BINS
-SLOT = 16
+SLOT = 4
 MIB = 1024 * 1024
 
 
@@ -122,12 +122,20 @@
     return [kept, near.at[0], far, near.at[1]]
 
 
-def prep_kernel(place, key, value, out_grad, kept, near, far, pieces):
+def pieces_kernel(out_grad, pieces, sems):
+    copies = []
+    for piece in range(pieces.shape[0]):
+        source = out_grad.at[:, piece * WIDE : (piece + 1) * WIDE]
+        copies.append(pltpu.make_async_copy(source, pieces.at[piece], sems.at[piece]))
+        copies[-1].start()
+    for copy in copies:
+        copy.wait()
+
+
+def mixed_kernel(place, key, value, kept, near, far):
     for hop, ship in enumerate(out_hops(kept, near, far)):
         at = (slice(None), lanes_at(place[0] ^ hop))
         ship[...] = (key[at].astype(F32) * value[at].astype(F32)).astype(BF16)
-    for piece in range(pieces.shape[0]):
-        pieces[piece] = out_grad[:, piece * WIDE : (piece + 1) * WIDE]
 
 
 def pick_kernel(far, near, out):
@@ -204,11 +212,8 @@
         summed = summed + part if chunk else part
     for j in range(reach):
         total[token_block(j), :] = summed[:, lane_block(j)] * scale
-    total[lags:, :] = jnp.zeros_like(total[lags:, :])
-    count = lag_grad.shape[0]
-    share = lags // count
-    for slot in range(count):
-        lag_grad[slot] = total[slot * share : slot * share + SLOT, :].astype(BF16)
+    for rows in range(lag_grad.shape[0]):
+        lag_grad[rows] = total[rows * SLOT : (rows + 1) * SLOT, :].astype(BF16)
 
 
 def back_kernel(scale, place, table, back, grad, halo, response, conv, *refs):
@@ -238,11 +243,12 @@
         gate_grad[at] = (cotangent[at].astype(F32) * conv).astype(BF16)
         key_grad[at] = (back * value[at].astype(F32)).astype(BF16)
         value_grad[at] = (back * key[at].astype(F32)).astype(BF16)
+    units = lag_grad.shape[0] // SLOT
     for block in range(BLOCKS):
-        total = parts[block].astype(F32)
-        for source in range(1, parts.shape[0] // BLOCKS):
-            total += parts[source * BLOCKS + block].astype(F32)
-        lag_grad[:, lane_block(block)] = total[: lag_grad.shape[0]]
+        for unit in range(units):
+            at = [source * units + unit for source in range(block, parts.shape[0] // units, BLOCKS)]
+            total = sum(parts[i].astype(F32) for i in at)
+            lag_grad[unit * SLOT : (unit + 1) * SLOT, lane_block(block)] = total
 
 
 def whole(shape):
@@ -321,7 +327,7 @@
     pieces = (channels // WIDE, held, WIDE)
     flat = (TOKENS, LANES)
     reach = (lags, LANES)
-    slots = (lags // share, SLOT, LANES)
+    slots = (lags // SLOT, SLOT, LANES)
     scalar = pl.BlockSpec(memory_space=pltpu.SMEM)
     anywhere = pl.BlockSpec(memory_space=pl.ANY)
     place = lax.axis_index(GROUP).reshape(1)
@@ -329,13 +335,20 @@
     part = (BLOCK, LANES)
     by_block = (BLOCKS, BLOCK, LANES)
     pair = (2,) + part
-    *ships, cotangent = call(
-        prep_kernel,
-        [scalar] + [whole(local)] * 2 + [whole(out_grad.shape)],
-        [whole(part), whole(pair), whole(part), whole(pieces)],
-        [shaped(part), shaped(pair), shaped(part), shaped(pieces)],
+    cotangent = call(
+        pieces_kernel,
+        [anywhere],
+        anywhere,
+        shaped(pieces),
+        [pltpu.SemaphoreType.DMA((pieces[0],))],
         limit=PREP_LIMIT,
-    )(place, key_input, value_input, out_grad)
+    )(out_grad)
+    ships = call(
+        mixed_kernel,
+        [scalar] + [whole(local)] * 2,
+        [whole(part), whole(pair), whole(part)],
+        [shaped(part), shaped(pair), shaped(part)],
+    )(place, key_input, value_input)
     cotangent = exchange(cotangent, CH).reshape(local)
     mixed, tail = call(
         join_kernel,
@@ -379,7 +392,7 @@
         [shaped(reach), shaped(slots)],
         [
             pltpu.VMEM(local, BF16),
-            pltpu.VMEM((lags + SLOT, LANES), F32),
+            pltpu.VMEM(reach, F32),
             pltpu.VMEM(by_bins, BF16),
             pltpu.SemaphoreType.DMA((STEPS,)),
         ],

time: 92.6 us -> 97.3 us (1.051)
  Pallas kernels: 12.5 us -> 19.8 us
  waiting for transfers between devices: 15.2 us -> 12.7 us
    pallas_call x1 -> x2, Pallas kernels: 1.93 us -> 9.19 us  [the longest x1 9.11 us: body(): call(pieces_kernel, [anywhere], anywhere, shaped(pieces), [pltpu.Semaphor...]
    all_to_all x3, waiting for transfers between devices: 5.01 us -> 2.77 us  [exchange(): return lax.all_to_all(value, axes, split_axis=0, concat_axis=0, tiled=True)]
  transfers between devices with their start and end apart: 10 -> 10, of which waited for: 6 -> 6; matrix products, arithmetic and copies ran while one was open for 1% -> 1% of each run, Pallas kernels for 7% -> 6%
where the time goes in v13:
time: 97.3 us; the launch traced here: 96.6 us
  starting transfers between devices  62.5 us (64%)
  Pallas kernels  19.8 us (20%)
  waiting for transfers between devices  12.7 us (13%)
    all_to_all x3, starting transfers between devices, exchange(): return lax.all_to_all(value, axes, split_axis=0, concat_axis=0, tiled=True)  42.2 us
    pallas_call x1, Pallas kernels, body(): call(pieces_kernel, [anywhere], anywhere, shaped(pieces), [pltpu.Semaphor...  9.11 us
    ppermute x3, starting transfers between devices, swap_direct(): lax.ppermute(ships[hop], GROUP, [(i, i ^ hop) for i in range(BLOCKS)])  7.87 us
    ppermute x2, starting transfers between devices, shift(): lax.ppermute(value, RUNS, [(i, i + steps) for i in range(first, last)])  6.25 us
    ppermute x2, starting transfers between devices, flip(): return lax.ppermute(value, axis, [(0, 1), (1, 0)])  6.2 us
    ppermute x3, waiting for transfers between devices, swap_direct(): lax.ppermute(ships[hop], GROUP, [(i, i ^ hop) for i in range(BLOCKS)])  5.61 us
    ppermute x2, waiting for transfers between devices, flip(): return lax.ppermute(value, axis, [(0, 1), (1, 0)])  4.37 us
    pallas_call x1, Pallas kernels, body(): call(functools.partial(cross_kernel, norm), [table, table, whole(flat), a...  3.31 us
  transfers between devices with their start and end apart: 10, of which 6 were waited for; matrix products, arithmetic and copies ran while one was open for 1% of the time, Pallas kernels for 6%

profile of v13, /device:TPU:1, one launch (start us, length us, event | category | flops | bytes accessed | tf_op | source)
XLA Modules:
  0.0 96.6 jit_solution(8402312356525524496)
XLA Ops:
  0.6 9.1 %shard_map.102 = bf16[8,32,512]{2,1,0:T(8,128)(2,1)} custom-call(bf16[32,4096]{1,0:T(8,128)(2,1)} %out_grad.1), custom_call_target="tpu_custom_call" | custom-call | tf_op jit(solution)/shard_map/pallas_call | solution.py:338
  9.8 0.0 copy-start
  9.8 0.0 copy-start.1
  9.8 18.2 %all-to-all-start = ((bf16[8,32,512]{2,1,0:T(8,128)(2,1)}), bf16[8,32,512]{2,1,0:T(8,128)(2,1)S(1)}, u32[]{:S(2)}, u32[]{:S(2)}) async-start(bf16[8,32,512]{2,1,0:T(8,128)(2,1)} %shard_map.102), calls=%async_computation | async-start | bytes 524288 | tf_op jit(solution)/shard_map/all_to_all | solution.py:317
  28.0 0.0 copy-done
  28.0 0.0 copy-done.1
  28.0 0.1 shard_map.103
  28.1 2.9 %collective-permute-start = (bf16[2,256,128]{2,1,0:T(8,128)(2,1)S(1)}, bf16[2,256,128]{2,1,0:T(8,128)(2,1)S(1)}, u32[]{:S(2)}, u32[]{:S(2)}) collective-permute-start(bf16[2,256,128]{2,1,0:T(8,128)(2,1)S(1)} %get-tuple-element.19), channel_id=1, source_target_pairs={{0,8},{8,0},{1,9},{9,1},{2,10},{10,2},{3,11},{11,3},{4,12},{12,4},... | collective-permute-start | bytes 393224 | tf_op jit(solution)/shard_map/ppermute | solution.py:297
  31.0 1.0 collective-permute-done.near
  32.0 0.0 copy-start.4
  32.0 3.3 %collective-permute-start.1 = (bf16[2,256,128]{2,1,0:T(8,128)(2,1)S(1)}, bf16[2,256,128]{2,1,0:T(8,128)(2,1)S(1)}, u32[]{:S(2)}, u32[]{:S(2)}) collective-permute-start(bf16[2,256,128]{2,1,0:T(8,128)(2,1)S(1)} %shard_map.104), channel_id=1, source_target_pairs={{0,16},{16,0},{1,17},{17,1},{2,18},{18,2},{3,19},{19,3},{4,20},{20... | collective-permute-start | bytes 393224 | tf_op jit(solution)/shard_map/ppermute | solution.py:297
  35.3 3.4 %collective-permute-done.1.far = bf16[2,256,128]{2,1,0:T(8,128)(2,1)S(1)} collective-permute-done((bf16[2,256,128]{2,1,0:T(8,128)(2,1)S(1)}, bf16[2,256,128]{2,1,0:T(8,128)(2,1)S(1)}, u32[]{:S(2)}, u32[]{:S(2)}) %collective-permute-start.1) | collective-permute-done | bytes 131104 | tf_op jit(solution)/shard_map/ppermute | solution.py:297
  38.8 0.0 copy-start.2
  38.8 0.0 copy-start.3
  38.8 5.0 %collective-permute-start.2 = (bf16[768,128]{1,0:T(8,128)(2,1)S(1)}, bf16[768,128]{1,0:T(8,128)(2,1)S(1)}, u32[]{:S(2)}, u32[]{:S(2)}) collective-permute-start(bf16[768,128]{1,0:T(8,128)(2,1)S(1)} %get-tuple-element.21), channel_id=1, source_target_pairs={{0,32},{32,64},{64,96},{96,128},{128,160},{160,192},{192,224},{224... | collective-permute-start | bytes 589832 | tf_op jit(solution)/shard_map/ppermute | solution.py:292
  43.8 0.0 all-to-all-done
  43.8 0.0 copy-done.4
  43.8 0.8 bitcast_bitcast_fusion
  44.6 5.1 %all-to-all-start.1 = ((bf16[4,256,128]{2,1,0:T(8,128)(2,1)}), bf16[4,256,128]{2,1,0:T(8,128)(2,1)S(1)}, u32[]{:S(2)}, u32[]{:S(2)}) async-start(bf16[4,256,128]{2,1,0:T(8,128)(2,1)} %bitcast_bitcast_fusion), calls=%async_computation.1 | async-start | bytes 524288 | tf_op jit(solution)/shard_map/all_to_all | solution.py:317
  49.7 0.0 collective-permute-done.2.halo
  49.7 0.0 copy-done.2
  49.7 0.0 copy-done.3
  49.7 3.3 %shard_map.106 = (bf16[1024,128]{1,0:T(8,128)(2,1)S(1)}, bf16[4,256,512]{2,1,0:T(8,128)(2,1)}, bf16[4,256,128]{2,1,0:T(8,128)(2,1)S(1)}) custom-call(s32[1]{0:T(128)} %bitcast.place, bf16[4,256,256]{2,1,0:T(8,128)(2,1)S(1)} %copy-done.2, bf16[4,256,256]{2,1,0:T(8,128)(2,1)S(1)} %copy-done.3, bf16[768,128]{1,0:T(8,128)(2,1)S(1)} %collective-permute-done.2.halo, ...), custom_call_target="tpu_custom_call" | custom-call | flops 24000000000 | tf_op jit(solution)/shard_map/pallas_call | solution.py:368
  52.9 1.9 %all-to-all-done.1 = bf16[4,256,128]{2,1,0:T(8,128)(2,1)S(1)} async-done(((bf16[4,256,128]{2,1,0:T(8,128)(2,1)}), bf16[4,256,128]{2,1,0:T(8,128)(2,1)S(1)}, u32[]{:S(2)}, u32[]{:S(2)}) %all-to-all-start.1) | async-done | bytes 262176 | tf_op jit(solution)/shard_map/all_to_all | solution.py:317
  54.8 3.3 %shard_map.107 = (bf16[768,128]{1,0:T(8,128)(2,1)S(1)}, bf16[192,4,128]{2,1,0:T(4,128)(2,1)}) custom-call(bf16[4,256,256]{2,1,0:T(8,128)(2,1)S(1)} %copy-done.2, bf16[4,256,256]{2,1,0:T(8,128)(2,1)S(1)} %copy-done.3, bf16[1024,128]{1,0:T(8,128)(2,1)S(1)} %bitcast.13, bf16[4,256,512]{2,1,0:T(8,128)(2,1)} %get-tuple-element.23.spectrum), custom_call_target="tpu_custom_call" | custom-call | tf_op jit(solution)/shard_map/pallas_call | solution.py:388
  58.1 1.3 %collective-permute-start.3 = (bf16[768,128]{1,0:T(8,128)(2,1)S(1)}, bf16[768,128]{1,0:T(8,128)(2,1)S(1)}, u32[]{:S(2)}, u32[]{:S(2)}) collective-permute-start(bf16[768,128]{1,0:T(8,128)(2,1)S(1)} %get-tuple-element.24), channel_id=1, source_target_pairs={{32,0},{64,32},{96,64},{128,96},{160,128},{192,160},{224,192},{256... | collective-permute-start | bytes 589832 | tf_op jit(solution)/shard_map/ppermute | solution.py:292
  59.4 18.8 %all-to-all-start.2 = ((bf16[192,4,128]{2,1,0:T(4,128)(2,1)}), bf16[192,4,128]{2,1,0:T(4,128)(2,1)S(1)}, u32[]{:S(2)}, u32[]{:S(2)}) async-start(bf16[192,4,128]{2,1,0:T(4,128)(2,1)} %get-tuple-element.31), calls=%async_computation.2 | async-start | bytes 393216 | tf_op jit(solution)/shard_map/all_to_all | solution.py:317
  78.3 0.0 collective-permute-done.3.halo
  78.3 2.9 %shard_map.108 = (bf16[512,128]{1,0:T(8,128)(2,1)S(1)}, bf16[512,128]{1,0:T(8,128)(2,1)S(1)}, bf16[512,128]{1,0:T(8,128)(2,1)S(1)}, bf16[512,128]{1,0:T(8,128)(2,1)S(1)}) custom-call(s32[1]{0:T(128)} %bitcast.place, bf16[4,256,256]{2,1,0:T(8,128)(2,1)S(1)} %copy-done.2, bf16[4,256,256]{2,1,0:T(8,128)(2,1)} %constant.17.clone.back, ...), custom_call_target="tpu_custom_call" | custom-call | flops 35000000512 | tf_op jit(solution)/shard_map/pallas_call | solution.py:404
  81.2 2.4 %collective-permute-start.4 = (bf16[512,128]{1,0:T(8,128)(2,1)S(1)}, bf16[512,128]{1,0:T(8,128)(2,1)S(1)}, u32[]{:S(2)}, u32[]{:S(2)}) collective-permute-start(bf16[512,128]{1,0:T(8,128)(2,1)S(1)} %get-tuple-element.28), channel_id=1, source_target_pairs={{0,8},{8,0},{16,24},{24,16},{1,9},{9,1},{17,25},{25,17},{2,10},{10... | collective-permute-start | bytes 393224 | tf_op jit(solution)/shard_map/ppermute | solution.py:311
  83.5 3.2 %collective-permute-start.5 = (bf16[512,128]{1,0:T(8,128)(2,1)S(1)}, bf16[512,128]{1,0:T(8,128)(2,1)S(1)}, u32[]{:S(2)}, u32[]{:S(2)}) collective-permute-start(bf16[512,128]{1,0:T(8,128)(2,1)S(1)} %get-tuple-element.29), channel_id=1, source_target_pairs={{0,16},{8,24},{16,0},{24,8},{1,17},{9,25},{17,1},{25,9},{2,18},{10... | collective-permute-start | bytes 393224 | tf_op jit(solution)/shard_map/ppermute | solution.py:311
  86.7 2.3 %collective-permute-start.6 = (bf16[512,128]{1,0:T(8,128)(2,1)S(1)}, bf16[512,128]{1,0:T(8,128)(2,1)S(1)}, u32[]{:S(2)}, u32[]{:S(2)}) collective-permute-start(bf16[512,128]{1,0:T(8,128)(2,1)S(1)} %get-tuple-element.30), channel_id=1, source_target_pairs={{0,24},{8,16},{16,8},{24,0},{1,25},{9,17},{17,9},{25,1},{2,26},{10... | collective-permute-start | bytes 393224 | tf_op jit(solution)/shard_map/ppermute | solution.py:311
  89.1 0.0 collective-permute-done.4.refs_1_
  89.1 2.0 %collective-permute-done.5.refs_2_ = bf16[512,128]{1,0:T(8,128)(2,1)S(1)} collective-permute-done((bf16[512,128]{1,0:T(8,128)(2,1)S(1)}, bf16[512,128]{1,0:T(8,128)(2,1)S(1)}, u32[]{:S(2)}, u32[]{:S(2)}) %collective-permute-start.5) | collective-permute-done | bytes 131104 | tf_op jit(solution)/shard_map/ppermute | solution.py:311
  91.1 3.6 %collective-permute-done.6.refs_3_ = bf16[512,128]{1,0:T(8,128)(2,1)S(1)} collective-permute-done((bf16[512,128]{1,0:T(8,128)(2,1)S(1)}, bf16[512,128]{1,0:T(8,128)(2,1)S(1)}, u32[]{:S(2)}, u32[]{:S(2)}) %collective-permute-start.6) | collective-permute-done | bytes 131104 | tf_op jit(solution)/shard_map/ppermute | solution.py:311
  94.7 0.9 all-to-all-done.2.refs_7_
  95.6 1.1 %shard_map.109 = (bf16[256,512]{1,0:T(8,128)(2,1)}, bf16[256,512]{1,0:T(8,128)(2,1)}, bf16[256,512]{1,0:T(8,128)(2,1)}, f32[12,512]{1,0:T(8,128)}) custom-call(s32[1]{0:T(128)} %bitcast.place, bf16[512,128]{1,0:T(8,128)(2,1)S(1)} %get-tuple-element.27.refs_0_, bf16[512,128]{1,0:T(8,128)(2,1)S(1)} %collective-permute-done.4.refs_1_, ...), custom_call_target="tpu_custom_call" | custom-call | tf_op jit(solution)/shard_map/pallas_call | solution.py:420
  (2 shorter events, 0.0 us)
Async XLA Ops:
  9.8 18.3 %copy-start = (bf16[256,512]{1,0:T(8,128)(2,1)S(1)}, bf16[256,512]{1,0:T(8,128)(2,1)}, u32[]{:S(2)}) copy-start(bf16[256,512]{1,0:T(8,128)(2,1)} %refs_5_.1) | copy-start | bytes 786436
  9.8 18.3 %copy-start.1 = (bf16[256,512]{1,0:T(8,128)(2,1)S(1)}, bf16[256,512]{1,0:T(8,128)(2,1)}, u32[]{:S(2)}) copy-start(bf16[256,512]{1,0:T(8,128)(2,1)} %refs_6_.1) | copy-start | bytes 786436
  9.8 34.0 %all-to-all-start = ((bf16[8,32,512]{2,1,0:T(8,128)(2,1)}), bf16[8,32,512]{2,1,0:T(8,128)(2,1)S(1)}, u32[]{:S(2)}, u32[]{:S(2)}) async-start(bf16[8,32,512]{2,1,0:T(8,128)(2,1)} %shard_map.102), calls=%async_computation | async-start | bytes 524288 | tf_op jit(solution)/shard_map/all_to_all | solution.py:317
  28.1 3.8 %collective-permute-start = (bf16[2,256,128]{2,1,0:T(8,128)(2,1)S(1)}, bf16[2,256,128]{2,1,0:T(8,128)(2,1)S(1)}, u32[]{:S(2)}, u32[]{:S(2)}) collective-permute-start(bf16[2,256,128]{2,1,0:T(8,128)(2,1)S(1)} %get-tuple-element.19), channel_id=1, source_target_pairs={{0,8},{8,0},{1,9},{9,1},{2,10},{10,2},{3,11},{11,3},{4,12},{12,4},... | collective-permute-start | bytes 393224 | tf_op jit(solution)/shard_map/ppermute | solution.py:297
  32.0 11.8 %copy-start.4 = (bf16[256,512]{1,0:T(8,128)(2,1)S(1)}, bf16[256,512]{1,0:T(8,128)(2,1)}, u32[]{:S(2)}) copy-start(bf16[256,512]{1,0:T(8,128)(2,1)} %param.7) | copy-start | bytes 786436
  32.0 6.7 %collective-permute-start.1 = (bf16[2,256,128]{2,1,0:T(8,128)(2,1)S(1)}, bf16[2,256,128]{2,1,0:T(8,128)(2,1)S(1)}, u32[]{:S(2)}, u32[]{:S(2)}) collective-permute-start(bf16[2,256,128]{2,1,0:T(8,128)(2,1)S(1)} %shard_map.104), channel_id=1, source_target_pairs={{0,16},{16,0},{1,17},{17,1},{2,18},{18,2},{3,19},{19,3},{4,20},{20... | collective-permute-start | bytes 393224 | tf_op jit(solution)/shard_map/ppermute | solution.py:297
  38.8 10.9 %copy-start.2 = (bf16[4,256,256]{2,1,0:T(8,128)(2,1)S(1)}, bf16[4,256,256]{2,1,0:T(8,128)(2,1)}, u32[]{:S(2)}) copy-start(bf16[4,256,256]{2,1,0:T(8,128)(2,1)} %constant.16.clone.table) | copy-start | bytes 1572868
  38.8 10.9 %copy-start.3 = (bf16[4,256,256]{2,1,0:T(8,128)(2,1)S(1)}, bf16[4,256,256]{2,1,0:T(8,128)(2,1)}, u32[]{:S(2)}) copy-start(bf16[4,256,256]{2,1,0:T(8,128)(2,1)} %constant.17.clone.back) | copy-start | bytes 1572868
  38.8 10.9 %collective-permute-start.2 = (bf16[768,128]{1,0:T(8,128)(2,1)S(1)}, bf16[768,128]{1,0:T(8,128)(2,1)S(1)}, u32[]{:S(2)}, u32[]{:S(2)}) collective-permute-start(bf16[768,128]{1,0:T(8,128)(2,1)S(1)} %get-tuple-element.21), channel_id=1, source_target_pairs={{0,32},{32,64},{64,96},{96,128},{128,160},{160,192},{192,224},{224... | collective-permute-start | bytes 589832 | tf_op jit(solution)/shard_map/ppermute | solution.py:292
  44.6 10.3 %all-to-all-start.1 = ((bf16[4,256,128]{2,1,0:T(8,128)(2,1)}), bf16[4,256,128]{2,1,0:T(8,128)(2,1)S(1)}, u32[]{:S(2)}, u32[]{:S(2)}) async-start(bf16[4,256,128]{2,1,0:T(8,128)(2,1)} %bitcast_bitcast_fusion), calls=%async_computation.1 | async-start | bytes 524288 | tf_op jit(solution)/shard_map/all_to_all | solution.py:317
  58.1 20.1 %collective-permute-start.3 = (bf16[768,128]{1,0:T(8,128)(2,1)S(1)}, bf16[768,128]{1,0:T(8,128)(2,1)S(1)}, u32[]{:S(2)}, u32[]{:S(2)}) collective-permute-start(bf16[768,128]{1,0:T(8,128)(2,1)S(1)} %get-tuple-element.24), channel_id=1, source_target_pairs={{32,0},{64,32},{96,64},{128,96},{160,128},{192,160},{224,192},{256... | collective-permute-start | bytes 589832 | tf_op jit(solution)/shard_map/ppermute | solution.py:292
  59.4 36.1 %all-to-all-start.2 = ((bf16[192,4,128]{2,1,0:T(4,128)(2,1)}), bf16[192,4,128]{2,1,0:T(4,128)(2,1)S(1)}, u32[]{:S(2)}, u32[]{:S(2)}) async-start(bf16[192,4,128]{2,1,0:T(4,128)(2,1)} %get-tuple-element.31), calls=%async_computation.2 | async-start | bytes 393216 | tf_op jit(solution)/shard_map/all_to_all | solution.py:317
  81.2 7.9 %collective-permute-start.4 = (bf16[512,128]{1,0:T(8,128)(2,1)S(1)}, bf16[512,128]{1,0:T(8,128)(2,1)S(1)}, u32[]{:S(2)}, u32[]{:S(2)}) collective-permute-start(bf16[512,128]{1,0:T(8,128)(2,1)S(1)} %get-tuple-element.28), channel_id=1, source_target_pairs={{0,8},{8,0},{16,24},{24,16},{1,9},{9,1},{17,25},{25,17},{2,10},{10... | collective-permute-start | bytes 393224 | tf_op jit(solution)/shard_map/ppermute | solution.py:311
  83.5 7.5 %collective-permute-start.5 = (bf16[512,128]{1,0:T(8,128)(2,1)S(1)}, bf16[512,128]{1,0:T(8,128)(2,1)S(1)}, u32[]{:S(2)}, u32[]{:S(2)}) collective-permute-start(bf16[512,128]{1,0:T(8,128)(2,1)S(1)} %get-tuple-element.29), channel_id=1, source_target_pairs={{0,16},{8,24},{16,0},{24,8},{1,17},{9,25},{17,1},{25,9},{2,18},{10... | collective-permute-start | bytes 393224 | tf_op jit(solution)/shard_map/ppermute | solution.py:311
  86.7 7.9 %collective-permute-start.6 = (bf16[512,128]{1,0:T(8,128)(2,1)S(1)}, bf16[512,128]{1,0:T(8,128)(2,1)S(1)}, u32[]{:S(2)}, u32[]{:S(2)}) collective-permute-start(bf16[512,128]{1,0:T(8,128)(2,1)S(1)} %get-tuple-element.30), channel_id=1, source_target_pairs={{0,24},{8,16},{16,8},{24,0},{1,25},{9,17},{17,9},{25,1},{2,26},{10... | collective-permute-start | bytes 393224 | tf_op jit(solution)/shard_map/ppermute | solution.py:311

commit v14 on v13

--- a/solution.py
+++ b/solution.py
@@ -122,14 +122,9 @@
     return [kept, near.at[0], far, near.at[1]]
 
 
-def pieces_kernel(out_grad, pieces, sems):
-    copies = []
+def pieces_kernel(out_grad, pieces):
     for piece in range(pieces.shape[0]):
-        source = out_grad.at[:, piece * WIDE : (piece + 1) * WIDE]
-        copies.append(pltpu.make_async_copy(source, pieces.at[piece], sems.at[piece]))
-        copies[-1].start()
-    for copy in copies:
-        copy.wait()
+        pieces[piece] = out_grad[:, piece * WIDE : (piece + 1) * WIDE]
 
 
 def mixed_kernel(place, key, value, kept, near, far):
@@ -337,10 +332,9 @@
     pair = (2,) + part
     cotangent = call(
         pieces_kernel,
-        [anywhere],
-        anywhere,
+        [whole(out_grad.shape)],
+        whole(pieces),
         shaped(pieces),
-        [pltpu.SemaphoreType.DMA((pieces[0],))],
         limit=PREP_LIMIT,
     )(out_grad)
     ships = call(

time: 97.3 us -> 89.8 us (0.923)
  Pallas kernels: 19.8 us -> 12.3 us
    pallas_call x1, Pallas kernels: 9.11 us -> 1.67 us  [body(): call(pieces_kernel, [whole(out_grad.shape)], whole(pieces), shaped(pieces...]
  transfers between devices with their start and end apart: 10 -> 10, of which waited for: 6 -> 6; matrix products, arithmetic and copies ran while one was open for 1% -> 1% of each run, Pallas kernels for 6% -> 7%
where the time goes in v14:
time: 89.8 us; the launch traced here: 89.1 us
  starting transfers between devices  62.5 us (70%)
  waiting for transfers between devices  12.7 us (14%)
  Pallas kernels  12.3 us (14%)
    all_to_all x3, starting transfers between devices, exchange(): return lax.all_to_all(value, axes, split_axis=0, concat_axis=0, tiled=True)  42.1 us
    ppermute x3, starting transfers between devices, swap_direct(): lax.ppermute(ships[hop], GROUP, [(i, i ^ hop) for i in range(BLOCKS)])  7.87 us
    ppermute x2, starting transfers between devices, shift(): lax.ppermute(value, RUNS, [(i, i + steps) for i in range(first, last)])  6.25 us
    ppermute x2, starting transfers between devices, flip(): return lax.ppermute(value, axis, [(0, 1), (1, 0)])  6.2 us
    ppermute x3, waiting for transfers between devices, swap_direct(): lax.ppermute(ships[hop], GROUP, [(i, i ^ hop) for i in range(BLOCKS)])  5.61 us
    ppermute x2, waiting for transfers between devices, flip(): return lax.ppermute(value, axis, [(0, 1), (1, 0)])  4.37 us
    pallas_call x1, Pallas kernels, body(): call(functools.partial(cross_kernel, norm), [table, table, whole(flat), a...  3.32 us
    pallas_call x1, Pallas kernels, body(): call(functools.partial(conv_kernel, norm), [table, table, whole(reach), w...  3.29 us
  transfers between devices with their start and end apart: 10, of which 6 were waited for; matrix products, arithmetic and copies ran while one was open for 1% of the time, Pallas kernels for 7%

profile of v14, /device:TPU:1, one launch (start us, length us, event | category | flops | bytes accessed | tf_op | source)
XLA Modules:
  0.0 89.1 jit_solution(17402835925079395242)
XLA Ops:
  0.6 1.7 %shard_map.102 = bf16[8,32,512]{2,1,0:T(8,128)(2,1)} custom-call(bf16[32,4096]{1,0:T(8,128)(2,1)} %out_grad.1), custom_call_target="tpu_custom_call" | custom-call | tf_op jit(solution)/shard_map/pallas_call | solution.py:333
  2.3 0.0 copy-start
  2.3 0.0 copy-start.1
  2.3 18.2 %all-to-all-start = ((bf16[8,32,512]{2,1,0:T(8,128)(2,1)}), bf16[8,32,512]{2,1,0:T(8,128)(2,1)S(1)}, u32[]{:S(2)}, u32[]{:S(2)}) async-start(bf16[8,32,512]{2,1,0:T(8,128)(2,1)} %shard_map.102), calls=%async_computation | async-start | bytes 524288 | tf_op jit(solution)/shard_map/all_to_all | solution.py:312
  20.5 0.0 copy-done
  20.5 0.0 copy-done.1
  20.6 0.1 shard_map.103
  20.6 2.9 %collective-permute-start = (bf16[2,256,128]{2,1,0:T(8,128)(2,1)S(1)}, bf16[2,256,128]{2,1,0:T(8,128)(2,1)S(1)}, u32[]{:S(2)}, u32[]{:S(2)}) collective-permute-start(bf16[2,256,128]{2,1,0:T(8,128)(2,1)S(1)} %get-tuple-element.19), channel_id=1, source_target_pairs={{0,8},{8,0},{1,9},{9,1},{2,10},{10,2},{3,11},{11,3},{4,12},{12,4},... | collective-permute-start | bytes 393224 | tf_op jit(solution)/shard_map/ppermute | solution.py:292
  23.5 1.0 %collective-permute-done.near = bf16[2,256,128]{2,1,0:T(8,128)(2,1)S(1)} collective-permute-done((bf16[2,256,128]{2,1,0:T(8,128)(2,1)S(1)}, bf16[2,256,128]{2,1,0:T(8,128)(2,1)S(1)}, u32[]{:S(2)}, u32[]{:S(2)}) %collective-permute-start) | collective-permute-done | bytes 131104 | tf_op jit(solution)/shard_map/ppermute | solution.py:292
  24.5 0.0 copy-start.4
  24.5 3.3 %collective-permute-start.1 = (bf16[2,256,128]{2,1,0:T(8,128)(2,1)S(1)}, bf16[2,256,128]{2,1,0:T(8,128)(2,1)S(1)}, u32[]{:S(2)}, u32[]{:S(2)}) collective-permute-start(bf16[2,256,128]{2,1,0:T(8,128)(2,1)S(1)} %shard_map.104), channel_id=1, source_target_pairs={{0,16},{16,0},{1,17},{17,1},{2,18},{18,2},{3,19},{19,3},{4,20},{20... | collective-permute-start | bytes 393224 | tf_op jit(solution)/shard_map/ppermute | solution.py:292
  27.8 3.4 %collective-permute-done.1.far = bf16[2,256,128]{2,1,0:T(8,128)(2,1)S(1)} collective-permute-done((bf16[2,256,128]{2,1,0:T(8,128)(2,1)S(1)}, bf16[2,256,128]{2,1,0:T(8,128)(2,1)S(1)}, u32[]{:S(2)}, u32[]{:S(2)}) %collective-permute-start.1) | collective-permute-done | bytes 131104 | tf_op jit(solution)/shard_map/ppermute | solution.py:292
  31.3 0.0 copy-start.2
  31.3 0.0 copy-start.3
  31.3 5.0 %collective-permute-start.2 = (bf16[768,128]{1,0:T(8,128)(2,1)S(1)}, bf16[768,128]{1,0:T(8,128)(2,1)S(1)}, u32[]{:S(2)}, u32[]{:S(2)}) collective-permute-start(bf16[768,128]{1,0:T(8,128)(2,1)S(1)} %get-tuple-element.21), channel_id=1, source_target_pairs={{0,32},{32,64},{64,96},{96,128},{128,160},{160,192},{192,224},{224... | collective-permute-start | bytes 589832 | tf_op jit(solution)/shard_map/ppermute | solution.py:287
  36.3 0.0 all-to-all-done
  36.3 0.0 copy-done.4
  36.3 0.8 bitcast_bitcast_fusion
  37.1 5.1 %all-to-all-start.1 = ((bf16[4,256,128]{2,1,0:T(8,128)(2,1)}), bf16[4,256,128]{2,1,0:T(8,128)(2,1)S(1)}, u32[]{:S(2)}, u32[]{:S(2)}) async-start(bf16[4,256,128]{2,1,0:T(8,128)(2,1)} %bitcast_bitcast_fusion), calls=%async_computation.1 | async-start | bytes 524288 | tf_op jit(solution)/shard_map/all_to_all | solution.py:312
  42.2 0.0 collective-permute-done.2.halo
  42.2 0.0 copy-done.2
  42.2 0.0 copy-done.3
  42.2 3.3 %shard_map.106 = (bf16[1024,128]{1,0:T(8,128)(2,1)S(1)}, bf16[4,256,512]{2,1,0:T(8,128)(2,1)}, bf16[4,256,128]{2,1,0:T(8,128)(2,1)S(1)}) custom-call(s32[1]{0:T(128)} %bitcast.place, bf16[4,256,256]{2,1,0:T(8,128)(2,1)S(1)} %copy-done.2, bf16[4,256,256]{2,1,0:T(8,128)(2,1)S(1)} %copy-done.3, bf16[768,128]{1,0:T(8,128)(2,1)S(1)} %collective-permute-done.2.halo, ...), custom_call_target="tpu_custom_call" | custom-call | flops 24000000000 | tf_op jit(solution)/shard_map/pallas_call | solution.py:362
  45.5 1.9 %all-to-all-done.1 = bf16[4,256,128]{2,1,0:T(8,128)(2,1)S(1)} async-done(((bf16[4,256,128]{2,1,0:T(8,128)(2,1)}), bf16[4,256,128]{2,1,0:T(8,128)(2,1)S(1)}, u32[]{:S(2)}, u32[]{:S(2)}) %all-to-all-start.1) | async-done | bytes 262176 | tf_op jit(solution)/shard_map/all_to_all | solution.py:312
  47.3 3.3 %shard_map.107 = (bf16[768,128]{1,0:T(8,128)(2,1)S(1)}, bf16[192,4,128]{2,1,0:T(4,128)(2,1)}) custom-call(bf16[4,256,256]{2,1,0:T(8,128)(2,1)S(1)} %copy-done.2, bf16[4,256,256]{2,1,0:T(8,128)(2,1)S(1)} %copy-done.3, bf16[1024,128]{1,0:T(8,128)(2,1)S(1)} %bitcast.13, bf16[4,256,512]{2,1,0:T(8,128)(2,1)} %get-tuple-element.23.spectrum), custom_call_target="tpu_custom_call" | custom-call | tf_op jit(solution)/shard_map/pallas_call | solution.py:382
  50.7 1.3 %collective-permute-start.3 = (bf16[768,128]{1,0:T(8,128)(2,1)S(1)}, bf16[768,128]{1,0:T(8,128)(2,1)S(1)}, u32[]{:S(2)}, u32[]{:S(2)}) collective-permute-start(bf16[768,128]{1,0:T(8,128)(2,1)S(1)} %get-tuple-element.24), channel_id=1, source_target_pairs={{32,0},{64,32},{96,64},{128,96},{160,128},{192,160},{224,192},{256... | collective-permute-start | bytes 589832 | tf_op jit(solution)/shard_map/ppermute | solution.py:287
  52.0 18.8 %all-to-all-start.2 = ((bf16[192,4,128]{2,1,0:T(4,128)(2,1)}), bf16[192,4,128]{2,1,0:T(4,128)(2,1)S(1)}, u32[]{:S(2)}, u32[]{:S(2)}) async-start(bf16[192,4,128]{2,1,0:T(4,128)(2,1)} %get-tuple-element.31), calls=%async_computation.2 | async-start | bytes 393216 | tf_op jit(solution)/shard_map/all_to_all | solution.py:312
  70.8 0.0 collective-permute-done.3.halo
  70.8 2.9 %shard_map.108 = (bf16[512,128]{1,0:T(8,128)(2,1)S(1)}, bf16[512,128]{1,0:T(8,128)(2,1)S(1)}, bf16[512,128]{1,0:T(8,128)(2,1)S(1)}, bf16[512,128]{1,0:T(8,128)(2,1)S(1)}) custom-call(s32[1]{0:T(128)} %bitcast.place, bf16[4,256,256]{2,1,0:T(8,128)(2,1)S(1)} %copy-done.2, bf16[4,256,256]{2,1,0:T(8,128)(2,1)} %constant.17.clone.back, ...), custom_call_target="tpu_custom_call" | custom-call | flops 35000000512 | tf_op jit(solution)/shard_map/pallas_call | solution.py:398
  73.7 2.4 %collective-permute-start.4 = (bf16[512,128]{1,0:T(8,128)(2,1)S(1)}, bf16[512,128]{1,0:T(8,128)(2,1)S(1)}, u32[]{:S(2)}, u32[]{:S(2)}) collective-permute-start(bf16[512,128]{1,0:T(8,128)(2,1)S(1)} %get-tuple-element.28), channel_id=1, source_target_pairs={{0,8},{8,0},{16,24},{24,16},{1,9},{9,1},{17,25},{25,17},{2,10},{10... | collective-permute-start | bytes 393224 | tf_op jit(solution)/shard_map/ppermute | solution.py:306
  76.0 3.2 %collective-permute-start.5 = (bf16[512,128]{1,0:T(8,128)(2,1)S(1)}, bf16[512,128]{1,0:T(8,128)(2,1)S(1)}, u32[]{:S(2)}, u32[]{:S(2)}) collective-permute-start(bf16[512,128]{1,0:T(8,128)(2,1)S(1)} %get-tuple-element.29), channel_id=1, source_target_pairs={{0,16},{8,24},{16,0},{24,8},{1,17},{9,25},{17,1},{25,9},{2,18},{10... | collective-permute-start | bytes 393224 | tf_op jit(solution)/shard_map/ppermute | solution.py:306
  79.3 2.3 %collective-permute-start.6 = (bf16[512,128]{1,0:T(8,128)(2,1)S(1)}, bf16[512,128]{1,0:T(8,128)(2,1)S(1)}, u32[]{:S(2)}, u32[]{:S(2)}) collective-permute-start(bf16[512,128]{1,0:T(8,128)(2,1)S(1)} %get-tuple-element.30), channel_id=1, source_target_pairs={{0,24},{8,16},{16,8},{24,0},{1,25},{9,17},{17,9},{25,1},{2,26},{10... | collective-permute-start | bytes 393224 | tf_op jit(solution)/shard_map/ppermute | solution.py:306
  81.6 0.0 collective-permute-done.4.refs_1_
  81.6 2.0 %collective-permute-done.5.refs_2_ = bf16[512,128]{1,0:T(8,128)(2,1)S(1)} collective-permute-done((bf16[512,128]{1,0:T(8,128)(2,1)S(1)}, bf16[512,128]{1,0:T(8,128)(2,1)S(1)}, u32[]{:S(2)}, u32[]{:S(2)}) %collective-permute-start.5) | collective-permute-done | bytes 131104 | tf_op jit(solution)/shard_map/ppermute | solution.py:306
  83.6 3.6 %collective-permute-done.6.refs_3_ = bf16[512,128]{1,0:T(8,128)(2,1)S(1)} collective-permute-done((bf16[512,128]{1,0:T(8,128)(2,1)S(1)}, bf16[512,128]{1,0:T(8,128)(2,1)S(1)}, u32[]{:S(2)}, u32[]{:S(2)}) %collective-permute-start.6) | collective-permute-done | bytes 131104 | tf_op jit(solution)/shard_map/ppermute | solution.py:306
  87.2 0.9 %all-to-all-done.2.refs_7_ = bf16[192,4,128]{2,1,0:T(4,128)(2,1)S(1)} async-done(((bf16[192,4,128]{2,1,0:T(4,128)(2,1)}), bf16[192,4,128]{2,1,0:T(4,128)(2,1)S(1)}, u32[]{:S(2)}, u32[]{:S(2)}) %all-to-all-start.2) | async-done | bytes 196640 | tf_op jit(solution)/shard_map/all_to_all | solution.py:312
  88.1 1.1 %shard_map.109 = (bf16[256,512]{1,0:T(8,128)(2,1)}, bf16[256,512]{1,0:T(8,128)(2,1)}, bf16[256,512]{1,0:T(8,128)(2,1)}, f32[12,512]{1,0:T(8,128)}) custom-call(s32[1]{0:T(128)} %bitcast.place, bf16[512,128]{1,0:T(8,128)(2,1)S(1)} %get-tuple-element.27.refs_0_, bf16[512,128]{1,0:T(8,128)(2,1)S(1)} %collective-permute-done.4.refs_1_, ...), custom_call_target="tpu_custom_call" | custom-call | tf_op jit(solution)/shard_map/pallas_call | solution.py:414
  (2 shorter events, 0.0 us)
Async XLA Ops:
  2.3 18.2 %copy-start = (bf16[256,512]{1,0:T(8,128)(2,1)S(1)}, bf16[256,512]{1,0:T(8,128)(2,1)}, u32[]{:S(2)}) copy-start(bf16[256,512]{1,0:T(8,128)(2,1)} %refs_5_.1) | copy-start | bytes 786436
  2.3 18.2 %copy-start.1 = (bf16[256,512]{1,0:T(8,128)(2,1)S(1)}, bf16[256,512]{1,0:T(8,128)(2,1)}, u32[]{:S(2)}) copy-start(bf16[256,512]{1,0:T(8,128)(2,1)} %refs_6_.1) | copy-start | bytes 786436
  2.3 34.0 %all-to-all-start = ((bf16[8,32,512]{2,1,0:T(8,128)(2,1)}), bf16[8,32,512]{2,1,0:T(8,128)(2,1)S(1)}, u32[]{:S(2)}, u32[]{:S(2)}) async-start(bf16[8,32,512]{2,1,0:T(8,128)(2,1)} %shard_map.102), calls=%async_computation | async-start | bytes 524288 | tf_op jit(solution)/shard_map/all_to_all | solution.py:312
  20.6 3.8 %collective-permute-start = (bf16[2,256,128]{2,1,0:T(8,128)(2,1)S(1)}, bf16[2,256,128]{2,1,0:T(8,128)(2,1)S(1)}, u32[]{:S(2)}, u32[]{:S(2)}) collective-permute-start(bf16[2,256,128]{2,1,0:T(8,128)(2,1)S(1)} %get-tuple-element.19), channel_id=1, source_target_pairs={{0,8},{8,0},{1,9},{9,1},{2,10},{10,2},{3,11},{11,3},{4,12},{12,4},... | collective-permute-start | bytes 393224 | tf_op jit(solution)/shard_map/ppermute | solution.py:292
  24.5 11.8 %copy-start.4 = (bf16[256,512]{1,0:T(8,128)(2,1)S(1)}, bf16[256,512]{1,0:T(8,128)(2,1)}, u32[]{:S(2)}) copy-start(bf16[256,512]{1,0:T(8,128)(2,1)} %param.7) | copy-start | bytes 786436
  24.5 6.7 %collective-permute-start.1 = (bf16[2,256,128]{2,1,0:T(8,128)(2,1)S(1)}, bf16[2,256,128]{2,1,0:T(8,128)(2,1)S(1)}, u32[]{:S(2)}, u32[]{:S(2)}) collective-permute-start(bf16[2,256,128]{2,1,0:T(8,128)(2,1)S(1)} %shard_map.104), channel_id=1, source_target_pairs={{0,16},{16,0},{1,17},{17,1},{2,18},{18,2},{3,19},{19,3},{4,20},{20... | collective-permute-start | bytes 393224 | tf_op jit(solution)/shard_map/ppermute | solution.py:292
  31.3 10.9 %copy-start.2 = (bf16[4,256,256]{2,1,0:T(8,128)(2,1)S(1)}, bf16[4,256,256]{2,1,0:T(8,128)(2,1)}, u32[]{:S(2)}) copy-start(bf16[4,256,256]{2,1,0:T(8,128)(2,1)} %constant.16.clone.table) | copy-start | bytes 1572868
  31.3 10.9 %copy-start.3 = (bf16[4,256,256]{2,1,0:T(8,128)(2,1)S(1)}, bf16[4,256,256]{2,1,0:T(8,128)(2,1)}, u32[]{:S(2)}) copy-start(bf16[4,256,256]{2,1,0:T(8,128)(2,1)} %constant.17.clone.back) | copy-start | bytes 1572868
  31.3 10.9 %collective-permute-start.2 = (bf16[768,128]{1,0:T(8,128)(2,1)S(1)}, bf16[768,128]{1,0:T(8,128)(2,1)S(1)}, u32[]{:S(2)}, u32[]{:S(2)}) collective-permute-start(bf16[768,128]{1,0:T(8,128)(2,1)S(1)} %get-tuple-element.21), channel_id=1, source_target_pairs={{0,32},{32,64},{64,96},{96,128},{128,160},{160,192},{192,224},{224... | collective-permute-start | bytes 589832 | tf_op jit(solution)/shard_map/ppermute | solution.py:287
  37.1 10.3 %all-to-all-start.1 = ((bf16[4,256,128]{2,1,0:T(8,128)(2,1)}), bf16[4,256,128]{2,1,0:T(8,128)(2,1)S(1)}, u32[]{:S(2)}, u32[]{:S(2)}) async-start(bf16[4,256,128]{2,1,0:T(8,128)(2,1)} %bitcast_bitcast_fusion), calls=%async_computation.1 | async-start | bytes 524288 | tf_op jit(solution)/shard_map/all_to_all | solution.py:312
  50.7 20.1 %collective-permute-start.3 = (bf16[768,128]{1,0:T(8,128)(2,1)S(1)}, bf16[768,128]{1,0:T(8,128)(2,1)S(1)}, u32[]{:S(2)}, u32[]{:S(2)}) collective-permute-start(bf16[768,128]{1,0:T(8,128)(2,1)S(1)} %get-tuple-element.24), channel_id=1, source_target_pairs={{32,0},{64,32},{96,64},{128,96},{160,128},{192,160},{224,192},{256... | collective-permute-start | bytes 589832 | tf_op jit(solution)/shard_map/ppermute | solution.py:287
  52.0 36.1 %all-to-all-start.2 = ((bf16[192,4,128]{2,1,0:T(4,128)(2,1)}), bf16[192,4,128]{2,1,0:T(4,128)(2,1)S(1)}, u32[]{:S(2)}, u32[]{:S(2)}) async-start(bf16[192,4,128]{2,1,0:T(4,128)(2,1)} %get-tuple-element.31), calls=%async_computation.2 | async-start | bytes 393216 | tf_op jit(solution)/shard_map/all_to_all | solution.py:312
  73.7 7.9 %collective-permute-start.4 = (bf16[512,128]{1,0:T(8,128)(2,1)S(1)}, bf16[512,128]{1,0:T(8,128)(2,1)S(1)}, u32[]{:S(2)}, u32[]{:S(2)}) collective-permute-start(bf16[512,128]{1,0:T(8,128)(2,1)S(1)} %get-tuple-element.28), channel_id=1, source_target_pairs={{0,8},{8,0},{16,24},{24,16},{1,9},{9,1},{17,25},{25,17},{2,10},{10... | collective-permute-start | bytes 393224 | tf_op jit(solution)/shard_map/ppermute | solution.py:306
  76.0 7.5 %collective-permute-start.5 = (bf16[512,128]{1,0:T(8,128)(2,1)S(1)}, bf16[512,128]{1,0:T(8,128)(2,1)S(1)}, u32[]{:S(2)}, u32[]{:S(2)}) collective-permute-start(bf16[512,128]{1,0:T(8,128)(2,1)S(1)} %get-tuple-element.29), channel_id=1, source_target_pairs={{0,16},{8,24},{16,0},{24,8},{1,17},{9,25},{17,1},{25,9},{2,18},{10... | collective-permute-start | bytes 393224 | tf_op jit(solution)/shard_map/ppermute | solution.py:306
  79.3 7.9 %collective-permute-start.6 = (bf16[512,128]{1,0:T(8,128)(2,1)S(1)}, bf16[512,128]{1,0:T(8,128)(2,1)S(1)}, u32[]{:S(2)}, u32[]{:S(2)}) collective-permute-start(bf16[512,128]{1,0:T(8,128)(2,1)S(1)} %get-tuple-element.30), channel_id=1, source_target_pairs={{0,24},{8,16},{16,8},{24,0},{1,25},{9,17},{17,9},{25,1},{2,26},{10... | collective-permute-start | bytes 393224 | tf_op jit(solution)/shard_map/ppermute | solution.py:306

commit v15 on v14

--- a/solution.py
+++ b/solution.py
@@ -254,12 +254,12 @@
     return jax.ShapeDtypeStruct(shape, dtype)
 
 
-def call(kernel, in_specs, out_specs, out_shape, scratch=(), flops=0, limit=None, scalars=0):
+def call(kernel, in_specs, out_specs, out_shape, scratch=(), flops=0, limit=None, scalars=0, steps=1):
     return pl.pallas_call(
         kernel,
         grid_spec=pltpu.PrefetchScalarGridSpec(
             num_scalar_prefetch=scalars,
-            grid=(1,),
+            grid=(steps,),
             in_specs=in_specs,
             out_specs=out_specs,
             scratch_shapes=scratch,
@@ -332,10 +332,11 @@
     pair = (2,) + part
     cotangent = call(
         pieces_kernel,
-        [whole(out_grad.shape)],
-        whole(pieces),
+        [pl.BlockSpec((held, channels // 2), lambda step: (0, step))],
+        pl.BlockSpec((pieces[0] // 2,) + pieces[1:], lambda step: (step, 0, 0)),
         shaped(pieces),
         limit=PREP_LIMIT,
+        steps=2,
     )(out_grad)
     ships = call(
         mixed_kernel,

time: 89.8 us -> 89.8 us (level)
  no operation moved by 1% of the time
where the time goes in v15:
time: 89.8 us; the launch traced here: 89.1 us
  starting transfers between devices  62.5 us (70%)
  waiting for transfers between devices  12.7 us (14%)
  Pallas kernels  12.3 us (14%)
    all_to_all x3, starting transfers between devices, exchange(): return lax.all_to_all(value, axes, split_axis=0, concat_axis=0, tiled=True)  42.1 us
    ppermute x3, starting transfers between devices, swap_direct(): lax.ppermute(ships[hop], GROUP, [(i, i ^ hop) for i in range(BLOCKS)])  7.87 us
    ppermute x2, starting transfers between devices, shift(): lax.ppermute(value, RUNS, [(i, i + steps) for i in range(first, last)])  6.25 us
    ppermute x2, starting transfers between devices, flip(): return lax.ppermute(value, axis, [(0, 1), (1, 0)])  6.2 us
    ppermute x3, waiting for transfers between devices, swap_direct(): lax.ppermute(ships[hop], GROUP, [(i, i ^ hop) for i in range(BLOCKS)])  5.61 us
    ppermute x2, waiting for transfers between devices, flip(): return lax.ppermute(value, axis, [(0, 1), (1, 0)])  4.37 us
    pallas_call x1, Pallas kernels, body(): call(functools.partial(cross_kernel, norm), [table, table, whole(flat), a...  3.32 us
    pallas_call x1, Pallas kernels, body(): call(functools.partial(conv_kernel, norm), [table, table, whole(reach), w...  3.3 us
  transfers between devices with their start and end apart: 10, of which 6 were waited for; matrix products, arithmetic and copies ran while one was open for 1% of the time, Pallas kernels for 7%

profile of v15, /device:TPU:1, one launch (start us, length us, event | category | flops | bytes accessed | tf_op | source)
XLA Modules:
  0.0 89.1 jit_solution(13731238278426945294)
XLA Ops:
  0.6 1.6 %shard_map.102 = bf16[8,32,512]{2,1,0:T(8,128)(2,1)} custom-call(bf16[32,4096]{1,0:T(8,128)(2,1)} %out_grad.1), custom_call_target="tpu_custom_call" | custom-call | tf_op jit(solution)/shard_map/pallas_call | solution.py:333
  2.3 0.0 copy-start
  2.3 0.0 copy-start.1
  2.3 18.2 %all-to-all-start = ((bf16[8,32,512]{2,1,0:T(8,128)(2,1)}), bf16[8,32,512]{2,1,0:T(8,128)(2,1)S(1)}, u32[]{:S(2)}, u32[]{:S(2)}) async-start(bf16[8,32,512]{2,1,0:T(8,128)(2,1)} %shard_map.102), calls=%async_computation | async-start | bytes 524288 | tf_op jit(solution)/shard_map/all_to_all | solution.py:312
  20.5 0.0 copy-done
  20.5 0.0 copy-done.1
  20.5 0.1 shard_map.103
  20.6 2.9 %collective-permute-start = (bf16[2,256,128]{2,1,0:T(8,128)(2,1)S(1)}, bf16[2,256,128]{2,1,0:T(8,128)(2,1)S(1)}, u32[]{:S(2)}, u32[]{:S(2)}) collective-permute-start(bf16[2,256,128]{2,1,0:T(8,128)(2,1)S(1)} %get-tuple-element.19), channel_id=1, source_target_pairs={{0,8},{8,0},{1,9},{9,1},{2,10},{10,2},{3,11},{11,3},{4,12},{12,4},... | collective-permute-start | bytes 393224 | tf_op jit(solution)/shard_map/ppermute | solution.py:292
  23.5 1.0 %collective-permute-done.near = bf16[2,256,128]{2,1,0:T(8,128)(2,1)S(1)} collective-permute-done((bf16[2,256,128]{2,1,0:T(8,128)(2,1)S(1)}, bf16[2,256,128]{2,1,0:T(8,128)(2,1)S(1)}, u32[]{:S(2)}, u32[]{:S(2)}) %collective-permute-start) | collective-permute-done | bytes 131104 | tf_op jit(solution)/shard_map/ppermute | solution.py:292
  24.5 0.0 copy-start.4
  24.5 3.3 %collective-permute-start.1 = (bf16[2,256,128]{2,1,0:T(8,128)(2,1)S(1)}, bf16[2,256,128]{2,1,0:T(8,128)(2,1)S(1)}, u32[]{:S(2)}, u32[]{:S(2)}) collective-permute-start(bf16[2,256,128]{2,1,0:T(8,128)(2,1)S(1)} %shard_map.104), channel_id=1, source_target_pairs={{0,16},{16,0},{1,17},{17,1},{2,18},{18,2},{3,19},{19,3},{4,20},{20... | collective-permute-start | bytes 393224 | tf_op jit(solution)/shard_map/ppermute | solution.py:292
  27.8 3.4 %collective-permute-done.1.far = bf16[2,256,128]{2,1,0:T(8,128)(2,1)S(1)} collective-permute-done((bf16[2,256,128]{2,1,0:T(8,128)(2,1)S(1)}, bf16[2,256,128]{2,1,0:T(8,128)(2,1)S(1)}, u32[]{:S(2)}, u32[]{:S(2)}) %collective-permute-start.1) | collective-permute-done | bytes 131104 | tf_op jit(solution)/shard_map/ppermute | solution.py:292
  31.3 0.0 copy-start.2
  31.3 0.0 copy-start.3
  31.3 5.0 %collective-permute-start.2 = (bf16[768,128]{1,0:T(8,128)(2,1)S(1)}, bf16[768,128]{1,0:T(8,128)(2,1)S(1)}, u32[]{:S(2)}, u32[]{:S(2)}) collective-permute-start(bf16[768,128]{1,0:T(8,128)(2,1)S(1)} %get-tuple-element.21), channel_id=1, source_target_pairs={{0,32},{32,64},{64,96},{96,128},{128,160},{160,192},{192,224},{224... | collective-permute-start | bytes 589832 | tf_op jit(solution)/shard_map/ppermute | solution.py:287
  36.2 0.0 all-to-all-done
  36.3 0.0 copy-done.4
  36.3 0.8 bitcast_bitcast_fusion
  37.1 5.1 %all-to-all-start.1 = ((bf16[4,256,128]{2,1,0:T(8,128)(2,1)}), bf16[4,256,128]{2,1,0:T(8,128)(2,1)S(1)}, u32[]{:S(2)}, u32[]{:S(2)}) async-start(bf16[4,256,128]{2,1,0:T(8,128)(2,1)} %bitcast_bitcast_fusion), calls=%async_computation.1 | async-start | bytes 524288 | tf_op jit(solution)/shard_map/all_to_all | solution.py:312
  42.1 0.0 collective-permute-done.2.halo
  42.1 0.0 copy-done.2
  42.2 0.0 copy-done.3
  42.2 3.3 %shard_map.106 = (bf16[1024,128]{1,0:T(8,128)(2,1)S(1)}, bf16[4,256,512]{2,1,0:T(8,128)(2,1)}, bf16[4,256,128]{2,1,0:T(8,128)(2,1)S(1)}) custom-call(s32[1]{0:T(128)} %bitcast.place, bf16[4,256,256]{2,1,0:T(8,128)(2,1)S(1)} %copy-done.2, bf16[4,256,256]{2,1,0:T(8,128)(2,1)S(1)} %copy-done.3, bf16[768,128]{1,0:T(8,128)(2,1)S(1)} %collective-permute-done.2.halo, ...), custom_call_target="tpu_custom_call" | custom-call | flops 24000000000 | tf_op jit(solution)/shard_map/pallas_call | solution.py:363
  45.5 1.9 %all-to-all-done.1 = bf16[4,256,128]{2,1,0:T(8,128)(2,1)S(1)} async-done(((bf16[4,256,128]{2,1,0:T(8,128)(2,1)}), bf16[4,256,128]{2,1,0:T(8,128)(2,1)S(1)}, u32[]{:S(2)}, u32[]{:S(2)}) %all-to-all-start.1) | async-done | bytes 262176 | tf_op jit(solution)/shard_map/all_to_all | solution.py:312
  47.3 3.3 %shard_map.107 = (bf16[768,128]{1,0:T(8,128)(2,1)S(1)}, bf16[192,4,128]{2,1,0:T(4,128)(2,1)}) custom-call(bf16[4,256,256]{2,1,0:T(8,128)(2,1)S(1)} %copy-done.2, bf16[4,256,256]{2,1,0:T(8,128)(2,1)S(1)} %copy-done.3, bf16[1024,128]{1,0:T(8,128)(2,1)S(1)} %bitcast.13, bf16[4,256,512]{2,1,0:T(8,128)(2,1)} %get-tuple-element.23.spectrum), custom_call_target="tpu_custom_call" | custom-call | tf_op jit(solution)/shard_map/pallas_call | solution.py:383
  50.6 1.3 %collective-permute-start.3 = (bf16[768,128]{1,0:T(8,128)(2,1)S(1)}, bf16[768,128]{1,0:T(8,128)(2,1)S(1)}, u32[]{:S(2)}, u32[]{:S(2)}) collective-permute-start(bf16[768,128]{1,0:T(8,128)(2,1)S(1)} %get-tuple-element.24), channel_id=1, source_target_pairs={{32,0},{64,32},{96,64},{128,96},{160,128},{192,160},{224,192},{256... | collective-permute-start | bytes 589832 | tf_op jit(solution)/shard_map/ppermute | solution.py:287
  51.9 18.8 %all-to-all-start.2 = ((bf16[192,4,128]{2,1,0:T(4,128)(2,1)}), bf16[192,4,128]{2,1,0:T(4,128)(2,1)S(1)}, u32[]{:S(2)}, u32[]{:S(2)}) async-start(bf16[192,4,128]{2,1,0:T(4,128)(2,1)} %get-tuple-element.31), calls=%async_computation.2 | async-start | bytes 393216 | tf_op jit(solution)/shard_map/all_to_all | solution.py:312
  70.8 0.0 collective-permute-done.3.halo
  70.8 2.9 %shard_map.108 = (bf16[512,128]{1,0:T(8,128)(2,1)S(1)}, bf16[512,128]{1,0:T(8,128)(2,1)S(1)}, bf16[512,128]{1,0:T(8,128)(2,1)S(1)}, bf16[512,128]{1,0:T(8,128)(2,1)S(1)}) custom-call(s32[1]{0:T(128)} %bitcast.place, bf16[4,256,256]{2,1,0:T(8,128)(2,1)S(1)} %copy-done.2, bf16[4,256,256]{2,1,0:T(8,128)(2,1)} %constant.17.clone.back, ...), custom_call_target="tpu_custom_call" | custom-call | flops 35000000512 | tf_op jit(solution)/shard_map/pallas_call | solution.py:399
  73.7 2.4 %collective-permute-start.4 = (bf16[512,128]{1,0:T(8,128)(2,1)S(1)}, bf16[512,128]{1,0:T(8,128)(2,1)S(1)}, u32[]{:S(2)}, u32[]{:S(2)}) collective-permute-start(bf16[512,128]{1,0:T(8,128)(2,1)S(1)} %get-tuple-element.28), channel_id=1, source_target_pairs={{0,8},{8,0},{16,24},{24,16},{1,9},{9,1},{17,25},{25,17},{2,10},{10... | collective-permute-start | bytes 393224 | tf_op jit(solution)/shard_map/ppermute | solution.py:306
  76.0 3.2 %collective-permute-start.5 = (bf16[512,128]{1,0:T(8,128)(2,1)S(1)}, bf16[512,128]{1,0:T(8,128)(2,1)S(1)}, u32[]{:S(2)}, u32[]{:S(2)}) collective-permute-start(bf16[512,128]{1,0:T(8,128)(2,1)S(1)} %get-tuple-element.29), channel_id=1, source_target_pairs={{0,16},{8,24},{16,0},{24,8},{1,17},{9,25},{17,1},{25,9},{2,18},{10... | collective-permute-start | bytes 393224 | tf_op jit(solution)/shard_map/ppermute | solution.py:306
  79.2 2.3 %collective-permute-start.6 = (bf16[512,128]{1,0:T(8,128)(2,1)S(1)}, bf16[512,128]{1,0:T(8,128)(2,1)S(1)}, u32[]{:S(2)}, u32[]{:S(2)}) collective-permute-start(bf16[512,128]{1,0:T(8,128)(2,1)S(1)} %get-tuple-element.30), channel_id=1, source_target_pairs={{0,24},{8,16},{16,8},{24,0},{1,25},{9,17},{17,9},{25,1},{2,26},{10... | collective-permute-start | bytes 393224 | tf_op jit(solution)/shard_map/ppermute | solution.py:306
  81.5 0.0 collective-permute-done.4.refs_1_
  81.6 2.0 %collective-permute-done.5.refs_2_ = bf16[512,128]{1,0:T(8,128)(2,1)S(1)} collective-permute-done((bf16[512,128]{1,0:T(8,128)(2,1)S(1)}, bf16[512,128]{1,0:T(8,128)(2,1)S(1)}, u32[]{:S(2)}, u32[]{:S(2)}) %collective-permute-start.5) | collective-permute-done | bytes 131104 | tf_op jit(solution)/shard_map/ppermute | solution.py:306
  83.6 3.6 %collective-permute-done.6.refs_3_ = bf16[512,128]{1,0:T(8,128)(2,1)S(1)} collective-permute-done((bf16[512,128]{1,0:T(8,128)(2,1)S(1)}, bf16[512,128]{1,0:T(8,128)(2,1)S(1)}, u32[]{:S(2)}, u32[]{:S(2)}) %collective-permute-start.6) | collective-permute-done | bytes 131104 | tf_op jit(solution)/shard_map/ppermute | solution.py:306
  87.2 0.9 %all-to-all-done.2.refs_7_ = bf16[192,4,128]{2,1,0:T(4,128)(2,1)S(1)} async-done(((bf16[192,4,128]{2,1,0:T(4,128)(2,1)}), bf16[192,4,128]{2,1,0:T(4,128)(2,1)S(1)}, u32[]{:S(2)}, u32[]{:S(2)}) %all-to-all-start.2) | async-done | bytes 196640 | tf_op jit(solution)/shard_map/all_to_all | solution.py:312
  88.1 1.1 %shard_map.109 = (bf16[256,512]{1,0:T(8,128)(2,1)}, bf16[256,512]{1,0:T(8,128)(2,1)}, bf16[256,512]{1,0:T(8,128)(2,1)}, f32[12,512]{1,0:T(8,128)}) custom-call(s32[1]{0:T(128)} %bitcast.place, bf16[512,128]{1,0:T(8,128)(2,1)S(1)} %get-tuple-element.27.refs_0_, bf16[512,128]{1,0:T(8,128)(2,1)S(1)} %collective-permute-done.4.refs_1_, ...), custom_call_target="tpu_custom_call" | custom-call | tf_op jit(solution)/shard_map/pallas_call | solution.py:415
  (2 shorter events, 0.0 us)
Async XLA Ops:
  2.3 18.2 %copy-start = (bf16[256,512]{1,0:T(8,128)(2,1)S(1)}, bf16[256,512]{1,0:T(8,128)(2,1)}, u32[]{:S(2)}) copy-start(bf16[256,512]{1,0:T(8,128)(2,1)} %refs_5_.1) | copy-start | bytes 786436
  2.3 18.2 %copy-start.1 = (bf16[256,512]{1,0:T(8,128)(2,1)S(1)}, bf16[256,512]{1,0:T(8,128)(2,1)}, u32[]{:S(2)}) copy-start(bf16[256,512]{1,0:T(8,128)(2,1)} %refs_6_.1) | copy-start | bytes 786436
  2.3 34.0 %all-to-all-start = ((bf16[8,32,512]{2,1,0:T(8,128)(2,1)}), bf16[8,32,512]{2,1,0:T(8,128)(2,1)S(1)}, u32[]{:S(2)}, u32[]{:S(2)}) async-start(bf16[8,32,512]{2,1,0:T(8,128)(2,1)} %shard_map.102), calls=%async_computation | async-start | bytes 524288 | tf_op jit(solution)/shard_map/all_to_all | solution.py:312
  20.6 3.8 %collective-permute-start = (bf16[2,256,128]{2,1,0:T(8,128)(2,1)S(1)}, bf16[2,256,128]{2,1,0:T(8,128)(2,1)S(1)}, u32[]{:S(2)}, u32[]{:S(2)}) collective-permute-start(bf16[2,256,128]{2,1,0:T(8,128)(2,1)S(1)} %get-tuple-element.19), channel_id=1, source_target_pairs={{0,8},{8,0},{1,9},{9,1},{2,10},{10,2},{3,11},{11,3},{4,12},{12,4},... | collective-permute-start | bytes 393224 | tf_op jit(solution)/shard_map/ppermute | solution.py:292
  24.5 11.8 %copy-start.4 = (bf16[256,512]{1,0:T(8,128)(2,1)S(1)}, bf16[256,512]{1,0:T(8,128)(2,1)}, u32[]{:S(2)}) copy-start(bf16[256,512]{1,0:T(8,128)(2,1)} %param.7) | copy-start | bytes 786436
  24.5 6.7 %collective-permute-start.1 = (bf16[2,256,128]{2,1,0:T(8,128)(2,1)S(1)}, bf16[2,256,128]{2,1,0:T(8,128)(2,1)S(1)}, u32[]{:S(2)}, u32[]{:S(2)}) collective-permute-start(bf16[2,256,128]{2,1,0:T(8,128)(2,1)S(1)} %shard_map.104), channel_id=1, source_target_pairs={{0,16},{16,0},{1,17},{17,1},{2,18},{18,2},{3,19},{19,3},{4,20},{20... | collective-permute-start | bytes 393224 | tf_op jit(solution)/shard_map/ppermute | solution.py:292
  31.3 10.9 %copy-start.2 = (bf16[4,256,256]{2,1,0:T(8,128)(2,1)S(1)}, bf16[4,256,256]{2,1,0:T(8,128)(2,1)}, u32[]{:S(2)}) copy-start(bf16[4,256,256]{2,1,0:T(8,128)(2,1)} %constant.16.clone.table) | copy-start | bytes 1572868
  31.3 10.9 %copy-start.3 = (bf16[4,256,256]{2,1,0:T(8,128)(2,1)S(1)}, bf16[4,256,256]{2,1,0:T(8,128)(2,1)}, u32[]{:S(2)}) copy-start(bf16[4,256,256]{2,1,0:T(8,128)(2,1)} %constant.17.clone.back) | copy-start | bytes 1572868
  31.3 10.9 %collective-permute-start.2 = (bf16[768,128]{1,0:T(8,128)(2,1)S(1)}, bf16[768,128]{1,0:T(8,128)(2,1)S(1)}, u32[]{:S(2)}, u32[]{:S(2)}) collective-permute-start(bf16[768,128]{1,0:T(8,128)(2,1)S(1)} %get-tuple-element.21), channel_id=1, source_target_pairs={{0,32},{32,64},{64,96},{96,128},{128,160},{160,192},{192,224},{224... | collective-permute-start | bytes 589832 | tf_op jit(solution)/shard_map/ppermute | solution.py:287
  37.1 10.3 %all-to-all-start.1 = ((bf16[4,256,128]{2,1,0:T(8,128)(2,1)}), bf16[4,256,128]{2,1,0:T(8,128)(2,1)S(1)}, u32[]{:S(2)}, u32[]{:S(2)}) async-start(bf16[4,256,128]{2,1,0:T(8,128)(2,1)} %bitcast_bitcast_fusion), calls=%async_computation.1 | async-start | bytes 524288 | tf_op jit(solution)/shard_map/all_to_all | solution.py:312
  50.6 20.1 %collective-permute-start.3 = (bf16[768,128]{1,0:T(8,128)(2,1)S(1)}, bf16[768,128]{1,0:T(8,128)(2,1)S(1)}, u32[]{:S(2)}, u32[]{:S(2)}) collective-permute-start(bf16[768,128]{1,0:T(8,128)(2,1)S(1)} %get-tuple-element.24), channel_id=1, source_target_pairs={{32,0},{64,32},{96,64},{128,96},{160,128},{192,160},{224,192},{256... | collective-permute-start | bytes 589832 | tf_op jit(solution)/shard_map/ppermute | solution.py:287
  51.9 36.1 %all-to-all-start.2 = ((bf16[192,4,128]{2,1,0:T(4,128)(2,1)}), bf16[192,4,128]{2,1,0:T(4,128)(2,1)S(1)}, u32[]{:S(2)}, u32[]{:S(2)}) async-start(bf16[192,4,128]{2,1,0:T(4,128)(2,1)} %get-tuple-element.31), calls=%async_computation.2 | async-start | bytes 393216 | tf_op jit(solution)/shard_map/all_to_all | solution.py:312
  73.7 7.9 %collective-permute-start.4 = (bf16[512,128]{1,0:T(8,128)(2,1)S(1)}, bf16[512,128]{1,0:T(8,128)(2,1)S(1)}, u32[]{:S(2)}, u32[]{:S(2)}) collective-permute-start(bf16[512,128]{1,0:T(8,128)(2,1)S(1)} %get-tuple-element.28), channel_id=1, source_target_pairs={{0,8},{8,0},{16,24},{24,16},{1,9},{9,1},{17,25},{25,17},{2,10},{10... | collective-permute-start | bytes 393224 | tf_op jit(solution)/shard_map/ppermute | solution.py:306
  76.0 7.5 %collective-permute-start.5 = (bf16[512,128]{1,0:T(8,128)(2,1)S(1)}, bf16[512,128]{1,0:T(8,128)(2,1)S(1)}, u32[]{:S(2)}, u32[]{:S(2)}) collective-permute-start(bf16[512,128]{1,0:T(8,128)(2,1)S(1)} %get-tuple-element.29), channel_id=1, source_target_pairs={{0,16},{8,24},{16,0},{24,8},{1,17},{9,25},{17,1},{25,9},{2,18},{10... | collective-permute-start | bytes 393224 | tf_op jit(solution)/shard_map/ppermute | solution.py:306
  79.2 7.9 %collective-permute-start.6 = (bf16[512,128]{1,0:T(8,128)(2,1)S(1)}, bf16[512,128]{1,0:T(8,128)(2,1)S(1)}, u32[]{:S(2)}, u32[]{:S(2)}) collective-permute-start(bf16[512,128]{1,0:T(8,128)(2,1)S(1)} %get-tuple-element.30), channel_id=1, source_target_pairs={{0,24},{8,16},{16,8},{24,0},{1,25},{9,17},{17,9},{25,1},{2,26},{10... | collective-permute-start | bytes 393224 | tf_op jit(solution)/shard_map/ppermute | solution.py:306
